TPU v7x, 32 devices: a whole 2x2x4 slice. The times are simulated.
32 devices in a mesh: dp: 16 (over z, x, core), tensor: 2 (over y).
Axes of the slice: x: 2, y: 2, z: 4, core: 2. Of those that a mesh axis runs over, the one named last changes fastest.
Arguments:
- tokens: bfloat16 [8192, 2048], P('dp'), may hold values from -6 to 6
- seq_lengths: int32 [16, 4], P('dp'), may hold values from 0 to 512, as said below
- first_gain: bfloat16 [2048], replicated, may hold values from 0.099609375 to 1.8984375
- query_weight: bfloat16 [2048, 2048], P('dp', 'tensor'), may hold values from -0.125 to 0.125
- key_matrix: bfloat16 [2048, 1024], P('dp', 'tensor'), may hold values from -0.125 to 0.125
- value_matrix: bfloat16 [2048, 1024], P('dp', 'tensor'), may hold values from -0.125 to 0.125
- query_norm_gain: bfloat16 [128], replicated, may hold values from 0.099609375 to 1.8984375
- key_gain: bfloat16 [128], replicated, may hold values from 0.099609375 to 1.8984375
- output_weight: bfloat16 [2048, 2048], P('tensor', 'dp'), may hold values from -1 to 1
- second_gain: bfloat16 [2048], replicated, may hold values from 0.099609375 to 1.8984375
- gate_weight: bfloat16 [2048, 6144], P('dp', 'tensor'), may hold values from -0.125 to 0.125
- up_weight: bfloat16 [2048, 6144], P('dp', 'tensor'), may hold values from -0.125 to 0.125
- down_weight: bfloat16 [6144, 2048], P('tensor', 'dp'), may hold values from -0.078125 to 0.078125
- cotangent: bfloat16 [8192, 2048], P('dp'), may hold values from -6 to 6
Outputs:
- block_output: bfloat16 [8192, 2048], P('dp')
- token_grad: float32 [8192, 2048], P('dp')
- first_gain_grad: float32 [2048], P('dp')
- query_weight_grad: float32 [2048, 2048], P('dp', 'tensor')
- key_weight_grad: float32 [2048, 1024], P('dp', 'tensor')
- value_weight_grad: float32 [2048, 1024], P('dp', 'tensor')
- query_gain_grad: float32 [128], P('dp')
- key_gain_grad: float32 [128], P('dp')
- output_weight_grad: float32 [2048, 2048], P('tensor', 'dp')
- second_gain_grad: float32 [2048], P('dp')
- gate_weight_grad: float32 [2048, 6144], P('dp', 'tensor')
- up_weight_grad: float32 [2048, 6144], P('dp', 'tensor')
- down_weight_grad: float32 [6144, 2048], P('tensor', 'dp')
Inputs may be any that keep to these rules, and one draw needn't show every extreme that they name: `seq_lengths`: row g lists the lengths of the sequences of data group g in slot order; a zero is an empty slot. Padded to multiples of 64, the sequences of a group fit in 512 rows. In every draw some group holds a single sequence of 512 tokens.
All inputs are finite; a program needn't handle non-finite values.
Results may differ from a plain program's by a relative error of at most 0.014.
Values may be sent and summed in bfloat16 or wider, within the bound.
No kernel may reach another device: no remote copies, remote signals or barrier semaphores. Data moves between devices by JAX's collectives and lax.ppermute only.
A program may use at most 256 MiB of HBM per device.

v0:
```python
import jax
import jax.numpy as jnp
from jax import lax
from jax.sharding import PartitionSpec as P

HEAD_SIZE = 128
BLK = 64


epsilon = 1e-06
rope_base = 1000000.0


def matrix_product(left, right):
    return jnp.dot(left, right, preferred_element_type=jnp.float32)


def inner_left(left, right):
    return lax.dot_general(
        left, right, (((0,), (0,)), ((), ())), preferred_element_type=jnp.float32
    )


def inner_right(left, right):
    return lax.dot_general(
        left, right, (((1,), (1,)), ((), ())), preferred_element_type=jnp.float32
    )


def rownorm_apply(inputs, gain_vector):
    return (
        inputs
        * lax.rsqrt(jnp.mean(inputs * inputs, axis=-1, keepdims=True) + epsilon)
        * gain_vector
    )


def layout(lengths, count_of_rows):
    padded = (lengths + BLK - 1) // BLK * BLK
    starts = jnp.cumsum(padded) - padded
    row_index = jnp.arange(count_of_rows, dtype=jnp.int32)
    inside = (row_index[:, None] >= starts[None, :]) & (
        row_index[:, None] < (starts + lengths)[None, :]
    )
    live_rows = jnp.any(inside, axis=1)
    slot_index = jnp.arange(lengths.shape[0], dtype=jnp.int32)
    owning = jnp.sum(jnp.where(inside, slot_index[None, :], 0), axis=1)
    position = jnp.sum(jnp.where(inside, row_index[:, None] - starts[None, :], 0), axis=1)
    segment = jnp.where(live_rows, owning, -1 - row_index)
    return (live_rows, segment, position)


def rotation(position, width):
    half_width = width // 2
    frequency = jnp.power(rope_base, -(jnp.arange(half_width, dtype=jnp.float32) * 2.0) / width)
    angles = position.astype(jnp.float32)[:, None] * frequency[None, :]
    return (jnp.cos(angles)[:, None, :], jnp.sin(angles)[:, None, :])


def rotary_apply(inputs, cosine_table, sinusoid_table):
    half_width = inputs.shape[-1] // 2
    leading = inputs[..., :half_width]
    trailing = inputs[..., half_width:]
    return jnp.concatenate(
        [
            leading * cosine_table - trailing * sinusoid_table,
            trailing * cosine_table + leading * sinusoid_table,
        ],
        axis=-1,
    )


def score_block(query_rows, key_tile_rows, segment):
    count_of_rows = query_rows.shape[0]
    scaling = query_rows.shape[-1] ** (-0.5)
    scores = (
        jnp.einsum("qhgd,khd->hgqk", query_rows, key_tile_rows, preferred_element_type=jnp.float32)
        * scaling
    )
    row_index = jnp.arange(count_of_rows, dtype=jnp.int32)
    allowed = (segment[:, None] == segment[None, :]) & (row_index[None, :] <= row_index[:, None])
    return jnp.where(allowed, scores, -1e30)


def attend(query_rows, key_tile_rows, value_tile_rows, segment):
    scores = score_block(query_rows, key_tile_rows, segment)
    largest = jnp.max(scores, axis=-1, keepdims=True)
    raised = jnp.exp(scores - largest)
    totals = jnp.sum(raised, axis=-1, keepdims=True)
    weights = raised / totals
    log_total = largest + jnp.log(totals)
    mixture = jnp.einsum(
        "hgqk,khd->qhgd",
        weights.astype(jnp.bfloat16),
        value_tile_rows,
        preferred_element_type=jnp.float32,
    )
    return (mixture, log_total)


def attend_back(query_rows, key_tile_rows, value_tile_rows, segment, log_total, back_mixture):
    scaling = query_rows.shape[-1] ** (-0.5)
    weights = jnp.exp(score_block(query_rows, key_tile_rows, segment) - log_total)
    back_weights = jnp.einsum(
        "qhgd,khd->hgqk", back_mixture, value_tile_rows, preferred_element_type=jnp.float32
    )
    back_values = jnp.einsum(
        "hgqk,qhgd->khd",
        weights.astype(jnp.bfloat16),
        back_mixture,
        preferred_element_type=jnp.float32,
    )
    center = jnp.sum(back_weights * weights, axis=-1, keepdims=True)
    back_scores = (weights * (back_weights - center)).astype(jnp.bfloat16)
    back_queries = (
        jnp.einsum("hgqk,khd->qhgd", back_scores, key_tile_rows, preferred_element_type=jnp.float32)
        * scaling
    )
    back_keys = (
        jnp.einsum("hgqk,qhgd->khd", back_scores, query_rows, preferred_element_type=jnp.float32)
        * scaling
    )
    return (back_queries, back_keys, back_values)


def shards(
    tokens,
    seq_lengths,
    first_gain,
    query_weight,
    key_matrix,
    value_matrix,
    query_norm_gain,
    key_gain,
    output_weight,
    second_gain,
    gate_weight,
    up_weight,
    down_weight,
    cotangent,
):
    count_of_rows = tokens.shape[0]
    head_count = query_weight.shape[1] // HEAD_SIZE
    key_heads = key_matrix.shape[1] // HEAD_SIZE
    heads_per_group = head_count // key_heads
    live_rows, segment, position = layout(seq_lengths[0], count_of_rows)
    cosine_table, sinusoid_table = rotation(position, HEAD_SIZE)
    residual = tokens.astype(jnp.float32)
    normed_one, pull_first = jax.vjp(rownorm_apply, residual, first_gain.astype(jnp.float32))
    input_one = normed_one.astype(jnp.bfloat16)
    query_full, key_full, value_full = (
        lax.all_gather(query_weight, "dp", axis=0, tiled=True),
        lax.all_gather(key_matrix, "dp", axis=0, tiled=True),
        lax.all_gather(value_matrix, "dp", axis=0, tiled=True),
    )
    query_raw = matrix_product(input_one, query_full)
    key_raw = matrix_product(input_one, key_full)
    value_raw = matrix_product(input_one, value_full)

    def positional(query_part, key_part, query_scale, key_scale):
        query_heads = rotary_apply(
            rownorm_apply(query_part.reshape(count_of_rows, head_count, HEAD_SIZE), query_scale),
            cosine_table,
            sinusoid_table,
        )
        key_rotated = rotary_apply(
            rownorm_apply(key_part.reshape(count_of_rows, key_heads, HEAD_SIZE), key_scale),
            cosine_table,
            sinusoid_table,
        )
        return (
            query_heads.reshape(count_of_rows, key_heads, heads_per_group, HEAD_SIZE),
            key_rotated,
        )

    (query_rot, key_rot), pull_rotary = jax.vjp(
        positional,
        query_raw,
        key_raw,
        query_norm_gain.astype(jnp.float32),
        key_gain.astype(jnp.float32),
    )
    query_low = query_rot.astype(jnp.bfloat16)
    key_low = key_rot.astype(jnp.bfloat16)
    value_low = value_raw.astype(jnp.bfloat16).reshape(count_of_rows, key_heads, HEAD_SIZE)
    mixture, log_total = attend(query_low, key_low, value_low, segment)
    mixture_low = mixture.reshape(count_of_rows, head_count * HEAD_SIZE).astype(jnp.bfloat16)
    output_full = lax.all_gather(output_weight, "dp", axis=1, tiled=True)
    branch = lax.psum(matrix_product(mixture_low, output_full), "tensor")
    middle = residual + branch
    normed_two, pull_second = jax.vjp(rownorm_apply, middle, second_gain.astype(jnp.float32))
    input_two = normed_two.astype(jnp.bfloat16)
    gate_full, up_full = (
        lax.all_gather(gate_weight, "dp", axis=0, tiled=True),
        lax.all_gather(up_weight, "dp", axis=0, tiled=True),
    )
    gate_value = matrix_product(input_two, gate_full)
    up_value = matrix_product(input_two, up_full)
    active, pull_swiglu = jax.vjp(
        lambda gate_part, up_part: jax.nn.silu(gate_part) * up_part, gate_value, up_value
    )
    hidden = active.astype(jnp.bfloat16)
    down_full = lax.all_gather(down_weight, "dp", axis=1, tiled=True)
    ffn_branch = lax.psum(matrix_product(hidden, down_full).astype(jnp.bfloat16), "tensor").astype(
        jnp.float32
    )
    block_output = (middle + ffn_branch).astype(jnp.bfloat16)
    upstream = cotangent.astype(jnp.float32) * live_rows[:, None].astype(jnp.float32)
    upstream_low = upstream.astype(jnp.bfloat16)
    grad_down = inner_left(hidden, upstream_low)
    grad_hidden = inner_right(upstream_low, down_full)
    grad_gate_value, grad_up_value = pull_swiglu(grad_hidden)
    gate_low = grad_gate_value.astype(jnp.bfloat16)
    up_low = grad_up_value.astype(jnp.bfloat16)
    grad_gate = inner_left(input_two, gate_low)
    grad_up = inner_left(input_two, up_low)
    back_two = lax.psum(inner_right(gate_low, gate_full) + inner_right(up_low, up_full), "tensor")
    back_middle, grad_second = pull_second(back_two)
    back_middle = back_middle + upstream
    branch_low = back_middle.astype(jnp.bfloat16)
    grad_output = inner_left(mixture_low, branch_low)
    back_mixture = (
        inner_right(branch_low, output_full)
        .astype(jnp.bfloat16)
        .reshape(count_of_rows, key_heads, heads_per_group, HEAD_SIZE)
    )
    back_queries, back_keys, back_values = attend_back(
        query_low, key_low, value_low, segment, log_total, back_mixture
    )
    value_grad_low = back_values.reshape(count_of_rows, key_heads * HEAD_SIZE).astype(jnp.bfloat16)
    back_query_raw, back_key_raw, grad_qgain, grad_kgain = pull_rotary((back_queries, back_keys))
    query_grad_low = back_query_raw.astype(jnp.bfloat16)
    key_grad_low = back_key_raw.astype(jnp.bfloat16)
    grad_query = inner_left(input_one, query_grad_low)
    grad_key = inner_left(input_one, key_grad_low)
    grad_value = inner_left(input_one, value_grad_low)
    partial_one = (
        inner_right(query_grad_low, query_full)
        + inner_right(key_grad_low, key_full)
        + inner_right(value_grad_low, value_full)
    )
    back_one, grad_qgain, grad_kgain = lax.psum((partial_one, grad_qgain, grad_kgain), "tensor")
    back_tokens, grad_first = pull_first(back_one)
    token_grad = back_middle + back_tokens
    (
        grad_query,
        grad_key,
        grad_value,
        grad_gate,
        grad_up,
        grad_first,
        grad_second,
        grad_qgain,
        grad_kgain,
    ) = (
        lax.psum_scatter(grad_query, "dp", scatter_dimension=0, tiled=True),
        lax.psum_scatter(grad_key, "dp", scatter_dimension=0, tiled=True),
        lax.psum_scatter(grad_value, "dp", scatter_dimension=0, tiled=True),
        lax.psum_scatter(grad_gate, "dp", scatter_dimension=0, tiled=True),
        lax.psum_scatter(grad_up, "dp", scatter_dimension=0, tiled=True),
        lax.psum_scatter(grad_first, "dp", scatter_dimension=0, tiled=True),
        lax.psum_scatter(grad_second, "dp", scatter_dimension=0, tiled=True),
        lax.psum_scatter(grad_qgain, "dp", scatter_dimension=0, tiled=True),
        lax.psum_scatter(grad_kgain, "dp", scatter_dimension=0, tiled=True),
    )
    grad_output, grad_down = (
        lax.psum_scatter(grad_output, "dp", scatter_dimension=1, tiled=True),
        lax.psum_scatter(grad_down, "dp", scatter_dimension=1, tiled=True),
    )
    return (
        block_output,
        token_grad,
        grad_first,
        grad_query,
        grad_key,
        grad_value,
        grad_qgain,
        grad_kgain,
        grad_output,
        grad_second,
        grad_gate,
        grad_up,
        grad_down,
    )


def solution(mesh):
    return jax.shard_map(
        shards,
        mesh=mesh,
        in_specs=(
            P("dp", None),
            P("dp", None),
            P(),
            P("dp", "tensor"),
            P("dp", "tensor"),
            P("dp", "tensor"),
            P(),
            P(),
            P("tensor", "dp"),
            P(),
            P("dp", "tensor"),
            P("dp", "tensor"),
            P("tensor", "dp"),
            P("dp", None),
        ),
        out_specs=(
            P("dp", None),
            P("dp", None),
            P("dp"),
            P("dp", "tensor"),
            P("dp", "tensor"),
            P("dp", "tensor"),
            P("dp"),
            P("dp"),
            P("tensor", "dp"),
            P("dp"),
            P("dp", "tensor"),
            P("dp", "tensor"),
            P("tensor", "dp"),
        ),
        check_vma=False,
    )
```

profile of v0, /device:TPU:0, one launch (start us, length us, event | category | flops | bytes accessed | tf_op | source)
XLA Modules:
  0.0 2129.3 jit_solution(18359063889235030145)
XLA Ops:
  13.8 2.1 fusion.17
  17.3 1.7 multiply_cosine_fusion
  19.1 35.3 %all-gather.10.cloned.1.call-done = bf16[2048,512]{1,0:T(8,128)(2,1)} async-done(((bf16[128,512]{1,0:T(8,128)(2,1)}), bf16[2048,512]{1,0:T(8,128)(2,1)}) %all-gather.10.cloned.1.call-update) | async-done | bytes 2097168 | tf_op jit(solution)/shard_map/all_gather | solution.py:153
  54.4 4.6 multiply_reduce_fusion.8
  58.9 1.7 copy.113
  61.9 2.4 subtract_convert_fusion.1
  64.3 32.4 %all-gather.8.cloned.1.call-done = bf16[2048,512]{1,0:T(8,128)(2,1)} async-done(((bf16[128,512]{1,0:T(8,128)(2,1)}), bf16[2048,512]{1,0:T(8,128)(2,1)}) %all-gather.8.cloned.1.call-update) | async-done | bytes 2097168 | tf_op jit(solution)/shard_map/all_gather | solution.py:154
  96.7 3.8 convolution_convert_fusion.2
  100.5 47.8 %all-gather.12.cloned.1.call-done = bf16[2048,1024]{1,0:T(8,128)(2,1)} async-done(((bf16[128,1024]{1,0:T(8,128)(2,1)}), bf16[2048,1024]{1,0:T(8,128)(2,1)}) %all-gather.12.cloned.1.call-update) | async-done | bytes 4194320 | tf_op jit(solution)/shard_map/all_gather | solution.py:152
  148.3 4.6 convolution_bitcast_fusion
  155.6 2.1 multiply_multiply_fusion
  159.9 2.3 fusion.66
  163.4 2.0 copy-done
  165.4 1.7 fusion.23
  167.2 34.9 %all-gather.14.cloned.1.call-done = bf16[1024,2048]{1,0:T(8,128)(2,1)} async-done(((bf16[1024,128]{1,0:T(8,128)(2,1)}), bf16[1024,2048]{1,0:T(8,128)(2,1)}) %all-gather.14.cloned.1.call-update) | async-done | bytes 4194320 | tf_op jit(solution)/shard_map/all_gather | solution.py:188
  202.0 6.6 fusion.67
  210.8 104.0 %all-reduce.15.cloned.1.call-done = f32[512,2048]{1,0:T(8,128)} async-done(((f32[512,2048]{1,0:T(8,128)}), f32[512,2048]{1,0:T(8,128)}) %all-reduce.15.cloned.1.call-update) | async-done | bytes 4194320 | tf_op jit(solution)/shard_map/psum | solution.py:189
  314.8 2.8 multiply_reduce_fusion.2
  317.6 2.0 copy-done.5
  320.1 97.9 %all-gather.18.cloned.1.call-done = bf16[2048,3072]{1,0:T(8,128)(2,1)} async-done(((bf16[128,3072]{1,0:T(8,128)(2,1)}), bf16[2048,3072]{1,0:T(8,128)(2,1)}) %all-gather.18.cloned.1.call-update) | async-done | bytes 12582928 | tf_op jit(solution)/shard_map/all_gather | solution.py:195
  418.0 11.3 fusion.69
  429.3 90.2 %all-gather.16.cloned.1.call-done = bf16[2048,3072]{1,0:T(8,128)(2,1)} async-done(((bf16[128,3072]{1,0:T(8,128)(2,1)}), bf16[2048,3072]{1,0:T(8,128)(2,1)}) %all-gather.16.cloned.1.call-update) | async-done | bytes 12582928 | tf_op jit(solution)/shard_map/all_gather | solution.py:194
  519.5 11.9 fusion.68
  531.4 92.6 %all-gather.20.cloned.1.call-done = bf16[3072,2048]{1,0:T(8,128)(2,1)} async-done(((bf16[3072,128]{1,0:T(8,128)(2,1)}), bf16[3072,2048]{1,0:T(8,128)(2,1)}) %all-gather.20.cloned.1.call-update) | async-done | bytes 12582928 | tf_op jit(solution)/shard_map/all_gather | solution.py:203
  624.0 22.6 %multiply_convert_fusion = (bf16[512,3072]{1,0:T(8,128)(2,1)}, bf16[512,3072]{1,0:T(8,128)(2,1)}, bf16[512,3072]{1,0:T(8,128)(2,1)}) fusion(f32[512,3072]{1,0:T(8,128)} %fusion.68, f32[512,3072]{1,0:T(8,128)} %fusion.69, bf16[3072,2048]{1,0:T(8,128)(2,1)} %all-gather.20.cloned.1.call-done, bf16[512,2048]{1,0:T(8,128)(2,1)S(1)} %copy-done.29, ...), kind=kOutput, calls=%fused_computation.22 | convolution fusion | flops 6470762496 | bytes 36702208 | tf_op jit(solution)/shard_map/dot_general | solution.py:25
  646.6 12.1 fusion.70
  658.8 11.9 convolution_add_fusion
  670.7 11.6 convolution_convert_fusion
  682.4 94.4 %all-reduce.19.cloned.1.call-done = f32[512,2048]{1,0:T(8,128)} async-done(((f32[512,2048]{1,0:T(8,128)}), f32[512,2048]{1,0:T(8,128)}) %all-reduce.19.cloned.1.call-update) | async-done | bytes 4194320 | tf_op jit(solution)/shard_map/psum | solution.py:217
  776.9 4.5 multiply_reduce_fusion
  781.4 61.2 %all-reduce.17.cloned.1.call-done = bf16[512,2048]{1,0:T(8,128)(2,1)} async-done(((bf16[512,2048]{1,0:T(8,128)(2,1)}), bf16[512,2048]{1,0:T(8,128)(2,1)}) %all-reduce.17.cloned.1.call-update) | async-done | bytes 2097168 | tf_op jit(solution)/shard_map/psum | solution.py:204
  842.6 6.3 fusion.13
  848.9 2.0 copy-done.6
  850.9 2.4 convolution_convert_fusion.1
  853.9 5.9 fusion.29
  859.8 5.4 fusion
  865.2 2.5 fusion.2
  871.5 3.3 copy.152
  876.2 1.8 fusion.32
  879.3 2.0 copy.153
  881.3 2.8 multiply_add_fusion.1
  884.2 2.3 multiply_reduce_fusion.3
  886.8 4.1 fusion.22
  893.5 2.4 fusion.35
  895.9 3.4 add_add_fusion.2
  899.4 1.5 copy-done.2
  900.9 3.6 fusion.56
  904.5 3.4 fusion.58
  909.2 7.8 fusion.37
  918.2 5.8 fusion.33
  924.1 14.3 fusion.43
  938.4 13.9 fusion.73
  952.7 14.5 fusion.72
  969.1 38.3 %all-reduce.21.cloned.1.call-done = f32[512,2048]{1,0:T(8,128)} async-done(((f32[512,2048]{1,0:T(8,128)}), f32[512,2048]{1,0:T(8,128)}) %all-reduce.21.cloned.1.call-update) | async-done | bytes 4194320 | tf_op jit(solution)/shard_map/psum | solution.py:242
  1007.4 3.5 fusion.12
  1010.9 62.4 %all-reduce.8 = (f32[2048]{0:T(1024)S(1)}, f32[128]{0:T(128)S(1)}, f32[128]{0:T(128)S(1)}, f32[2048]{0:T(1024)S(1)}) all-reduce(f32[2048]{0:T(1024)S(1)} %get-tuple-element.15, f32[128]{0:T(128)S(1)} %get-tuple-element.17, f32[128]{0:T(128)S(1)} %get-tuple-element.19, ...), channel_id=2, replica_groups=mesh['dp'=16,'tensor'=2] {'dp'}, use_global_device_ids=true, to_apply=%region_20.21.clone | all-reduce | flops 4352 | bytes 34816
  1074.1 5.4 all-reduce.9
  1080.7 6.5 fusion.14
  1087.3 74.3 %reduce-scatter.10.cloned.1.call-done = f32[128,512]{1,0:T(8,128)} async-done(((f32[2048,512]{1,0:T(8,128)}), f32[128,512]{1,0:T(8,128)}) %reduce-scatter.10.cloned.1.call-update) | async-done | bytes 262160 | tf_op jit(solution)/shard_map/reduce_scatter | solution.py:257
  1161.6 108.4 %reduce-scatter.14.cloned.1.call-done = f32[1024,128]{1,0:T(8,128)} async-done(((f32[1024,2048]{1,0:T(8,128)}), f32[1024,128]{1,0:T(8,128)}) %reduce-scatter.14.cloned.1.call-update) | async-done | bytes 524304 | tf_op jit(solution)/shard_map/reduce_scatter | solution.py:267
  1269.9 109.0 %reduce-scatter.8.cloned.1.call-done = f32[128,1024]{1,0:T(8,128)} async-done(((f32[2048,1024]{1,0:T(8,128)}), f32[128,1024]{1,0:T(8,128)}) %reduce-scatter.8.cloned.1.call-update) | async-done | bytes 524304 | tf_op jit(solution)/shard_map/reduce_scatter | solution.py:256
  1378.9 248.1 %reduce-scatter.20.cloned.1.call-done = f32[3072,128]{1,0:T(8,128)} async-done(((f32[3072,2048]{1,0:T(8,128)}), f32[3072,128]{1,0:T(8,128)}) %reduce-scatter.20.cloned.1.call-update) | async-done | bytes 1572880 | tf_op jit(solution)/shard_map/reduce_scatter | solution.py:268
  1626.9 247.5 %reduce-scatter.18.cloned.1.call-done = f32[128,3072]{1,0:T(8,128)} async-done(((f32[2048,3072]{1,0:T(8,128)}), f32[128,3072]{1,0:T(8,128)}) %reduce-scatter.18.cloned.1.call-update) | async-done | bytes 1572880 | tf_op jit(solution)/shard_map/reduce_scatter | solution.py:260
  1874.5 247.5 %reduce-scatter.16.cloned.1.call-done = f32[128,3072]{1,0:T(8,128)} async-done(((f32[2048,3072]{1,0:T(8,128)}), f32[128,3072]{1,0:T(8,128)}) %reduce-scatter.16.cloned.1.call-update) | async-done | bytes 1572880 | tf_op jit(solution)/shard_map/reduce_scatter | solution.py:259
  (200 shorter events, 33.2 us)
Async XLA Ops:
  7.2 47.2 %all-gather.10.cloned.1.call-start = ((), (), s32[]{:S(2)}) async-start(), calls=%async_computation.8 | async-start | bytes 2228224 | tf_op jit(solution)/shard_map/all_gather | solution.py:153
  7.9 88.8 %all-gather.8.cloned.1.call-start = ((), (), s32[]{:S(2)}) async-start(), calls=%async_computation.7 | async-start | bytes 2228224 | tf_op jit(solution)/shard_map/all_gather | solution.py:154
  8.7 139.6 %all-gather.12.cloned.1.call-start = ((), (), s32[]{:S(2)}) async-start(), calls=%async_computation.9 | async-start | bytes 4456448 | tf_op jit(solution)/shard_map/all_gather | solution.py:152
  9.4 192.6 %all-gather.14.cloned.1.call-start = ((), (), s32[]{:S(2)}) async-start(), calls=%async_computation.10 | async-start | bytes 4456448 | tf_op jit(solution)/shard_map/all_gather | solution.py:188
  10.0 304.8 %all-reduce.15.cloned.1.call-start = ((), (), s32[]{:S(2)}) async-start(), calls=%async_computation.11 | async-start | bytes 8388608 | tf_op jit(solution)/shard_map/psum | solution.py:189
  10.7 144.9 %copy-start.49 = (f32[128]{0:T(128)}, f32[128]{0:T(128)S(1)}, u32[]{:S(2)}) copy-start(f32[128]{0:T(128)S(1)} %convert_element_type.119) | copy-start | bytes 1540
  11.3 49.3 %copy-start.51 = (f32[128]{0:T(128)}, f32[128]{0:T(128)S(1)}, u32[]{:S(2)}) copy-start(f32[128]{0:T(128)S(1)} %convert_element_type.117) | copy-start | bytes 1540
  13.6 134.6 %copy-start.35 = (f32[2048]{0:T(1024)}, f32[2048]{0:T(1024)S(1)}, u32[]{:S(2)}) copy-start(f32[2048]{0:T(1024)S(1)} %convert_element_type.114) | copy-start | bytes 24580
  16.4 131.8 %copy-start.43 = (f32[512]{0:T(512)}, f32[512]{0:T(512)S(1)}, u32[]{:S(2)}) copy-start(f32[512]{0:T(512)S(1)} %fusion.50) | copy-start | bytes 6148
  19.1 138.6 %copy-start.14 = (f32[512,64]{1,0:T(8,128)}, f32[512,64]{1,0:T(8,128)S(1)}, u32[]{:S(2)}) copy-start(f32[512,64]{1,0:T(8,128)S(1)} %get-tuple-element.46) | copy-start | bytes 393220
  58.9 41.6 %copy-start.45 = (f32[512,4]{0,1:T(4,128)}, f32[512,4]{0,1:T(4,128)S(1)}, u32[]{:S(2)}) copy-start(f32[512,4]{0,1:T(4,128)S(1)} %get-tuple-element.50) | copy-start | bytes 24580
  58.9 37.8 %copy-start.1 = (bf16[512,2048]{1,0:T(8,128)(2,1)S(1)}, bf16[512,2048]{1,0:T(8,128)(2,1)}, u32[]{:S(2)}) copy-start(bf16[512,2048]{1,0:T(8,128)(2,1)} %param.14) | copy-start | bytes 6291460
  60.7 39.9 %copy-start.9 = (f32[512,4,128]{2,0,1:T(8,128)}, f32[512,4,128]{2,0,1:T(8,128)S(1)}, u32[]{:S(2)}) copy-start(f32[512,4,128]{2,0,1:T(8,128)S(1)} %copy.113) | copy-start | bytes 3145732
  153.3 4.4 copy-start.16
  155.4 3.1 copy-start.39
  155.6 3.0 copy-start.25
  159.4 2.8 copy-start.12
  162.2 3.2 copy-start
  162.2 3.2 copy-start.37
  167.1 41.5 %copy-start.18 = (bf16[4,128,2,512]{3,1,2,0:T(8,128)(2,1)}, bf16[4,128,2,512]{3,1,2,0:T(8,128)(2,1)S(1)}, u32[]{:S(2)}) copy-start(bf16[4,128,2,512]{3,1,2,0:T(8,128)(2,1)S(1)} %fusion.23) | copy-start | bytes 3145732
  208.6 2.2 copy-start.53
  208.6 209.4 %all-gather.18.cloned.1.call-start = ((), (), s32[]{:S(2)}) async-start(), calls=%async_computation.13 | async-start | bytes 13369344 | tf_op jit(solution)/shard_map/all_gather | solution.py:195
  209.2 310.3 %all-gather.16.cloned.1.call-start = ((), (), s32[]{:S(2)}) async-start(), calls=%async_computation.12 | async-start | bytes 13369344 | tf_op jit(solution)/shard_map/all_gather | solution.py:194
  209.9 414.1 %all-gather.20.cloned.1.call-start = ((), (), s32[]{:S(2)}) async-start(), calls=%async_computation.14 | async-start | bytes 13369344 | tf_op jit(solution)/shard_map/all_gather | solution.py:203
  210.7 566.2 %all-reduce.19.cloned.1.call-start = ((), (), s32[]{:S(2)}) async-start(), calls=%async_computation.16 | async-start | bytes 8388608 | tf_op jit(solution)/shard_map/psum | solution.py:217
  317.6 2.0 copy-start.5
  320.1 97.9 %copy-start.30 = (bf16[512,2048]{1,0:T(8,128)(2,1)}, bf16[512,2048]{1,0:T(8,128)(2,1)S(1)}, u32[]{:S(2)}) copy-start(bf16[512,2048]{1,0:T(8,128)(2,1)S(1)} %multiply_convert_fusion.2) | copy-start | bytes 6291460
  429.3 194.7 %copy-start.29 = (bf16[512,2048]{1,0:T(8,128)(2,1)S(1)}, bf16[512,2048]{1,0:T(8,128)(2,1)}, u32[]{:S(2)}) copy-start(bf16[512,2048]{1,0:T(8,128)(2,1)} %param.27) | copy-start | bytes 6291460
  646.6 12.1 copy-start.56
  670.7 171.9 %all-reduce.17.cloned.1.call-start = ((), (), s32[]{:S(2)}) async-start(), calls=%async_computation.15 | async-start | bytes 4194304 | tf_op jit(solution)/shard_map/psum | solution.py:204
  682.4 325.0 %all-reduce.21.cloned.1.call-start = ((), (), s32[]{:S(2)}) async-start(), calls=%async_computation.17 | async-start | bytes 8388608 | tf_op jit(solution)/shard_map/psum | solution.py:242
  842.6 8.4 copy-start.11
  848.9 2.0 copy-start.6
  853.9 5.9 copy-start.38
  853.9 11.3 slice-start
  859.8 5.4 slice-start.1
  865.2 2.5 copy-start.13
  870.0 4.8 copy-start.15
  870.0 4.8 copy-start.17
  871.5 3.8 copy-start.10
  871.5 3.8 copy-start.42
  871.5 3.8 copy-start.52
  875.2 4.1 copy-start.27
  881.3 2.9 copy-start.4
  881.3 2.9 copy-start.26
  881.3 2.9 copy-start.50
  884.2 2.4 copy-start.7
  884.2 2.4 copy-start.8
  884.2 2.4 copy-start.40
  886.8 4.1 copy-start.31
  890.9 2.6 copy-start.54
  893.5 2.4 copy-start.20
  893.5 2.4 copy-start.32
  899.3 1.6 copy-start.2
  899.3 1.6 copy-start.36
  899.3 1.6 copy-start.44
  899.3 187.9 %reduce-scatter.12.cloned.1.call-start = ((), (), s32[]{:S(2)}) async-start(), calls=%async_computation.20 | async-start | bytes 4456448 | tf_op jit(solution)/shard_map/reduce_scatter | solution.py:258
  904.5 257.1 %reduce-scatter.10.cloned.1.call-start = ((), (), s32[]{:S(2)}) async-start(), calls=%async_computation.19 | async-start | bytes 4456448 | tf_op jit(solution)/shard_map/reduce_scatter | solution.py:257
  908.0 361.9 %reduce-scatter.14.cloned.1.call-start = ((), (), s32[]{:S(2)}) async-start(), calls=%async_computation.21 | async-start | bytes 8912896 | tf_op jit(solution)/shard_map/reduce_scatter | solution.py:267
  917.0 461.9 %reduce-scatter.8.cloned.1.call-start = ((), (), s32[]{:S(2)}) async-start(), calls=%async_computation.18 | async-start | bytes 8912896 | tf_op jit(solution)/shard_map/reduce_scatter | solution.py:256
  924.0 702.9 %reduce-scatter.20.cloned.1.call-start = ((), (), s32[]{:S(2)}) async-start(), calls=%async_computation.24 | async-start | bytes 26738688 | tf_op jit(solution)/shard_map/reduce_scatter | solution.py:268
  938.4 936.1 %reduce-scatter.18.cloned.1.call-start = ((), (), s32[]{:S(2)}) async-start(), calls=%async_computation.23 | async-start | bytes 26738688 | tf_op jit(solution)/shard_map/reduce_scatter | solution.py:260
  952.4 1169.6 %reduce-scatter.16.cloned.1.call-start = ((), (), s32[]{:S(2)}) async-start(), calls=%async_computation.22 | async-start | bytes 26738688 | tf_op jit(solution)/shard_map/reduce_scatter | solution.py:259
  967.2 113.5 %copy-start.48 = (f32[512]{0:T(512)S(1)}, f32[512]{0:T(512)}, u32[]{:S(2)}) copy-start(f32[512]{0:T(512)} %copy-done.47) | copy-start | bytes 6148
  (13 other events, 14.8 us)
Sparse Core Ops, SparseCore 0:
  10.2 44.1 all-gather.9
  56.5 40.1 all-gather.7
  98.9 49.3 all-gather.11
  150.3 51.6 all-gather.13
  208.7 106.0 all-reduce.14
  317.2 100.7 all-gather.17
  420.5 98.9 all-gather.15
  521.9 102.1 all-gather.19
  670.8 106.0 all-reduce.18
  779.6 62.8 all-reduce.16
  899.4 107.8 all-reduce.20
  1011.6 73.0 reduce-scatter.11
  1089.6 71.8 reduce-scatter.9
  1166.1 103.8 reduce-scatter.13
  1274.4 104.4 reduce-scatter.7
  1383.4 243.4 reduce-scatter.19
  1631.5 242.9 reduce-scatter.17
  1879.0 242.9 reduce-scatter.15
where the time goes:
time: 2140 us; the launch traced here: 2130 us
  waiting for transfers between devices  1770 us (83%)
  matrix products  191 us (9%)
  blocking collectives  67.9 us (3%)
  other arithmetic  55.6 us (3%)
  local copies, waits for them, and re-layouts  28.2 us (1%)
    reduce_scatter x1, waiting for transfers between devices, shards(): lax.psum_scatter(grad_down, 'dp', scatter_dimension=1, tiled=True)  248 us
    reduce_scatter x1, waiting for transfers between devices, shards(): lax.psum_scatter(grad_up, 'dp', scatter_dimension=0, tiled=True)  248 us
    reduce_scatter x1, waiting for transfers between devices, shards(): lax.psum_scatter(grad_gate, 'dp', scatter_dimension=0, tiled=True)  248 us
    reduce_scatter x1, waiting for transfers between devices, shards(): lax.psum_scatter(grad_query, 'dp', scatter_dimension=0, tiled=True)  109 us
    reduce_scatter x1, waiting for transfers between devices, shards(): lax.psum_scatter(grad_output, 'dp', scatter_dimension=1, tiled=True)  108 us
    psum x1, waiting for transfers between devices, shards(): branch = lax.psum(matrix_product(mixture_low, output_full), 'tensor')  104 us
    all_gather x1, waiting for transfers between devices, shards(): lax.all_gather(up_weight, 'dp', axis=0, tiled=True)  97.9 us
    psum x1, waiting for transfers between devices, shards(): lax.psum(inner_right(gate_low, gate_full) + inner_right(up_low, up_full),...  94.4 us
  transfers between devices with their start and end apart: 18, of which 17 were waited for; matrix products, arithmetic and copies ran while one was open for 7% of the time, Pallas kernels for 0%

commit v1 on v0

v1 whole, which is shorter than its diff:
```python
import functools

import jax
import jax.numpy as jnp
from jax import lax
from jax.experimental import pallas as pl
from jax.experimental.pallas import tpu as pltpu
from jax.sharding import PartitionSpec as P

HEAD_SIZE = 128
BLK = 64


epsilon = 1e-06
rope_base = 1000000.0


def matrix_product(left, right):
    return jnp.dot(left, right, preferred_element_type=jnp.float32)


def inner_left(left, right):
    return lax.dot_general(
        left, right, (((0,), (0,)), ((), ())), preferred_element_type=jnp.float32
    )


def inner_right(left, right):
    return lax.dot_general(
        left, right, (((1,), (1,)), ((), ())), preferred_element_type=jnp.float32
    )


def layout(lengths, count_of_rows):
    padded = (lengths + BLK - 1) // BLK * BLK
    starts = jnp.cumsum(padded) - padded
    row_index = jnp.arange(count_of_rows, dtype=jnp.int32)
    inside = (row_index[:, None] >= starts[None, :]) & (
        row_index[:, None] < (starts + lengths)[None, :]
    )
    live_rows = jnp.any(inside, axis=1)
    slot_index = jnp.arange(lengths.shape[0], dtype=jnp.int32)
    owning = jnp.sum(jnp.where(inside, slot_index[None, :], 0), axis=1)
    position = jnp.sum(jnp.where(inside, row_index[:, None] - starts[None, :], 0), axis=1)
    segment = jnp.where(live_rows, owning, -1 - row_index)
    return (live_rows, segment, position)


def rotation(position, width):
    half_width = width // 2
    frequency = jnp.power(rope_base, -(jnp.arange(half_width, dtype=jnp.float32) * 2.0) / width)
    angles = position.astype(jnp.float32)[:, None] * frequency[None, :]
    return (jnp.cos(angles)[:, None, :], jnp.sin(angles)[:, None, :])


CHUNKS = 3
PARTS = 4
LANES = 128
VMEM_LIMIT = 56 * 1024 * 1024


def add_low(left, right):
    return (left.astype(jnp.float32) + right.astype(jnp.float32)).astype(jnp.bfloat16)


class Ring:
    def __init__(self, size):
        self.size = size
        self.steps = size // 4
        index = lax.axis_index("dp")
        self.place = index // 4
        self.side = (index // 2) % 2
        self.core = index % 2
        self.places = [(self.place - 1 - i) % self.steps for i in range(self.steps)]
        self.groups = [
            [place * 4 + side * 2 + core for place in range(self.steps) for core in range(2)]
            for side in range(2)
        ]

    def swap_core(self, value):
        return lax.ppermute(value, "dp", [(i, i ^ 1) for i in range(self.size)])

    def swap_side(self, value):
        return lax.ppermute(value, "dp", [(i, i ^ 2) for i in range(self.size)])

    def shift(self, value, places):
        return lax.ppermute(
            value, "dp", [(i, (i + 4 * places) % self.size) for i in range(self.size)]
        )

    def pick(self, value, axis):
        low, high = jnp.split(value, 2, axis=axis)
        return (
            jnp.where(self.side == 0, low, high),
            jnp.where(self.side == 0, high, low),
        )

    def ordered(self, mine, other, axis):
        return jnp.where(
            self.side == 0,
            jnp.concatenate([mine, other], axis=axis),
            jnp.concatenate([other, mine], axis=axis),
        )

    def block(self, back, core, side):
        return ((self.place - back) % self.steps) * 4 + core * 2 + side

    def place_in(self, whole, back, core, side, value):
        start = (self.block(back, core, side), 0, 0)
        return lax.dynamic_update_slice(whole, value[None], start)


class Gather:
    def __init__(self, ring, piece):
        self.ring = ring
        self.current, self.across, self.index = piece, None, 0
        self.whole = jnp.zeros((ring.size,) + piece.shape, piece.dtype)

    def put(self, back, core, side, value):
        self.whole = self.ring.place_in(self.whole, back, core, side, value)

    def start(self):
        ring, moves = self.ring, {}
        if self.index < ring.steps:
            moves["side"] = ring.swap_side(self.current)
            moves["core"] = ring.swap_core(self.current)
            if self.index < ring.steps - 1:
                moves["hop"] = ring.shift(self.current, 1)
        if self.across is not None:
            moves["both"] = ring.swap_core(self.across)
        return moves

    def finish(self, moves):
        ring, back = self.ring, self.index
        core, side = ring.core, ring.side
        if "both" in moves:
            self.put(back - 1, 1 - core, 1 - side, moves["both"])
        self.across = None
        if "side" in moves:
            self.put(back, core, side, self.current)
            self.put(back, core, 1 - side, moves["side"])
            self.put(back, 1 - core, side, moves["core"])
            self.across, self.current = moves["side"], moves.get("hop")
        self.index += 1

    def result(self):
        return self.whole.reshape(-1, self.whole.shape[2])


class Scatter:
    def __init__(self, ring, mine, other):
        self.ring = ring
        count = mine.shape[0] // ring.steps
        self.mine = [mine[i * count : (i + 1) * count] for i in range(ring.steps)]
        self.other = [other[i * count : (i + 1) * count] for i in range(ring.steps)]
        self.term, self.index, self.total = None, 0, None

    def start(self):
        moves = {}
        if self.index < self.ring.steps:
            moves["side"] = self.ring.swap_side(self.other[self.index])
        if self.term is not None:
            moves["hop"] = self.ring.shift(self.term, 1)
        return moves

    def finish(self, moves):
        value = self.mine[self.index].astype(jnp.float32) + moves["side"].astype(jnp.float32)
        if "hop" in moves:
            value = value + moves["hop"].astype(jnp.float32)
        self.index += 1
        self.total = value
        self.term = value.astype(jnp.bfloat16) if self.index < self.ring.steps else None


def settle(*values):
    return lax.optimization_barrier(values)


def swap_tensor(value):
    return lax.ppermute(value, "tensor", [(0, 1), (1, 0)])


def arrange(value, steps, width):
    blocks = [value[:, i * width : (i + 1) * width] for i in range(4 * steps)]
    order = [4 * place + k for place in range(steps) for k in (0, 2, 1, 3)]
    return jnp.concatenate([blocks[i] for i in order], axis=1)


def arrange_vector(vector, steps):
    return vector.reshape(steps, 2, 2, -1).swapaxes(1, 2).reshape(-1)


def row_call(kernel, rows, block, ins, outs, sums=(), ties=()):
    in_specs = [
        pl.BlockSpec((block, a.shape[1]), lambda i: (i, 0))
        if kind == "rows"
        else pl.BlockSpec(a.shape, lambda i: (0, 0))
        for a, kind in ins
    ]
    out_specs = [pl.BlockSpec((block, c), lambda i: (i, 0)) for c, _ in outs]
    out_specs += [pl.BlockSpec((1, c), lambda i: (0, 0)) for c in sums]
    out_shape = [jax.ShapeDtypeStruct((rows, c), d) for c, d in outs]
    out_shape += [jax.ShapeDtypeStruct((1, c), jnp.float32) for c in sums]
    moved = sum(a.size * a.dtype.itemsize for a, _ in ins)
    moved += sum(rows * c * jnp.dtype(d).itemsize for c, d in outs)
    count = len(ins)

    def body(*refs):
        kernel(*refs[:count], *refs[count + len(ties) :])

    return pl.pallas_call(
        body,
        grid=(rows // block,),
        in_specs=in_specs + [pl.BlockSpec(memory_space=pl.ANY) for _ in ties],
        out_specs=out_specs,
        out_shape=out_shape,
        compiler_params=pltpu.CompilerParams(vmem_limit_bytes=VMEM_LIMIT),
        cost_estimate=pl.CostEstimate(flops=0, bytes_accessed=moved, transcendentals=0),
    )(*[a for a, _ in ins], *ties)


def inverse_rms(value):
    return lax.rsqrt(jnp.mean(value * value, axis=-1, keepdims=True) + epsilon)


def first_kernel(turn, tokens, cotangent, live, gain, tokens_out, upstream_out, normed_out):
    value = turn(tokens[...])
    tokens_out[...] = value
    value = value.astype(jnp.float32)
    normed_out[...] = (value * inverse_rms(value) * gain[...]).astype(jnp.bfloat16)
    back = turn(cotangent[...]).astype(jnp.float32)
    upstream_out[...] = (back * live[...]).astype(jnp.bfloat16)


def middle_kernel(tokens, mine, other, gain, middle_out, normed_out):
    branch = mine[...].astype(jnp.float32) + other[...].astype(jnp.float32)
    value = tokens[...].astype(jnp.float32) + branch
    middle_out[...] = value
    normed_out[...] = (value * inverse_rms(value) * gain[...]).astype(jnp.bfloat16)


def back_rms(value, gain, back):
    scale = inverse_rms(value)
    normed = value * scale
    pulled = back * gain
    center = jnp.mean(pulled * normed, axis=-1, keepdims=True)
    return scale * (pulled - normed * center), back * normed


def add_sum(out_ref, value):
    @pl.when(pl.program_id(0) == 0)
    def _():
        out_ref[...] = jnp.zeros_like(out_ref)

    out_ref[...] += jnp.sum(value, axis=0, keepdims=True)


def back_middle_kernel(mine, other, middle, upstream, gain, back_out, low_out, gain_out):
    back = mine[...].astype(jnp.float32) + other[...].astype(jnp.float32)
    value, gain_term = back_rms(middle[...], gain[...], back)
    value = value + upstream[...].astype(jnp.float32)
    back_out[...] = value
    low_out[...] = value.astype(jnp.bfloat16)
    add_sum(gain_out, gain_term)


def output_kernel(turn, middle, mine, other, out):
    value = middle[...] + mine[...].astype(jnp.float32) + other[...].astype(jnp.float32)
    out[...] = turn(value).astype(jnp.bfloat16)


def token_kernel(turn, mine, other, tokens, back_middle, gain, out):
    back = mine[...].astype(jnp.float32) + other[...].astype(jnp.float32)
    value, _ = back_rms(tokens[...].astype(jnp.float32), gain[...], back)
    out[...] = turn(value + back_middle[...])


def feed_kernel(chunk, normed, upstream, full, out):
    gate = matrix_product(normed[...], full[:, :chunk])
    up = matrix_product(normed[...], full[:, chunk : 2 * chunk])
    back = matrix_product(upstream[...], full[:, 2 * chunk :])
    share = jax.nn.sigmoid(gate)
    active = gate * share
    out[:, :chunk] = (back * up * (share * (1.0 + gate * (1.0 - share)))).astype(jnp.bfloat16)
    out[:, chunk : 2 * chunk] = (back * active).astype(jnp.bfloat16)
    out[:, 2 * chunk :] = (active * up).astype(jnp.bfloat16)


def feed_call(normed, upstream, full, ties=()):
    rows, model_width = normed.shape
    columns = full.shape[1]
    block = 256
    return pl.pallas_call(
        lambda a, b, c, *rest: feed_kernel(columns // 3, a, b, c, rest[-1]),
        grid=(rows // block,),
        in_specs=[
            pl.BlockSpec((block, model_width), lambda i: (i, 0)),
            pl.BlockSpec((block, model_width), lambda i: (i, 0)),
            pl.BlockSpec(full.shape, lambda i: (0, 0)),
        ]
        + [pl.BlockSpec(memory_space=pl.ANY) for _ in ties],
        out_specs=pl.BlockSpec((block, columns), lambda i: (i, 0)),
        out_shape=jax.ShapeDtypeStruct((rows, columns), jnp.bfloat16),
        compiler_params=pltpu.CompilerParams(vmem_limit_bytes=VMEM_LIMIT),
        cost_estimate=pl.CostEstimate(
            flops=2 * rows * model_width * columns,
            bytes_accessed=2 * (2 * normed.size + full.size + rows * columns),
            transcendentals=rows * columns // 3,
        ),
    )(normed, upstream, full, *ties)


def wide_kernel(count, started, *refs):
    out, total = refs[-1], None
    for act, full in zip(refs[:count], refs[count : 2 * count]):
        term = inner_right(act[...], full[...])
        total = term if total is None else total + term
    if started:
        total = total + refs[2 * count][...]
    out[...] = total.astype(out.dtype)


def wide_call(acts, fulls, span, out_dtype, start=None, ties=()):
    lo, hi = span
    size, index = hi - lo, lo // (hi - lo)
    rows, model_width, count = acts[0].shape[0], fulls[0].shape[0], len(acts)
    tile = 512
    ins = list(acts) + list(fulls)
    specs = [pl.BlockSpec((rows, size), lambda i: (0, index))] * count
    specs += [pl.BlockSpec((tile, size), lambda i: (i, index))] * count
    if start is not None:
        ins.append(start)
        specs.append(pl.BlockSpec((rows, tile), lambda i: (0, i)))
    ins += list(ties)
    specs += [pl.BlockSpec(memory_space=pl.ANY) for _ in ties]
    return pl.pallas_call(
        functools.partial(wide_kernel, count, start is not None),
        grid=(model_width // tile,),
        in_specs=specs,
        out_specs=pl.BlockSpec((rows, tile), lambda i: (0, i)),
        out_shape=jax.ShapeDtypeStruct((rows, model_width), out_dtype),
        compiler_params=pltpu.CompilerParams(vmem_limit_bytes=VMEM_LIMIT),
        cost_estimate=pl.CostEstimate(
            flops=2 * rows * model_width * size * count,
            bytes_accessed=2 * (rows + model_width) * size * count + rows * model_width * 6,
            transcendentals=0,
        ),
    )(*ins)


def grad_kernel(split, *refs):
    out = refs[-1]
    for columns, lefts in ((slice(0, split), refs[0:2]), (slice(split, None), refs[2:4])):
        total = 0.0
        for left, act in zip(lefts, refs[4:6]):
            total = total + inner_left(left[...], act[:, columns])
        out[:, columns] = total.astype(jnp.bfloat16)


def grad_call(normed, upstream, acts, ties=()):
    rows, model_width = normed[0].shape
    columns = acts[0].shape[1]
    tall = 512
    return pl.pallas_call(
        functools.partial(grad_kernel, columns // 3 * 2),
        grid=(model_width // tall,),
        in_specs=[pl.BlockSpec((rows, tall), lambda i: (0, i))] * 4
        + [pl.BlockSpec((rows, columns), lambda i: (0, 0))] * 2
        + [pl.BlockSpec(memory_space=pl.ANY) for _ in ties],
        out_specs=pl.BlockSpec((tall, columns), lambda i: (i, 0)),
        out_shape=jax.ShapeDtypeStruct((model_width, columns), jnp.bfloat16),
        compiler_params=pltpu.CompilerParams(vmem_limit_bytes=VMEM_LIMIT),
        cost_estimate=pl.CostEstimate(
            flops=4 * rows * model_width * columns,
            bytes_accessed=2 * (8 * rows * model_width + 4 * rows * columns + model_width * columns),
            transcendentals=0,
        ),
    )(*normed, *upstream, *acts, *ties)


def norm_rope(raw, gain, cosine, sine):
    scale = inverse_rms(raw)
    normed = raw * scale
    scaled = normed * gain
    return scaled * cosine + pltpu.roll(scaled, HEAD_SIZE // 2, 1) * sine, normed, scale


def back_norm_rope(back, normed, scale, gain, cosine, sine):
    back = back * cosine - pltpu.roll(back, HEAD_SIZE // 2, 1) * sine
    pulled = back * gain
    center = jnp.mean(pulled * normed, axis=-1, keepdims=True)
    return scale * (pulled - normed * center), back * normed


def softmax_rows(query, key, allowed):
    scores = jnp.where(allowed, inner_right(query, key) * HEAD_SIZE ** (-0.5), -1e30)
    raised = jnp.exp(scores - jnp.max(scores, axis=-1, keepdims=True))
    return raised / jnp.sum(raised, axis=-1, keepdims=True)


def allowed_pairs(segment_column, segment_row):
    count = segment_column.shape[0]
    row = lax.broadcasted_iota(jnp.int32, (count, count), 0)
    column = lax.broadcasted_iota(jnp.int32, (count, count), 1)
    return (segment_column[...] == segment_row[...]) & (column <= row)


def attend_kernel(
    queries, keys, values, query_gain, key_gain, cosine, sine, seg_column, seg_row, out
):
    allowed = allowed_pairs(seg_column, seg_row)
    cosine, sine = cosine[...], sine[...]
    key = norm_rope(keys[...], key_gain[...], cosine, sine)[0].astype(jnp.bfloat16)
    value = values[...].astype(jnp.bfloat16)
    for lo in range(0, queries.shape[1], HEAD_SIZE):
        span = slice(lo, lo + HEAD_SIZE)
        query = norm_rope(queries[:, span], query_gain[...], cosine, sine)[0]
        weights = softmax_rows(query.astype(jnp.bfloat16), key, allowed)
        out[:, span] = matrix_product(weights.astype(jnp.bfloat16), value).astype(jnp.bfloat16)


def attend_back_kernel(
    first,
    query_columns,
    key_columns,
    queries,
    keys,
    values,
    query_gain,
    key_gain,
    cosine,
    sine,
    seg_column,
    seg_row,
    back_mixture,
    *rest,
):
    out, query_gain_out, key_gain_out = rest[-3:]
    head = first + pl.program_id(0)
    wide = queries.shape[1]
    scaling = HEAD_SIZE ** (-0.5)
    allowed = allowed_pairs(seg_column, seg_row)
    cosine, sine = cosine[...], sine[...]
    key, key_normed, key_scale = norm_rope(keys[...], key_gain[...], cosine, sine)
    key = key.astype(jnp.bfloat16)
    value = values[...].astype(jnp.bfloat16)
    back_key, back_value, query_term = 0.0, 0.0, 0.0
    for lo in range(0, wide, HEAD_SIZE):
        span = slice(lo, lo + HEAD_SIZE)
        query, normed, scale = norm_rope(queries[:, span], query_gain[...], cosine, sine)
        query = query.astype(jnp.bfloat16)
        weights = softmax_rows(query, key, allowed)
        back = back_mixture[:, span]
        back_weights = inner_right(back, value)
        back_value = back_value + inner_left(weights.astype(jnp.bfloat16), back)
        center = jnp.sum(back_weights * weights, axis=-1, keepdims=True)
        back_scores = (weights * (back_weights - center)).astype(jnp.bfloat16)
        back_query = matrix_product(back_scores, key) * scaling
        back_key = back_key + inner_left(back_scores, query) * scaling
        back_query, term = back_norm_rope(
            back_query, normed, scale, query_gain[...], cosine, sine
        )
        query_term = query_term + term
        start = pl.multiple_of(head * wide + lo, HEAD_SIZE)
        out[:, pl.ds(start, HEAD_SIZE)] = back_query.astype(jnp.bfloat16)
    back_key, key_term = back_norm_rope(
        back_key, key_normed, key_scale, key_gain[...], cosine, sine
    )
    start = pl.multiple_of(query_columns + head * HEAD_SIZE, HEAD_SIZE)
    out[:, pl.ds(start, HEAD_SIZE)] = back_key.astype(jnp.bfloat16)
    start = pl.multiple_of(query_columns + key_columns + head * HEAD_SIZE, HEAD_SIZE)
    out[:, pl.ds(start, HEAD_SIZE)] = back_value.astype(jnp.bfloat16)
    add_sum(query_gain_out, query_term)
    add_sum(key_gain_out, key_term)


def attention_call(raw, query_columns, key_columns, gains, tables, segment, heads, back=None):
    rows, columns = raw.shape
    first, count = heads
    wide = query_columns * HEAD_SIZE // key_columns
    first_key = query_columns // HEAD_SIZE + first
    first_value = first_key + key_columns // HEAD_SIZE
    ins = [raw, raw, raw, *gains, *tables, segment[:, None], segment[None, :]]
    specs = [
        pl.BlockSpec((rows, wide), lambda h: (0, first + h)),
        pl.BlockSpec((rows, HEAD_SIZE), lambda h: (0, first_key + h)),
        pl.BlockSpec((rows, HEAD_SIZE), lambda h: (0, first_value + h)),
    ] + [pl.BlockSpec(a.shape, lambda h: (0, 0)) for a in ins[3:]]
    params = dict(
        grid=(count,),
        compiler_params=pltpu.CompilerParams(vmem_limit_bytes=VMEM_LIMIT),
    )
    pairs = count * wide // HEAD_SIZE * rows * rows
    if back is None:
        return pl.pallas_call(
            attend_kernel,
            in_specs=specs,
            out_specs=pl.BlockSpec((rows, wide), lambda h: (0, h)),
            out_shape=jax.ShapeDtypeStruct((rows, count * wide), jnp.bfloat16),
            cost_estimate=pl.CostEstimate(
                flops=4 * pairs * HEAD_SIZE, bytes_accessed=5 * raw.size, transcendentals=pairs
            ),
            **params,
        )(*ins)
    gain_spec = pl.BlockSpec((1, HEAD_SIZE), lambda h: (0, 0))
    gain_shape = jax.ShapeDtypeStruct((1, HEAD_SIZE), jnp.float32)
    return pl.pallas_call(
        functools.partial(attend_back_kernel, first, query_columns, key_columns),
        in_specs=specs + [pl.BlockSpec((rows, wide), lambda h: (0, first + h))],
        out_specs=[pl.BlockSpec((rows, columns), lambda h: (0, 0)), gain_spec, gain_spec],
        out_shape=[jax.ShapeDtypeStruct((rows, columns), jnp.bfloat16), gain_shape, gain_shape],
        cost_estimate=pl.CostEstimate(
            flops=12 * pairs * HEAD_SIZE, bytes_accessed=8 * raw.size, transcendentals=pairs
        ),
        **params,
    )(*ins, back)


def back_first_kernel(raw_grad, full, tokens, out, gain_out):
    value = tokens[...].astype(jnp.float32)
    tile = out.shape[1]
    column = pl.program_id(0) * tile
    back = inner_right(raw_grad[...], full[...])
    out[...] = back.astype(jnp.bfloat16)
    part = tokens[:, pl.ds(pl.multiple_of(column, tile), tile)].astype(jnp.float32)
    gain_out[...] = jnp.sum(back * (part * inverse_rms(value)), axis=0, keepdims=True)


def back_first_call(raw_grad, full, tokens):
    rows, model_width = tokens.shape
    tile = 512
    return pl.pallas_call(
        back_first_kernel,
        grid=(model_width // tile,),
        in_specs=[
            pl.BlockSpec(raw_grad.shape, lambda i: (0, 0)),
            pl.BlockSpec((tile, full.shape[1]), lambda i: (i, 0)),
            pl.BlockSpec(tokens.shape, lambda i: (0, 0)),
        ],
        out_specs=[
            pl.BlockSpec((rows, tile), lambda i: (0, i)),
            pl.BlockSpec((1, tile), lambda i: (0, i)),
        ],
        out_shape=[
            jax.ShapeDtypeStruct((rows, model_width), jnp.bfloat16),
            jax.ShapeDtypeStruct((1, model_width), jnp.float32),
        ],
        compiler_params=pltpu.CompilerParams(vmem_limit_bytes=VMEM_LIMIT),
        cost_estimate=pl.CostEstimate(
            flops=2 * rows * full.size, bytes_accessed=2 * full.size + 8 * tokens.size, transcendentals=0
        ),
    )(raw_grad, full, tokens)


def scatter_kernel(width, info, left, right, *rest):
    mine_out, other_out, whole = rest[-3:]
    whole[...] = inner_left(left[...], right[...])
    mine = whole[pl.ds(pl.multiple_of(info[1] * width, width), width), :]
    other = whole[pl.ds(pl.multiple_of((1 - info[1]) * width, width), width), :]
    if len(rest) > 3:
        mine = mine + rest[0][...].astype(jnp.float32)
        other = other + rest[1][...].astype(jnp.float32)
    mine_out[...] = mine.astype(jnp.bfloat16)
    other_out[...] = other.astype(jnp.bfloat16)


def scatter_call(ring, width, left, right, core, got=()):
    rows, columns = right.shape
    steps = ring.steps
    if 2 * width % LANES:
        blocks = left.reshape(rows, steps, 2, 2, width)
        outs = []
        for k, side in enumerate((ring.side, 1 - ring.side)):
            parts = [
                lax.dynamic_slice(blocks, (0, place, core, side, 0), (rows, 1, 1, 1, width))
                for place in ring.places
            ]
            picked = jnp.concatenate([p.reshape(rows, width) for p in parts], axis=1)
            total = inner_left(picked, right)
            if got:
                total = total + got[k].astype(jnp.float32)
            outs.append(total.astype(jnp.bfloat16))
        return outs
    info = jnp.stack([core, ring.side] + ring.places).astype(jnp.int32)
    half = pl.BlockSpec((width, columns), lambda i, info: (i, 0))
    shape = jax.ShapeDtypeStruct((steps * width, columns), jnp.bfloat16)
    return pl.pallas_call(
        functools.partial(scatter_kernel, width),
        grid_spec=pltpu.PrefetchScalarGridSpec(
            num_scalar_prefetch=1,
            grid=(steps,),
            in_specs=[
                pl.BlockSpec((rows, 2 * width), lambda i, info: (0, info[2 + i] * 2 + info[0])),
                pl.BlockSpec((rows, columns), lambda i, info: (0, 0)),
            ]
            + [half for _ in got],
            out_specs=[half, half],
            scratch_shapes=[pltpu.VMEM((2 * width, columns), jnp.float32)],
        ),
        out_shape=[shape, shape],
        compiler_params=pltpu.CompilerParams(vmem_limit_bytes=VMEM_LIMIT),
        cost_estimate=pl.CostEstimate(
            flops=4 * rows * steps * width * columns,
            bytes_accessed=2 * (right.size + left.size) + 4 * steps * width * columns,
            transcendentals=0,
        ),
    )(info, left, right, *got)


def shards(
    dp_size,
    tokens,
    seq_lengths,
    first_gain,
    query_weight,
    key_matrix,
    value_matrix,
    query_norm_gain,
    key_gain,
    output_weight,
    second_gain,
    gate_weight,
    up_weight,
    down_weight,
    cotangent,
):
    ring = Ring(dp_size)
    steps = ring.steps
    rows, model_width = tokens.shape
    width = query_weight.shape[0]
    key_heads = key_matrix.shape[1] // HEAD_SIZE
    query_columns, key_columns = query_weight.shape[1], key_matrix.shape[1]
    part = rows // PARTS
    tiled = width % LANES == 0
    turned = functools.partial(arrange, steps=steps, width=width)
    turn = turned if tiled else (lambda value: value)
    if not tiled:
        tokens, cotangent = turned(tokens), turned(cotangent)

    def parts_of(value):
        return [value[i * part : (i + 1) * part] for i in range(PARTS)]

    hidden_width = gate_weight.shape[1] // 2
    chunk = hidden_width // CHUNKS
    pieces = [ring.pick(w, 1) for w in (gate_weight, up_weight, down_weight.T)]
    feed_mine, feed_other = (
        [
            jnp.concatenate([p[k][:, j * chunk : (j + 1) * chunk] for p in pieces], axis=1)
            for j in range(CHUNKS)
        ]
        for k in range(2)
    )
    feed_full = [None] * CHUNKS

    def feed_gather(j, got):
        block = ring.ordered(feed_mine[j], got, 0)
        feed_full[j] = lax.all_gather(
            block, "dp", axis=0, tiled=True, axis_index_groups=ring.groups
        )

    attention = Gather(ring, jnp.concatenate([query_weight, key_matrix, value_matrix], axis=1))
    output = Gather(ring, output_weight.T)

    def step(movers, *others):
        moves = [mover.start() for mover in movers]
        moves, others = lax.optimization_barrier((moves, others))
        for mover, move in zip(movers, moves):
            mover.finish(move)
        return others

    live_rows, segment, position = layout(seq_lengths[0], rows)
    cosine_table, sinusoid_table = rotation(position, HEAD_SIZE)
    gain_one = arrange_vector(first_gain.astype(jnp.float32), steps)[None]
    gain_two = arrange_vector(second_gain.astype(jnp.float32), steps)[None]
    tables = (
        jnp.concatenate([cosine_table[:, 0], cosine_table[:, 0]], axis=1),
        jnp.concatenate([-sinusoid_table[:, 0], sinusoid_table[:, 0]], axis=1),
    )
    head_gains = (
        query_norm_gain.astype(jnp.float32)[None],
        key_gain.astype(jnp.float32)[None],
    )
    token_rows, upstream, input_one = row_call(
        functools.partial(first_kernel, turn),
        rows,
        128,
        [
            (tokens, "rows"),
            (cotangent, "rows"),
            (live_rows[:, None].astype(jnp.float32), "rows"),
            (gain_one, "all"),
        ],
        [(model_width, jnp.bfloat16)] * 3,
    )
    for i in range(steps):
        if i == 0:
            token_rows, upstream, input_one, tables = step(
                [attention], token_rows, upstream, input_one, tables
            )
        elif i == steps - 2:
            (got,) = step([attention], ring.swap_side(feed_other[0]))
            feed_gather(0, got)
        elif i == steps - 1:
            step([attention, output])
        else:
            step([attention])
    step([attention])
    attention_full = attention.result()
    upstream_parts = parts_of(upstream)
    upstream_other = []

    raw = matrix_product(input_one, attention_full)
    raw, got, back = step(
        [output], raw, ring.swap_side(feed_other[1]), ring.swap_side(upstream_parts[0])
    )
    upstream_other.append(back)
    feed_gather(1, got)
    half = key_heads // 2
    attend_args = (raw, query_columns, key_columns, head_gains, tables, segment)
    mixture_low = []
    for i in range(2):
        (mixed,) = step([output], attention_call(*attend_args, (i * half, half)))
        mixture_low.append(mixed)
    while output.index <= steps:
        step([output])
    mixture_low = jnp.concatenate(mixture_low, axis=1)
    branch = inner_right(mixture_low, output.result()).astype(jnp.bfloat16)
    extra = [ring.swap_side(w) for w in feed_other[2:]]
    branch, extra = settle(branch, extra)
    for j, got in enumerate(extra):
        feed_gather(2 + j, got)

    branch_parts, token_parts = parts_of(branch), parts_of(token_rows)
    middle_parts, normed_parts = [], []
    got = None
    for i in range(PARTS + 1):
        work = []
        if i:
            work = row_call(
                middle_kernel,
                part,
                part,
                [
                    (token_parts[i - 1], "rows"),
                    (branch_parts[i - 1], "rows"),
                    (got, "rows"),
                    (gain_two, "all"),
                ],
                [(model_width, jnp.float32), (model_width, jnp.bfloat16)],
            )
        if i < PARTS:
            moves = [swap_tensor(branch_parts[i])]
            if i + 1 < PARTS:
                moves.append(ring.swap_side(upstream_parts[i + 1]))
            moves, work, branch_parts = settle(moves, work, branch_parts)
            got = moves[0]
            upstream_other += moves[1:]
        if i:
            middle_parts.append(work[0])
            normed_parts.append(work[1])
    normed_other = [ring.swap_side(p) for p in normed_parts]
    middle = jnp.concatenate(middle_parts, axis=0)
    normed = jnp.concatenate(normed_parts, axis=0)

    span, out_span = (0, 2 * chunk), (2 * chunk, 3 * chunk)
    acts = [feed_call(normed, upstream, feed_full[0])]
    for j in range(1, CHUNKS - 1):
        acts.append(feed_call(normed, upstream, feed_full[j], acts[-1:]))
    normed_other = jnp.concatenate(normed_other, axis=0)
    upstream_other = jnp.concatenate(upstream_other, axis=0)
    sides = (normed, normed_other), (upstream, upstream_other)
    acts_other, feed_grads = [], []
    for j in range(CHUNKS - 1):
        acts_other.append(
            feed_call(normed_other, upstream_other, feed_full[j], (acts[-1:] + feed_grads)[-1:])
        )
        feed_grads.append(grad_call(*sides, (acts[j], acts_other[j])))
    early_other = wide_call(acts_other, feed_full[:-1], span, jnp.float32, ties=feed_grads[-1:])
    early_mine = wide_call(acts, feed_full[:-1], span, jnp.float32, ties=(early_other,))
    acts_other.append(feed_call(normed_other, upstream_other, feed_full[-1], (early_mine,)))
    back_other = wide_call(acts_other[-1:], feed_full[-1:], span, jnp.bfloat16, early_other)
    acts.append(feed_call(normed, upstream, feed_full[-1], (back_other,)))

    back_other = parts_of(back_other)
    back_mine = wide_call(acts[-1:], feed_full[-1:], span, jnp.float32, early_mine)
    got, back_mine = settle(ring.swap_side(back_other[0]), back_mine)
    back_mine = parts_of(back_mine)
    mine = add_low(back_mine[0], got)
    back_parts, low_parts, mixed_parts, grad_second = [], [], [], 0.0
    out_other, out_mine, out_sums, out_got = None, None, [], []

    def back_middle_call(i, mine, other):
        return row_call(
            back_middle_kernel,
            part,
            part,
            [
                (mine, "rows"),
                (other, "rows"),
                (middle_parts[i], "rows"),
                (upstream_parts[i], "rows"),
                (gain_two, "all"),
            ],
            [(model_width, jnp.float32), (model_width, jnp.bfloat16)],
            [model_width],
        )

    output_full = output.result()
    for i in range(PARTS):
        work = []
        if i == 0:
            work = [grad_call(*sides, (acts[-1], acts_other[-1]), (mine,))]
        if i == 1:
            work = [wide_call(acts_other, feed_full, out_span, jnp.bfloat16, ties=(mine,))]
        if i == 2:
            work = [wide_call(acts, feed_full, out_span, jnp.float32, ties=(mine,))]
        done = []
        if i:
            back, low, term = back_middle_call(i - 1, last[0], last[1])
            done = [back, low, term, matrix_product(low, output_full).astype(jnp.bfloat16)]
        moves = [swap_tensor(mine)]
        moves.append(ring.swap_side(back_other[i + 1] if i + 1 < PARTS else out_other[0]))
        moves, work, done = settle(moves, work, done)
        last = (mine, moves[0])
        if i + 1 < PARTS:
            mine = add_low(back_mine[i + 1], moves[1])
        else:
            out_got.append(moves[1])
        if i == 0:
            feed_grads.append(work[0])
        if i == 1:
            out_other = parts_of(work[0])
        if i == 2:
            out_mine = parts_of(work[0])
        if done:
            back_parts.append(done[0])
            low_parts.append(done[1])
            grad_second = grad_second + done[2]
            mixed_parts.append(done[3])
    back, low, term = back_middle_call(PARTS - 1, last[0], last[1])
    back_parts.append(back)
    low_parts.append(low)
    grad_second = grad_second + term
    mixed_parts.append(matrix_product(low, output_full).astype(jnp.bfloat16))
    back_middle = jnp.concatenate(back_parts, axis=0)
    branch_low = jnp.concatenate(low_parts, axis=0)
    back_mixture = jnp.concatenate(mixed_parts, axis=0)

    scattered = [
        lax.psum_scatter(
            grad, "dp", scatter_dimension=0, tiled=True, axis_index_groups=ring.groups
        )
        for grad in feed_grads
    ]

    core = ring.core
    far = scatter_call(ring, width, branch_low, mixture_low, 1 - core)
    out_sums.append(add_low(out_mine[0], out_got[0]))
    raw_grads, head_terms, far_got, out_done = [], [], None, []
    for i in range(2):
        moves = [ring.swap_side(out_other[1 + i]), swap_tensor(out_sums[i])]
        if i == 0:
            moves += [ring.swap_core(f) for f in far]
        work = attention_call(*attend_args, (i * half, half), back_mixture)
        moves, work = settle(moves, work)
        out_sums.append(add_low(out_mine[1 + i], moves[0]))
        out_done.append(moves[1])
        if i == 0:
            near = scatter_call(ring, width, branch_low, mixture_low, core, moves[2:])
        raw_grads.append(work[0])
        head_terms.append(work[1:])
    heads_done = half * HEAD_SIZE
    queries_done = query_columns // 2

    def join(first, second, start, size, cut):
        return [first[:, start : start + cut], second[:, start + cut : start + size]]

    raw_grad = jnp.concatenate(
        join(*raw_grads, 0, query_columns, queries_done)
        + join(*raw_grads, query_columns, key_columns, heads_done)
        + join(*raw_grads, query_columns + key_columns, key_columns, heads_done),
        axis=1,
    )
    grad_qgain = head_terms[0][0] + head_terms[1][0]
    grad_kgain = head_terms[0][1] + head_terms[1][1]

    output_sum = Scatter(ring, *near)
    far = scatter_call(ring, width, input_one, raw_grad, 1 - core)
    moves = [ring.swap_core(f) for f in far] + [
        ring.swap_side(out_other[3]),
        swap_tensor(out_sums[2]),
    ]
    back_one, grad_first, moves = settle(
        *back_first_call(raw_grad, attention_full, token_rows), moves
    )
    out_sums.append(add_low(out_mine[3], moves[2]))
    out_done.append(moves[3])
    attention_sum = Scatter(
        ring, *scatter_call(ring, width, input_one, raw_grad, core, moves[:2])
    )
    back_one = parts_of(back_one)
    back_one_other = []
    gains = jnp.concatenate(
        [
            arrange_vector(grad_first[0], steps),
            arrange_vector(grad_second[0], steps) * 0.5,
            grad_qgain[0],
            grad_kgain[0],
        ]
    )
    (out_last,) = step([output_sum], swap_tensor(out_sums[3]))
    out_done.append(out_last)
    pairs = [ring.pick(total, 0) for total in scattered]
    pairs_got = []
    gains = gains + swap_tensor(gains)
    distance = 1
    for i in range(steps):
        movers = [attention_sum] + ([output_sum] if output_sum.index < steps else [])
        others = []
        if i < PARTS:
            others.append(swap_tensor(back_one[i]))
        if distance < dp_size:
            others.append(
                lax.ppermute(gains, "dp", [(k, k ^ distance) for k in range(dp_size)])
            )
        final = i - (steps - 1 - CHUNKS)
        if 0 < final < CHUNKS:
            others.insert(0, ring.swap_side(pairs[final - 1][1]))
        others = list(step(movers, *others))
        if 0 < final < CHUNKS:
            pairs_got.append(others.pop(0))
        if distance < dp_size:
            gains = gains + others.pop()
            distance *= 2
        back_one_other += others
    (token_grad,) = row_call(
        functools.partial(token_kernel, turn),
        rows,
        128,
        [
            (jnp.concatenate(back_one, axis=0), "rows"),
            (jnp.concatenate(back_one_other, axis=0), "rows"),
            (token_rows, "rows"),
            (back_middle, "rows"),
            (gain_one, "all"),
        ],
        [(model_width, jnp.float32)],
    )
    (block_output,) = row_call(
        functools.partial(output_kernel, turn),
        rows,
        128,
        [
            (middle, "rows"),
            (jnp.concatenate(out_sums, axis=0), "rows"),
            (jnp.concatenate(out_done, axis=0), "rows"),
        ],
        [(model_width, jnp.bfloat16)],
    )
    if not tiled:
        token_grad, block_output = turned(token_grad), turned(block_output)
    grad_output = output_sum.total
    grad_attention = attention_sum.total
    grad_query = grad_attention[:, :query_columns]
    grad_key = grad_attention[:, query_columns : query_columns + key_columns]
    grad_value = grad_attention[:, query_columns + key_columns :]

    chunk_grads = []
    pairs_got.append(ring.swap_side(pairs[-1][1]))
    for (mine, _), other in zip(pairs, pairs_got):
        both = (
            jnp.where(ring.side == 0, mine, other),
            jnp.where(ring.side == 0, other, mine),
        )
        chunk_grads.append([b.astype(jnp.float32) for b in both])
    grad_gate, grad_up, grad_down = (
        jnp.concatenate(
            [
                chunk_grads[j][side][:, k * chunk : (k + 1) * chunk]
                for side in range(2)
                for j in range(CHUNKS)
            ],
            axis=1,
        )
        for k in range(3)
    )

    while distance < dp_size:
        gains = gains + lax.ppermute(gains, "dp", [(k, k ^ distance) for k in range(dp_size)])
        distance *= 2
    index = lax.axis_index("dp")

    def own_part(start, size):
        return lax.dynamic_slice_in_dim(gains, start + index * (size // dp_size), size // dp_size)

    return (
        block_output,
        token_grad,
        own_part(0, model_width),
        grad_query,
        grad_key,
        grad_value,
        own_part(2 * model_width, HEAD_SIZE),
        own_part(2 * model_width + HEAD_SIZE, HEAD_SIZE),
        grad_output.T,
        own_part(model_width, model_width),
        grad_gate,
        grad_up,
        grad_down.T,
    )


def solution(mesh):
    return jax.shard_map(
        functools.partial(shards, mesh.shape["dp"]),
        mesh=mesh,
        in_specs=(
            P("dp", None),
            P("dp", None),
            P(),
            P("dp", "tensor"),
            P("dp", "tensor"),
            P("dp", "tensor"),
            P(),
            P(),
            P("tensor", "dp"),
            P(),
            P("dp", "tensor"),
            P("dp", "tensor"),
            P("tensor", "dp"),
            P("dp", None),
        ),
        out_specs=(
            P("dp", None),
            P("dp", None),
            P("dp"),
            P("dp", "tensor"),
            P("dp", "tensor"),
            P("dp", "tensor"),
            P("dp"),
            P("dp"),
            P("tensor", "dp"),
            P("dp"),
            P("dp", "tensor"),
            P("dp", "tensor"),
            P("tensor", "dp"),
        ),
        check_vma=False,
    )
```

time: 2140 us -> 680 us (0.32)
  waiting for transfers between devices: 1770 us -> 172 us
  Pallas kernels: 0 us -> 257 us
  matrix products: 191 us -> 13.1 us
  starting transfers between devices: 1.19 us -> 87.6 us
  blocking collectives: 67.9 us -> 0 us
  local copies, waits for them, and re-layouts: 28.2 us -> 70.5 us
    reduce_scatter x7 -> x3, waiting for transfers between devices: 1030 us -> 0.02 us  [shards(): lax.psum_scatter(grad, 'dp', scatter_dimension=0, tiled=True, axis_index_...]
    all_gather x7 -> x3, waiting for transfers between devices: 431 us -> 0.01 us  [feed_gather(): lax.all_gather(block, 'dp', axis=0, tiled=True, axis_index_groups=ring.gr...]
    psum x4 -> x0, waiting for transfers between devices: 298 us -> none  [the longest x1 104 us: shards(): branch = lax.psum(matrix_product(mixture_low, output_full), 'tensor')]
    pallas_call x0 -> x35, Pallas kernels: none -> 257 us  [the longest x6 49 us: wide_call(): pl.pallas_call(functools.partial(wide_kernel, count, start is not None),...]
    ppermute x0 -> x91, waiting for transfers between devices: none -> 172 us  [the longest x38 139 us: swap_side(): return lax.ppermute(value, 'dp', [(i, i ^ 2) for i in range(self.size)])]
    ppermute x0 -> x91, starting transfers between devices: none -> 86.7 us  [the longest x38 44.4 us: swap_side(): return lax.ppermute(value, 'dp', [(i, i ^ 2) for i in range(self.size)])]
    dot_general x13 -> x0, matrix products: 80.9 us -> none  [the longest x7 63.3 us: inner_left(): lax.dot_general(left, right, (((0,), (0,)), ((), ())), preferred_element_...]
    unnamed x1 -> x0, blocking collectives: 62.4 us -> none
  transfers between devices with their start and end apart: 18 -> 97, of which waited for: 17 -> 30; matrix products, arithmetic and copies ran while one was open for 7% -> 17% of each run, Pallas kernels for 0% -> 38%
where the time goes in v1:
time: 680 us; the launch traced here: 669 us
  Pallas kernels  257 us (38%)
  waiting for transfers between devices  172 us (25%)
  starting transfers between devices  87.6 us (13%)
  local copies, waits for them, and re-layouts  70.5 us (10%)
  other arithmetic  52.8 us (8%)
  between operations  16 us (2%)
  matrix products  13.1 us (2%)
    ppermute x38, waiting for transfers between devices, swap_side(): return lax.ppermute(value, 'dp', [(i, i ^ 2) for i in range(self.size)])  139 us
    pallas_call x6, Pallas kernels, wide_call(): pl.pallas_call(functools.partial(wide_kernel, count, start is not None),...  49 us
    pallas_call x6, Pallas kernels, feed_call(): pl.pallas_call(lambda a, b, c, *rest: feed_kernel(columns // 3, a, b, c,...  48.4 us
    ppermute x38, starting transfers between devices, swap_side(): return lax.ppermute(value, 'dp', [(i, i ^ 2) for i in range(self.size)])  44.4 us
    pallas_call x11, Pallas kernels, row_call(): pl.pallas_call(body, grid=(rows // block,), in_specs=in_specs + [pl.Block...  44.2 us
    pallas_call x3, Pallas kernels, grad_call(): pl.pallas_call(functools.partial(grad_kernel, columns // 3 * 2), grid=(mo...  34.7 us
    unnamed x223, local copies, waits for them, and re-layouts  31.9 us
    pallas_call x4, Pallas kernels, scatter_call(): pl.pallas_call(functools.partial(scatter_kernel, width), grid_spec=pltpu....  28.1 us
  transfers between devices with their start and end apart: 97, of which 30 were waited for; matrix products, arithmetic and copies ran while one was open for 17% of the time, Pallas kernels for 38%

profile of v1, /device:TPU:0, one launch (start us, length us, event | category | flops | bytes accessed | tf_op | source)
XLA Modules:
  0.0 669.1 jit_solution(14494528241821635203)
XLA Ops:
  10.1 3.0 collective-permute-start.2
  22.8 5.7 shard_map.237
  34.4 9.2 %collective-permute-done.6 = bf16[128,2048]{1,0:T(8,128)(2,1)S(1)} collective-permute-done((bf16[128,2048]{1,0:T(8,128)(2,1)}, bf16[128,2048]{1,0:T(8,128)(2,1)S(1)}, u32[]{:S(2)}, u32[]{:S(2)}) %collective-permute-start.6) | collective-permute-done | bytes 524320 | tf_op jit(solution)/shard_map/ppermute | solution.py:84
  47.5 4.6 collective-permute-done.11
  52.1 10.8 %collective-permute-done.10 = bf16[128,2048]{1,0:T(8,128)(2,1)S(1)} collective-permute-done((bf16[128,2048]{1,0:T(8,128)(2,1)S(1)}, bf16[128,2048]{1,0:T(8,128)(2,1)S(1)}, u32[]{:S(2)}, u32[]{:S(2)}) %collective-permute-start.10) | collective-permute-done | bytes 524320 | tf_op jit(solution)/shard_map/ppermute | solution.py:84
  81.6 9.8 %collective-permute-done.14 = bf16[128,2048]{1,0:T(8,128)(2,1)S(1)} collective-permute-done((bf16[128,2048]{1,0:T(8,128)(2,1)S(1)}, bf16[128,2048]{1,0:T(8,128)(2,1)S(1)}, u32[]{:S(2)}, u32[]{:S(2)}) %collective-permute-start.14) | collective-permute-done | bytes 524320 | tf_op jit(solution)/shard_map/ppermute | solution.py:84
  96.6 3.2 collective-permute-done.23
  99.8 6.1 fusion.22.queries.keys.values
  106.0 5.1 collective-permute-done.24
  111.9 2.9 collective-permute-done.21
  124.9 9.3 %shard_map.239 = bf16[512,512]{1,0:T(8,128)(2,1)} custom-call(f32[512,2048]{1,0:T(8,128)} %fusion.22.queries.keys.values, f32[512,2048]{1,0:T(8,128)} %fusion.22.queries.keys.values, f32[512,2048]{1,0:T(8,128)} %fusion.22.queries.keys.values, f32[1,128]{1,0:T(1,128)} %get-tuple-element.505.query_gain, f32[1,128]{1,0:T(1,128)} %get-tuple-element.504.key_gain, ...), custom_call_target="tpu_custom_call" | custom-call | flops 536870912 | bytes 5242880 | tf_op jit(solution)/shard_map/pallas_call | solution.py:495
  135.2 9.4 %shard_map.238 = bf16[512,512]{1,0:T(8,128)(2,1)} custom-call(f32[512,2048]{1,0:T(8,128)} %fusion.22.queries.keys.values, f32[512,2048]{1,0:T(8,128)} %fusion.22.queries.keys.values, f32[512,2048]{1,0:T(8,128)} %fusion.22.queries.keys.values, f32[1,128]{1,0:T(1,128)} %get-tuple-element.505.query_gain, f32[1,128]{1,0:T(1,128)} %get-tuple-element.504.key_gain, ...), custom_call_target="tpu_custom_call" | custom-call | flops 536870912 | bytes 5242880 | tf_op jit(solution)/shard_map/pallas_call | solution.py:495
  148.1 4.9 collective-permute-done.31
  165.9 8.8 %collective-permute-done.35 = bf16[128,2048]{1,0:T(8,128)(2,1)S(1)} collective-permute-done((bf16[128,2048]{1,0:T(8,128)(2,1)S(1)}, bf16[128,2048]{1,0:T(8,128)(2,1)S(1)}, u32[]{:S(2)}, u32[]{:S(2)}) %collective-permute-start.35) | collective-permute-done | bytes 524320 | tf_op jit(solution)/shard_map/ppermute | solution.py:84
  178.4 2.7 shard_map.240
  181.2 15.3 %collective-permute-done.37 = bf16[128,2048]{1,0:T(8,128)(2,1)S(1)} collective-permute-done((bf16[128,2048]{1,0:T(8,128)(2,1)S(1)}, bf16[128,2048]{1,0:T(8,128)(2,1)S(1)}, u32[]{:S(2)}, u32[]{:S(2)}) %collective-permute-start.37) | collective-permute-done | bytes 524320 | tf_op jit(solution)/shard_map/ppermute | solution.py:84
  202.9 2.8 shard_map.241
  205.7 4.1 collective-permute-done.38.refs_2_
  216.0 3.2 shard_map.242
  219.2 2.9 collective-permute-done.40.refs_2_
  222.9 2.7 shard_map.243
  230.8 17.8 %collective-permute-done.43 = bf16[128,2048]{1,0:T(8,128)(2,1)S(1)} collective-permute-done((bf16[128,2048]{1,0:T(8,128)(2,1)}, bf16[128,2048]{1,0:T(8,128)(2,1)S(1)}, u32[]{:S(2)}, u32[]{:S(2)}) %collective-permute-start.43) | collective-permute-done | bytes 524320 | tf_op jit(solution)/shard_map/ppermute | solution.py:84
  250.3 8.1 %shard_map.244.rest_0_.refs_4_.refs_0_ = bf16[512,1536]{1,0:T(8,128)(2,1)} custom-call(bf16[512,2048]{1,0:T(8,128)(2,1)} %copy-done.3, bf16[512,2048]{1,0:T(8,128)(2,1)} %get-tuple-element.204.b.refs_2_, bf16[2048,1536]{1,0:T(8,128)(2,1)} %all-gather.6.cloned.1.call-done.c.refs_2_.refs_3_), custom_call_target="tpu_custom_call" | custom-call | flops 3221225472 | bytes 12058624 | tf_op jit(solution)/shard_map/pallas_call | solution.py:293
  258.4 8.1 %shard_map.245.rest_0_.refs_4_.refs_1_ = bf16[512,1536]{1,0:T(8,128)(2,1)} custom-call(bf16[512,2048]{1,0:T(8,128)(2,1)} %copy-done.3, bf16[512,2048]{1,0:T(8,128)(2,1)} %get-tuple-element.204.b.refs_2_, bf16[2048,1536]{1,0:T(8,128)(2,1)} %all-gather.8.cloned.1.call-done.c.refs_3_.refs_4_, bf16[512,1536]{1,0:T(8,128)(2,1)} %shard_map.244.rest_0_.refs_4_.refs_0_), custom_call_target="tpu_custom_call" | custom-call | flops 3221225472 | bytes 12058624 | tf_op jit(solution)/shard_map/pallas_call | solution.py:293
  266.4 8.1 %shard_map.246.refs_5_.refs_0_ = bf16[512,1536]{1,0:T(8,128)(2,1)} custom-call(bf16[512,2048]{1,0:T(8,128)(2,1)} %constant_dynamic-update-slice_fusion.5.a.refs_1_, bf16[512,2048]{1,0:T(8,128)(2,1)} %copy-done.4, bf16[2048,1536]{1,0:T(8,128)(2,1)} %all-gather.6.cloned.1.call-done.c.refs_2_.refs_3_, bf16[512,1536]{1,0:T(8,128)(2,1)} %shard_map.245.rest_0_.refs_4_.refs_1_), custom_call_target="tpu_custom_call" | custom-call | flops 3221225472 | bytes 12058624 | tf_op jit(solution)/shard_map/pallas_call | solution.py:293
  274.5 11.6 %shard_map.247.rest_0_ = bf16[2048,1536]{1,0:T(8,128)(2,1)} custom-call(bf16[512,2048]{1,0:T(8,128)(2,1)} %copy-done.3, bf16[512,2048]{1,0:T(8,128)(2,1)} %constant_dynamic-update-slice_fusion.5.a.refs_1_, bf16[512,2048]{1,0:T(8,128)(2,1)} %get-tuple-element.204.b.refs_2_, bf16[512,2048]{1,0:T(8,128)(2,1)} %copy-done.4, ...), custom_call_target="tpu_custom_call" | custom-call | flops 6442450944 | bytes 29360128 | tf_op jit(solution)/shard_map/pallas_call | solution.py:364
  286.1 8.0 %shard_map.248.refs_5_.refs_1_ = bf16[512,1536]{1,0:T(8,128)(2,1)} custom-call(bf16[512,2048]{1,0:T(8,128)(2,1)} %constant_dynamic-update-slice_fusion.5.a.refs_1_, bf16[512,2048]{1,0:T(8,128)(2,1)} %copy-done.4, bf16[2048,1536]{1,0:T(8,128)(2,1)} %all-gather.8.cloned.1.call-done.c.refs_3_.refs_4_, bf16[2048,1536]{1,0:T(8,128)(2,1)} %shard_map.247.rest_0_), custom_call_target="tpu_custom_call" | custom-call | flops 3221225472 | bytes 12058624 | tf_op jit(solution)/shard_map/pallas_call | solution.py:293
  294.2 11.6 %shard_map.249.refs_4_ = bf16[2048,1536]{1,0:T(8,128)(2,1)} custom-call(bf16[512,2048]{1,0:T(8,128)(2,1)} %copy-done.3, bf16[512,2048]{1,0:T(8,128)(2,1)} %constant_dynamic-update-slice_fusion.5.a.refs_1_, bf16[512,2048]{1,0:T(8,128)(2,1)} %get-tuple-element.204.b.refs_2_, bf16[512,2048]{1,0:T(8,128)(2,1)} %copy-done.4, ...), custom_call_target="tpu_custom_call" | custom-call | flops 6442450944 | bytes 29360128 | tf_op jit(solution)/shard_map/pallas_call | solution.py:364
  306.0 9.3 %shard_map.250.refs_4_.refs_2_ = f32[512,2048]{1,0:T(8,128)} custom-call(bf16[512,1536]{1,0:T(8,128)(2,1)} %shard_map.246.refs_5_.refs_0_, bf16[512,1536]{1,0:T(8,128)(2,1)} %shard_map.248.refs_5_.refs_1_, bf16[2048,1536]{1,0:T(8,128)(2,1)} %all-gather.6.cloned.1.call-done.c.refs_2_.refs_3_, ...), custom_call_target="tpu_custom_call" | custom-call | flops 4294967296 | bytes 16777216 | tf_op jit(solution)/shard_map/pallas_call | solution.py:336
  315.3 9.2 %shard_map.251.rest_0_.refs_2_ = f32[512,2048]{1,0:T(8,128)} custom-call(bf16[512,1536]{1,0:T(8,128)(2,1)} %shard_map.244.rest_0_.refs_4_.refs_0_, bf16[512,1536]{1,0:T(8,128)(2,1)} %shard_map.245.rest_0_.refs_4_.refs_1_, bf16[2048,1536]{1,0:T(8,128)(2,1)} %all-gather.6.cloned.1.call-done.c.refs_2_.refs_3_, ...), custom_call_target="tpu_custom_call" | custom-call | flops 4294967296 | bytes 16777216 | tf_op jit(solution)/shard_map/pallas_call | solution.py:336
  324.4 8.1 %shard_map.252.refs_0_.refs_5_.refs_2_ = bf16[512,1536]{1,0:T(8,128)(2,1)} custom-call(bf16[512,2048]{1,0:T(8,128)(2,1)} %constant_dynamic-update-slice_fusion.5.a.refs_1_, bf16[512,2048]{1,0:T(8,128)(2,1)} %copy-done.4, bf16[2048,1536]{1,0:T(8,128)(2,1)} %all-gather.4.cloned.1.call-done.c.refs_1_.refs_5_, f32[512,2048]{1,0:T(8,128)} %shard_map.251.rest_0_.refs_2_), custom_call_target="tpu_custom_call" | custom-call | flops 3221225472 | bytes 12058624 | tf_op jit(solution)/shard_map/pallas_call | solution.py:293
  332.5 7.0 %shard_map.253.rest_0_ = bf16[512,2048]{1,0:T(8,128)(2,1)} custom-call(bf16[512,1536]{1,0:T(8,128)(2,1)} %shard_map.252.refs_0_.refs_5_.refs_2_, bf16[2048,1536]{1,0:T(8,128)(2,1)} %all-gather.4.cloned.1.call-done.c.refs_1_.refs_5_, f32[512,2048]{1,0:T(8,128)} %shard_map.250.refs_4_.refs_2_), custom_call_target="tpu_custom_call" | custom-call | flops 2147483648 | bytes 11534336 | tf_op jit(solution)/shard_map/pallas_call | solution.py:336
  347.5 8.1 %shard_map.254.refs_0_.refs_4_.refs_2_ = bf16[512,1536]{1,0:T(8,128)(2,1)} custom-call(bf16[512,2048]{1,0:T(8,128)(2,1)} %copy-done.3, bf16[512,2048]{1,0:T(8,128)(2,1)} %get-tuple-element.204.b.refs_2_, bf16[2048,1536]{1,0:T(8,128)(2,1)} %all-gather.4.cloned.1.call-done.c.refs_1_.refs_5_, bf16[512,2048]{1,0:T(8,128)(2,1)} %shard_map.253.rest_0_), custom_call_target="tpu_custom_call" | custom-call | flops 3221225472 | bytes 12058624 | tf_op jit(solution)/shard_map/pallas_call | solution.py:293
  355.6 7.5 %shard_map.255 = f32[512,2048]{1,0:T(8,128)} custom-call(bf16[512,1536]{1,0:T(8,128)(2,1)} %shard_map.254.refs_0_.refs_4_.refs_2_, bf16[2048,1536]{1,0:T(8,128)(2,1)} %all-gather.4.cloned.1.call-done.c.refs_1_.refs_5_, f32[512,2048]{1,0:T(8,128)} %shard_map.251.rest_0_.refs_2_), custom_call_target="tpu_custom_call" | custom-call | flops 2147483648 | bytes 11534336 | tf_op jit(solution)/shard_map/pallas_call | solution.py:336
  366.0 11.6 %shard_map.256 = bf16[2048,1536]{1,0:T(8,128)(2,1)} custom-call(bf16[512,2048]{1,0:T(8,128)(2,1)} %copy-done.3, bf16[512,2048]{1,0:T(8,128)(2,1)} %constant_dynamic-update-slice_fusion.5.a.refs_1_, bf16[512,2048]{1,0:T(8,128)(2,1)} %get-tuple-element.204.b.refs_2_, bf16[512,2048]{1,0:T(8,128)(2,1)} %copy-done.4, ...), custom_call_target="tpu_custom_call" | custom-call | flops 6442450944 | bytes 29360128 | tf_op jit(solution)/shard_map/pallas_call | solution.py:364
  377.6 9.6 %collective-permute-done.47 = bf16[128,2048]{1,0:T(8,128)(2,1)S(1)} collective-permute-done((bf16[128,2048]{1,0:T(8,128)(2,1)S(1)}, bf16[128,2048]{1,0:T(8,128)(2,1)S(1)}, u32[]{:S(2)}, u32[]{:S(2)}) %collective-permute-start.47) | collective-permute-done | bytes 524320 | tf_op jit(solution)/shard_map/ppermute | solution.py:84
  390.3 3.6 shard_map.258
  393.9 7.8 %shard_map.257 = bf16[512,2048]{1,0:T(8,128)(2,1)} custom-call(bf16[512,1536]{1,0:T(8,128)(2,1)} %shard_map.246.refs_5_.refs_0_, bf16[512,1536]{1,0:T(8,128)(2,1)} %shard_map.248.refs_5_.refs_1_, bf16[512,1536]{1,0:T(8,128)(2,1)} %shard_map.252.refs_0_.refs_5_.refs_2_, bf16[2048,1536]{1,0:T(8,128)(2,1)} %all-gather.6.cloned.1.call-done.c.refs_2_.refs_3_, ...), custom_call_target="tpu_custom_call" | custom-call | flops 3221225472 | bytes 14155776 | tf_op jit(solution)/shard_map/pallas_call | solution.py:336
  410.5 3.6 shard_map.260
  414.2 8.3 %shard_map.259 = f32[512,2048]{1,0:T(8,128)} custom-call(bf16[512,1536]{1,0:T(8,128)(2,1)} %shard_map.244.rest_0_.refs_4_.refs_0_, bf16[512,1536]{1,0:T(8,128)(2,1)} %shard_map.245.rest_0_.refs_4_.refs_1_, bf16[512,1536]{1,0:T(8,128)(2,1)} %shard_map.254.refs_0_.refs_4_.refs_2_, bf16[2048,1536]{1,0:T(8,128)(2,1)} %all-gather.6.cloned.1.call-done.c.refs_2_.refs_3_, ...), custom_call_target="tpu_custom_call" | custom-call | flops 3221225472 | bytes 14155776 | tf_op jit(solution)/shard_map/pallas_call | solution.py:336
  427.0 3.6 shard_map.261
  432.4 7.4 %collective-permute-done.53 = bf16[128,2048]{1,0:T(8,128)(2,1)} collective-permute-done((bf16[128,2048]{1,0:T(8,128)(2,1)}, bf16[128,2048]{1,0:T(8,128)(2,1)}, u32[]{:S(2)}, u32[]{:S(2)}) %collective-permute-start.53) | collective-permute-done | bytes 524320 | tf_op jit(solution)/shard_map/ppermute | solution.py:84
  439.8 3.6 shard_map.262
  445.8 5.7 shard_map.263
  456.6 11.8 %shard_map.264 = (bf16[512,2048]{1,0:T(8,128)(2,1)}, f32[1,128]{1,0:T(1,128)}, f32[1,128]{1,0:T(1,128)}) custom-call(f32[512,2048]{1,0:T(8,128)} %fusion.22.queries.keys.values, f32[512,2048]{1,0:T(8,128)} %fusion.22.queries.keys.values, f32[512,2048]{1,0:T(8,128)} %fusion.22.queries.keys.values, f32[1,128]{1,0:T(1,128)} %get-tuple-element.505.query_gain, ...), custom_call_target="tpu_custom_call" | custom-call | flops 1610612736 | bytes 8388608 | tf_op jit(solution)/shard_map/pallas_call | solution.py:507
  476.1 12.0 %shard_map.265 = (bf16[512,2048]{1,0:T(8,128)(2,1)}, f32[1,128]{1,0:T(1,128)}, f32[1,128]{1,0:T(1,128)}) custom-call(f32[512,2048]{1,0:T(8,128)} %fusion.22.queries.keys.values, f32[512,2048]{1,0:T(8,128)} %fusion.22.queries.keys.values, f32[512,2048]{1,0:T(8,128)} %fusion.22.queries.keys.values, f32[1,128]{1,0:T(1,128)} %get-tuple-element.505.query_gain, ...), custom_call_target="tpu_custom_call" | custom-call | flops 1610612736 | bytes 8388608 | tf_op jit(solution)/shard_map/pallas_call | solution.py:507
  492.9 7.3 %shard_map.267 = (bf16[512,2048]{1,0:T(8,128)(2,1)}, bf16[512,2048]{1,0:T(8,128)(2,1)}) custom-call(s32[6]{0:T(128)} %stack.24.info, bf16[512,2048]{1,0:T(8,128)(2,1)} %get-tuple-element.195.left, bf16[512,2048]{1,0:T(8,128)(2,1)} %copy-done.17), custom_call_target="tpu_custom_call" | custom-call | flops 2147483648 | bytes 8388608 | tf_op jit(solution)/shard_map/pallas_call | solution.py:587
  500.8 4.0 pad_maximum_fusion.1.refs_3_
  504.8 6.6 shard_map.268
  516.7 10.4 %shard_map.266 = (bf16[512,2048]{1,0:T(8,128)(2,1)}, f32[1,2048]{1,0:T(1,128)}) custom-call(bf16[512,2048]{1,0:T(8,128)(2,1)} %copy-done.17, bf16[2048,2048]{1,0:T(8,128)(2,1)} %bitcast.131, bf16[512,2048]{1,0:T(8,128)(2,1)} %get-tuple-element.224.tokens.refs_2_), custom_call_target="tpu_custom_call" | custom-call | flops 4294967296 | bytes 16777216 | tf_op jit(solution)/shard_map/pallas_call | solution.py:532
  531.2 8.6 %shard_map.270 = (bf16[512,2048]{1,0:T(8,128)(2,1)}, bf16[512,2048]{1,0:T(8,128)(2,1)}) custom-call(s32[6]{0:T(128)} %stack.26.info, bf16[512,2048]{1,0:T(8,128)(2,1)} %get-tuple-element.195.left, bf16[512,2048]{1,0:T(8,128)(2,1)} %copy-done.17, bf16[512,2048]{1,0:T(8,128)(2,1)} %copy-done.31, bf16[512,2048]{1,0:T(8,128)(2,1)} %collective-permute-done.61.rest_1_), custom_call_target="tpu_custom_call" | custom-call | flops 2147483648 | bytes 8388608 | tf_op jit(solution)/shard_map/pallas_call | solution.py:587
  539.8 2.9 fusion.6
  550.5 10.0 %collective-permute-done.65 = bf16[128,2048]{1,0:T(8,128)(2,1)S(1)} collective-permute-done((bf16[128,2048]{1,0:T(8,128)(2,1)S(1)}, bf16[128,2048]{1,0:T(8,128)(2,1)S(1)}, u32[]{:S(2)}, u32[]{:S(2)}) %collective-permute-start.65) | collective-permute-done | bytes 524320 | tf_op jit(solution)/shard_map/ppermute | solution.py:180
  560.6 2.8 pad_maximum_fusion.3.refs_2_
  563.4 5.2 shard_map.269
  579.4 7.6 %collective-permute-done.73 = bf16[128,2048]{1,0:T(8,128)(2,1)} collective-permute-done((bf16[128,2048]{1,0:T(8,128)(2,1)}, bf16[128,2048]{1,0:T(8,128)(2,1)}, u32[]{:S(2)}, u32[]{:S(2)}) %collective-permute-start.73) | collective-permute-done | bytes 524320 | tf_op jit(solution)/shard_map/ppermute | solution.py:84
  592.9 6.1 collective-permute-done.76
  606.4 9.5 %collective-permute-done.80 = bf16[128,2048]{1,0:T(8,128)(2,1)S(1)} collective-permute-done((bf16[128,2048]{1,0:T(8,128)(2,1)}, bf16[128,2048]{1,0:T(8,128)(2,1)S(1)}, u32[]{:S(2)}, u32[]{:S(2)}) %collective-permute-start.80) | collective-permute-done | bytes 524320 | tf_op jit(solution)/shard_map/ppermute | solution.py:84
  618.1 4.5 collective-permute-done.83
  627.4 2.7 collective-permute-start.86
  632.2 6.4 collective-permute-done.86
  638.7 2.7 pad_maximum_fusion.4.refs_1_
  646.4 7.5 %shard_map.271 = f32[512,2048]{1,0:T(8,128)} custom-call(bf16[512,2048]{1,0:T(8,128)(2,1)} %get-tuple-element.311.refs_0_, bf16[512,2048]{1,0:T(8,128)(2,1)} %pad_maximum_fusion.4.refs_1_, bf16[512,2048]{1,0:T(8,128)(2,1)} %get-tuple-element.224.tokens.refs_2_, f32[512,2048]{1,0:T(8,128)} %pad_maximum_fusion.1.refs_3_, f32[1,2048]{1,0:T(1,128)} %bitcast.145), custom_call_target="tpu_custom_call" | custom-call | bytes 14688256 | tf_op jit(solution)/shard_map/pallas_call | solution.py:211
  659.0 3.0 copy.62
  (528 shorter events, 208.0 us)
Async XLA Ops:
  7.2 243.1 %all-gather.6.cloned.1.call-start = ((), (), s32[]{:S(2)}) async-start(), calls=%async_computation.4 | async-start | bytes 7077888 | tf_op jit(solution)/shard_map/all_gather | solution.py:657
  10.1 18.5 %collective-permute-start.2 = (bf16[128,2048]{1,0:T(8,128)(2,1)S(1)}, bf16[128,2048]{1,0:T(8,128)(2,1)}, u32[]{:S(2)}, u32[]{:S(2)}) collective-permute-start(bf16[128,2048]{1,0:T(8,128)(2,1)S(1)} %constant_dynamic-update-slice_fusion), channel_id=1, source_target_pairs={{0,4},{2,6},{4,0},{6,2},{8,12},{10,14},{12,8},{14,10},{16,20},{18,... | collective-permute-start | bytes 1572872 | tf_op jit(solution)/shard_map/ppermute | solution.py:84
  13.1 15.5 %collective-permute-start.1 = (bf16[128,2048]{1,0:T(8,128)(2,1)S(1)}, bf16[128,2048]{1,0:T(8,128)(2,1)}, u32[]{:S(2)}, u32[]{:S(2)}) collective-permute-start(bf16[128,2048]{1,0:T(8,128)(2,1)S(1)} %constant_dynamic-update-slice_fusion), channel_id=1, source_target_pairs={{0,8},{2,10},{4,12},{6,14},{8,16},{10,18},{12,20},{14,22},{16,24},... | collective-permute-start | bytes 1572872 | tf_op jit(solution)/shard_map/ppermute | solution.py:87
  28.7 15.0 %collective-permute-start.6 = (bf16[128,2048]{1,0:T(8,128)(2,1)}, bf16[128,2048]{1,0:T(8,128)(2,1)S(1)}, u32[]{:S(2)}, u32[]{:S(2)}) collective-permute-start(bf16[128,2048]{1,0:T(8,128)(2,1)} %collective-permute-done.1), channel_id=1, source_target_pairs={{0,4},{2,6},{4,0},{6,2},{8,12},{10,14},{12,8},{14,10},{16,20},{18,... | collective-permute-start | bytes 1572872 | tf_op jit(solution)/shard_map/ppermute | solution.py:84
  29.3 16.1 %collective-permute-start.5 = (bf16[128,2048]{1,0:T(8,128)(2,1)}, bf16[128,2048]{1,0:T(8,128)(2,1)S(1)}, u32[]{:S(2)}, u32[]{:S(2)}) collective-permute-start(bf16[128,2048]{1,0:T(8,128)(2,1)} %collective-permute-done.1), channel_id=1, source_target_pairs={{0,8},{2,10},{4,12},{6,14},{8,16},{10,18},{12,20},{14,22},{16,24},... | collective-permute-start | bytes 1572872 | tf_op jit(solution)/shard_map/ppermute | solution.py:87
  32.8 19.2 %collective-permute-start.11 = (bf16[128,1536]{1,0:T(8,128)(2,1)S(1)}, bf16[128,1536]{1,0:T(8,128)(2,1)S(1)}, u32[]{:S(2)}, u32[]{:S(2)}) collective-permute-start(bf16[128,1536]{1,0:T(8,128)(2,1)S(1)} %pad_maximum_fusion.6), channel_id=1, source_target_pairs={{0,4},{2,6},{4,0},{6,2},{8,12},{10,14},{12,8},{14,10},{16,20},{18,... | collective-permute-start | bytes 1179656 | tf_op jit(solution)/shard_map/ppermute | solution.py:84
  45.3 17.6 %collective-permute-start.10 = (bf16[128,2048]{1,0:T(8,128)(2,1)S(1)}, bf16[128,2048]{1,0:T(8,128)(2,1)S(1)}, u32[]{:S(2)}, u32[]{:S(2)}) collective-permute-start(bf16[128,2048]{1,0:T(8,128)(2,1)S(1)} %collective-permute-done.5), channel_id=1, source_target_pairs={{0,4},{2,6},{4,0},{6,2},{8,12},{10,14},{12,8},{14,10},{16,20},{18,... | collective-permute-start | bytes 1572872 | tf_op jit(solution)/shard_map/ppermute | solution.py:84
  46.8 16.1 %collective-permute-start.9 = (bf16[128,2048]{1,0:T(8,128)(2,1)S(1)}, bf16[128,2048]{1,0:T(8,128)(2,1)S(1)}, u32[]{:S(2)}, u32[]{:S(2)}) collective-permute-start(bf16[128,2048]{1,0:T(8,128)(2,1)S(1)} %collective-permute-done.5), channel_id=1, source_target_pairs={{0,8},{2,10},{4,12},{6,14},{8,16},{10,18},{12,20},{14,22},{16,24},... | collective-permute-start | bytes 1572872 | tf_op jit(solution)/shard_map/ppermute | solution.py:87
  46.8 16.1 %collective-permute-start.8 = (bf16[128,2048]{1,0:T(8,128)(2,1)S(1)}, bf16[128,2048]{1,0:T(8,128)(2,1)S(1)}, u32[]{:S(2)}, u32[]{:S(2)}) collective-permute-start(bf16[128,2048]{1,0:T(8,128)(2,1)S(1)} %collective-permute-done.5), channel_id=1, source_target_pairs={{0,2},{2,0},{4,6},{6,4},{8,10},{10,8},{12,14},{14,12},{16,18},{18,... | collective-permute-start | bytes 1572872 | tf_op jit(solution)/shard_map/ppermute | solution.py:81
  65.6 192.8 %all-gather.8.cloned.1.call-start = ((), (), s32[]{:S(2)}) async-start(), calls=%async_computation.5 | async-start | bytes 7077888 | tf_op jit(solution)/shard_map/all_gather | solution.py:657
  76.5 14.9 %collective-permute-start.14 = (bf16[128,2048]{1,0:T(8,128)(2,1)S(1)}, bf16[128,2048]{1,0:T(8,128)(2,1)S(1)}, u32[]{:S(2)}, u32[]{:S(2)}) collective-permute-start(bf16[128,2048]{1,0:T(8,128)(2,1)S(1)} %collective-permute-done.9), channel_id=1, source_target_pairs={{0,4},{2,6},{4,0},{6,2},{8,12},{10,14},{12,8},{14,10},{16,20},{18,... | collective-permute-start | bytes 1572872 | tf_op jit(solution)/shard_map/ppermute | solution.py:84
  79.0 20.8 %collective-permute-start.23 = (bf16[128,1536]{1,0:T(8,128)(2,1)S(1)}, bf16[128,1536]{1,0:T(8,128)(2,1)S(1)}, u32[]{:S(2)}, u32[]{:S(2)}) collective-permute-start(bf16[128,1536]{1,0:T(8,128)(2,1)S(1)} %pad_maximum_fusion.7), channel_id=1, source_target_pairs={{0,4},{2,6},{4,0},{6,2},{8,12},{10,14},{12,8},{14,10},{16,20},{18,... | collective-permute-start | bytes 1179656 | tf_op jit(solution)/shard_map/ppermute | solution.py:84
  81.3 29.7 %collective-permute-start.24 = (bf16[128,2048]{1,0:T(8,128)(2,1)S(1)}, bf16[128,2048]{1,0:T(8,128)(2,1)S(1)}, u32[]{:S(2)}, u32[]{:S(2)}) collective-permute-start(bf16[128,2048]{1,0:T(8,128)(2,1)S(1)} %get-tuple-element.432.refs_3_), channel_id=1, source_target_pairs={{0,4},{2,6},{4,0},{6,2},{8,12},{10,14},{12,8},{14,10},{16,20},{18,... | collective-permute-start | bytes 1572872 | tf_op jit(solution)/shard_map/ppermute | solution.py:84
  91.4 23.4 %collective-permute-start.21 = (bf16[128,1024]{1,0:T(8,128)(2,1)}, bf16[128,1024]{1,0:T(8,128)(2,1)S(1)}, u32[]{:S(2)}, u32[]{:S(2)}) collective-permute-start(bf16[128,1024]{1,0:T(8,128)(2,1)} %collective-permute-done.16), channel_id=1, source_target_pairs={{0,4},{2,6},{4,0},{6,2},{8,12},{10,14},{12,8},{14,10},{16,20},{18,... | collective-permute-start | bytes 786440 | tf_op jit(solution)/shard_map/ppermute | solution.py:84
  93.0 21.8 %collective-permute-start.20 = (bf16[128,1024]{1,0:T(8,128)(2,1)}, bf16[128,1024]{1,0:T(8,128)(2,1)S(1)}, u32[]{:S(2)}, u32[]{:S(2)}) collective-permute-start(bf16[128,1024]{1,0:T(8,128)(2,1)} %collective-permute-done.16), channel_id=1, source_target_pairs={{0,8},{2,10},{4,12},{6,14},{8,16},{10,18},{12,20},{14,22},{16,24},... | collective-permute-start | bytes 786440 | tf_op jit(solution)/shard_map/ppermute | solution.py:87
  96.4 18.4 %collective-permute-start.19 = (bf16[128,1024]{1,0:T(8,128)(2,1)}, bf16[128,1024]{1,0:T(8,128)(2,1)S(1)}, u32[]{:S(2)}, u32[]{:S(2)}) collective-permute-start(bf16[128,1024]{1,0:T(8,128)(2,1)} %collective-permute-done.16), channel_id=1, source_target_pairs={{0,2},{2,0},{4,6},{6,4},{8,10},{10,8},{12,14},{14,12},{16,18},{18,... | collective-permute-start | bytes 786440 | tf_op jit(solution)/shard_map/ppermute | solution.py:81
  115.9 208.6 %all-gather.4.cloned.1.call-start = ((), (), s32[]{:S(2)}) async-start(), calls=%async_computation.3 | async-start | bytes 7077888 | tf_op jit(solution)/shard_map/all_gather | solution.py:657
  116.7 40.2 %collective-permute-start.33 = (bf16[128,1536]{1,0:T(8,128)(2,1)}, bf16[128,1536]{1,0:T(8,128)(2,1)}, u32[]{:S(2)}, u32[]{:S(2)}) collective-permute-start(bf16[128,1536]{1,0:T(8,128)(2,1)} %pad_maximum_fusion.8), channel_id=1, source_target_pairs={{0,4},{2,6},{4,0},{6,2},{8,12},{10,14},{12,8},{14,10},{16,20},{18,... | collective-permute-start | bytes 1179656 | tf_op jit(solution)/shard_map/ppermute | solution.py:84
  121.9 22.7 %collective-permute-start.28 = (bf16[128,1024]{1,0:T(8,128)(2,1)S(1)}, bf16[128,1024]{1,0:T(8,128)(2,1)S(1)}, u32[]{:S(2)}, u32[]{:S(2)}) collective-permute-start(bf16[128,1024]{1,0:T(8,128)(2,1)S(1)} %collective-permute-done.20), channel_id=1, source_target_pairs={{0,4},{2,6},{4,0},{6,2},{8,12},{10,14},{12,8},{14,10},{16,20},{18,... | collective-permute-start | bytes 786440 | tf_op jit(solution)/shard_map/ppermute | solution.py:84
  122.6 22.1 %collective-permute-start.27 = (bf16[128,1024]{1,0:T(8,128)(2,1)S(1)}, bf16[128,1024]{1,0:T(8,128)(2,1)S(1)}, u32[]{:S(2)}, u32[]{:S(2)}) collective-permute-start(bf16[128,1024]{1,0:T(8,128)(2,1)S(1)} %collective-permute-done.20), channel_id=1, source_target_pairs={{0,8},{2,10},{4,12},{6,14},{8,16},{10,18},{12,20},{14,22},{16,24},... | collective-permute-start | bytes 786440 | tf_op jit(solution)/shard_map/ppermute | solution.py:87
  124.4 20.3 %collective-permute-start.26 = (bf16[128,1024]{1,0:T(8,128)(2,1)S(1)}, bf16[128,1024]{1,0:T(8,128)(2,1)S(1)}, u32[]{:S(2)}, u32[]{:S(2)}) collective-permute-start(bf16[128,1024]{1,0:T(8,128)(2,1)S(1)} %collective-permute-done.20), channel_id=1, source_target_pairs={{0,2},{2,0},{4,6},{6,4},{8,10},{10,8},{12,14},{14,12},{16,18},{18,... | collective-permute-start | bytes 786440 | tf_op jit(solution)/shard_map/ppermute | solution.py:81
  124.4 20.2 %collective-permute-start.25 = (bf16[128,1024]{1,0:T(8,128)(2,1)S(1)}, bf16[128,1024]{1,0:T(8,128)(2,1)S(1)}, u32[]{:S(2)}, u32[]{:S(2)}) collective-permute-start(bf16[128,1024]{1,0:T(8,128)(2,1)S(1)} %collective-permute-done.21), channel_id=1, source_target_pairs={{0,2},{2,0},{4,6},{6,4},{8,10},{10,8},{12,14},{14,12},{16,18},{18,... | collective-permute-start | bytes 786440 | tf_op jit(solution)/shard_map/ppermute | solution.py:81
  159.3 416.9 %reduce-scatter.4.cloned.1.call-start = ((), (), s32[]{:S(2)}) async-start(), calls=%async_computation.6 | async-start | bytes 7077888 | tf_op jit(solution)/shard_map/reduce_scatter | solution.py:850
  163.9 41.8 %collective-permute-start.39 = (bf16[128,2048]{1,0:T(8,128)(2,1)S(1)}, bf16[128,2048]{1,0:T(8,128)(2,1)}, u32[]{:S(2)}, u32[]{:S(2)}) collective-permute-start(bf16[128,2048]{1,0:T(8,128)(2,1)S(1)} %copy-done.32), channel_id=1, source_target_pairs={{0,4},{2,6},{4,0},{6,2},{8,12},{10,14},{12,8},{14,10},{16,20},{18,... | collective-permute-start | bytes 1572872 | tf_op jit(solution)/shard_map/ppermute | solution.py:84
  164.4 32.0 %collective-permute-start.37 = (bf16[128,2048]{1,0:T(8,128)(2,1)S(1)}, bf16[128,2048]{1,0:T(8,128)(2,1)S(1)}, u32[]{:S(2)}, u32[]{:S(2)}) collective-permute-start(bf16[128,2048]{1,0:T(8,128)(2,1)S(1)} %copy-done.33), channel_id=1, source_target_pairs={{0,4},{2,6},{4,0},{6,2},{8,12},{10,14},{12,8},{14,10},{16,20},{18,... | collective-permute-start | bytes 1572872 | tf_op jit(solution)/shard_map/ppermute | solution.py:84
  175.4 21.0 %collective-permute-start.36 = (bf16[128,2048]{1,0:T(8,128)(2,1)S(1)}, bf16[128,2048]{1,0:T(8,128)(2,1)S(1)}, u32[]{:S(2)}, u32[]{:S(2)}) collective-permute-start(bf16[128,2048]{1,0:T(8,128)(2,1)S(1)} %get-tuple-element.233.refs_1_), channel_id=1, source_target_pairs={{0,1},{1,0},{2,3},{3,2},{4,5},{5,4},{6,7},{7,6},{8,9},{9,8},{10,11... | collective-permute-start | bytes 1572872 | tf_op jit(solution)/shard_map/ppermute | solution.py:180
  199.1 15.9 %collective-permute-start.41 = (bf16[128,2048]{1,0:T(8,128)(2,1)}, bf16[128,2048]{1,0:T(8,128)(2,1)S(1)}, u32[]{:S(2)}, u32[]{:S(2)}) collective-permute-start(bf16[128,2048]{1,0:T(8,128)(2,1)} %get-tuple-element.248), channel_id=1, source_target_pairs={{0,4},{2,6},{4,0},{6,2},{8,12},{10,14},{12,8},{14,10},{16,20},{18,... | collective-permute-start | bytes 1572872 | tf_op jit(solution)/shard_map/ppermute | solution.py:84
  211.3 18.6 %collective-permute-start.42 = (bf16[128,2048]{1,0:T(8,128)(2,1)}, bf16[128,2048]{1,0:T(8,128)(2,1)S(1)}, u32[]{:S(2)}, u32[]{:S(2)}) collective-permute-start(bf16[128,2048]{1,0:T(8,128)(2,1)} %get-tuple-element.249), channel_id=1, source_target_pairs={{0,4},{2,6},{4,0},{6,2},{8,12},{10,14},{12,8},{14,10},{16,20},{18,... | collective-permute-start | bytes 1572872 | tf_op jit(solution)/shard_map/ppermute | solution.py:84
  225.6 23.8 %collective-permute-start.44 = (bf16[128,2048]{1,0:T(8,128)(2,1)}, bf16[128,2048]{1,0:T(8,128)(2,1)S(1)}, u32[]{:S(2)}, u32[]{:S(2)}) collective-permute-start(bf16[128,2048]{1,0:T(8,128)(2,1)} %get-tuple-element.251), channel_id=1, source_target_pairs={{0,4},{2,6},{4,0},{6,2},{8,12},{10,14},{12,8},{14,10},{16,20},{18,... | collective-permute-start | bytes 1572872 | tf_op jit(solution)/shard_map/ppermute | solution.py:84
  227.1 21.5 %collective-permute-start.43 = (bf16[128,2048]{1,0:T(8,128)(2,1)}, bf16[128,2048]{1,0:T(8,128)(2,1)S(1)}, u32[]{:S(2)}, u32[]{:S(2)}) collective-permute-start(bf16[128,2048]{1,0:T(8,128)(2,1)} %get-tuple-element.250), channel_id=1, source_target_pairs={{0,4},{2,6},{4,0},{6,2},{8,12},{10,14},{12,8},{14,10},{16,20},{18,... | collective-permute-start | bytes 1572872 | tf_op jit(solution)/shard_map/ppermute | solution.py:84
  286.1 301.5 %reduce-scatter.6.cloned.1.call-start = ((), (), s32[]{:S(2)}) async-start(), calls=%async_computation.7 | async-start | bytes 7077888 | tf_op jit(solution)/shard_map/reduce_scatter | solution.py:850
  305.8 337.2 %reduce-scatter.8.cloned.1.call-start = ((), (), s32[]{:S(2)}) async-start(), calls=%async_computation.8 | async-start | bytes 7077888 | tf_op jit(solution)/shard_map/reduce_scatter | solution.py:850
  342.2 20.9 %collective-permute-start.45 = (bf16[128,2048]{1,0:T(8,128)(2,1)S(1)}, bf16[128,2048]{1,0:T(8,128)(2,1)S(1)}, u32[]{:S(2)}, u32[]{:S(2)}) collective-permute-start(bf16[128,2048]{1,0:T(8,128)(2,1)S(1)} %get-tuple-element.424), channel_id=1, source_target_pairs={{0,4},{2,6},{4,0},{6,2},{8,12},{10,14},{12,8},{14,10},{16,20},{18,... | collective-permute-start | bytes 1572872 | tf_op jit(solution)/shard_map/ppermute | solution.py:84
  345.0 79.0 %collective-permute-start.51 = (bf16[128,2048]{1,0:T(8,128)(2,1)}, bf16[128,2048]{1,0:T(8,128)(2,1)}, u32[]{:S(2)}, u32[]{:S(2)}) collective-permute-start(bf16[128,2048]{1,0:T(8,128)(2,1)} %get-tuple-element.421), channel_id=1, source_target_pairs={{0,4},{2,6},{4,0},{6,2},{8,12},{10,14},{12,8},{14,10},{16,20},{18,... | collective-permute-start | bytes 1572872 | tf_op jit(solution)/shard_map/ppermute | solution.py:84
  345.5 57.0 %collective-permute-start.49 = (bf16[128,2048]{1,0:T(8,128)(2,1)}, bf16[128,2048]{1,0:T(8,128)(2,1)S(1)}, u32[]{:S(2)}, u32[]{:S(2)}) collective-permute-start(bf16[128,2048]{1,0:T(8,128)(2,1)} %get-tuple-element.422), channel_id=1, source_target_pairs={{0,4},{2,6},{4,0},{6,2},{8,12},{10,14},{12,8},{14,10},{16,20},{18,... | collective-permute-start | bytes 1572872 | tf_op jit(solution)/shard_map/ppermute | solution.py:84
  347.0 40.2 %collective-permute-start.47 = (bf16[128,2048]{1,0:T(8,128)(2,1)S(1)}, bf16[128,2048]{1,0:T(8,128)(2,1)S(1)}, u32[]{:S(2)}, u32[]{:S(2)}) collective-permute-start(bf16[128,2048]{1,0:T(8,128)(2,1)S(1)} %get-tuple-element.423), channel_id=1, source_target_pairs={{0,4},{2,6},{4,0},{6,2},{8,12},{10,14},{12,8},{14,10},{16,20},{18,... | collective-permute-start | bytes 1572872 | tf_op jit(solution)/shard_map/ppermute | solution.py:84
  364.4 22.8 %collective-permute-start.46 = (bf16[128,2048]{1,0:T(8,128)(2,1)S(1)}, bf16[128,2048]{1,0:T(8,128)(2,1)S(1)}, u32[]{:S(2)}, u32[]{:S(2)}) collective-permute-start(bf16[128,2048]{1,0:T(8,128)(2,1)S(1)} %add_convert_fusion.10.refs_6_.refs_0_), channel_id=1, source_target_pairs={{0,1},{1,0},{2,3},{3,2},{4,5},{5,4},{6,7},{7,6},{8,9},{9,8},{10,11... | collective-permute-start | bytes 1572872 | tf_op jit(solution)/shard_map/ppermute | solution.py:180
  405.0 18.9 %collective-permute-start.50 = (bf16[128,2048]{1,0:T(8,128)(2,1)S(1)}, bf16[128,2048]{1,0:T(8,128)(2,1)}, u32[]{:S(2)}, u32[]{:S(2)}) collective-permute-start(bf16[128,2048]{1,0:T(8,128)(2,1)S(1)} %add_convert_fusion.8.refs_6_.refs_0_), channel_id=1, source_target_pairs={{0,1},{1,0},{2,3},{3,2},{4,5},{5,4},{6,7},{7,6},{8,9},{9,8},{10,11... | collective-permute-start | bytes 1572872 | tf_op jit(solution)/shard_map/ppermute | solution.py:180
  407.0 81.1 %collective-permute-start.58 = (bf16[128,2048]{1,0:T(8,128)(2,1)}, bf16[128,2048]{1,0:T(8,128)(2,1)}, u32[]{:S(2)}, u32[]{:S(2)}) collective-permute-start(bf16[128,2048]{1,0:T(8,128)(2,1)} %get-tuple-element.418), channel_id=1, source_target_pairs={{0,4},{2,6},{4,0},{6,2},{8,12},{10,14},{12,8},{14,10},{16,20},{18,... | collective-permute-start | bytes 1572872 | tf_op jit(solution)/shard_map/ppermute | solution.py:84
  408.5 59.9 %collective-permute-start.54 = (bf16[128,2048]{1,0:T(8,128)(2,1)}, bf16[128,2048]{1,0:T(8,128)(2,1)}, u32[]{:S(2)}, u32[]{:S(2)}) collective-permute-start(bf16[128,2048]{1,0:T(8,128)(2,1)} %get-tuple-element.419), channel_id=1, source_target_pairs={{0,4},{2,6},{4,0},{6,2},{8,12},{10,14},{12,8},{14,10},{16,20},{18,... | collective-permute-start | bytes 1572872 | tf_op jit(solution)/shard_map/ppermute | solution.py:84
  409.1 30.7 %collective-permute-start.53 = (bf16[128,2048]{1,0:T(8,128)(2,1)}, bf16[128,2048]{1,0:T(8,128)(2,1)}, u32[]{:S(2)}, u32[]{:S(2)}) collective-permute-start(bf16[128,2048]{1,0:T(8,128)(2,1)} %get-tuple-element.420), channel_id=1, source_target_pairs={{0,4},{2,6},{4,0},{6,2},{8,12},{10,14},{12,8},{14,10},{16,20},{18,... | collective-permute-start | bytes 1572872 | tf_op jit(solution)/shard_map/ppermute | solution.py:84
  451.4 17.0 %collective-permute-start.56 = (bf16[512,1024]{1,0:T(8,128)(2,1)}, bf16[512,1024]{1,0:T(8,128)(2,1)S(1)}, u32[]{:S(2)}, u32[]{:S(2)}) collective-permute-start(bf16[512,1024]{1,0:T(8,128)(2,1)} %get-tuple-element.284), channel_id=1, source_target_pairs={{0,2},{2,0},{4,6},{6,4},{8,10},{10,8},{12,14},{14,12},{16,18},{18,... | collective-permute-start | bytes 3145736 | tf_op jit(solution)/shard_map/ppermute | solution.py:81
  451.4 17.0 %collective-permute-start.57 = (bf16[512,1024]{1,0:T(8,128)(2,1)}, bf16[512,1024]{1,0:T(8,128)(2,1)S(1)}, u32[]{:S(2)}, u32[]{:S(2)}) collective-permute-start(bf16[512,1024]{1,0:T(8,128)(2,1)} %get-tuple-element.285), channel_id=1, source_target_pairs={{0,2},{2,0},{4,6},{6,4},{8,10},{10,8},{12,14},{14,12},{16,18},{18,... | collective-permute-start | bytes 3145736 | tf_op jit(solution)/shard_map/ppermute | solution.py:81
  453.4 15.0 %collective-permute-start.55 = (bf16[128,2048]{1,0:T(8,128)(2,1)S(1)}, bf16[128,2048]{1,0:T(8,128)(2,1)}, u32[]{:S(2)}, u32[]{:S(2)}) collective-permute-start(bf16[128,2048]{1,0:T(8,128)(2,1)S(1)} %add_convert_fusion.6), channel_id=1, source_target_pairs={{0,1},{1,0},{2,3},{3,2},{4,5},{5,4},{6,7},{7,6},{8,9},{9,8},{10,11... | collective-permute-start | bytes 1572872 | tf_op jit(solution)/shard_map/ppermute | solution.py:180
  471.3 16.9 %collective-permute-start.59 = (bf16[128,2048]{1,0:T(8,128)(2,1)S(1)}, bf16[128,2048]{1,0:T(8,128)(2,1)S(1)}, u32[]{:S(2)}, u32[]{:S(2)}) collective-permute-start(bf16[128,2048]{1,0:T(8,128)(2,1)S(1)} %add_convert_fusion.5), channel_id=1, source_target_pairs={{0,1},{1,0},{2,3},{3,2},{4,5},{5,4},{6,7},{7,6},{8,9},{9,8},{10,11... | collective-permute-start | bytes 1572872 | tf_op jit(solution)/shard_map/ppermute | solution.py:180
  474.5 52.5 %collective-permute-start.62 = (bf16[128,2048]{1,0:T(8,128)(2,1)}, bf16[128,2048]{1,0:T(8,128)(2,1)}, u32[]{:S(2)}, u32[]{:S(2)}) collective-permute-start(bf16[128,2048]{1,0:T(8,128)(2,1)} %get-tuple-element.417), channel_id=1, source_target_pairs={{0,4},{2,6},{4,0},{6,2},{8,12},{10,14},{12,8},{14,10},{16,20},{18,... | collective-permute-start | bytes 1572872 | tf_op jit(solution)/shard_map/ppermute | solution.py:84
  500.2 28.9 %collective-permute-start.60 = (bf16[512,2048]{1,0:T(8,128)(2,1)}, bf16[512,2048]{1,0:T(8,128)(2,1)S(1)}, u32[]{:S(2)}, u32[]{:S(2)}) collective-permute-start(bf16[512,2048]{1,0:T(8,128)(2,1)} %get-tuple-element.301), channel_id=1, source_target_pairs={{0,2},{2,0},{4,6},{6,4},{8,10},{10,8},{12,14},{14,12},{16,18},{18,... | collective-permute-start | bytes 6291464 | tf_op jit(solution)/shard_map/ppermute | solution.py:81
  500.2 28.9 %collective-permute-start.61 = (bf16[512,2048]{1,0:T(8,128)(2,1)}, bf16[512,2048]{1,0:T(8,128)(2,1)}, u32[]{:S(2)}, u32[]{:S(2)}) collective-permute-start(bf16[512,2048]{1,0:T(8,128)(2,1)} %get-tuple-element.302), channel_id=1, source_target_pairs={{0,2},{2,0},{4,6},{6,4},{8,10},{10,8},{12,14},{14,12},{16,18},{18,... | collective-permute-start | bytes 6291464 | tf_op jit(solution)/shard_map/ppermute | solution.py:81
  513.7 54.9 %collective-permute-start.68 = (bf16[128,1024]{1,0:T(8,128)(2,1)}, bf16[128,1024]{1,0:T(8,128)(2,1)}, u32[]{:S(2)}, u32[]{:S(2)}) collective-permute-start(bf16[128,1024]{1,0:T(8,128)(2,1)} %get-tuple-element.447), channel_id=1, source_target_pairs={{0,4},{2,6},{4,0},{6,2},{8,12},{10,14},{12,8},{14,10},{16,20},{18,... | collective-permute-start | bytes 786440 | tf_op jit(solution)/shard_map/ppermute | solution.py:84
  527.1 23.3 %collective-permute-start.64 = (bf16[128,1024]{1,0:T(8,128)(2,1)}, bf16[128,1024]{1,0:T(8,128)(2,1)S(1)}, u32[]{:S(2)}, u32[]{:S(2)}) collective-permute-start(bf16[128,1024]{1,0:T(8,128)(2,1)} %get-tuple-element.448), channel_id=1, source_target_pairs={{0,4},{2,6},{4,0},{6,2},{8,12},{10,14},{12,8},{14,10},{16,20},{18,... | collective-permute-start | bytes 786440 | tf_op jit(solution)/shard_map/ppermute | solution.py:84
  529.8 19.1 %collective-permute-start.70 = (f32[4352]{0:T(1024)S(1)}, f32[4352]{0:T(1024)S(1)}, u32[]{:S(2)}, u32[]{:S(2)}) collective-permute-start(f32[4352]{0:T(1024)S(1)} %pad_maximum_fusion.11), channel_id=1, source_target_pairs={{0,1},{1,0},{2,3},{3,2},{4,5},{5,4},{6,7},{7,6},{8,9},{9,8},{10,11... | collective-permute-start | bytes 52232 | tf_op jit(solution)/shard_map/ppermute | solution.py:180
  542.7 28.0 %collective-permute-start.66 = (bf16[128,2048]{1,0:T(8,128)(2,1)}, bf16[128,2048]{1,0:T(8,128)(2,1)S(1)}, u32[]{:S(2)}, u32[]{:S(2)}) collective-permute-start(bf16[128,2048]{1,0:T(8,128)(2,1)} %get-tuple-element.416), channel_id=1, source_target_pairs={{0,4},{2,6},{4,0},{6,2},{8,12},{10,14},{12,8},{14,10},{16,20},{18,... | collective-permute-start | bytes 1572872 | tf_op jit(solution)/shard_map/ppermute | solution.py:84
  549.0 22.3 %collective-permute-start.69 = (bf16[128,2048]{1,0:T(8,128)(2,1)S(1)}, bf16[128,2048]{1,0:T(8,128)(2,1)S(1)}, u32[]{:S(2)}, u32[]{:S(2)}) collective-permute-start(bf16[128,2048]{1,0:T(8,128)(2,1)S(1)} %get-tuple-element.412), channel_id=1, source_target_pairs={{0,1},{1,0},{2,3},{3,2},{4,5},{5,4},{6,7},{7,6},{8,9},{9,8},{10,11... | collective-permute-start | bytes 1572872 | tf_op jit(solution)/shard_map/ppermute | solution.py:180
  550.4 18.8 %collective-permute-start.71 = (f32[4352]{0:T(1024)S(1)}, f32[4352]{0:T(1024)S(1)}, u32[]{:S(2)}, u32[]{:S(2)}) collective-permute-start(f32[4352]{0:T(1024)S(1)} %fusion.3), channel_id=1, source_target_pairs={{0,2},{2,0},{4,6},{6,4},{8,10},{10,8},{12,14},{14,12},{16,18},{18,... | collective-permute-start | bytes 52232 | tf_op jit(solution)/shard_map/ppermute | solution.py:924
  569.2 17.8 %collective-permute-start.73 = (bf16[128,2048]{1,0:T(8,128)(2,1)}, bf16[128,2048]{1,0:T(8,128)(2,1)}, u32[]{:S(2)}, u32[]{:S(2)}) collective-permute-start(bf16[128,2048]{1,0:T(8,128)(2,1)} %get-tuple-element.415), channel_id=1, source_target_pairs={{0,4},{2,6},{4,0},{6,2},{8,12},{10,14},{12,8},{14,10},{16,20},{18,... | collective-permute-start | bytes 1572872 | tf_op jit(solution)/shard_map/ppermute | solution.py:84
  570.7 18.0 %collective-permute-start.77 = (bf16[128,2048]{1,0:T(8,128)(2,1)}, bf16[128,2048]{1,0:T(8,128)(2,1)}, u32[]{:S(2)}, u32[]{:S(2)}) collective-permute-start(bf16[128,2048]{1,0:T(8,128)(2,1)} %get-tuple-element.411), channel_id=1, source_target_pairs={{0,1},{1,0},{2,3},{3,2},{4,5},{5,4},{6,7},{7,6},{8,9},{9,8},{10,11... | collective-permute-start | bytes 1572872 | tf_op jit(solution)/shard_map/ppermute | solution.py:180
  572.0 18.3 %collective-permute-start.78 = (f32[4352]{0:T(1024)}, f32[4352]{0:T(1024)}, u32[]{:S(2)}, u32[]{:S(2)}) collective-permute-start(f32[4352]{0:T(1024)} %add.459), channel_id=1, source_target_pairs={{0,4},{2,6},{4,0},{6,2},{8,12},{10,14},{12,8},{14,10},{16,20},{18,... | collective-permute-start | bytes 52232 | tf_op jit(solution)/shard_map/ppermute | solution.py:924
  573.9 17.4 %collective-permute-start.72 = (bf16[128,2048]{1,0:T(8,128)(2,1)S(1)}, bf16[128,2048]{1,0:T(8,128)(2,1)}, u32[]{:S(2)}, u32[]{:S(2)}) collective-permute-start(bf16[128,2048]{1,0:T(8,128)(2,1)S(1)} %add_convert_fusion.2), channel_id=1, source_target_pairs={{0,8},{2,10},{4,12},{6,14},{8,16},{10,18},{12,20},{14,22},{16,24},... | collective-permute-start | bytes 1572872 | tf_op jit(solution)/shard_map/ppermute | solution.py:87
  588.7 15.9 %collective-permute-start.82 = (bf16[128,1024]{1,0:T(8,128)(2,1)}, bf16[128,1024]{1,0:T(8,128)(2,1)S(1)}, u32[]{:S(2)}, u32[]{:S(2)}) collective-permute-start(bf16[128,1024]{1,0:T(8,128)(2,1)} %get-tuple-element.445), channel_id=1, source_target_pairs={{0,4},{2,6},{4,0},{6,2},{8,12},{10,14},{12,8},{14,10},{16,20},{18,... | collective-permute-start | bytes 786440 | tf_op jit(solution)/shard_map/ppermute | solution.py:84
  590.3 25.6 %collective-permute-start.80 = (bf16[128,2048]{1,0:T(8,128)(2,1)}, bf16[128,2048]{1,0:T(8,128)(2,1)S(1)}, u32[]{:S(2)}, u32[]{:S(2)}) collective-permute-start(bf16[128,2048]{1,0:T(8,128)(2,1)} %get-tuple-element.414), channel_id=1, source_target_pairs={{0,4},{2,6},{4,0},{6,2},{8,12},{10,14},{12,8},{14,10},{16,20},{18,... | collective-permute-start | bytes 1572872 | tf_op jit(solution)/shard_map/ppermute | solution.py:84
  590.8 26.7 %collective-permute-start.84 = (bf16[128,2048]{1,0:T(8,128)(2,1)}, bf16[128,2048]{1,0:T(8,128)(2,1)S(1)}, u32[]{:S(2)}, u32[]{:S(2)}) collective-permute-start(bf16[128,2048]{1,0:T(8,128)(2,1)} %get-tuple-element.410), channel_id=1, source_target_pairs={{0,1},{1,0},{2,3},{3,2},{4,5},{5,4},{6,7},{7,6},{8,9},{9,8},{10,11... | collective-permute-start | bytes 1572872 | tf_op jit(solution)/shard_map/ppermute | solution.py:180
  591.3 31.4 %collective-permute-start.83 = (bf16[128,1536]{1,0:T(8,128)(2,1)S(1)}, bf16[128,1536]{1,0:T(8,128)(2,1)S(1)}, u32[]{:S(2)}, u32[]{:S(2)}) collective-permute-start(bf16[128,1536]{1,0:T(8,128)(2,1)S(1)} %broadcast_select_fusion.4), channel_id=1, source_target_pairs={{0,4},{2,6},{4,0},{6,2},{8,12},{10,14},{12,8},{14,10},{16,20},{18,... | collective-permute-start | bytes 1179656 | tf_op jit(solution)/shard_map/ppermute | solution.py:84
  600.1 23.7 %collective-permute-start.81 = (bf16[128,1024]{1,0:T(8,128)(2,1)S(1)}, bf16[128,1024]{1,0:T(8,128)(2,1)S(1)}, u32[]{:S(2)}, u32[]{:S(2)}) collective-permute-start(bf16[128,1024]{1,0:T(8,128)(2,1)S(1)} %add_convert_fusion.11), channel_id=1, source_target_pairs={{0,8},{2,10},{4,12},{6,14},{8,16},{10,18},{12,20},{14,22},{16,24},... | collective-permute-start | bytes 786440 | tf_op jit(solution)/shard_map/ppermute | solution.py:87
  604.7 19.1 %collective-permute-start.79 = (bf16[128,2048]{1,0:T(8,128)(2,1)S(1)}, bf16[128,2048]{1,0:T(8,128)(2,1)S(1)}, u32[]{:S(2)}, u32[]{:S(2)}) collective-permute-start(bf16[128,2048]{1,0:T(8,128)(2,1)S(1)} %add_convert_fusion.1), channel_id=1, source_target_pairs={{0,8},{2,10},{4,12},{6,14},{8,16},{10,18},{12,20},{14,22},{16,24},... | collective-permute-start | bytes 1572872 | tf_op jit(solution)/shard_map/ppermute | solution.py:87
  (130 other events, 1161.7 us)
Sparse Core Ops, SparseCore 0:
  65.7 75.1 all-gather.5
  143.1 63.3 all-gather.7
  208.2 63.3 all-gather.3
  286.2 69.5 reduce-scatter.3
  358.0 68.1 reduce-scatter.5
  474.6 68.4 reduce-scatter.7

commit v2 on v1

v2 whole, which is shorter than its diff:
```python
import functools

import jax
import jax.numpy as jnp
from jax import lax
from jax.experimental import pallas as pl
from jax.experimental.pallas import tpu as pltpu
from jax.sharding import PartitionSpec as P

HEAD_SIZE = 128
BLK = 64


epsilon = 1e-06
rope_base = 1000000.0


def matrix_product(left, right):
    return jnp.dot(left, right, preferred_element_type=jnp.float32)


def inner_left(left, right):
    return lax.dot_general(
        left, right, (((0,), (0,)), ((), ())), preferred_element_type=jnp.float32
    )


def inner_right(left, right):
    return lax.dot_general(
        left, right, (((1,), (1,)), ((), ())), preferred_element_type=jnp.float32
    )


def layout(lengths, count_of_rows):
    padded = (lengths + BLK - 1) // BLK * BLK
    starts = jnp.cumsum(padded) - padded
    row_index = jnp.arange(count_of_rows, dtype=jnp.int32)
    inside = (row_index[:, None] >= starts[None, :]) & (
        row_index[:, None] < (starts + lengths)[None, :]
    )
    live_rows = jnp.any(inside, axis=1)
    slot_index = jnp.arange(lengths.shape[0], dtype=jnp.int32)
    owning = jnp.sum(jnp.where(inside, slot_index[None, :], 0), axis=1)
    position = jnp.sum(jnp.where(inside, row_index[:, None] - starts[None, :], 0), axis=1)
    segment = jnp.where(live_rows, owning, -1 - row_index)
    return (live_rows, segment, position)


def rotation(position, width):
    half_width = width // 2
    frequency = jnp.power(rope_base, -(jnp.arange(half_width, dtype=jnp.float32) * 2.0) / width)
    angles = position.astype(jnp.float32)[:, None] * frequency[None, :]
    return (jnp.cos(angles)[:, None, :], jnp.sin(angles)[:, None, :])


CHUNKS = 3
PARTS = 4
LANES = 128
VMEM_LIMIT = 56 * 1024 * 1024


def add_low(left, right):
    return (left.astype(jnp.float32) + right.astype(jnp.float32)).astype(jnp.bfloat16)


class Ring:
    def __init__(self, size):
        self.size = size
        self.steps = size // 4
        index = lax.axis_index("dp")
        self.place = index // 4
        self.side = (index // 2) % 2
        self.core = index % 2
        self.places = [(self.place - 1 - i) % self.steps for i in range(self.steps)]
        self.groups = [
            [place * 4 + side * 2 + core for place in range(self.steps) for core in range(2)]
            for side in range(2)
        ]

    def swap_core(self, value):
        return lax.ppermute(value, "dp", [(i, i ^ 1) for i in range(self.size)])

    def swap_side(self, value):
        return lax.ppermute(value, "dp", [(i, i ^ 2) for i in range(self.size)])

    def shift(self, value, places):
        return lax.ppermute(
            value, "dp", [(i, (i + 4 * places) % self.size) for i in range(self.size)]
        )

    def pick(self, value, axis):
        low, high = jnp.split(value, 2, axis=axis)
        return (
            jnp.where(self.side == 0, low, high),
            jnp.where(self.side == 0, high, low),
        )

    def ordered(self, mine, other, axis):
        return jnp.where(
            self.side == 0,
            jnp.concatenate([mine, other], axis=axis),
            jnp.concatenate([other, mine], axis=axis),
        )

    def block(self, back, core, side):
        return ((self.place - back) % self.steps) * 4 + core * 2 + side


class Gather:
    def __init__(self, ring, piece):
        self.ring = ring
        self.hops, self.across, self.index = [piece], None, 0
        self.pieces, self.order = [], []

    def put(self, back, core, side, value):
        self.pieces.append(value)
        self.order.append(self.ring.block(back, core, side))

    def start(self, stages, hop=True, swap=True):
        ring, moves = self.ring, {}
        self.hops = list(stages.hold(*self.hops))
        if hop and len(self.hops) < ring.steps:
            moves["hop"] = ring.shift(self.hops[-1], 1)
        if swap and self.index < ring.steps:
            moves["side"] = ring.swap_side(self.hops[self.index])
            moves["core"] = ring.swap_core(self.hops[self.index])
        if swap and self.across is not None:
            moves["both"] = ring.swap_core(self.across)
        return moves

    def finish(self, moves):
        ring, back = self.ring, self.index
        core, side = ring.core, ring.side
        if "hop" in moves:
            self.hops.append(moves["hop"])
        if "both" in moves:
            self.put(back - 1, 1 - core, 1 - side, moves["both"])
            self.across = None
        if "side" in moves:
            self.put(back, core, side, self.hops[back])
            self.put(back, core, 1 - side, moves["side"])
            self.put(back, 1 - core, side, moves["core"])
            self.across = moves["side"]
            self.index += 1

    @property
    def done(self):
        return len(self.pieces) == self.ring.size


class Scatter:
    def __init__(self, ring, mine, other, crossed=None):
        self.ring = ring
        self.mine, self.other, self.crossed = mine, other, crossed
        self.term, self.index, self.total = None, 0, None
        if crossed is not None:
            self.add({"side": crossed[0]})

    def start(self, stages):
        moves = {}
        if self.index < self.ring.steps and self.crossed is None:
            (other,) = stages.hold(self.other[self.index])
            moves["side"] = self.ring.swap_side(other)
        if self.term is not None:
            moves["hop"] = self.ring.shift(self.term, 1)
        return moves

    def finish(self, moves):
        if self.crossed is not None:
            moves = dict(moves, side=self.crossed[self.index])
        self.add(moves)

    def add(self, moves):
        value = self.mine[self.index].astype(jnp.float32) + moves["side"].astype(jnp.float32)
        if "hop" in moves:
            value = value + moves["hop"].astype(jnp.float32)
        self.index += 1
        self.total = value
        self.term = value.astype(jnp.bfloat16) if self.index < self.ring.steps else None


class Stages:
    def __init__(self, mark):
        self.mark = mark

    def settle(self, *values):
        values, self.mark = lax.optimization_barrier((values, self.mark))
        return values

    def step(self, movers, *others):
        movers = [mover if isinstance(mover, tuple) else (mover, {}) for mover in movers]
        moves = [mover.start(self, **kind) for mover, kind in movers]
        moves, others = self.settle(moves, others)
        for (mover, _), move in zip(movers, moves):
            mover.finish(move)
        return others

    def hold(self, *values):
        return lax.optimization_barrier((values, self.mark))[0]

    @property
    def ties(self):
        return (self.mark,)


def swap_tensor(value):
    return lax.ppermute(value, "tensor", [(0, 1), (1, 0)])


def arrange(value, steps, width):
    blocks = [value[:, i * width : (i + 1) * width] for i in range(4 * steps)]
    order = [4 * place + k for place in range(steps) for k in (0, 2, 1, 3)]
    return jnp.concatenate([blocks[i] for i in order], axis=1)


def arrange_vector(vector, steps):
    return vector.reshape(steps, 2, 2, -1).swapaxes(1, 2).reshape(-1)


def loose(ties):
    return [pl.BlockSpec(memory_space=pl.ANY) for _ in ties]


def row_call(kernel, rows, block, ins, outs, sums=(), ties=(), into=None):
    arrays, specs, places, cuts = [], [], [], 1
    for value, kind in ins:
        places.append(len(arrays))
        if kind == "parts":
            cuts = len(value)
            span = rows // cuts // block
            for k, piece in enumerate(value):
                arrays.append(piece)
                specs.append(
                    pl.BlockSpec(
                        (block, piece.shape[1]),
                        lambda i, k=k, span=span: (jnp.clip(i - k * span, 0, span - 1), 0),
                    )
                )
            continue
        arrays.append(value)
        if kind == "all":
            specs.append(pl.BlockSpec(value.shape, lambda i: (0, 0)))
        else:
            first = 0 if kind == "rows" else kind
            specs.append(
                pl.BlockSpec((block, value.shape[1]), lambda i, first=first: (first + i, 0))
            )
    base, all_rows, aliases = 0, rows, {}
    count = len(arrays)
    if into is not None:
        given, base, all_rows = into
        if given is not None:
            ties = (given, *ties)
            aliases = {count: 0}
    out_specs = [pl.BlockSpec((block, c), lambda i: (base + i, 0)) for c, _ in outs]
    out_specs += [pl.BlockSpec((1, c), lambda i: (0, 0)) for c in sums]
    out_shape = [jax.ShapeDtypeStruct((all_rows, c), d) for c, d in outs]
    out_shape += [jax.ShapeDtypeStruct((1, c), jnp.float32) for c in sums]
    moved = sum(a.size * a.dtype.itemsize for a in arrays)
    moved += sum(rows * c * jnp.dtype(d).itemsize for c, d in outs)

    def body(*refs):
        given = refs[count + len(ties) :]
        if cuts == 1:
            kernel(*refs[:count], *given)
            return
        turn = pl.program_id(0) // (rows // cuts // block)
        for k in range(cuts):
            chosen = [
                refs[place + k] if kind == "parts" else refs[place]
                for place, (_, kind) in zip(places, ins)
            ]
            pl.when(turn == k)(functools.partial(kernel, *chosen, *given))

    return pl.pallas_call(
        body,
        grid=(rows // block,),
        in_specs=specs + loose(ties),
        out_specs=out_specs,
        out_shape=out_shape,
        input_output_aliases=aliases,
        compiler_params=pltpu.CompilerParams(vmem_limit_bytes=VMEM_LIMIT),
        cost_estimate=pl.CostEstimate(flops=0, bytes_accessed=moved, transcendentals=0),
    )(*arrays, *ties)


def inverse_rms(value):
    return lax.rsqrt(jnp.mean(value * value, axis=-1, keepdims=True) + epsilon)


def first_kernel(turn, tokens, cotangent, live, gain, tokens_out, upstream_out, normed_out):
    value = turn(tokens[...])
    tokens_out[...] = value
    value = value.astype(jnp.float32)
    normed_out[...] = (value * inverse_rms(value) * gain[...]).astype(jnp.bfloat16)
    back = turn(cotangent[...]).astype(jnp.float32)
    upstream_out[...] = (back * live[...]).astype(jnp.bfloat16)


def middle_kernel(tokens, mine, other, gain, middle_out, normed_out):
    branch = mine[...].astype(jnp.float32) + other[...].astype(jnp.float32)
    value = tokens[...].astype(jnp.float32) + branch
    middle_out[...] = value
    normed_out[...] = (value * inverse_rms(value) * gain[...]).astype(jnp.bfloat16)


def back_rms(value, gain, back):
    scale = inverse_rms(value)
    normed = value * scale
    pulled = back * gain
    center = jnp.mean(pulled * normed, axis=-1, keepdims=True)
    return scale * (pulled - normed * center), back * normed


def add_sum(out_ref, value):
    @pl.when(pl.program_id(0) == 0)
    def _():
        out_ref[...] = jnp.zeros_like(out_ref)

    out_ref[...] += jnp.sum(value, axis=0, keepdims=True)


def back_middle_kernel(
    mine, other, middle, upstream, gain, full, back_out, low_out, mixed_out, gain_out
):
    back = mine[...].astype(jnp.float32) + other[...].astype(jnp.float32)
    value, gain_term = back_rms(middle[...], gain[...], back)
    value = value + upstream[...].astype(jnp.float32)
    back_out[...] = value
    low = value.astype(jnp.bfloat16)
    low_out[...] = low
    mixed_out[...] = matrix_product(low, full[...]).astype(jnp.bfloat16)
    add_sum(gain_out, gain_term)


def output_kernel(turn, middle, mine, other, out):
    value = middle[...] + mine[...].astype(jnp.float32) + other[...].astype(jnp.float32)
    out[...] = turn(value).astype(jnp.bfloat16)


def token_kernel(turn, mine, other, tokens, back_middle, gain, out):
    back = mine[...].astype(jnp.float32) + other[...].astype(jnp.float32)
    value, _ = back_rms(tokens[...].astype(jnp.float32), gain[...], back)
    out[...] = turn(value + back_middle[...])


def feed_kernel(chunk, count, many, *refs):
    full, out = refs[count], refs[-1]
    block = out.shape[0]

    def picked(group, step):
        refs_of = refs[group[0] : group[1]]
        if len(refs_of) == 1:
            return refs_of[0][...]
        each = block // refs_of[0].shape[0]
        return jnp.concatenate([r[...] for r in refs_of[step * each : (step + 1) * each]], axis=0)

    def run(step):
        normed, upstream = picked((0, many), step), picked((many, count), step)
        gate = matrix_product(normed, full[:, :chunk])
        up = matrix_product(normed, full[:, chunk : 2 * chunk])
        back = matrix_product(upstream, full[:, 2 * chunk :])
        share = jax.nn.sigmoid(gate)
        active = gate * share
        out[:, :chunk] = (back * up * (share * (1.0 + gate * (1.0 - share)))).astype(jnp.bfloat16)
        out[:, chunk : 2 * chunk] = (back * active).astype(jnp.bfloat16)
        out[:, 2 * chunk :] = (active * up).astype(jnp.bfloat16)

    for step in range(2):
        pl.when(pl.program_id(0) == step)(functools.partial(run, step))


def feed_call(normed, upstream, full, ties=()):
    groups = [g if isinstance(g, list) else [g] for g in (normed, upstream)]
    rows, model_width = sum(a.shape[0] for a in groups[0]), full.shape[0]
    columns = full.shape[1]
    block = rows // 2
    specs = []
    for group in groups:
        if len(group) == 1:
            specs.append(pl.BlockSpec((block, model_width), lambda i: (i, 0)))
        else:
            specs += [pl.BlockSpec(a.shape, lambda i: (0, 0)) for a in group]
    return pl.pallas_call(
        functools.partial(feed_kernel, columns // 3, len(specs), len(groups[0])),
        grid=(2,),
        in_specs=specs + [pl.BlockSpec(full.shape, lambda i: (0, 0))] + loose(ties),
        out_specs=pl.BlockSpec((block, columns), lambda i: (i, 0)),
        out_shape=jax.ShapeDtypeStruct((rows, columns), jnp.bfloat16),
        compiler_params=pltpu.CompilerParams(vmem_limit_bytes=VMEM_LIMIT),
        cost_estimate=pl.CostEstimate(
            flops=2 * rows * model_width * columns,
            bytes_accessed=2 * (2 * rows * model_width + full.size + rows * columns),
            transcendentals=rows * columns // 3,
        ),
    )(*groups[0], *groups[1], full, *ties)


def wide_kernel(count, started, parts, *refs):
    outs, total = refs[-parts:], None
    for act, full in zip(refs[:count], refs[count : 2 * count]):
        term = inner_right(act[...], full[...])
        total = term if total is None else total + term
    if started:
        total = total + refs[2 * count][...]
    part = outs[0].shape[0]
    for i, out in enumerate(outs):
        out[...] = total[i * part : (i + 1) * part].astype(out.dtype)


def wide_call(acts, fulls, span, out_dtype, start=None, ties=(), parts=PARTS):
    lo, hi = span
    size, index = hi - lo, lo // (hi - lo)
    rows, model_width, count = acts[0].shape[0], fulls[0].shape[0], len(acts)
    tile = 512
    ins = list(acts) + list(fulls)
    specs = [pl.BlockSpec((rows, size), lambda i: (0, index))] * count
    specs += [pl.BlockSpec((tile, size), lambda i: (i, index))] * count
    if start is not None:
        ins.append(start)
        specs.append(pl.BlockSpec((rows, tile), lambda i: (0, i)))
    ins += list(ties)
    specs += [pl.BlockSpec(memory_space=pl.ANY) for _ in ties]
    return pl.pallas_call(
        functools.partial(wide_kernel, count, start is not None, parts),
        grid=(model_width // tile,),
        in_specs=specs,
        out_specs=[pl.BlockSpec((rows // parts, tile), lambda i: (0, i))] * parts,
        out_shape=[jax.ShapeDtypeStruct((rows // parts, model_width), out_dtype)] * parts,
        compiler_params=pltpu.CompilerParams(vmem_limit_bytes=VMEM_LIMIT),
        cost_estimate=pl.CostEstimate(
            flops=2 * rows * model_width * size * count,
            bytes_accessed=2 * (rows + model_width) * size * count + rows * model_width * 6,
            transcendentals=0,
        ),
    )(*ins)


def grad_kernel(split, counts, *refs):
    out = refs[-1]
    acts = refs[sum(counts) : sum(counts) + 2]
    first = 0
    total = [0.0, 0.0]
    for group, count in enumerate(counts):
        rows, act = 0, acts[group % 2]
        columns = slice(0, split) if group < 2 else slice(split, None)
        parts = [r[...] for r in refs[first : first + count]]
        left = parts[0] if count == 1 else jnp.concatenate(parts, axis=0)
        total[group // 2] = total[group // 2] + inner_left(left, act[:, columns])
        first += count
    out[:, :split] = total[0].astype(jnp.bfloat16)
    out[:, split:] = total[1].astype(jnp.bfloat16)


def grad_call(normed, upstream, acts, ties=(), place=0, places=1, into=None):
    groups = [g if isinstance(g, list) else [g] for g in (*normed, *upstream)]
    lefts = [a for group in groups for a in group]
    rows, model_width = acts[0].shape[0], lefts[0].shape[1]
    columns = acts[0].shape[1]
    tall = 512
    ins = lefts + list(acts)
    specs = [pl.BlockSpec((a.shape[0], tall), lambda i: (0, i)) for a in lefts]
    specs += [pl.BlockSpec((rows, columns), lambda i: (0, 0))] * 2
    aliases = {}
    if into is not None:
        aliases = {len(ins): 0}
        ins.append(into)
        specs.append(pl.BlockSpec(memory_space=pl.ANY))
    return pl.pallas_call(
        functools.partial(grad_kernel, columns // 3 * 2, [len(g) for g in groups]),
        grid=(model_width // tall,),
        in_specs=specs + loose(ties),
        out_specs=pl.BlockSpec((tall, columns), lambda i: (i, place)),
        out_shape=jax.ShapeDtypeStruct((model_width, places * columns), jnp.bfloat16),
        input_output_aliases=aliases,
        compiler_params=pltpu.CompilerParams(vmem_limit_bytes=VMEM_LIMIT),
        cost_estimate=pl.CostEstimate(
            flops=4 * rows * model_width * columns,
            bytes_accessed=2 * (4 * rows * model_width + 2 * rows * columns + model_width * columns),
            transcendentals=0,
        ),
    )(*ins, *ties)


def norm_rope(raw, gain, cosine, sine):
    scale = inverse_rms(raw)
    normed = raw * scale
    scaled = normed * gain
    return scaled * cosine + pltpu.roll(scaled, HEAD_SIZE // 2, 1) * sine, normed, scale


def back_norm_rope(back, normed, scale, gain, cosine, sine):
    back = back * cosine - pltpu.roll(back, HEAD_SIZE // 2, 1) * sine
    pulled = back * gain
    center = jnp.mean(pulled * normed, axis=-1, keepdims=True)
    return scale * (pulled - normed * center), back * normed


def softmax_rows(query, key, allowed):
    scores = jnp.where(allowed, inner_right(query, key) * HEAD_SIZE ** (-0.5), -1e30)
    raised = jnp.exp(scores - jnp.max(scores, axis=-1, keepdims=True))
    return raised / jnp.sum(raised, axis=-1, keepdims=True)


def allowed_pairs(segment_column, segment_row):
    count = segment_column.shape[0]
    row = lax.broadcasted_iota(jnp.int32, (count, count), 0)
    column = lax.broadcasted_iota(jnp.int32, (count, count), 1)
    return (segment_column[...] == segment_row[...]) & (column <= row)


def attend_kernel(
    queries, keys, values, query_gain, key_gain, cosine, sine, seg_column, seg_row, *rest
):
    out = rest[-1]
    allowed = allowed_pairs(seg_column, seg_row)
    cosine, sine = cosine[...], sine[...]
    key = norm_rope(keys[...], key_gain[...], cosine, sine)[0].astype(jnp.bfloat16)
    value = values[...].astype(jnp.bfloat16)
    for lo in range(0, queries.shape[1], HEAD_SIZE):
        span = slice(lo, lo + HEAD_SIZE)
        query = norm_rope(queries[:, span], query_gain[...], cosine, sine)[0]
        weights = softmax_rows(query.astype(jnp.bfloat16), key, allowed)
        out[:, span] = matrix_product(weights.astype(jnp.bfloat16), value).astype(jnp.bfloat16)


def attend_back_kernel(
    first,
    query_columns,
    key_columns,
    queries,
    keys,
    values,
    query_gain,
    key_gain,
    cosine,
    sine,
    seg_column,
    seg_row,
    *rest,
):
    out, query_gain_out, key_gain_out = rest[-3:]
    back_parts = rest[:PARTS]
    head = first + pl.program_id(0)
    wide = queries.shape[1]
    scaling = HEAD_SIZE ** (-0.5)
    allowed = allowed_pairs(seg_column, seg_row)
    cosine, sine = cosine[...], sine[...]
    key, key_normed, key_scale = norm_rope(keys[...], key_gain[...], cosine, sine)
    key = key.astype(jnp.bfloat16)
    value = values[...].astype(jnp.bfloat16)
    back_key, back_value, query_term = 0.0, 0.0, 0.0
    for lo in range(0, wide, HEAD_SIZE):
        span = slice(lo, lo + HEAD_SIZE)
        query, normed, scale = norm_rope(queries[:, span], query_gain[...], cosine, sine)
        query = query.astype(jnp.bfloat16)
        weights = softmax_rows(query, key, allowed)
        back = jnp.concatenate([b[:, span] for b in back_parts], axis=0)
        back_weights = inner_right(back, value)
        back_value = back_value + inner_left(weights.astype(jnp.bfloat16), back)
        center = jnp.sum(back_weights * weights, axis=-1, keepdims=True)
        back_scores = (weights * (back_weights - center)).astype(jnp.bfloat16)
        back_query = matrix_product(back_scores, key) * scaling
        back_key = back_key + inner_left(back_scores, query) * scaling
        back_query, term = back_norm_rope(
            back_query, normed, scale, query_gain[...], cosine, sine
        )
        query_term = query_term + term
        start = pl.multiple_of(head * wide + lo, HEAD_SIZE)
        out[:, pl.ds(start, HEAD_SIZE)] = back_query.astype(jnp.bfloat16)
    back_key, key_term = back_norm_rope(
        back_key, key_normed, key_scale, key_gain[...], cosine, sine
    )
    start = pl.multiple_of(query_columns + head * HEAD_SIZE, HEAD_SIZE)
    out[:, pl.ds(start, HEAD_SIZE)] = back_key.astype(jnp.bfloat16)
    start = pl.multiple_of(query_columns + key_columns + head * HEAD_SIZE, HEAD_SIZE)
    out[:, pl.ds(start, HEAD_SIZE)] = back_value.astype(jnp.bfloat16)
    add_sum(query_gain_out, query_term)
    add_sum(key_gain_out, key_term)


def attention_call(raw, query_columns, key_columns, gains, tables, segment, heads, back=None, ties=()):
    rows, columns = raw.shape
    first, count = heads
    wide = query_columns * HEAD_SIZE // key_columns
    first_key = query_columns // HEAD_SIZE + first
    first_value = first_key + key_columns // HEAD_SIZE
    ins = [raw, raw, raw, *gains, *tables, segment[:, None], segment[None, :]]
    specs = [
        pl.BlockSpec((rows, wide), lambda h: (0, first + h)),
        pl.BlockSpec((rows, HEAD_SIZE), lambda h: (0, first_key + h)),
        pl.BlockSpec((rows, HEAD_SIZE), lambda h: (0, first_value + h)),
    ] + [pl.BlockSpec(a.shape, lambda h: (0, 0)) for a in ins[3:]]
    params = dict(
        grid=(count,),
        compiler_params=pltpu.CompilerParams(vmem_limit_bytes=VMEM_LIMIT),
    )
    pairs = count * wide // HEAD_SIZE * rows * rows
    if back is None:
        return pl.pallas_call(
            attend_kernel,
            in_specs=specs + loose(ties),
            out_specs=pl.BlockSpec((rows, wide), lambda h: (0, h)),
            out_shape=jax.ShapeDtypeStruct((rows, count * wide), jnp.bfloat16),
            cost_estimate=pl.CostEstimate(
                flops=4 * pairs * HEAD_SIZE, bytes_accessed=5 * raw.size, transcendentals=pairs
            ),
            **params,
        )(*ins, *ties)
    gain_spec = pl.BlockSpec((1, HEAD_SIZE), lambda h: (0, 0))
    gain_shape = jax.ShapeDtypeStruct((1, HEAD_SIZE), jnp.float32)
    return pl.pallas_call(
        functools.partial(attend_back_kernel, first, query_columns, key_columns),
        in_specs=specs
        + [pl.BlockSpec((b.shape[0], wide), lambda h: (0, first + h)) for b in back]
        + loose(ties),
        out_specs=[pl.BlockSpec((rows, columns), lambda h: (0, 0)), gain_spec, gain_spec],
        out_shape=[jax.ShapeDtypeStruct((rows, columns), jnp.bfloat16), gain_shape, gain_shape],
        cost_estimate=pl.CostEstimate(
            flops=12 * pairs * HEAD_SIZE, bytes_accessed=8 * raw.size, transcendentals=pairs
        ),
        **params,
    )(*ins, *back, *ties)


def back_first_kernel(raw_grad, full, tokens, *rest):
    outs, gain_out, scale = rest[-2 - PARTS : -2], rest[-2], rest[-1]
    part, tile = outs[0].shape

    @pl.when(pl.program_id(0) == 0)
    def _():
        scale[...] = inverse_rms(tokens[...].astype(jnp.float32))

    back = inner_right(raw_grad[...], full[...])
    for i, out in enumerate(outs):
        out[...] = back[i * part : (i + 1) * part].astype(jnp.bfloat16)
    start = pl.multiple_of(pl.program_id(0) * tile, tile)
    normed = tokens[:, pl.ds(start, tile)].astype(jnp.float32) * scale[...]
    gain_out[...] = jnp.sum(back * normed, axis=0, keepdims=True)


def back_first_call(raw_grad, full, tokens, ties=()):
    rows, model_width = tokens.shape
    tile, part = 512, rows // PARTS
    return pl.pallas_call(
        back_first_kernel,
        grid=(model_width // tile,),
        in_specs=[
            pl.BlockSpec(raw_grad.shape, lambda i: (0, 0)),
            pl.BlockSpec((tile, full.shape[1]), lambda i: (i, 0)),
            pl.BlockSpec(tokens.shape, lambda i: (0, 0)),
        ]
        + [pl.BlockSpec(memory_space=pl.ANY) for _ in ties],
        out_specs=[pl.BlockSpec((part, tile), lambda i: (0, i))] * PARTS
        + [pl.BlockSpec((1, tile), lambda i: (0, i))],
        out_shape=[jax.ShapeDtypeStruct((part, model_width), jnp.bfloat16)] * PARTS
        + [jax.ShapeDtypeStruct((1, model_width), jnp.float32)],
        scratch_shapes=[pltpu.VMEM((rows, 1), jnp.float32)],
        compiler_params=pltpu.CompilerParams(vmem_limit_bytes=VMEM_LIMIT),
        cost_estimate=pl.CostEstimate(
            flops=2 * rows * full.size,
            bytes_accessed=2 * full.size + 8 * tokens.size,
            transcendentals=0,
        ),
    )(raw_grad, full, tokens, *ties)


def scatter_kernel(width, steps, lefts, gots, ties, info, *refs):
    turned, outs = refs[-1], refs[lefts + 1 + gots + ties : -1]
    left, right, got = refs[:lefts], refs[lefts], refs[lefts + 1 : lefts + 1 + gots]
    size = steps * width

    @pl.when(pl.program_id(0) == 0)
    def _():
        for k in range(2):
            side = info[1] if k == 0 else 1 - info[1]
            for i in range(steps):
                start = pl.multiple_of((info[2 + i] * 4 + info[0] * 2 + side) * width, width)
                first = 0
                for part in left:
                    block = part[:, pl.ds(start, width)].T
                    row = k * size + i * width
                    turned[row : row + width, first : first + part.shape[0]] = block
                    first += part.shape[0]

    total = matrix_product(turned[...], right[...])
    for k in range(2):
        value = total[k * size : (k + 1) * size]
        if gots:
            value = value + got[k][...].astype(jnp.float32)
        value = value.astype(jnp.bfloat16)
        each = len(outs) // 2
        rows = size // each
        for i in range(each):
            outs[k * each + i][...] = value[i * rows : (i + 1) * rows]


def scatter_call(ring, width, left, right, core, got=(), ties=(), apart=True):
    rows, columns = right.shape
    steps = ring.steps
    each = steps if apart else 1
    if 2 * width % LANES:
        blocks = jnp.concatenate(left, axis=0).reshape(rows, steps, 2, 2, width)
        outs = []
        for k, side in enumerate((ring.side, 1 - ring.side)):
            for i, place in enumerate(ring.places):
                picked = lax.dynamic_slice(
                    blocks, (0, place, core, side, 0), (rows, 1, 1, 1, width)
                )
                total = inner_left(picked.reshape(rows, width), right)
                if got:
                    total = total + got[k][i * width : (i + 1) * width].astype(jnp.float32)
                outs.append(total.astype(jnp.bfloat16))
        if apart:
            return outs[:steps], outs[steps:]
        return [jnp.concatenate(outs[:steps])], [jnp.concatenate(outs[steps:])]
    info = jnp.stack([core, ring.side] + ring.places).astype(jnp.int32)
    tile, tall = 512, steps * width // each
    outs = pl.pallas_call(
        functools.partial(scatter_kernel, width, steps, len(left), len(got), len(ties)),
        grid_spec=pltpu.PrefetchScalarGridSpec(
            num_scalar_prefetch=1,
            grid=(columns // tile,),
            in_specs=[pl.BlockSpec(a.shape, lambda i, info: (0, 0)) for a in left]
            + [pl.BlockSpec((rows, tile), lambda i, info: (0, i))]
            + [pl.BlockSpec((steps * width, tile), lambda i, info: (0, i)) for _ in got]
            + loose(ties),
            out_specs=[pl.BlockSpec((tall, tile), lambda i, info: (0, i))] * (2 * each),
            scratch_shapes=[pltpu.VMEM((2 * steps * width, rows), jnp.bfloat16)],
        ),
        out_shape=[jax.ShapeDtypeStruct((tall, columns), jnp.bfloat16)] * (2 * each),
        compiler_params=pltpu.CompilerParams(vmem_limit_bytes=VMEM_LIMIT),
        cost_estimate=pl.CostEstimate(
            flops=4 * rows * steps * width * columns,
            bytes_accessed=2 * (right.size + rows * 16 * width) + 4 * steps * width * columns,
            transcendentals=0,
        ),
    )(info, *left, right, *got, *ties)
    return outs[:each], outs[each:]


def finish_kernel(chunk, counts, info, *refs):
    count = len(counts)
    totals, others, (gate, up, down) = refs[:count], refs[count:-3], refs[-3:]
    side, width = info[0], gate.shape[0]
    half = gate.shape[1] // 2
    values = []
    for total, chunks in zip(totals, counts):
        mine = total[pl.ds(pl.multiple_of(side * width, width), width), :]
        values += [(mine[:, 3 * j * chunk : 3 * (j + 1) * chunk], side) for j in range(chunks)]
    values += [(other[...], 1 - side) for other in others]
    for j, (value, at) in enumerate(values):
        value = value.astype(jnp.float32)
        start = pl.multiple_of(at * half + j % CHUNKS * chunk, chunk)
        gate[:, pl.ds(start, chunk)] = value[:, :chunk]
        up[:, pl.ds(start, chunk)] = value[:, chunk : 2 * chunk]
        down[pl.ds(start, chunk), :] = value[:, 2 * chunk :].T


def finish_call(ring, chunk, totals, others):
    width, hidden = others[0].shape[0], 2 * CHUNKS * chunk
    counts = [a.shape[1] // (3 * chunk) for a in totals]
    shapes = [(width, hidden), (width, hidden), (hidden, width)]
    whole = [pl.BlockSpec(a.shape, lambda i, info: (0, 0)) for a in (*totals, *others)]
    return pl.pallas_call(
        functools.partial(finish_kernel, chunk, counts),
        grid_spec=pltpu.PrefetchScalarGridSpec(
            num_scalar_prefetch=1,
            grid=(1,),
            in_specs=whole,
            out_specs=[pl.BlockSpec(shape, lambda i, info: (0, 0)) for shape in shapes],
        ),
        out_shape=[jax.ShapeDtypeStruct(shape, jnp.float32) for shape in shapes],
        compiler_params=pltpu.CompilerParams(vmem_limit_bytes=VMEM_LIMIT),
        cost_estimate=pl.CostEstimate(
            flops=0, bytes_accessed=18 * hidden * width, transcendentals=0
        ),
    )(jnp.stack([ring.side]).astype(jnp.int32), *totals, *others)


def join_kernel(width, count, order, left, *rest):
    pieces, (product, whole) = rest[:count], rest[count:]
    for i, piece in enumerate(pieces):
        whole[pl.ds(pl.multiple_of(order[i] * width, width), width), :] = piece[...]
    product[...] = matrix_product(left[...], whole[...])


def join_call(gather, left):
    width, columns = gather.pieces[0].shape
    rows, model_width = left.shape
    tile = columns // 4
    count = len(gather.pieces)
    return pl.pallas_call(
        functools.partial(join_kernel, width, count),
        grid_spec=pltpu.PrefetchScalarGridSpec(
            num_scalar_prefetch=1,
            grid=(columns // tile,),
            in_specs=[pl.BlockSpec((rows, model_width), lambda i, order: (0, 0))]
            + [pl.BlockSpec((width, tile), lambda i, order: (0, i))] * count,
            out_specs=[
                pl.BlockSpec((rows, tile), lambda i, order: (0, i)),
                pl.BlockSpec((model_width, tile), lambda i, order: (0, i)),
            ],
        ),
        out_shape=[
            jax.ShapeDtypeStruct((rows, columns), jnp.float32),
            jax.ShapeDtypeStruct((model_width, columns), jnp.bfloat16),
        ],
        compiler_params=pltpu.CompilerParams(vmem_limit_bytes=VMEM_LIMIT),
        cost_estimate=pl.CostEstimate(
            flops=2 * rows * model_width * columns,
            bytes_accessed=4 * model_width * columns + 4 * rows * columns,
            transcendentals=0,
        ),
    )(jnp.stack(gather.order).astype(jnp.int32), left, *gather.pieces)


def join_wide_kernel(width, count, order, first, second, *rest):
    pieces, mixture, whole = rest[:count], rest[count], rest[count + 1]
    total, outs = rest[-1], rest[count + 2 : -1]
    for i, piece in enumerate(pieces):
        whole[pl.ds(pl.multiple_of(order[i] * width, width), width), :] = piece[...]

    @pl.when(pl.program_id(0) == 0)
    def _():
        mixture[...] = first[...]
        total[...] = inner_right(first[...], whole[...])

    @pl.when(pl.program_id(0) == 1)
    def _():
        mixture[...] = second[...]
        total[...] += inner_right(second[...], whole[...])
        part = outs[0].shape[0]
        for i, out in enumerate(outs):
            out[...] = total[i * part : (i + 1) * part, :].astype(jnp.bfloat16)


def join_wide_call(gather, left):
    width, columns = gather.pieces[0].shape
    rows, model_width = left[0].shape[0], width * len(gather.pieces)
    tile, part = columns // 2, rows // PARTS
    count = len(gather.pieces)
    return pl.pallas_call(
        functools.partial(join_wide_kernel, width, count),
        grid_spec=pltpu.PrefetchScalarGridSpec(
            num_scalar_prefetch=1,
            grid=(2,),
            in_specs=[pl.BlockSpec((rows, tile), lambda i, order: (0, 0))] * 2
            + [pl.BlockSpec((width, tile), lambda i, order: (0, i))] * count,
            out_specs=[
                pl.BlockSpec((rows, tile), lambda i, order: (0, i)),
                pl.BlockSpec((model_width, tile), lambda i, order: (0, i)),
            ]
            + [pl.BlockSpec((part, model_width), lambda i, order: (0, 0))] * PARTS,
            scratch_shapes=[pltpu.VMEM((rows, model_width), jnp.float32)],
        ),
        out_shape=[
            jax.ShapeDtypeStruct((rows, columns), jnp.bfloat16),
            jax.ShapeDtypeStruct((model_width, columns), jnp.bfloat16),
        ]
        + [jax.ShapeDtypeStruct((part, model_width), jnp.bfloat16)] * PARTS,
        compiler_params=pltpu.CompilerParams(vmem_limit_bytes=VMEM_LIMIT),
        cost_estimate=pl.CostEstimate(
            flops=2 * rows * model_width * columns,
            bytes_accessed=4 * model_width * columns + 4 * rows * model_width,
            transcendentals=0,
        ),
    )(jnp.stack(gather.order).astype(jnp.int32), *left, *gather.pieces)


def shards(
    dp_size,
    tokens,
    seq_lengths,
    first_gain,
    query_weight,
    key_matrix,
    value_matrix,
    query_norm_gain,
    key_gain,
    output_weight,
    second_gain,
    gate_weight,
    up_weight,
    down_weight,
    cotangent,
):
    ring = Ring(dp_size)
    steps = ring.steps
    rows, model_width = tokens.shape
    width = query_weight.shape[0]
    key_heads = key_matrix.shape[1] // HEAD_SIZE
    query_columns, key_columns = query_weight.shape[1], key_matrix.shape[1]
    part = rows // PARTS
    tiled = width % LANES == 0
    turned = functools.partial(arrange, steps=steps, width=width)
    turn = turned if tiled else (lambda value: value)
    if not tiled:
        tokens, cotangent = turned(tokens), turned(cotangent)

    hidden_width = gate_weight.shape[1] // 2
    chunk = hidden_width // CHUNKS
    pieces = [ring.pick(w, 1) for w in (gate_weight, up_weight, down_weight.T)]
    feed_mine, feed_other = (
        [
            jnp.concatenate([p[k][:, j * chunk : (j + 1) * chunk] for p in pieces], axis=1)
            for j in range(CHUNKS)
        ]
        for k in range(2)
    )
    feed_full = [None] * CHUNKS

    def feed_gather(j, got):
        block = ring.ordered(feed_mine[j], got, 0)
        feed_full[j] = lax.all_gather(
            block, "dp", axis=0, tiled=True, axis_index_groups=ring.groups
        )

    attention = Gather(ring, jnp.concatenate([query_weight, key_matrix, value_matrix], axis=1))
    output = Gather(ring, output_weight.T)

    live_rows, segment, position = layout(seq_lengths[0], rows)
    cosine_table, sinusoid_table = rotation(position, HEAD_SIZE)
    gain_one = arrange_vector(first_gain.astype(jnp.float32), steps)[None]
    gain_two = arrange_vector(second_gain.astype(jnp.float32), steps)[None]
    tables = (
        jnp.concatenate([cosine_table[:, 0], cosine_table[:, 0]], axis=1),
        jnp.concatenate([-sinusoid_table[:, 0], sinusoid_table[:, 0]], axis=1),
    )
    head_gains = (
        query_norm_gain.astype(jnp.float32)[None],
        key_gain.astype(jnp.float32)[None],
    )
    stages = Stages(jnp.broadcast_to(gain_one[:, :LANES], (8, LANES)) + 0.0)
    settle, step = stages.settle, stages.step
    token_rows, upstream, input_one = row_call(
        functools.partial(first_kernel, turn),
        rows,
        128,
        [
            (tokens, "rows"),
            (cotangent, "rows"),
            (live_rows[:, None].astype(jnp.float32), "rows"),
            (gain_one, "all"),
        ],
        [(model_width, jnp.bfloat16)] * 3,
    )
    for i in range(steps):
        ahead = (output, dict(hop=i != 2, swap=i == 2))
        movers = [attention, ahead]
        if i == 0:
            token_rows, upstream, input_one, tables = step(
                movers, token_rows, upstream, input_one, tables
            )
        elif i == 1:
            (got,) = step(movers, ring.swap_side(feed_other[0]))
            feed_gather(0, got)
        else:
            step(movers)
    step([attention])
    place = lax.axis_index("tensor")
    sent = [
        lax.dynamic_slice_in_dim(upstream, place * (rows // 2) + k * part, part) for k in range(2)
    ]

    late = stages.hold(*feed_other[1:])
    raw, attention_full = step([output], *join_call(attention, input_one))
    half = key_heads // 2
    attend_args = (raw, query_columns, key_columns, head_gains, tables, segment)
    mixture_low = []
    for i in range(2):
        mixed = attention_call(*attend_args, (i * half, half), ties=stages.ties)
        mixed, got = step([output], mixed, [ring.swap_side(late[0])] if i == 0 else [])
        mixture_low.append(mixed)
        if i == 0:
            feed_gather(1, got[0])
    late = stages.hold(*late)
    while not output.done:
        step([output])
    joined, got = settle(
        join_wide_call(output, mixture_low), [ring.swap_side(w) for w in late[1:]]
    )
    mixture_low, output_full, *branch_parts = joined
    for j, value in enumerate(got):
        feed_gather(2 + j, value)

    middle_parts, normed_parts, normed_other = [], [], []
    got = None
    for i in range(PARTS + 1):
        work = []
        if i:
            work = row_call(
                middle_kernel,
                part,
                part,
                [
                    (token_rows, i - 1),
                    (branch_parts[i - 1], "rows"),
                    (got, "rows"),
                    (gain_two, "all"),
                ],
                [(model_width, jnp.float32), (model_width, jnp.bfloat16)],
            )
        if i < PARTS:
            moves = [swap_tensor(branch_parts[i])]
            if i < 2:
                moves.append(ring.swap_side(stages.hold(sent[i])[0]))
            else:
                moves.append(ring.swap_side(normed_parts[i - 2]))
            moves, work, branch_parts = settle(moves, work, branch_parts)
            got = moves[0]
            if i < 2:
                sent[i] = moves[1]
            else:
                normed_other.append(moves[1])
        if i:
            middle_parts.append(work[0])
            normed_parts.append(work[1])
    got = [swap_tensor(v) for v in stages.hold(*sent)]

    span, out_span = (0, 2 * chunk), (2 * chunk, 3 * chunk)
    rest = [ring.swap_side(p) for p in normed_parts[len(normed_other) :]]
    acts = []
    for j in range(CHUNKS - 1):
        act, got, rest[j : j + 1] = settle(
            feed_call(normed_parts, upstream, feed_full[j], stages.ties), got, rest[j : j + 1]
        )
        acts.append(act)
    rest, upstream_other = settle(
        rest, [jnp.where(place == 0, a, b) for a, b in zip(sent + got, got + sent)]
    )
    normed_other += rest
    sides = (normed_parts, normed_other), (upstream, upstream_other)
    acts_other = [feed_call(normed_other, upstream_other, feed_full[0], stages.ties)]
    feed_grads = [grad_call(*sides, (acts[0], acts_other[0]))]
    for j in range(1, CHUNKS):
        acts_other.append(
            feed_call(normed_other, upstream_other, feed_full[j], (feed_grads + acts_other[1:])[-1:])
        )
    back_other = wide_call(acts_other, feed_full, span, jnp.bfloat16)
    last_grads = None
    (acts_last,) = settle(
        feed_call(normed_parts, upstream, feed_full[-1], tuple(back_other[:1]))
    )
    acts.append(acts_last)
    back_other = [back_other[0], *stages.hold(*back_other[1:])]

    back_mine = wide_call(acts, feed_full, span, jnp.float32, ties=stages.ties)
    got, back_mine = settle(ring.swap_side(back_other[0]), back_mine)
    mine = add_low(back_mine[0], got)
    back_parts, low_parts, mixed_parts, grad_second = [], [], [], 0.0
    out_other, out_mine, out_sums, out_got = None, None, [], []

    def back_middle_call(i, mine, other):
        return row_call(
            back_middle_kernel,
            part,
            part,
            [
                (mine, "rows"),
                (other, "rows"),
                (middle_parts[i], "rows"),
                (upstream, i),
                (gain_two, "all"),
                (output_full, "all"),
            ],
            [
                (model_width, jnp.float32),
                (model_width, jnp.bfloat16),
                (query_columns, jnp.bfloat16),
            ],
            [model_width],
            stages.ties,
        )

    for i in range(PARTS):
        work = []
        if i + 1 < CHUNKS:
            last_grads = grad_call(
                *sides,
                (acts[i + 1], acts_other[i + 1]),
                (mine,) + stages.ties,
                i,
                CHUNKS - 1,
                last_grads,
            )
            work = [last_grads]
        if i == PARTS - 2:
            work = [wide_call(acts_other, feed_full, out_span, jnp.bfloat16, ties=(mine,))]
        if i == PARTS - 1:
            work = [wide_call(acts, feed_full, out_span, jnp.float32, ties=(mine,))]
        done = back_middle_call(i - 1, *last) if i else []
        moves = [swap_tensor(mine)]
        if i + 1 < PARTS:
            moves.append(ring.swap_side(back_other[i + 1]))
        if i == PARTS - 1:
            moves.append(ring.swap_side(out_other[0]))
            out_other[2:] = stages.hold(*out_other[2:])
        moves, work, done = settle(moves, work, done)
        back_other[i + 2 :] = stages.hold(*back_other[i + 2 :])
        last = (mine, moves[0])
        if i + 1 < PARTS:
            mine = add_low(back_mine[i + 1], moves[1])
        if i == PARTS - 1:
            out_got.append(moves[-1])
        if i + 1 < CHUNKS:
            last_grads = work[0]
        if i == PARTS - 2:
            out_other = list(work[0])
        if i == PARTS - 1:
            out_mine = work[0]
        if i:
            back_parts.append(done[0])
            low_parts.append(done[1])
            mixed_parts.append(done[2])
            grad_second = grad_second + done[3]
    done = back_middle_call(PARTS - 1, *last)
    back_parts.append(done[0])
    low_parts.append(done[1])
    mixed_parts.append(done[2])
    grad_second = grad_second + done[3]
    feed_grads.append(last_grads)

    scattered = [
        lax.psum_scatter(
            grad, "dp", scatter_dimension=0, tiled=True, axis_index_groups=ring.groups
        )
        for grad in feed_grads
    ]

    core = ring.core
    out_other[2:] = stages.hold(*out_other[2:])
    out_sums = [add_low(out_mine[0], out_got[0])]
    far = scatter_call(
        ring, width, low_parts, mixture_low, 1 - core, ties=stages.ties, apart=False
    )
    (far,) = settle([ring.swap_core(f[0]) for f in far])
    out_other[3:] = stages.hold(*out_other[3:])
    near, across = scatter_call(
        ring, width, low_parts, mixture_low, core, far, stages.ties, apart=False
    )
    def picked(total):
        return lax.dynamic_slice_in_dim(total, (1 - ring.side) * width, width)

    work, scattered[0], got, out_next, pair = settle(
        attention_call(
            *attend_args, (0, key_heads), mixed_parts, stages.ties + tuple(near)
        ),
        scattered[0],
        [ring.swap_side(w) for w in out_other[1:]],
        swap_tensor(out_sums[0]),
        ring.swap_side(picked(*stages.hold(scattered[0]))),
    )
    raw_grad, grad_qgain, grad_kgain = work
    out_sums += [add_low(m, g) for m, g in zip(out_mine[1:], got)]
    out_done = [out_next]
    pairs_got = [pair]
    across = stages.hold(*across)

    far = scatter_call(
        ring, width, [input_one], raw_grad, 1 - core, ties=stages.ties, apart=False
    )
    far, work, out_next = settle(
        [ring.swap_core(f[0]) for f in far],
        back_first_call(
            raw_grad, attention_full, token_rows, stages.ties + (far[0][0],)
        ),
        swap_tensor(out_sums[1]),
    )
    out_done.append(out_next)
    *back_one, grad_first = work
    gains = jnp.concatenate(
        [
            arrange_vector(grad_first[0], steps),
            arrange_vector(grad_second[0], steps) * 0.5,
            grad_qgain[0],
            grad_kgain[0],
        ]
    )
    back_one_other = []
    near_one, across, gains_got = settle(
        scatter_call(ring, width, [input_one], raw_grad, core, far, stages.ties),
        ring.swap_side(across[0]),
        swap_tensor(gains),
    )
    gains = gains + gains_got
    attention_sum = Scatter(ring, *near_one)

    def places_of(value):
        return [value[i * width : (i + 1) * width] for i in range(steps)]

    output_sum = Scatter(ring, places_of(near[0]), None, places_of(across))
    def token_call(first, last, into, ties):
        ins = [
            (back_one[first:last], "parts"),
            (back_one_other[first:last], "parts"),
            (token_rows, first),
            (back_parts[first:last], "parts"),
            (gain_one, "all"),
        ]
        return row_call(
            functools.partial(token_kernel, turn),
            (last - first) * part,
            part,
            ins,
            [(model_width, jnp.float32)],
            ties=ties,
            into=(into, first, rows),
        )[0]

    distance = 1
    token_grad = block_output = None
    for i in range(steps):
        movers = [attention_sum] + ([output_sum] if output_sum.index < steps else [])
        others = []
        if i < PARTS:
            others.append(swap_tensor(*stages.hold(back_one[i])))
        if i < 2:
            others.append(swap_tensor(out_sums[2 + i]))
        if 0 < i < CHUNKS:
            pair = picked(scattered[1])[:, (i - 1) * 3 * chunk : i * 3 * chunk]
            others.append(ring.swap_side(*stages.hold(pair)))
        if i == 2:
            (block_output,) = row_call(
                functools.partial(output_kernel, turn),
                rows,
                128,
                [(middle_parts, "parts"), (out_sums, "parts"), (out_done, "parts")],
                [(model_width, jnp.bfloat16)],
                ties=stages.ties,
            )
            others.append(block_output)
        if i == steps - 1:
            early = len(back_one_other)
            token_grad = token_call(0, early, None, stages.ties)
            grads = finish_call(ring, chunk, scattered, pairs_got)
            others += [token_grad, grads]
        if distance < dp_size:
            others.append(
                lax.ppermute(gains, "dp", [(k, k ^ distance) for k in range(dp_size)])
            )
        others = list(step(movers, *others))
        if distance < dp_size:
            gains = gains + others.pop()
            distance *= 2
        if i == steps - 1:
            grads = others.pop()
            token_grad = others.pop()
        if i == 2:
            block_output = others.pop()
        if 0 < i < CHUNKS:
            pairs_got.append(others.pop())
        if i < 2:
            out_done.append(others.pop())
        if i < PARTS:
            back_one_other.append(others.pop())
    if early < PARTS:
        token_grad = token_call(early, PARTS, token_grad, stages.ties)
    if not tiled:
        token_grad, block_output = turned(token_grad), turned(block_output)
    grad_output = output_sum.total
    grad_attention = attention_sum.total
    grad_query = grad_attention[:, :query_columns]
    grad_key = grad_attention[:, query_columns : query_columns + key_columns]
    grad_value = grad_attention[:, query_columns + key_columns :]

    grad_gate, grad_up, grad_down = grads

    while distance < dp_size:
        gains = gains + lax.ppermute(gains, "dp", [(k, k ^ distance) for k in range(dp_size)])
        distance *= 2
    index = lax.axis_index("dp")

    def own_part(start, size):
        return lax.dynamic_slice_in_dim(gains, start + index * (size // dp_size), size // dp_size)

    return (
        block_output,
        token_grad,
        own_part(0, model_width),
        grad_query,
        grad_key,
        grad_value,
        own_part(2 * model_width, HEAD_SIZE),
        own_part(2 * model_width + HEAD_SIZE, HEAD_SIZE),
        grad_output.T,
        own_part(model_width, model_width),
        grad_gate,
        grad_up,
        grad_down,
    )


def solution(mesh):
    return jax.shard_map(
        functools.partial(shards, mesh.shape["dp"]),
        mesh=mesh,
        in_specs=(
            P("dp", None),
            P("dp", None),
            P(),
            P("dp", "tensor"),
            P("dp", "tensor"),
            P("dp", "tensor"),
            P(),
            P(),
            P("tensor", "dp"),
            P(),
            P("dp", "tensor"),
            P("dp", "tensor"),
            P("tensor", "dp"),
            P("dp", None),
        ),
        out_specs=(
            P("dp", None),
            P("dp", None),
            P("dp"),
            P("dp", "tensor"),
            P("dp", "tensor"),
            P("dp", "tensor"),
            P("dp"),
            P("dp"),
            P("tensor", "dp"),
            P("dp"),
            P("dp", "tensor"),
            P("dp", "tensor"),
            P("tensor", "dp"),
        ),
        check_vma=False,
    )
```

time: 680 us -> 574 us (0.84)
  local copies, waits for them, and re-layouts: 70.5 us -> 21.8 us
  other arithmetic: 52.8 us -> 24.7 us
  Pallas kernels: 257 us -> 280 us
  waiting for transfers between devices: 172 us -> 152 us
  starting transfers between devices: 87.6 us -> 72 us
  matrix products: 13.1 us -> 0 us
    ppermute x38 -> x33, waiting for transfers between devices: 139 us -> 45.2 us  [swap_side(): return lax.ppermute(value, 'dp', [(i, i ^ 2) for i in range(self.size)])]
    ppermute x12, waiting for transfers between devices: 8.14 us -> 66.9 us  [shift(): lax.ppermute(value, 'dp', [(i, (i + 4 * places) % self.size) for i in ran...]
    pallas_call x32 -> x34, Pallas kernels: 223 us -> 249 us  [the longest x12 53.2 us: row_call(): pl.pallas_call(body, grid=(rows // block,), in_specs=specs + loose(ties),...]
    unnamed x223 -> x205, local copies, waits for them, and re-layouts: 31.9 us -> 10.7 us
    concatenate x6 -> x1, other arithmetic: 14.6 us -> 1.19 us  [shards(): jnp.concatenate([query_weight, key_matrix, value_matrix], axis=1)]
    dot_general x6 -> x0, matrix products: 13.1 us -> none  [the longest x5 10.7 us: matrix_product(): return jnp.dot(left, right, preferred_element_type=jnp.float32)]
    ppermute x17 -> x19, waiting for transfers between devices: 17.9 us -> 29.8 us  [swap_tensor(): return lax.ppermute(value, 'tensor', [(0, 1), (1, 0)])]
    slice x8 -> x1, local copies, waits for them, and re-layouts: 13.1 us -> 1.3 us  [shards(): pair = picked(scattered[1])[:, (i - 1) * 3 * chunk:i * 3 * chunk]]
  transfers between devices with their start and end apart: 97 -> 93, of which waited for: 30 -> 28; matrix products, arithmetic and copies ran while one was open for 17% -> 5% of each run, Pallas kernels for 38% -> 49%
where the time goes in v2:
time: 574 us; the launch traced here: 565 us
  Pallas kernels  280 us (49%)
  waiting for transfers between devices  152 us (26%)
  starting transfers between devices  72 us (13%)
  other arithmetic  24.7 us (4%)
  local copies, waits for them, and re-layouts  21.8 us (4%)
  between operations  15.4 us (3%)
    ppermute x12, waiting for transfers between devices, shift(): lax.ppermute(value, 'dp', [(i, (i + 4 * places) % self.size) for i in ran...  66.9 us
    pallas_call x12, Pallas kernels, row_call(): pl.pallas_call(body, grid=(rows // block,), in_specs=specs + loose(ties),...  53.2 us
    pallas_call x6, Pallas kernels, feed_call(): pl.pallas_call(functools.partial(feed_kernel, columns // 3, len(specs), l...  52.7 us
    ppermute x33, waiting for transfers between devices, swap_side(): return lax.ppermute(value, 'dp', [(i, i ^ 2) for i in range(self.size)])  45.2 us
    pallas_call x4, Pallas kernels, wide_call(): pl.pallas_call(functools.partial(wide_kernel, count, start is not None, p...  38.7 us
    pallas_call x3, Pallas kernels, grad_call(): pl.pallas_call(functools.partial(grad_kernel, columns // 3 * 2, [len(g) f...  35.1 us
    ppermute x33, starting transfers between devices, swap_side(): return lax.ppermute(value, 'dp', [(i, i ^ 2) for i in range(self.size)])  34.3 us
    ppermute x19, waiting for transfers between devices, swap_tensor(): return lax.ppermute(value, 'tensor', [(0, 1), (1, 0)])  29.8 us
  transfers between devices with their start and end apart: 93, of which 28 were waited for; matrix products, arithmetic and copies ran while one was open for 5% of the time, Pallas kernels for 49%

profile of v2, /device:TPU:0, one launch (start us, length us, event | category | flops | bytes accessed | tf_op | source)
XLA Modules:
  0.0 565.4 jit_solution(12695156891227590775)
XLA Ops:
  9.9 2.9 collective-permute-start.2
  14.4 1.8 copy.53
  23.7 5.7 %shard_map.237 = (bf16[512,2048]{1,0:T(8,128)(2,1)}, bf16[512,2048]{1,0:T(8,128)(2,1)}, bf16[512,2048]{1,0:T(8,128)(2,1)}) custom-call(bf16[512,2048]{1,0:T(8,128)(2,1)} %refs_0_.1, bf16[512,2048]{1,0:T(8,128)(2,1)} %refs_1_.1, f32[512,1]{1,0:T(8,128)} %copy.54.refs_2_, f32[1,2048]{1,0:T(1,128)} %bitcast.71), custom_call_target="tpu_custom_call" | custom-call | bytes 10496000 | tf_op jit(solution)/shard_map/pallas_call | solution.py:275
  30.4 3.4 collective-permute-done.3.rest_4_
  36.4 18.2 %collective-permute-done.8.rest_8_ = bf16[128,1024]{1,0:T(8,128)(2,1)S(1)} collective-permute-done((bf16[128,1024]{1,0:T(8,128)(2,1)}, bf16[128,1024]{1,0:T(8,128)(2,1)S(1)}, u32[]{:S(2)}, u32[]{:S(2)}) %collective-permute-start.8) | collective-permute-done | bytes 262176 | tf_op jit(solution)/shard_map/ppermute | solution.py:87
  55.8 2.2 maximum_select_fusion
  60.7 6.9 %collective-permute-done.15.rest_1_ = bf16[128,1024]{1,0:T(8,128)(2,1)S(1)} collective-permute-done((bf16[128,1024]{1,0:T(8,128)(2,1)}, bf16[128,1024]{1,0:T(8,128)(2,1)S(1)}, u32[]{:S(2)}, u32[]{:S(2)}) %collective-permute-start.15) | collective-permute-done | bytes 262176 | tf_op jit(solution)/shard_map/ppermute | solution.py:84
  67.6 1.7 collective-permute-done.14.rest_2_
  69.3 6.5 %collective-permute-done.13.rest_9_ = bf16[128,2048]{1,0:T(8,128)(2,1)S(1)} collective-permute-done((bf16[128,2048]{1,0:T(8,128)(2,1)}, bf16[128,2048]{1,0:T(8,128)(2,1)S(1)}, u32[]{:S(2)}, u32[]{:S(2)}) %collective-permute-start.13) | collective-permute-done | bytes 524320 | tf_op jit(solution)/shard_map/ppermute | solution.py:84
  75.8 5.7 %collective-permute-done.12.rest_12_ = bf16[128,2048]{1,0:T(8,128)(2,1)S(1)} collective-permute-done((bf16[128,2048]{1,0:T(8,128)(2,1)}, bf16[128,2048]{1,0:T(8,128)(2,1)S(1)}, u32[]{:S(2)}, u32[]{:S(2)}) %collective-permute-start.12) | collective-permute-done | bytes 524320 | tf_op jit(solution)/shard_map/ppermute | solution.py:87
  83.9 15.4 %collective-permute-done.20.rest_12_ = bf16[128,1024]{1,0:T(8,128)(2,1)} collective-permute-done((bf16[128,1024]{1,0:T(8,128)(2,1)S(1)}, bf16[128,1024]{1,0:T(8,128)(2,1)}, u32[]{:S(2)}, u32[]{:S(2)}) %collective-permute-start.20) | collective-permute-done | bytes 262176 | tf_op jit(solution)/shard_map/ppermute | solution.py:87
  104.1 12.0 %shard_map.238 = (f32[512,2048]{1,0:T(8,128)}, bf16[2048,2048]{1,0:T(8,128)(2,1)}) custom-call(s32[16]{0:T(128)} %stack.138.order, bf16[512,2048]{1,0:T(8,128)(2,1)} %get-tuple-element.351.left.refs_0_, bf16[128,2048]{1,0:T(8,128)(2,1)} %copy-done.40, bf16[128,2048]{1,0:T(8,128)(2,1)} %collective-permute-done.2.rest_1_, ...), custom_call_target="tpu_custom_call" | custom-call | flops 4294967296 | bytes 20971520 | tf_op jit(solution)/shard_map/pallas_call | solution.py:793
  118.5 9.3 %shard_map.239.first = bf16[512,512]{1,0:T(8,128)(2,1)} custom-call(f32[512,2048]{1,0:T(8,128)} %get-tuple-element.389.queries.keys.values, f32[512,2048]{1,0:T(8,128)} %get-tuple-element.389.queries.keys.values, f32[512,2048]{1,0:T(8,128)} %get-tuple-element.389.queries.keys.values, f32[1,128]{1,0:T(1,128)} %get-tuple-element.781.query_gain, ...), custom_call_target="tpu_custom_call" | custom-call | flops 536870912 | bytes 5242880 | tf_op jit(solution)/shard_map/pallas_call | solution.py:600
  132.1 9.3 %shard_map.240.second = bf16[512,512]{1,0:T(8,128)(2,1)} custom-call(f32[512,2048]{1,0:T(8,128)} %get-tuple-element.389.queries.keys.values, f32[512,2048]{1,0:T(8,128)} %get-tuple-element.389.queries.keys.values, f32[512,2048]{1,0:T(8,128)} %get-tuple-element.389.queries.keys.values, f32[1,128]{1,0:T(1,128)} %get-tuple-element.781.query_gain, ...), custom_call_target="tpu_custom_call" | custom-call | flops 536870912 | bytes 5242880 | tf_op jit(solution)/shard_map/pallas_call | solution.py:600
  143.9 7.8 %shard_map.241 = (bf16[512,1024]{1,0:T(8,128)(2,1)}, bf16[2048,1024]{1,0:T(8,128)(2,1)}, bf16[128,2048]{1,0:T(8,128)(2,1)}, bf16[128,2048]{1,0:T(8,128)(2,1)}, b...) custom-call(s32[16]{0:T(128)} %stack.138.order, bf16[512,512]{1,0:T(8,128)(2,1)} %shard_map.239.first, ...), custom_call_target="tpu_custom_call" | custom-call | flops 2147483648 | bytes 12582912 | tf_op jit(solution)/shard_map/pallas_call | solution.py:843
  156.9 11.1 %collective-permute-done.34 = bf16[128,2048]{1,0:T(8,128)(2,1)S(1)} collective-permute-done((bf16[128,2048]{1,0:T(8,128)(2,1)S(1)}, bf16[128,2048]{1,0:T(8,128)(2,1)S(1)}, u32[]{:S(2)}, u32[]{:S(2)}) %collective-permute-start.34) | collective-permute-done | bytes 524320 | tf_op jit(solution)/shard_map/ppermute | solution.py:84
  172.1 2.8 shard_map.242
  174.9 6.6 %collective-permute-done.36 = bf16[128,2048]{1,0:T(8,128)(2,1)S(1)} collective-permute-done((bf16[128,2048]{1,0:T(8,128)(2,1)S(1)}, bf16[128,2048]{1,0:T(8,128)(2,1)S(1)}, u32[]{:S(2)}, u32[]{:S(2)}) %collective-permute-start.36) | collective-permute-done | bytes 524320 | tf_op jit(solution)/shard_map/ppermute | solution.py:84
  185.1 2.7 shard_map.243
  187.8 6.5 %collective-permute-done.37.refs_2_ = bf16[128,2048]{1,0:T(8,128)(2,1)S(1)} collective-permute-done((bf16[128,2048]{1,0:T(8,128)(2,1)S(1)}, bf16[128,2048]{1,0:T(8,128)(2,1)S(1)}, u32[]{:S(2)}, u32[]{:S(2)}) %collective-permute-start.37) | collective-permute-done | bytes 524320 | tf_op jit(solution)/shard_map/ppermute | solution.py:207
  197.1 2.8 shard_map.244
  199.9 7.1 %collective-permute-done.39.refs_2_ = bf16[128,2048]{1,0:T(8,128)(2,1)S(1)} collective-permute-done((bf16[128,2048]{1,0:T(8,128)(2,1)S(1)}, bf16[128,2048]{1,0:T(8,128)(2,1)S(1)}, u32[]{:S(2)}, u32[]{:S(2)}) %collective-permute-start.39) | collective-permute-done | bytes 524320 | tf_op jit(solution)/shard_map/ppermute | solution.py:207
  210.3 2.8 shard_map.245
  213.9 9.0 %shard_map.246.refs_13_.refs_0_ = bf16[512,1536]{1,0:T(8,128)(2,1)} custom-call(bf16[128,2048]{1,0:T(8,128)(2,1)} %get-tuple-element.441.refs_0_, bf16[128,2048]{1,0:T(8,128)(2,1)} %get-tuple-element.450.refs_1_, bf16[128,2048]{1,0:T(8,128)(2,1)} %get-tuple-element.457.refs_2_, bf16[128,2048]{1,0:T(8,128)(2,1)} %get-tuple-element.460.refs_3_, ...), custom_call_target="tpu_custom_call" | custom-call | flops 3221225472 | bytes 12058624 | tf_op jit(solution)/shard_map/pallas_call | solution.py:384
  222.9 5.6 collective-permute-done.42
  228.5 8.5 %shard_map.247.refs_1_.refs_13_ = bf16[512,1536]{1,0:T(8,128)(2,1)} custom-call(bf16[128,2048]{1,0:T(8,128)(2,1)} %get-tuple-element.441.refs_0_, bf16[128,2048]{1,0:T(8,128)(2,1)} %get-tuple-element.450.refs_1_, bf16[128,2048]{1,0:T(8,128)(2,1)} %get-tuple-element.457.refs_2_, bf16[128,2048]{1,0:T(8,128)(2,1)} %get-tuple-element.460.refs_3_, ...), custom_call_target="tpu_custom_call" | custom-call | flops 3221225472 | bytes 12058624 | tf_op jit(solution)/shard_map/pallas_call | solution.py:384
  239.2 8.8 %shard_map.248.refs_14_.refs_0_ = bf16[512,1536]{1,0:T(8,128)(2,1)} custom-call(bf16[128,2048]{1,0:T(8,128)(2,1)} %copy-done.1, bf16[128,2048]{1,0:T(8,128)(2,1)} %copy-done.2, bf16[128,2048]{1,0:T(8,128)(2,1)} %copy-done.3, bf16[128,2048]{1,0:T(8,128)(2,1)} %copy-done.4, bf16[128,2048]{1,0:T(8,128)(2,1)} %get-tuple-element.478.refs_4_.refs_9_, ...), custom_call_target="tpu_custom_call" | custom-call | flops 3221225472 | bytes 12058624 | tf_op jit(solution)/shard_map/pallas_call | solution.py:384
  248.0 11.6 %shard_map.249.refs_9_ = bf16[2048,1536]{1,0:T(8,128)(2,1)} custom-call(bf16[128,2048]{1,0:T(8,128)(2,1)} %get-tuple-element.441.refs_0_, bf16[128,2048]{1,0:T(8,128)(2,1)} %get-tuple-element.450.refs_1_, bf16[128,2048]{1,0:T(8,128)(2,1)} %get-tuple-element.457.refs_2_, bf16[128,2048]{1,0:T(8,128)(2,1)} %get-tuple-element.460.refs_3_, ...), custom_call_target="tpu_custom_call" | custom-call | flops 6442450944 | bytes 17825792 | tf_op jit(solution)/shard_map/pallas_call | solution.py:469
  259.7 8.9 %shard_map.250.refs_9_.refs_1_.refs_14_ = bf16[512,1536]{1,0:T(8,128)(2,1)} custom-call(bf16[128,2048]{1,0:T(8,128)(2,1)} %copy-done.1, bf16[128,2048]{1,0:T(8,128)(2,1)} %copy-done.2, bf16[128,2048]{1,0:T(8,128)(2,1)} %copy-done.3, bf16[128,2048]{1,0:T(8,128)(2,1)} %copy-done.4, bf16[128,2048]{1,0:T(8,128)(2,1)} %get-tuple-element.478.refs_4_.refs_9_, ...), custom_call_target="tpu_custom_call" | custom-call | flops 3221225472 | bytes 12058624 | tf_op jit(solution)/shard_map/pallas_call | solution.py:384
  268.6 9.0 %shard_map.251.refs_2_.refs_14_ = bf16[512,1536]{1,0:T(8,128)(2,1)} custom-call(bf16[128,2048]{1,0:T(8,128)(2,1)} %copy-done.1, bf16[128,2048]{1,0:T(8,128)(2,1)} %copy-done.2, bf16[128,2048]{1,0:T(8,128)(2,1)} %copy-done.3, bf16[128,2048]{1,0:T(8,128)(2,1)} %copy-done.4, bf16[128,2048]{1,0:T(8,128)(2,1)} %get-tuple-element.478.refs_4_.refs_9_, ...), custom_call_target="tpu_custom_call" | custom-call | flops 3221225472 | bytes 12058624 | tf_op jit(solution)/shard_map/pallas_call | solution.py:384
  277.7 11.4 %shard_map.252 = (bf16[128,2048]{1,0:T(8,128)(2,1)}, bf16[128,2048]{1,0:T(8,128)(2,1)}, bf16[128,2048]{1,0:T(8,128)(2,1)}, bf16[128,2048]{1,0:T(8,128)(2,1)}) custom-call(bf16[512,1536]{1,0:T(8,128)(2,1)} %shard_map.248.refs_14_.refs_0_, bf16[512,1536]{1,0:T(8,128)(2,1)} %shard_map.250.refs_9_.refs_1_.refs_14_, ...), custom_call_target="tpu_custom_call" | custom-call | flops 6442450944 | bytes 22020096 | tf_op jit(solution)/shard_map/pallas_call | solution.py:424
  289.1 1.7 collective-permute-start.45
  290.8 8.4 %shard_map.253.refs_2_.refs_13_ = bf16[512,1536]{1,0:T(8,128)(2,1)} custom-call(bf16[128,2048]{1,0:T(8,128)(2,1)} %get-tuple-element.441.refs_0_, bf16[128,2048]{1,0:T(8,128)(2,1)} %get-tuple-element.450.refs_1_, bf16[128,2048]{1,0:T(8,128)(2,1)} %get-tuple-element.457.refs_2_, bf16[128,2048]{1,0:T(8,128)(2,1)} %get-tuple-element.460.refs_3_, ...), custom_call_target="tpu_custom_call" | custom-call | flops 3221225472 | bytes 12058624 | tf_op jit(solution)/shard_map/pallas_call | solution.py:384
  299.6 11.9 %shard_map.254 = (f32[128,2048]{1,0:T(8,128)}, f32[128,2048]{1,0:T(8,128)}, f32[128,2048]{1,0:T(8,128)}, f32[128,2048]{1,0:T(8,128)}) custom-call(bf16[512,1536]{1,0:T(8,128)(2,1)} %shard_map.246.refs_13_.refs_0_, bf16[512,1536]{1,0:T(8,128)(2,1)} %shard_map.247.refs_1_.refs_13_, bf16[512,1536]{1,0:T(8,128)(2,1)} %shard_map.253.refs_2_.refs_13_, ...), custom_call_target="tpu_custom_call" | custom-call | flops 6442450944 | bytes 22020096 | tf_op jit(solution)/shard_map/pallas_call | solution.py:424
  314.2 11.8 %shard_map.255.refs_15_ = bf16[2048,3072]{1,0:T(8,128)(2,1)} custom-call(bf16[128,2048]{1,0:T(8,128)(2,1)} %get-tuple-element.441.refs_0_, bf16[128,2048]{1,0:T(8,128)(2,1)} %get-tuple-element.450.refs_1_, bf16[128,2048]{1,0:T(8,128)(2,1)} %get-tuple-element.457.refs_2_, bf16[128,2048]{1,0:T(8,128)(2,1)} %get-tuple-element.460.refs_3_, ...), custom_call_target="tpu_custom_call" | custom-call | flops 6442450944 | bytes 17825792 | tf_op jit(solution)/shard_map/pallas_call | solution.py:469
  328.8 5.2 shard_map.257
  333.9 11.6 %shard_map.256 = bf16[2048,3072]{1,0:T(8,128)(2,1)} custom-call(bf16[128,2048]{1,0:T(8,128)(2,1)} %get-tuple-element.441.refs_0_, bf16[128,2048]{1,0:T(8,128)(2,1)} %get-tuple-element.450.refs_1_, bf16[128,2048]{1,0:T(8,128)(2,1)} %get-tuple-element.457.refs_2_, bf16[128,2048]{1,0:T(8,128)(2,1)} %get-tuple-element.460.refs_3_, ...), custom_call_target="tpu_custom_call", output_to_operand_aliasing={{}: (15, {})} | custom-call | flops 6442450944 | bytes 17825792 | tf_op jit(solution)/shard_map/pallas_call | solution.py:469
  348.7 5.2 shard_map.259
  353.8 7.5 %shard_map.258 = (bf16[128,2048]{1,0:T(8,128)(2,1)}, bf16[128,2048]{1,0:T(8,128)(2,1)}, bf16[128,2048]{1,0:T(8,128)(2,1)}, bf16[128,2048]{1,0:T(8,128)(2,1)}) custom-call(bf16[512,1536]{1,0:T(8,128)(2,1)} %shard_map.248.refs_14_.refs_0_, bf16[512,1536]{1,0:T(8,128)(2,1)} %shard_map.250.refs_9_.refs_1_.refs_14_, ...), custom_call_target="tpu_custom_call" | custom-call | flops 3221225472 | bytes 14155776 | tf_op jit(solution)/shard_map/pallas_call | solution.py:424
  362.8 1.6 collective-permute-start.53
  365.0 5.2 shard_map.261
  370.2 7.8 %shard_map.260 = (f32[128,2048]{1,0:T(8,128)}, f32[128,2048]{1,0:T(8,128)}, f32[128,2048]{1,0:T(8,128)}, f32[128,2048]{1,0:T(8,128)}) custom-call(bf16[512,1536]{1,0:T(8,128)(2,1)} %shard_map.246.refs_13_.refs_0_, bf16[512,1536]{1,0:T(8,128)(2,1)} %shard_map.247.refs_1_.refs_13_, bf16[512,1536]{1,0:T(8,128)(2,1)} %shard_map.253.refs_2_.refs_13_, ...), custom_call_target="tpu_custom_call" | custom-call | flops 3221225472 | bytes 14155776 | tf_op jit(solution)/shard_map/pallas_call | solution.py:424
  378.9 5.2 shard_map.262
  384.1 5.1 shard_map.263
  393.1 1.8 collective-permute-start.57
  396.4 1.8 collective-permute-start.60
  398.1 5.7 %shard_map.264 = (bf16[512,1024]{1,0:T(8,128)(2,1)}, bf16[512,1024]{1,0:T(8,128)(2,1)}) custom-call(s32[6]{0:T(128)} %stack.58.info, bf16[128,2048]{1,0:T(8,128)(2,1)} %get-tuple-element.550.refs_0_, bf16[128,2048]{1,0:T(8,128)(2,1)} %get-tuple-element.551.refs_1_, bf16[128,2048]{1,0:T(8,128)(2,1)} %get-tuple-element.552.refs_2_, ...), custom_call_target="tpu_custom_call" | custom-call | flops 1073741824 | bytes 5242880 | tf_op jit(solution)/shard_map/pallas_call | solution.py:719
  403.9 20.9 %shard_map.265 = (bf16[512,2048]{1,0:T(8,128)(2,1)}, f32[1,128]{1,0:T(1,128)}, f32[1,128]{1,0:T(1,128)}) custom-call(f32[512,2048]{1,0:T(8,128)} %get-tuple-element.389.queries.keys.values, f32[512,2048]{1,0:T(8,128)} %get-tuple-element.389.queries.keys.values, f32[512,2048]{1,0:T(8,128)} %get-tuple-element.389.queries.keys.values, ...), custom_call_target="tpu_custom_call" | custom-call | flops 3221225472 | bytes 8388608 | tf_op jit(solution)/shard_map/pallas_call | solution.py:612
  424.9 3.0 collective-permute-done.58
  427.8 7.5 %collective-permute-done.60.refs_2_ = bf16[128,1536]{1,0:T(8,128)(2,1)S(1)} collective-permute-done((bf16[128,1536]{1,0:T(8,128)(2,1)S(1)}, bf16[128,1536]{1,0:T(8,128)(2,1)S(1)}, u32[]{:S(2)}, u32[]{:S(2)}) %collective-permute-start.60) | collective-permute-done | bytes 393248 | tf_op jit(solution)/shard_map/ppermute | solution.py:84
  435.4 7.2 %shard_map.266 = (bf16[512,2048]{1,0:T(8,128)(2,1)}, bf16[512,2048]{1,0:T(8,128)(2,1)}) custom-call(s32[6]{0:T(128)} %stack.140.info, bf16[512,2048]{1,0:T(8,128)(2,1)} %get-tuple-element.351.left.refs_0_, bf16[512,2048]{1,0:T(8,128)(2,1)} %get-tuple-element.575.refs_1_.raw_grad, ...), custom_call_target="tpu_custom_call" | custom-call | flops 2147483648 | bytes 8388608 | tf_op jit(solution)/shard_map/pallas_call | solution.py:719
  447.3 9.9 %shard_map.267 = (bf16[128,2048]{1,0:T(8,128)(2,1)}, bf16[128,2048]{1,0:T(8,128)(2,1)}, bf16[128,2048]{1,0:T(8,128)(2,1)}, bf16[128,2048]{1,0:T(8,128)(2,1)}, f32[1,2048]{1,0:T(1,128)}) custom-call(bf16[512,2048]{1,0:T(8,128)(2,1)} %get-tuple-element.575.refs_1_.raw_grad, bf16[2048,2048]{1,0:T(8,128)(2,1)} %get-tuple-element.579.full, ...), custom_call_target="tpu_custom_call" | custom-call | flops 4294967296 | bytes 16777216 | tf_op jit(solution)/shard_map/pallas_call | solution.py:645
  460.4 8.5 %shard_map.268 = (bf16[128,2048]{1,0:T(8,128)(2,1)}, bf16[128,2048]{1,0:T(8,128)(2,1)}, bf16[128,2048]{1,0:T(8,128)(2,1)}, bf16[128,2048]{1,0:T(8,128)(2,1)}, bf...) custom-call(s32[6]{0:T(128)} %stack.58.info, ...), custom_call_target="tpu_custom_call" | custom-call | flops 2147483648 | bytes 8388608 | tf_op jit(solution)/shard_map/pallas_call | solution.py:719
  472.7 9.5 %collective-permute-done.67 = bf16[128,1024]{1,0:T(8,128)(2,1)S(1)} collective-permute-done((bf16[128,1024]{1,0:T(8,128)(2,1)S(1)}, bf16[128,1024]{1,0:T(8,128)(2,1)S(1)}, u32[]{:S(2)}, u32[]{:S(2)}) %collective-permute-start.67) | collective-permute-done | bytes 262176 | tf_op jit(solution)/shard_map/ppermute | solution.py:87
  482.3 2.5 collective-permute-done.68.refs_3_
  491.2 4.9 collective-permute-done.75.refs_11_
  496.6 13.5 %collective-permute-done.73 = bf16[128,1024]{1,0:T(8,128)(2,1)S(1)} collective-permute-done((bf16[128,1024]{1,0:T(8,128)(2,1)S(1)}, bf16[128,1024]{1,0:T(8,128)(2,1)S(1)}, u32[]{:S(2)}, u32[]{:S(2)}) %collective-permute-start.73) | collective-permute-done | bytes 262176 | tf_op jit(solution)/shard_map/ppermute | solution.py:87
  516.2 7.4 %collective-permute-done.83 = f32[4352]{0:T(1024)S(1)} collective-permute-done((f32[4352]{0:T(1024)S(1)}, f32[4352]{0:T(1024)S(1)}, u32[]{:S(2)}, u32[]{:S(2)}) %collective-permute-start.83) | collective-permute-done | bytes 17440 | tf_op jit(solution)/shard_map/ppermute | solution.py:1240
  523.7 2.5 collective-permute-start.80
  526.1 5.5 shard_map.269
  535.9 2.3 collective-permute-start.84
  539.7 6.9 %shard_map.270.refs_5_ = f32[512,2048]{1,0:T(8,128)} custom-call(bf16[128,2048]{1,0:T(8,128)(2,1)} %get-tuple-element.614.refs_0_, bf16[128,2048]{1,0:T(8,128)(2,1)} %get-tuple-element.624.refs_1_, bf16[128,2048]{1,0:T(8,128)(2,1)} %get-tuple-element.637.refs_2_, bf16[128,2048]{1,0:T(8,128)(2,1)} %copy-done.31, ...), custom_call_target="tpu_custom_call" | custom-call | bytes 11542528 | tf_op jit(solution)/shard_map/pallas_call | solution.py:275
  546.6 4.5 shard_map.271
  555.4 3.3 shard_map.272
  (441 shorter events, 108.5 us)
Async XLA Ops:
  7.2 206.7 %all-gather.4.cloned.1.call-start = ((), (), s32[]{:S(2)}) async-start(), calls=%async_computation.2 | async-start | bytes 7077888 | tf_op jit(solution)/shard_map/all_gather | solution.py:915
  9.9 23.9 %collective-permute-start.2 = (bf16[128,2048]{1,0:T(8,128)(2,1)S(1)}, bf16[128,2048]{1,0:T(8,128)(2,1)}, u32[]{:S(2)}, u32[]{:S(2)}) collective-permute-start(bf16[128,2048]{1,0:T(8,128)(2,1)S(1)} %pad_maximum_fusion.rest_0_), channel_id=1, source_target_pairs={{0,4},{2,6},{4,0},{6,2},{8,12},{10,14},{12,8},{14,10},{16,20},{18,... | collective-permute-start | bytes 1572872 | tf_op jit(solution)/shard_map/ppermute | solution.py:84
  12.8 21.0 %collective-permute-start.1 = (bf16[128,2048]{1,0:T(8,128)(2,1)S(1)}, bf16[128,2048]{1,0:T(8,128)(2,1)}, u32[]{:S(2)}, u32[]{:S(2)}) collective-permute-start(bf16[128,2048]{1,0:T(8,128)(2,1)S(1)} %pad_maximum_fusion.rest_0_), channel_id=1, source_target_pairs={{0,8},{2,10},{4,12},{6,14},{8,16},{10,18},{12,20},{14,22},{16,24},... | collective-permute-start | bytes 1572872 | tf_op jit(solution)/shard_map/ppermute | solution.py:87
  14.4 19.4 %collective-permute-start = (bf16[128,2048]{1,0:T(8,128)(2,1)S(1)}, bf16[128,2048]{1,0:T(8,128)(2,1)}, u32[]{:S(2)}, u32[]{:S(2)}) collective-permute-start(bf16[128,2048]{1,0:T(8,128)(2,1)S(1)} %pad_maximum_fusion.rest_0_), channel_id=1, source_target_pairs={{0,2},{2,0},{4,6},{6,4},{8,10},{10,8},{12,14},{14,12},{16,18},{18,... | collective-permute-start | bytes 1572872 | tf_op jit(solution)/shard_map/ppermute | solution.py:81
  16.2 17.6 %collective-permute-start.3 = (bf16[128,1024]{1,0:T(8,128)(2,1)}, bf16[128,1024]{1,0:T(8,128)(2,1)}, u32[]{:S(2)}, u32[]{:S(2)}) collective-permute-start(bf16[128,1024]{1,0:T(8,128)(2,1)} %bitcast.10.rest_0_), channel_id=1, source_target_pairs={{0,8},{2,10},{4,12},{6,14},{8,16},{10,18},{12,20},{14,22},{16,24},... | collective-permute-start | bytes 786440 | tf_op jit(solution)/shard_map/ppermute | solution.py:87
  20.9 14.1 %collective-permute-start.9 = (bf16[128,1536]{1,0:T(8,128)(2,1)}, bf16[128,1536]{1,0:T(8,128)(2,1)}, u32[]{:S(2)}, u32[]{:S(2)}) collective-permute-start(bf16[128,1536]{1,0:T(8,128)(2,1)} %pad_maximum_fusion.1), channel_id=1, source_target_pairs={{0,4},{2,6},{4,0},{6,2},{8,12},{10,14},{12,8},{14,10},{16,20},{18,... | collective-permute-start | bytes 1179656 | tf_op jit(solution)/shard_map/ppermute | solution.py:84
  33.8 20.7 %collective-permute-start.7 = (bf16[128,2048]{1,0:T(8,128)(2,1)}, bf16[128,2048]{1,0:T(8,128)(2,1)}, u32[]{:S(2)}, u32[]{:S(2)}) collective-permute-start(bf16[128,2048]{1,0:T(8,128)(2,1)} %collective-permute-done.1.rest_4_), channel_id=1, source_target_pairs={{0,4},{2,6},{4,0},{6,2},{8,12},{10,14},{12,8},{14,10},{16,20},{18,... | collective-permute-start | bytes 1572872 | tf_op jit(solution)/shard_map/ppermute | solution.py:84
  34.4 20.1 %collective-permute-start.6 = (bf16[128,2048]{1,0:T(8,128)(2,1)}, bf16[128,2048]{1,0:T(8,128)(2,1)S(1)}, u32[]{:S(2)}, u32[]{:S(2)}) collective-permute-start(bf16[128,2048]{1,0:T(8,128)(2,1)} %collective-permute-done.1.rest_4_), channel_id=1, source_target_pairs={{0,8},{2,10},{4,12},{6,14},{8,16},{10,18},{12,20},{14,22},{16,24},... | collective-permute-start | bytes 1572872 | tf_op jit(solution)/shard_map/ppermute | solution.py:87
  34.4 20.2 %collective-permute-start.5 = (bf16[128,2048]{1,0:T(8,128)(2,1)}, bf16[128,2048]{1,0:T(8,128)(2,1)S(1)}, u32[]{:S(2)}, u32[]{:S(2)}) collective-permute-start(bf16[128,2048]{1,0:T(8,128)(2,1)} %collective-permute-done.1.rest_4_), channel_id=1, source_target_pairs={{0,2},{2,0},{4,6},{6,4},{8,10},{10,8},{12,14},{14,12},{16,18},{18,... | collective-permute-start | bytes 1572872 | tf_op jit(solution)/shard_map/ppermute | solution.py:81
  34.4 20.2 %collective-permute-start.4 = (bf16[128,2048]{1,0:T(8,128)(2,1)}, bf16[128,2048]{1,0:T(8,128)(2,1)S(1)}, u32[]{:S(2)}, u32[]{:S(2)}) collective-permute-start(bf16[128,2048]{1,0:T(8,128)(2,1)} %collective-permute-done.2.rest_1_), channel_id=1, source_target_pairs={{0,2},{2,0},{4,6},{6,4},{8,10},{10,8},{12,14},{14,12},{16,18},{18,... | collective-permute-start | bytes 1572872 | tf_op jit(solution)/shard_map/ppermute | solution.py:81
  35.0 19.6 %collective-permute-start.8 = (bf16[128,1024]{1,0:T(8,128)(2,1)}, bf16[128,1024]{1,0:T(8,128)(2,1)S(1)}, u32[]{:S(2)}, u32[]{:S(2)}) collective-permute-start(bf16[128,1024]{1,0:T(8,128)(2,1)} %collective-permute-done.3.rest_4_), channel_id=1, source_target_pairs={{0,8},{2,10},{4,12},{6,14},{8,16},{10,18},{12,20},{14,22},{16,24},... | collective-permute-start | bytes 786440 | tf_op jit(solution)/shard_map/ppermute | solution.py:87
  58.0 170.5 %all-gather.6.cloned.1.call-start = ((), (), s32[]{:S(2)}) async-start(), calls=%async_computation.3 | async-start | bytes 7077888 | tf_op jit(solution)/shard_map/all_gather | solution.py:915
  59.4 16.5 %collective-permute-start.13 = (bf16[128,2048]{1,0:T(8,128)(2,1)}, bf16[128,2048]{1,0:T(8,128)(2,1)S(1)}, u32[]{:S(2)}, u32[]{:S(2)}) collective-permute-start(bf16[128,2048]{1,0:T(8,128)(2,1)} %copy-done.75), channel_id=1, source_target_pairs={{0,4},{2,6},{4,0},{6,2},{8,12},{10,14},{12,8},{14,10},{16,20},{18,... | collective-permute-start | bytes 1572872 | tf_op jit(solution)/shard_map/ppermute | solution.py:84
  60.1 21.4 %collective-permute-start.12 = (bf16[128,2048]{1,0:T(8,128)(2,1)}, bf16[128,2048]{1,0:T(8,128)(2,1)S(1)}, u32[]{:S(2)}, u32[]{:S(2)}) collective-permute-start(bf16[128,2048]{1,0:T(8,128)(2,1)} %copy-done.75), channel_id=1, source_target_pairs={{0,8},{2,10},{4,12},{6,14},{8,16},{10,18},{12,20},{14,22},{16,24},... | collective-permute-start | bytes 1572872 | tf_op jit(solution)/shard_map/ppermute | solution.py:87
  60.1 21.4 %collective-permute-start.11 = (bf16[128,2048]{1,0:T(8,128)(2,1)}, bf16[128,2048]{1,0:T(8,128)(2,1)S(1)}, u32[]{:S(2)}, u32[]{:S(2)}) collective-permute-start(bf16[128,2048]{1,0:T(8,128)(2,1)} %copy-done.75), channel_id=1, source_target_pairs={{0,2},{2,0},{4,6},{6,4},{8,10},{10,8},{12,14},{14,12},{16,18},{18,... | collective-permute-start | bytes 1572872 | tf_op jit(solution)/shard_map/ppermute | solution.py:81
  60.1 21.4 %collective-permute-start.10 = (bf16[128,2048]{1,0:T(8,128)(2,1)}, bf16[128,2048]{1,0:T(8,128)(2,1)S(1)}, u32[]{:S(2)}, u32[]{:S(2)}) collective-permute-start(bf16[128,2048]{1,0:T(8,128)(2,1)} %collective-permute-done.7.rest_5_), channel_id=1, source_target_pairs={{0,2},{2,0},{4,6},{6,4},{8,10},{10,8},{12,14},{14,12},{16,18},{18,... | collective-permute-start | bytes 1572872 | tf_op jit(solution)/shard_map/ppermute | solution.py:81
  81.6 17.7 %collective-permute-start.19 = (bf16[128,2048]{1,0:T(8,128)(2,1)S(1)}, bf16[128,2048]{1,0:T(8,128)(2,1)}, u32[]{:S(2)}, u32[]{:S(2)}) collective-permute-start(bf16[128,2048]{1,0:T(8,128)(2,1)S(1)} %collective-permute-done.12.rest_12_), channel_id=1, source_target_pairs={{0,4},{2,6},{4,0},{6,2},{8,12},{10,14},{12,8},{14,10},{16,20},{18,... | collective-permute-start | bytes 1572872 | tf_op jit(solution)/shard_map/ppermute | solution.py:84
  82.3 16.9 %collective-permute-start.18 = (bf16[128,2048]{1,0:T(8,128)(2,1)S(1)}, bf16[128,2048]{1,0:T(8,128)(2,1)}, u32[]{:S(2)}, u32[]{:S(2)}) collective-permute-start(bf16[128,2048]{1,0:T(8,128)(2,1)S(1)} %collective-permute-done.12.rest_12_), channel_id=1, source_target_pairs={{0,2},{2,0},{4,6},{6,4},{8,10},{10,8},{12,14},{14,12},{16,18},{18,... | collective-permute-start | bytes 1572872 | tf_op jit(solution)/shard_map/ppermute | solution.py:81
  82.3 16.9 %collective-permute-start.17 = (bf16[128,2048]{1,0:T(8,128)(2,1)S(1)}, bf16[128,2048]{1,0:T(8,128)(2,1)}, u32[]{:S(2)}, u32[]{:S(2)}) collective-permute-start(bf16[128,2048]{1,0:T(8,128)(2,1)S(1)} %collective-permute-done.13.rest_9_), channel_id=1, source_target_pairs={{0,2},{2,0},{4,6},{6,4},{8,10},{10,8},{12,14},{14,12},{16,18},{18,... | collective-permute-start | bytes 1572872 | tf_op jit(solution)/shard_map/ppermute | solution.py:81
  82.8 16.4 %collective-permute-start.20 = (bf16[128,1024]{1,0:T(8,128)(2,1)S(1)}, bf16[128,1024]{1,0:T(8,128)(2,1)}, u32[]{:S(2)}, u32[]{:S(2)}) collective-permute-start(bf16[128,1024]{1,0:T(8,128)(2,1)S(1)} %collective-permute-done.8.rest_8_), channel_id=1, source_target_pairs={{0,8},{2,10},{4,12},{6,14},{8,16},{10,18},{12,20},{14,22},{16,24},... | collective-permute-start | bytes 786440 | tf_op jit(solution)/shard_map/ppermute | solution.py:87
  101.6 14.5 %collective-permute-start.16 = (bf16[128,1024]{1,0:T(8,128)(2,1)S(1)}, bf16[128,1024]{1,0:T(8,128)(2,1)S(1)}, u32[]{:S(2)}, u32[]{:S(2)}) collective-permute-start(bf16[128,1024]{1,0:T(8,128)(2,1)S(1)} %copy-done.89), channel_id=1, source_target_pairs={{0,2},{2,0},{4,6},{6,4},{8,10},{10,8},{12,14},{14,12},{16,18},{18,... | collective-permute-start | bytes 786440 | tf_op jit(solution)/shard_map/ppermute | solution.py:81
  102.1 14.0 %collective-permute-start.23 = (bf16[128,1024]{1,0:T(8,128)(2,1)}, bf16[128,1024]{1,0:T(8,128)(2,1)S(1)}, u32[]{:S(2)}, u32[]{:S(2)}) collective-permute-start(bf16[128,1024]{1,0:T(8,128)(2,1)} %collective-permute-done.3.rest_4_), channel_id=1, source_target_pairs={{0,4},{2,6},{4,0},{6,2},{8,12},{10,14},{12,8},{14,10},{16,20},{18,... | collective-permute-start | bytes 786440 | tf_op jit(solution)/shard_map/ppermute | solution.py:84
  103.4 24.5 %collective-permute-start.27 = (bf16[128,1536]{1,0:T(8,128)(2,1)S(1)}, bf16[128,1536]{1,0:T(8,128)(2,1)S(1)}, u32[]{:S(2)}, u32[]{:S(2)}) collective-permute-start(bf16[128,1536]{1,0:T(8,128)(2,1)S(1)} %pad_maximum_fusion.2), channel_id=1, source_target_pairs={{0,4},{2,6},{4,0},{6,2},{8,12},{10,14},{12,8},{14,10},{16,20},{18,... | collective-permute-start | bytes 1179656 | tf_op jit(solution)/shard_map/ppermute | solution.py:84
  130.5 138.2 %all-gather.8.cloned.1.call-start = ((), (), s32[]{:S(2)}) async-start(), calls=%async_computation.4 | async-start | bytes 7077888 | tf_op jit(solution)/shard_map/all_gather | solution.py:915
  154.2 241.0 %reduce-scatter.3.cloned.1.call-start = ((), (), s32[]{:S(2)}) async-start(), calls=%async_computation.5 | async-start | bytes 7077888 | tf_op jit(solution)/shard_map/reduce_scatter | solution.py:1125
  154.3 13.7 %collective-permute-start.34 = (bf16[128,2048]{1,0:T(8,128)(2,1)S(1)}, bf16[128,2048]{1,0:T(8,128)(2,1)S(1)}, u32[]{:S(2)}, u32[]{:S(2)}) collective-permute-start(bf16[128,2048]{1,0:T(8,128)(2,1)S(1)} %get-tuple-element.426), channel_id=1, source_target_pairs={{0,4},{2,6},{4,0},{6,2},{8,12},{10,14},{12,8},{14,10},{16,20},{18,... | collective-permute-start | bytes 1572872 | tf_op jit(solution)/shard_map/ppermute | solution.py:84
  207.0 15.9 %collective-permute-start.41 = (bf16[128,2048]{1,0:T(8,128)(2,1)S(1)}, bf16[128,2048]{1,0:T(8,128)(2,1)S(1)}, u32[]{:S(2)}, u32[]{:S(2)}) collective-permute-start(bf16[128,2048]{1,0:T(8,128)(2,1)S(1)} %collective-permute-done.34), channel_id=1, source_target_pairs={{0,1},{1,0},{2,3},{3,2},{4,5},{5,4},{6,7},{7,6},{8,9},{9,8},{10,11... | collective-permute-start | bytes 1572872 | tf_op jit(solution)/shard_map/ppermute | solution.py:207
  208.0 20.4 %collective-permute-start.42 = (bf16[128,2048]{1,0:T(8,128)(2,1)S(1)}, bf16[128,2048]{1,0:T(8,128)(2,1)S(1)}, u32[]{:S(2)}, u32[]{:S(2)}) collective-permute-start(bf16[128,2048]{1,0:T(8,128)(2,1)S(1)} %collective-permute-done.36), channel_id=1, source_target_pairs={{0,1},{1,0},{2,3},{3,2},{4,5},{5,4},{6,7},{7,6},{8,9},{9,8},{10,11... | collective-permute-start | bytes 1572872 | tf_op jit(solution)/shard_map/ppermute | solution.py:207
  209.0 19.4 %collective-permute-start.43 = (bf16[128,2048]{1,0:T(8,128)(2,1)}, bf16[128,2048]{1,0:T(8,128)(2,1)S(1)}, u32[]{:S(2)}, u32[]{:S(2)}) collective-permute-start(bf16[128,2048]{1,0:T(8,128)(2,1)} %get-tuple-element.457.refs_2_), channel_id=1, source_target_pairs={{0,4},{2,6},{4,0},{6,2},{8,12},{10,14},{12,8},{14,10},{16,20},{18,... | collective-permute-start | bytes 1572872 | tf_op jit(solution)/shard_map/ppermute | solution.py:84
  213.1 23.9 %collective-permute-start.44 = (bf16[128,2048]{1,0:T(8,128)(2,1)}, bf16[128,2048]{1,0:T(8,128)(2,1)S(1)}, u32[]{:S(2)}, u32[]{:S(2)}) collective-permute-start(bf16[128,2048]{1,0:T(8,128)(2,1)} %get-tuple-element.460.refs_3_), channel_id=1, source_target_pairs={{0,4},{2,6},{4,0},{6,2},{8,12},{10,14},{12,8},{14,10},{16,20},{18,... | collective-permute-start | bytes 1572872 | tf_op jit(solution)/shard_map/ppermute | solution.py:84
  259.7 230.2 %reduce-scatter.5.cloned.1.call-start = ((), (), s32[]{:S(2)}) async-start(), calls=%async_computation.6 | async-start | bytes 14155776 | tf_op jit(solution)/shard_map/reduce_scatter | solution.py:1125
  289.1 22.5 %collective-permute-start.45 = (bf16[128,2048]{1,0:T(8,128)(2,1)}, bf16[128,2048]{1,0:T(8,128)(2,1)S(1)}, u32[]{:S(2)}, u32[]{:S(2)}) collective-permute-start(bf16[128,2048]{1,0:T(8,128)(2,1)} %get-tuple-element.485.refs_6_), channel_id=1, source_target_pairs={{0,4},{2,6},{4,0},{6,2},{8,12},{10,14},{12,8},{14,10},{16,20},{18,... | collective-permute-start | bytes 1572872 | tf_op jit(solution)/shard_map/ppermute | solution.py:84
  299.2 26.8 %collective-permute-start.47 = (bf16[128,2048]{1,0:T(8,128)(2,1)S(1)}, bf16[128,2048]{1,0:T(8,128)(2,1)S(1)}, u32[]{:S(2)}, u32[]{:S(2)}) collective-permute-start(bf16[128,2048]{1,0:T(8,128)(2,1)S(1)} %copy-done.86), channel_id=1, source_target_pairs={{0,4},{2,6},{4,0},{6,2},{8,12},{10,14},{12,8},{14,10},{16,20},{18,... | collective-permute-start | bytes 1572872 | tf_op jit(solution)/shard_map/ppermute | solution.py:84
  326.0 19.5 %collective-permute-start.49 = (bf16[128,2048]{1,0:T(8,128)(2,1)S(1)}, bf16[128,2048]{1,0:T(8,128)(2,1)S(1)}, u32[]{:S(2)}, u32[]{:S(2)}) collective-permute-start(bf16[128,2048]{1,0:T(8,128)(2,1)S(1)} %copy-done.85), channel_id=1, source_target_pairs={{0,4},{2,6},{4,0},{6,2},{8,12},{10,14},{12,8},{14,10},{16,20},{18,... | collective-permute-start | bytes 1572872 | tf_op jit(solution)/shard_map/ppermute | solution.py:84
  327.4 18.2 %collective-permute-start.48 = (bf16[128,2048]{1,0:T(8,128)(2,1)S(1)}, bf16[128,2048]{1,0:T(8,128)(2,1)S(1)}, u32[]{:S(2)}, u32[]{:S(2)}) collective-permute-start(bf16[128,2048]{1,0:T(8,128)(2,1)S(1)} %add_convert_fusion.9.refs_16_.refs_0_), channel_id=1, source_target_pairs={{0,1},{1,0},{2,3},{3,2},{4,5},{5,4},{6,7},{7,6},{8,9},{9,8},{10,11... | collective-permute-start | bytes 1572872 | tf_op jit(solution)/shard_map/ppermute | solution.py:207
  346.8 14.5 %collective-permute-start.51 = (bf16[128,2048]{1,0:T(8,128)(2,1)S(1)}, bf16[128,2048]{1,0:T(8,128)(2,1)S(1)}, u32[]{:S(2)}, u32[]{:S(2)}) collective-permute-start(bf16[128,2048]{1,0:T(8,128)(2,1)S(1)} %copy-done.83), channel_id=1, source_target_pairs={{0,4},{2,6},{4,0},{6,2},{8,12},{10,14},{12,8},{14,10},{16,20},{18,... | collective-permute-start | bytes 1572872 | tf_op jit(solution)/shard_map/ppermute | solution.py:84
  347.4 14.0 %collective-permute-start.50 = (bf16[128,2048]{1,0:T(8,128)(2,1)S(1)}, bf16[128,2048]{1,0:T(8,128)(2,1)S(1)}, u32[]{:S(2)}, u32[]{:S(2)}) collective-permute-start(bf16[128,2048]{1,0:T(8,128)(2,1)S(1)} %add_convert_fusion.8.refs_6_.refs_0_), channel_id=1, source_target_pairs={{0,1},{1,0},{2,3},{3,2},{4,5},{5,4},{6,7},{7,6},{8,9},{9,8},{10,11... | collective-permute-start | bytes 1572872 | tf_op jit(solution)/shard_map/ppermute | solution.py:207
  361.5 16.6 %collective-permute-start.52 = (bf16[128,2048]{1,0:T(8,128)(2,1)S(1)}, bf16[128,2048]{1,0:T(8,128)(2,1)S(1)}, u32[]{:S(2)}, u32[]{:S(2)}) collective-permute-start(bf16[128,2048]{1,0:T(8,128)(2,1)S(1)} %add_convert_fusion.7.refs_6_.refs_0_), channel_id=1, source_target_pairs={{0,1},{1,0},{2,3},{3,2},{4,5},{5,4},{6,7},{7,6},{8,9},{9,8},{10,11... | collective-permute-start | bytes 1572872 | tf_op jit(solution)/shard_map/ppermute | solution.py:207
  362.8 15.3 %collective-permute-start.53 = (bf16[128,2048]{1,0:T(8,128)(2,1)S(1)}, bf16[128,2048]{1,0:T(8,128)(2,1)S(1)}, u32[]{:S(2)}, u32[]{:S(2)}) collective-permute-start(bf16[128,2048]{1,0:T(8,128)(2,1)S(1)} %copy-done.84), channel_id=1, source_target_pairs={{0,4},{2,6},{4,0},{6,2},{8,12},{10,14},{12,8},{14,10},{16,20},{18,... | collective-permute-start | bytes 1572872 | tf_op jit(solution)/shard_map/ppermute | solution.py:84
  390.4 34.4 %collective-permute-start.56 = (bf16[128,2048]{1,0:T(8,128)(2,1)}, bf16[128,2048]{1,0:T(8,128)(2,1)S(1)}, u32[]{:S(2)}, u32[]{:S(2)}) collective-permute-start(bf16[128,2048]{1,0:T(8,128)(2,1)} %get-tuple-element.564), channel_id=1, source_target_pairs={{0,4},{2,6},{4,0},{6,2},{8,12},{10,14},{12,8},{14,10},{16,20},{18,... | collective-permute-start | bytes 1572872 | tf_op jit(solution)/shard_map/ppermute | solution.py:84
  392.0 32.8 %collective-permute-start.59 = (bf16[128,2048]{1,0:T(8,128)(2,1)S(1)}, bf16[128,2048]{1,0:T(8,128)(2,1)S(1)}, u32[]{:S(2)}, u32[]{:S(2)}) collective-permute-start(bf16[128,2048]{1,0:T(8,128)(2,1)S(1)} %add_convert_fusion.6.refs_4_), channel_id=1, source_target_pairs={{0,1},{1,0},{2,3},{3,2},{4,5},{5,4},{6,7},{7,6},{8,9},{9,8},{10,11... | collective-permute-start | bytes 1572872 | tf_op jit(solution)/shard_map/ppermute | solution.py:207
  393.1 31.7 %collective-permute-start.57 = (bf16[128,2048]{1,0:T(8,128)(2,1)}, bf16[128,2048]{1,0:T(8,128)(2,1)}, u32[]{:S(2)}, u32[]{:S(2)}) collective-permute-start(bf16[128,2048]{1,0:T(8,128)(2,1)} %get-tuple-element.569), channel_id=1, source_target_pairs={{0,4},{2,6},{4,0},{6,2},{8,12},{10,14},{12,8},{14,10},{16,20},{18,... | collective-permute-start | bytes 1572872 | tf_op jit(solution)/shard_map/ppermute | solution.py:84
  394.9 32.9 %collective-permute-start.58 = (bf16[128,2048]{1,0:T(8,128)(2,1)}, bf16[128,2048]{1,0:T(8,128)(2,1)S(1)}, u32[]{:S(2)}, u32[]{:S(2)}) collective-permute-start(bf16[128,2048]{1,0:T(8,128)(2,1)} %get-tuple-element.571), channel_id=1, source_target_pairs={{0,4},{2,6},{4,0},{6,2},{8,12},{10,14},{12,8},{14,10},{16,20},{18,... | collective-permute-start | bytes 1572872 | tf_op jit(solution)/shard_map/ppermute | solution.py:84
  396.4 39.0 %collective-permute-start.60 = (bf16[128,1536]{1,0:T(8,128)(2,1)S(1)}, bf16[128,1536]{1,0:T(8,128)(2,1)S(1)}, u32[]{:S(2)}, u32[]{:S(2)}) collective-permute-start(bf16[128,1536]{1,0:T(8,128)(2,1)S(1)} %constant_dynamic-slice_fusion), channel_id=1, source_target_pairs={{0,4},{2,6},{4,0},{6,2},{8,12},{10,14},{12,8},{14,10},{16,20},{18,... | collective-permute-start | bytes 1179656 | tf_op jit(solution)/shard_map/ppermute | solution.py:84
  442.7 15.6 %collective-permute-start.62 = (bf16[512,2048]{1,0:T(8,128)(2,1)}, bf16[512,2048]{1,0:T(8,128)(2,1)}, u32[]{:S(2)}, u32[]{:S(2)}) collective-permute-start(bf16[512,2048]{1,0:T(8,128)(2,1)} %get-tuple-element.578), channel_id=1, source_target_pairs={{0,2},{2,0},{4,6},{6,4},{8,10},{10,8},{12,14},{14,12},{16,18},{18,... | collective-permute-start | bytes 6291464 | tf_op jit(solution)/shard_map/ppermute | solution.py:81
  442.8 15.5 %collective-permute-start.61 = (bf16[512,2048]{1,0:T(8,128)(2,1)}, bf16[512,2048]{1,0:T(8,128)(2,1)}, u32[]{:S(2)}, u32[]{:S(2)}) collective-permute-start(bf16[512,2048]{1,0:T(8,128)(2,1)} %get-tuple-element.577.rest_1_), channel_id=1, source_target_pairs={{0,2},{2,0},{4,6},{6,4},{8,10},{10,8},{12,14},{14,12},{16,18},{18,... | collective-permute-start | bytes 6291464 | tf_op jit(solution)/shard_map/ppermute | solution.py:81
  443.5 14.8 %collective-permute-start.63 = (bf16[128,2048]{1,0:T(8,128)(2,1)S(1)}, bf16[128,2048]{1,0:T(8,128)(2,1)S(1)}, u32[]{:S(2)}, u32[]{:S(2)}) collective-permute-start(bf16[128,2048]{1,0:T(8,128)(2,1)S(1)} %add_convert_fusion.5.refs_5_), channel_id=1, source_target_pairs={{0,1},{1,0},{2,3},{3,2},{4,5},{5,4},{6,7},{7,6},{8,9},{9,8},{10,11... | collective-permute-start | bytes 1572872 | tf_op jit(solution)/shard_map/ppermute | solution.py:207
  444.8 25.1 %collective-permute-start.64 = (bf16[512,1024]{1,0:T(8,128)(2,1)}, bf16[512,1024]{1,0:T(8,128)(2,1)S(1)}, u32[]{:S(2)}, u32[]{:S(2)}) collective-permute-start(bf16[512,1024]{1,0:T(8,128)(2,1)} %get-tuple-element.599), channel_id=1, source_target_pairs={{0,4},{2,6},{4,0},{6,2},{8,12},{10,14},{12,8},{14,10},{16,20},{18,... | collective-permute-start | bytes 3145736 | tf_op jit(solution)/shard_map/ppermute | solution.py:84
  446.3 25.3 %collective-permute-start.69 = (bf16[128,2048]{1,0:T(8,128)(2,1)S(1)}, bf16[128,2048]{1,0:T(8,128)(2,1)S(1)}, u32[]{:S(2)}, u32[]{:S(2)}) collective-permute-start(bf16[128,2048]{1,0:T(8,128)(2,1)S(1)} %add_convert_fusion.4.refs_6_), channel_id=1, source_target_pairs={{0,1},{1,0},{2,3},{3,2},{4,5},{5,4},{6,7},{7,6},{8,9},{9,8},{10,11... | collective-permute-start | bytes 1572872 | tf_op jit(solution)/shard_map/ppermute | solution.py:207
  470.0 14.8 %collective-permute-start.68 = (bf16[128,2048]{1,0:T(8,128)(2,1)S(1)}, bf16[128,2048]{1,0:T(8,128)(2,1)S(1)}, u32[]{:S(2)}, u32[]{:S(2)}) collective-permute-start(bf16[128,2048]{1,0:T(8,128)(2,1)S(1)} %copy-done.27), channel_id=1, source_target_pairs={{0,1},{1,0},{2,3},{3,2},{4,5},{5,4},{6,7},{7,6},{8,9},{9,8},{10,11... | collective-permute-start | bytes 1572872 | tf_op jit(solution)/shard_map/ppermute | solution.py:207
  470.8 14.2 %collective-permute-start.66 = (bf16[128,2048]{1,0:T(8,128)(2,1)}, bf16[128,2048]{1,0:T(8,128)(2,1)S(1)}, u32[]{:S(2)}, u32[]{:S(2)}) collective-permute-start(bf16[128,2048]{1,0:T(8,128)(2,1)} %get-tuple-element.611), channel_id=1, source_target_pairs={{0,4},{2,6},{4,0},{6,2},{8,12},{10,14},{12,8},{14,10},{16,20},{18,... | collective-permute-start | bytes 1572872 | tf_op jit(solution)/shard_map/ppermute | solution.py:84
  471.6 24.5 %collective-permute-start.75 = (bf16[128,2048]{1,0:T(8,128)(2,1)S(1)}, bf16[128,2048]{1,0:T(8,128)(2,1)}, u32[]{:S(2)}, u32[]{:S(2)}) collective-permute-start(bf16[128,2048]{1,0:T(8,128)(2,1)S(1)} %add_convert_fusion.2.refs_7_), channel_id=1, source_target_pairs={{0,1},{1,0},{2,3},{3,2},{4,5},{5,4},{6,7},{7,6},{8,9},{9,8},{10,11... | collective-permute-start | bytes 1572872 | tf_op jit(solution)/shard_map/ppermute | solution.py:207
  486.1 24.0 %collective-permute-start.72 = (bf16[128,2048]{1,0:T(8,128)(2,1)}, bf16[128,2048]{1,0:T(8,128)(2,1)}, u32[]{:S(2)}, u32[]{:S(2)}) collective-permute-start(bf16[128,2048]{1,0:T(8,128)(2,1)} %get-tuple-element.621), channel_id=1, source_target_pairs={{0,4},{2,6},{4,0},{6,2},{8,12},{10,14},{12,8},{14,10},{16,20},{18,... | collective-permute-start | bytes 1572872 | tf_op jit(solution)/shard_map/ppermute | solution.py:84
  487.6 22.5 %collective-permute-start.74 = (bf16[128,2048]{1,0:T(8,128)(2,1)S(1)}, bf16[128,2048]{1,0:T(8,128)(2,1)}, u32[]{:S(2)}, u32[]{:S(2)}) collective-permute-start(bf16[128,2048]{1,0:T(8,128)(2,1)S(1)} %copy-done.28), channel_id=1, source_target_pairs={{0,1},{1,0},{2,3},{3,2},{4,5},{5,4},{6,7},{7,6},{8,9},{9,8},{10,11... | collective-permute-start | bytes 1572872 | tf_op jit(solution)/shard_map/ppermute | solution.py:207
  489.8 20.3 %collective-permute-start.71 = (bf16[128,2048]{1,0:T(8,128)(2,1)}, bf16[128,2048]{1,0:T(8,128)(2,1)}, u32[]{:S(2)}, u32[]{:S(2)}) collective-permute-start(bf16[128,2048]{1,0:T(8,128)(2,1)} %add_convert_fusion.3), channel_id=1, source_target_pairs={{0,8},{2,10},{4,12},{6,14},{8,16},{10,18},{12,20},{14,22},{16,24},... | collective-permute-start | bytes 1572872 | tf_op jit(solution)/shard_map/ppermute | solution.py:87
  496.1 14.0 %collective-permute-start.76 = (bf16[128,1536]{1,0:T(8,128)(2,1)S(1)}, bf16[128,1536]{1,0:T(8,128)(2,1)S(1)}, u32[]{:S(2)}, u32[]{:S(2)}) collective-permute-start(bf16[128,1536]{1,0:T(8,128)(2,1)S(1)} %get-tuple-element.628), channel_id=1, source_target_pairs={{0,4},{2,6},{4,0},{6,2},{8,12},{10,14},{12,8},{14,10},{16,20},{18,... | collective-permute-start | bytes 1179656 | tf_op jit(solution)/shard_map/ppermute | solution.py:84
  496.5 13.6 %collective-permute-start.73 = (bf16[128,1024]{1,0:T(8,128)(2,1)S(1)}, bf16[128,1024]{1,0:T(8,128)(2,1)S(1)}, u32[]{:S(2)}, u32[]{:S(2)}) collective-permute-start(bf16[128,1024]{1,0:T(8,128)(2,1)S(1)} %add_convert_fusion.12), channel_id=1, source_target_pairs={{0,8},{2,10},{4,12},{6,14},{8,16},{10,18},{12,20},{14,22},{16,24},... | collective-permute-start | bytes 786440 | tf_op jit(solution)/shard_map/ppermute | solution.py:87
  510.2 22.8 %collective-permute-start.79 = (bf16[128,2048]{1,0:T(8,128)(2,1)S(1)}, bf16[128,2048]{1,0:T(8,128)(2,1)S(1)}, u32[]{:S(2)}, u32[]{:S(2)}) collective-permute-start(bf16[128,2048]{1,0:T(8,128)(2,1)S(1)} %copy-done.82), channel_id=1, source_target_pairs={{0,4},{2,6},{4,0},{6,2},{8,12},{10,14},{12,8},{14,10},{16,20},{18,... | collective-permute-start | bytes 1572872 | tf_op jit(solution)/shard_map/ppermute | solution.py:84
  511.0 21.9 %collective-permute-start.81 = (bf16[128,2048]{1,0:T(8,128)(2,1)S(1)}, bf16[128,2048]{1,0:T(8,128)(2,1)S(1)}, u32[]{:S(2)}, u32[]{:S(2)}) collective-permute-start(bf16[128,2048]{1,0:T(8,128)(2,1)S(1)} %copy-done.29), channel_id=1, source_target_pairs={{0,1},{1,0},{2,3},{3,2},{4,5},{5,4},{6,7},{7,6},{8,9},{9,8},{10,11... | collective-permute-start | bytes 1572872 | tf_op jit(solution)/shard_map/ppermute | solution.py:207
  513.6 19.4 %collective-permute-start.78 = (bf16[128,2048]{1,0:T(8,128)(2,1)S(1)}, bf16[128,2048]{1,0:T(8,128)(2,1)S(1)}, u32[]{:S(2)}, u32[]{:S(2)}) collective-permute-start(bf16[128,2048]{1,0:T(8,128)(2,1)S(1)} %add_convert_fusion.1), channel_id=1, source_target_pairs={{0,8},{2,10},{4,12},{6,14},{8,16},{10,18},{12,20},{14,22},{16,24},... | collective-permute-start | bytes 1572872 | tf_op jit(solution)/shard_map/ppermute | solution.py:87
  515.2 17.7 %collective-permute-start.82 = (bf16[128,1536]{1,0:T(8,128)(2,1)S(1)}, bf16[128,1536]{1,0:T(8,128)(2,1)S(1)}, u32[]{:S(2)}, u32[]{:S(2)}) collective-permute-start(bf16[128,1536]{1,0:T(8,128)(2,1)S(1)} %get-tuple-element.638), channel_id=1, source_target_pairs={{0,4},{2,6},{4,0},{6,2},{8,12},{10,14},{12,8},{14,10},{16,20},{18,... | collective-permute-start | bytes 1179656 | tf_op jit(solution)/shard_map/ppermute | solution.py:84
  532.9 18.2 %collective-permute-start.85 = (bf16[128,2048]{1,0:T(8,128)(2,1)}, bf16[128,2048]{1,0:T(8,128)(2,1)}, u32[]{:S(2)}, u32[]{:S(2)}) collective-permute-start(bf16[128,2048]{1,0:T(8,128)(2,1)} %get-tuple-element.651), channel_id=1, source_target_pairs={{0,4},{2,6},{4,0},{6,2},{8,12},{10,14},{12,8},{14,10},{16,20},{18,... | collective-permute-start | bytes 1572872 | tf_op jit(solution)/shard_map/ppermute | solution.py:84
  534.0 17.1 %collective-permute-start.86 = (bf16[128,2048]{1,0:T(8,128)(2,1)S(1)}, bf16[128,2048]{1,0:T(8,128)(2,1)}, u32[]{:S(2)}, u32[]{:S(2)}) collective-permute-start(bf16[128,2048]{1,0:T(8,128)(2,1)S(1)} %copy-done.25), channel_id=1, source_target_pairs={{0,1},{1,0},{2,3},{3,2},{4,5},{5,4},{6,7},{7,6},{8,9},{9,8},{10,11... | collective-permute-start | bytes 1572872 | tf_op jit(solution)/shard_map/ppermute | solution.py:207
  535.9 15.2 %collective-permute-start.84 = (bf16[128,2048]{1,0:T(8,128)(2,1)}, bf16[128,2048]{1,0:T(8,128)(2,1)}, u32[]{:S(2)}, u32[]{:S(2)}) collective-permute-start(bf16[128,2048]{1,0:T(8,128)(2,1)} %add_convert_fusion), channel_id=1, source_target_pairs={{0,8},{2,10},{4,12},{6,14},{8,16},{10,18},{12,20},{14,22},{16,24},... | collective-permute-start | bytes 1572872 | tf_op jit(solution)/shard_map/ppermute | solution.py:87
  (130 other events, 1244.2 us)
Sparse Core Ops, SparseCore 0:
  58.1 73.1 all-gather.3
  133.5 63.7 all-gather.5
  199.0 63.3 all-gather.7
  264.6 68.4 reduce-scatter.2
  345.8 130.2 reduce-scatter.4

commit v3 on v2

--- a/solution.py
+++ b/solution.py
@@ -56,6 +56,7 @@
 CHUNKS = 3
 PARTS = 4
 LANES = 128
+ROW_BLOCK = 256
 VMEM_LIMIT = 56 * 1024 * 1024
 
 
@@ -148,37 +149,6 @@
         return len(self.pieces) == self.ring.size
 
 
-class Scatter:
-    def __init__(self, ring, mine, other, crossed=None):
-        self.ring = ring
-        self.mine, self.other, self.crossed = mine, other, crossed
-        self.term, self.index, self.total = None, 0, None
-        if crossed is not None:
-            self.add({"side": crossed[0]})
-
-    def start(self, stages):
-        moves = {}
-        if self.index < self.ring.steps and self.crossed is None:
-            (other,) = stages.hold(self.other[self.index])
-            moves["side"] = self.ring.swap_side(other)
-        if self.term is not None:
-            moves["hop"] = self.ring.shift(self.term, 1)
-        return moves
-
-    def finish(self, moves):
-        if self.crossed is not None:
-            moves = dict(moves, side=self.crossed[self.index])
-        self.add(moves)
-
-    def add(self, moves):
-        value = self.mine[self.index].astype(jnp.float32) + moves["side"].astype(jnp.float32)
-        if "hop" in moves:
-            value = value + moves["hop"].astype(jnp.float32)
-        self.index += 1
-        self.total = value
-        self.term = value.astype(jnp.bfloat16) if self.index < self.ring.steps else None
-
-
 class Stages:
     def __init__(self, mark):
         self.mark = mark
@@ -217,6 +187,63 @@
     return vector.reshape(steps, 2, 2, -1).swapaxes(1, 2).reshape(-1)
 
 
+def sums_kernel(kinds, counts, *refs):
+    ins, outs = refs[: sum(counts)], list(refs[sum(counts) :])
+    for kind, count in zip(kinds, counts):
+        group, ins = ins[:count], ins[count:]
+        total = group[0][...].astype(jnp.float32)
+        for ref in group[1:]:
+            total = total + ref[...].astype(jnp.float32)
+        if kind == "low":
+            outs.pop(0)[...] = total.astype(jnp.bfloat16)
+        elif kind == "turned":
+            outs.pop(0)[...] = total.T
+        elif kind[0] == "open":
+            joined = outs.pop(0)
+            joined[:, : total.shape[1]] = total.astype(jnp.bfloat16)
+        elif kind[0] == "close":
+            joined[:, kind[1] : kind[1] + total.shape[1]] = total.astype(jnp.bfloat16)
+        else:
+            first = 0
+            for width in kind:
+                outs.pop(0)[...] = total[:, first : first + width]
+                first += width
+
+
+def sums_call(*groups):
+    shapes = []
+    for kind, arrays in groups:
+        rows, columns = arrays[-1][-1] if isinstance(arrays[-1], tuple) else arrays[-1].shape
+        if kind[0] == "open":
+            shapes.append(jax.ShapeDtypeStruct((rows, kind[1]), jnp.bfloat16))
+        elif kind[0] == "close":
+            continue
+        elif kind == "low":
+            shapes.append(jax.ShapeDtypeStruct((rows, columns), jnp.bfloat16))
+        elif kind == "turned":
+            shapes.append(jax.ShapeDtypeStruct((columns, rows), jnp.float32))
+        else:
+            shapes += [jax.ShapeDtypeStruct((rows, w), jnp.float32) for w in kind]
+    ins, specs = [], []
+    for _, arrays in groups:
+        shape = arrays[-1][-1] if isinstance(arrays[-1], tuple) else arrays[-1].shape
+        for a in arrays:
+            a, *block = a if isinstance(a, tuple) else (a, (0, 0))
+            ins.append(a)
+            specs.append(pl.BlockSpec(shape, lambda i, block=block[0]: block))
+    return pl.pallas_call(
+        functools.partial(sums_kernel, [k for k, _ in groups], [len(a) for _, a in groups]),
+        grid=(1,),
+        in_specs=specs,
+        out_specs=[pl.BlockSpec(shape.shape, lambda i: (0, 0)) for shape in shapes],
+        out_shape=shapes,
+        compiler_params=pltpu.CompilerParams(vmem_limit_bytes=VMEM_LIMIT),
+        cost_estimate=pl.CostEstimate(
+            flops=0, bytes_accessed=4 * sum(a.size for a in ins), transcendentals=0
+        ),
+    )(*ins)
+
+
 def loose(ties):
     return [pl.BlockSpec(memory_space=pl.ANY) for _ in ties]
 
@@ -225,9 +252,10 @@
     arrays, specs, places, cuts = [], [], [], 1
     for value, kind in ins:
         places.append(len(arrays))
-        if kind == "parts":
-            cuts = len(value)
-            span = rows // cuts // block
+        if kind in ("parts", "halves"):
+            if kind == "parts":
+                cuts = len(value)
+            span = rows // len(value) // block
             for k, piece in enumerate(value):
                 arrays.append(piece)
                 specs.append(
@@ -267,8 +295,10 @@
         turn = pl.program_id(0) // (rows // cuts // block)
         for k in range(cuts):
             chosen = [
-                refs[place + k] if kind == "parts" else refs[place]
-                for place, (_, kind) in zip(places, ins)
+                refs[place + k * len(value) // cuts]
+                if kind in ("parts", "halves")
+                else refs[place]
+                for place, (value, kind) in zip(places, ins)
             ]
             pl.when(turn == k)(functools.partial(kernel, *chosen, *given))
 
@@ -496,36 +526,44 @@
     return scale * (pulled - normed * center), back * normed
 
 
-def softmax_rows(query, key, allowed):
-    scores = jnp.where(allowed, inner_right(query, key) * HEAD_SIZE ** (-0.5), -1e30)
-    raised = jnp.exp(scores - jnp.max(scores, axis=-1, keepdims=True))
-    return raised / jnp.sum(raised, axis=-1, keepdims=True)
-
-
-def allowed_pairs(segment_column, segment_row):
-    count = segment_column.shape[0]
-    row = lax.broadcasted_iota(jnp.int32, (count, count), 0)
-    column = lax.broadcasted_iota(jnp.int32, (count, count), 1)
-    return (segment_column[...] == segment_row[...]) & (column <= row)
+def allowed_pairs(segment_column, segment_row, first, count):
+    height = first + count
+    key = lax.broadcasted_iota(jnp.int32, (height, count), 0)
+    query = lax.broadcasted_iota(jnp.int32, (height, count), 1) + first
+    same = segment_column[:height, :] == segment_row[:, first:height]
+    return same & (key <= query)
 
 
 def attend_kernel(
     queries, keys, values, query_gain, key_gain, cosine, sine, seg_column, seg_row, *rest
 ):
-    out = rest[-1]
-    allowed = allowed_pairs(seg_column, seg_row)
+    out, total_out = rest[-2:]
+    rows = queries.shape[0]
     cosine, sine = cosine[...], sine[...]
     key = norm_rope(keys[...], key_gain[...], cosine, sine)[0].astype(jnp.bfloat16)
-    value = values[...].astype(jnp.bfloat16)
-    for lo in range(0, queries.shape[1], HEAD_SIZE):
-        span = slice(lo, lo + HEAD_SIZE)
-        query = norm_rope(queries[:, span], query_gain[...], cosine, sine)[0]
-        weights = softmax_rows(query.astype(jnp.bfloat16), key, allowed)
-        out[:, span] = matrix_product(weights.astype(jnp.bfloat16), value).astype(jnp.bfloat16)
+    value = values[...].T.astype(jnp.bfloat16)
+    spans = [slice(lo, lo + HEAD_SIZE) for lo in range(0, queries.shape[1], HEAD_SIZE)]
+    heads = [
+        norm_rope(queries[:, span], query_gain[...], cosine, sine)[0].astype(jnp.bfloat16)
+        for span in spans
+    ]
+    for first in range(0, rows, ROW_BLOCK):
+        end = first + ROW_BLOCK
+        allowed = allowed_pairs(seg_column, seg_row, first, ROW_BLOCK)
+        for k, (span, query) in enumerate(zip(spans, heads)):
+            scores = inner_right(key[:end], query[first:end]) * HEAD_SIZE ** (-0.5)
+            scores = jnp.where(allowed, scores, -1e30)
+            largest = jnp.max(scores, axis=0, keepdims=True)
+            raised = jnp.exp(scores - largest)
+            total = jnp.sum(raised, axis=0, keepdims=True)
+            weights = (raised * (1.0 / total)).astype(jnp.bfloat16)
+            mixed = matrix_product(value[:, :end], weights)
+            out[first:end, span] = mixed.T.astype(jnp.bfloat16)
+            total_out[k : k + 1, first:end] = largest + jnp.log(total)
 
 
 def attend_back_kernel(
-    first,
+    first_head,
     query_columns,
     key_columns,
     queries,
@@ -537,38 +575,55 @@
     sine,
     seg_column,
     seg_row,
+    totals,
     *rest,
 ):
     out, query_gain_out, key_gain_out = rest[-3:]
     back_parts = rest[:PARTS]
-    head = first + pl.program_id(0)
-    wide = queries.shape[1]
+    head = first_head + pl.program_id(0)
+    rows, wide = queries.shape
     scaling = HEAD_SIZE ** (-0.5)
-    allowed = allowed_pairs(seg_column, seg_row)
     cosine, sine = cosine[...], sine[...]
     key, key_normed, key_scale = norm_rope(keys[...], key_gain[...], cosine, sine)
+    turned = key.T.astype(jnp.bfloat16)
     key = key.astype(jnp.bfloat16)
     value = values[...].astype(jnp.bfloat16)
-    back_key, back_value, query_term = 0.0, 0.0, 0.0
-    for lo in range(0, wide, HEAD_SIZE):
-        span = slice(lo, lo + HEAD_SIZE)
-        query, normed, scale = norm_rope(queries[:, span], query_gain[...], cosine, sine)
-        query = query.astype(jnp.bfloat16)
-        weights = softmax_rows(query, key, allowed)
-        back = jnp.concatenate([b[:, span] for b in back_parts], axis=0)
-        back_weights = inner_right(back, value)
-        back_value = back_value + inner_left(weights.astype(jnp.bfloat16), back)
-        center = jnp.sum(back_weights * weights, axis=-1, keepdims=True)
-        back_scores = (weights * (back_weights - center)).astype(jnp.bfloat16)
-        back_query = matrix_product(back_scores, key) * scaling
-        back_key = back_key + inner_left(back_scores, query) * scaling
+    back_mixture = jnp.concatenate([b[...] for b in back_parts], axis=0)
+    spans = [slice(lo, lo + HEAD_SIZE) for lo in range(0, wide, HEAD_SIZE)]
+    heads = [norm_rope(queries[:, span], query_gain[...], cosine, sine) for span in spans]
+    back_queries = [[] for _ in spans]
+    back_key, back_value = None, None
+    for first in range(0, rows, ROW_BLOCK):
+        end = first + ROW_BLOCK
+        allowed = allowed_pairs(seg_column, seg_row, first, ROW_BLOCK)
+        key_term, value_term = 0.0, 0.0
+        for k, span in enumerate(spans):
+            query = heads[k][0][first:end].astype(jnp.bfloat16)
+            back = back_mixture[first:end, span]
+            scores = inner_right(key[:end], query) * scaling
+            weights = jnp.where(allowed, jnp.exp(scores - totals[k : k + 1, first:end]), 0.0)
+            terms = inner_right(value[:end], back) * weights
+            value_term = value_term + matrix_product(weights.astype(jnp.bfloat16), back)
+            center = jnp.sum(terms, axis=0, keepdims=True)
+            back_scores = (terms - weights * center).astype(jnp.bfloat16)
+            back_queries[k].append(matrix_product(turned[:, :end], back_scores).T * scaling)
+            key_term = key_term + matrix_product(back_scores, query) * scaling
+        if back_key is None:
+            back_key, back_value = key_term, value_term
+        else:
+            back_key = jnp.concatenate([back_key + key_term[:first], key_term[first:]], axis=0)
+            back_value = jnp.concatenate(
+                [back_value + value_term[:first], value_term[first:]], axis=0
+            )
+    query_term = 0.0
+    for k, (lo, (_, normed, scale)) in enumerate(zip(range(0, wide, HEAD_SIZE), heads)):
         back_query, term = back_norm_rope(
-            back_query, normed, scale, query_gain[...], cosine, sine
+            jnp.concatenate(back_queries[k], axis=0), normed, scale, query_gain[...], cosine, sine
         )
         query_term = query_term + term
         start = pl.multiple_of(head * wide + lo, HEAD_SIZE)
         out[:, pl.ds(start, HEAD_SIZE)] = back_query.astype(jnp.bfloat16)
-    back_key, key_term = back_norm_rope(
+    back_key, key_sum = back_norm_rope(
         back_key, key_normed, key_scale, key_gain[...], cosine, sine
     )
     start = pl.multiple_of(query_columns + head * HEAD_SIZE, HEAD_SIZE)
@@ -576,10 +631,10 @@
     start = pl.multiple_of(query_columns + key_columns + head * HEAD_SIZE, HEAD_SIZE)
     out[:, pl.ds(start, HEAD_SIZE)] = back_value.astype(jnp.bfloat16)
     add_sum(query_gain_out, query_term)
-    add_sum(key_gain_out, key_term)
-
-
-def attention_call(raw, query_columns, key_columns, gains, tables, segment, heads, back=None, ties=()):
+    add_sum(key_gain_out, key_sum)
+
+
+def attention_call(raw, query_columns, key_columns, gains, tables, segment, heads, back=None, totals=None, ties=()):
     rows, columns = raw.shape
     first, count = heads
     wide = query_columns * HEAD_SIZE // key_columns
@@ -600,8 +655,14 @@
         return pl.pallas_call(
             attend_kernel,
             in_specs=specs + loose(ties),
-            out_specs=pl.BlockSpec((rows, wide), lambda h: (0, h)),
-            out_shape=jax.ShapeDtypeStruct((rows, count * wide), jnp.bfloat16),
+            out_specs=[
+                pl.BlockSpec((rows, wide), lambda h: (0, h)),
+                pl.BlockSpec((8, rows), lambda h: (h, 0)),
+            ],
+            out_shape=[
+                jax.ShapeDtypeStruct((rows, count * wide), jnp.bfloat16),
+                jax.ShapeDtypeStruct((count * 8, rows), jnp.float32),
+            ],
             cost_estimate=pl.CostEstimate(
                 flops=4 * pairs * HEAD_SIZE, bytes_accessed=5 * raw.size, transcendentals=pairs
             ),
@@ -612,6 +673,7 @@
     return pl.pallas_call(
         functools.partial(attend_back_kernel, first, query_columns, key_columns),
         in_specs=specs
+        + [pl.BlockSpec((8, rows), lambda h: (h, 0))]
         + [pl.BlockSpec((b.shape[0], wide), lambda h: (0, first + h)) for b in back]
         + loose(ties),
         out_specs=[pl.BlockSpec((rows, columns), lambda h: (0, 0)), gain_spec, gain_spec],
@@ -620,7 +682,7 @@
             flops=12 * pairs * HEAD_SIZE, bytes_accessed=8 * raw.size, transcendentals=pairs
         ),
         **params,
-    )(*ins, *back, *ties)
+    )(*ins, totals, *back, *ties)
 
 
 def back_first_kernel(raw_grad, full, tokens, *rest):
@@ -757,25 +819,43 @@
         down[pl.ds(start, chunk), :] = value[:, 2 * chunk :].T
 
 
-def finish_call(ring, chunk, totals, others):
+def finish_last_kernel(chunk, info, other, _gate, _up, _down, gate, up, down):
+    value = other[...].astype(jnp.float32)
+    gate[...] = value[:, :chunk]
+    up[...] = value[:, chunk : 2 * chunk]
+    down[...] = value[:, 2 * chunk :].T
+
+
+def finish_call(ring, chunk, totals, others, into=None):
     width, hidden = others[0].shape[0], 2 * CHUNKS * chunk
-    counts = [a.shape[1] // (3 * chunk) for a in totals]
     shapes = [(width, hidden), (width, hidden), (hidden, width)]
-    whole = [pl.BlockSpec(a.shape, lambda i, info: (0, 0)) for a in (*totals, *others)]
+    if into is None:
+        counts = [a.shape[1] // (3 * chunk) for a in totals]
+        kernel = functools.partial(finish_kernel, chunk, counts)
+        ins = [*totals, *others]
+        specs = [pl.BlockSpec(a.shape, lambda i, info: (0, 0)) for a in ins]
+        out_specs = [pl.BlockSpec(shape, lambda i, info: (0, 0)) for shape in shapes]
+        aliases = {}
+    else:
+        kernel = functools.partial(finish_last_kernel, chunk)
+        ins = [*others, *into]
+        specs = [pl.BlockSpec(others[0].shape, lambda i, info: (0, 0))] + loose(into)
+        last = lambda info: (1 - info[0]) * CHUNKS + CHUNKS - 1
+        out_specs = [pl.BlockSpec((width, chunk), lambda i, info: (0, last(info)))] * 2
+        out_specs.append(pl.BlockSpec((chunk, width), lambda i, info: (last(info), 0)))
+        aliases = {2: 0, 3: 1, 4: 2}
     return pl.pallas_call(
-        functools.partial(finish_kernel, chunk, counts),
+        kernel,
         grid_spec=pltpu.PrefetchScalarGridSpec(
-            num_scalar_prefetch=1,
-            grid=(1,),
-            in_specs=whole,
-            out_specs=[pl.BlockSpec(shape, lambda i, info: (0, 0)) for shape in shapes],
+            num_scalar_prefetch=1, grid=(1,), in_specs=specs, out_specs=out_specs
         ),
         out_shape=[jax.ShapeDtypeStruct(shape, jnp.float32) for shape in shapes],
+        input_output_aliases=aliases,
         compiler_params=pltpu.CompilerParams(vmem_limit_bytes=VMEM_LIMIT),
         cost_estimate=pl.CostEstimate(
             flops=0, bytes_accessed=18 * hidden * width, transcendentals=0
         ),
-    )(jnp.stack([ring.side]).astype(jnp.int32), *totals, *others)
+    )(jnp.stack([ring.side]).astype(jnp.int32), *ins)
 
 
 def join_kernel(width, count, order, left, *rest):
@@ -946,43 +1026,40 @@
         [(model_width, jnp.bfloat16)] * 3,
     )
     for i in range(steps):
-        ahead = (output, dict(hop=i != 2, swap=i == 2))
-        movers = [attention, ahead]
+        movers = [attention]
+        if i != 2:
+            movers.append((output, dict(swap=i > 2)))
+        others = []
+        if i in (1, 2):
+            others.append(ring.swap_side(*stages.hold(feed_other[i - 1])))
         if i == 0:
-            token_rows, upstream, input_one, tables = step(
-                movers, token_rows, upstream, input_one, tables
-            )
-        elif i == 1:
-            (got,) = step(movers, ring.swap_side(feed_other[0]))
-            feed_gather(0, got)
-        else:
-            step(movers)
+            others = [token_rows, upstream, input_one, tables]
+        others = step(movers, *others)
+        if i == 0:
+            token_rows, upstream, input_one, tables = others
+        if i in (1, 2):
+            feed_gather(i - 1, others[0])
     step([attention])
     place = lax.axis_index("tensor")
     sent = [
         lax.dynamic_slice_in_dim(upstream, place * (rows // 2) + k * part, part) for k in range(2)
     ]
 
-    late = stages.hold(*feed_other[1:])
+    late = stages.hold(*feed_other[2:])
     raw, attention_full = step([output], *join_call(attention, input_one))
     half = key_heads // 2
     attend_args = (raw, query_columns, key_columns, head_gains, tables, segment)
-    mixture_low = []
+    mixture_low, row_totals = [], []
     for i in range(2):
         mixed = attention_call(*attend_args, (i * half, half), ties=stages.ties)
-        mixed, got = step([output], mixed, [ring.swap_side(late[0])] if i == 0 else [])
-        mixture_low.append(mixed)
-        if i == 0:
-            feed_gather(1, got[0])
-    late = stages.hold(*late)
+        mixed, got = step([output], mixed, [ring.swap_side(w) for w in late] if i == 0 else [])
+        mixture_low.append(mixed[0])
+        row_totals.append(mixed[1])
+        for j, value in enumerate(got):
+            feed_gather(2 + j, value)
     while not output.done:
         step([output])
-    joined, got = settle(
-        join_wide_call(output, mixture_low), [ring.swap_side(w) for w in late[1:]]
-    )
-    mixture_low, output_full, *branch_parts = joined
-    for j, value in enumerate(got):
-        feed_gather(2 + j, value)
+    mixture_low, output_full, *branch_parts = join_wide_call(output, mixture_low)
 
     middle_parts, normed_parts, normed_other = [], [], []
     got = None
@@ -1022,10 +1099,13 @@
     rest = [ring.swap_side(p) for p in normed_parts[len(normed_other) :]]
     acts = []
     for j in range(CHUNKS - 1):
-        act, got, rest[j : j + 1] = settle(
-            feed_call(normed_parts, upstream, feed_full[j], stages.ties), got, rest[j : j + 1]
+        act, rest[j : j + 1], there = settle(
+            feed_call(normed_parts, upstream, feed_full[j], stages.ties),
+            rest[j : j + 1],
+            got if j == CHUNKS - 2 else [],
         )
         acts.append(act)
+    got = there
     rest, upstream_other = settle(
         rest, [jnp.where(place == 0, a, b) for a, b in zip(sent + got, got + sent)]
     )
@@ -1086,23 +1166,20 @@
             )
             work = [last_grads]
         if i == PARTS - 2:
-            work = [wide_call(acts_other, feed_full, out_span, jnp.bfloat16, ties=(mine,))]
+            work = [
+                wide_call(acts_other, feed_full, out_span, jnp.bfloat16, ties=(mine,), parts=2)
+            ]
         if i == PARTS - 1:
-            work = [wide_call(acts, feed_full, out_span, jnp.float32, ties=(mine,))]
+            work = [wide_call(acts, feed_full, out_span, jnp.float32, ties=(mine,), parts=2)]
         done = back_middle_call(i - 1, *last) if i else []
         moves = [swap_tensor(mine)]
         if i + 1 < PARTS:
             moves.append(ring.swap_side(back_other[i + 1]))
-        if i == PARTS - 1:
-            moves.append(ring.swap_side(out_other[0]))
-            out_other[2:] = stages.hold(*out_other[2:])
         moves, work, done = settle(moves, work, done)
         back_other[i + 2 :] = stages.hold(*back_other[i + 2 :])
         last = (mine, moves[0])
         if i + 1 < PARTS:
             mine = add_low(back_mine[i + 1], moves[1])
-        if i == PARTS - 1:
-            out_got.append(moves[-1])
         if i + 1 < CHUNKS:
             last_grads = work[0]
         if i == PARTS - 2:
@@ -1129,46 +1206,55 @@
     ]
 
     core = ring.core
-    out_other[2:] = stages.hold(*out_other[2:])
-    out_sums = [add_low(out_mine[0], out_got[0])]
     far = scatter_call(
         ring, width, low_parts, mixture_low, 1 - core, ties=stages.ties, apart=False
     )
-    (far,) = settle([ring.swap_core(f[0]) for f in far])
-    out_other[3:] = stages.hold(*out_other[3:])
-    near, across = scatter_call(
-        ring, width, low_parts, mixture_low, core, far, stages.ties, apart=False
-    )
+    (got,) = settle(ring.swap_side(out_other[0]))
+    (held,) = stages.hold(out_other[1])
+    out_sums = [add_low(out_mine[0], got)]
+
     def picked(total):
         return lax.dynamic_slice_in_dim(total, (1 - ring.side) * width, width)
 
-    work, scattered[0], got, out_next, pair = settle(
+    work, scattered[0], far, got, out_next = settle(
         attention_call(
-            *attend_args, (0, key_heads), mixed_parts, stages.ties + tuple(near)
+            *attend_args,
+            (0, key_heads),
+            mixed_parts,
+            jnp.concatenate(row_totals, axis=0),
+            stages.ties + (far[0][0],),
         ),
         scattered[0],
-        [ring.swap_side(w) for w in out_other[1:]],
+        [ring.swap_core(f[0]) for f in far],
+        ring.swap_side(held),
         swap_tensor(out_sums[0]),
-        ring.swap_side(picked(*stages.hold(scattered[0]))),
     )
     raw_grad, grad_qgain, grad_kgain = work
-    out_sums += [add_low(m, g) for m, g in zip(out_mine[1:], got)]
+    out_sums.append(add_low(out_mine[1], got))
     out_done = [out_next]
+    far_one = scatter_call(
+        ring, width, [input_one], raw_grad, 1 - core, ties=stages.ties, apart=False
+    )
+    (near,), across = scatter_call(
+        ring,
+        width,
+        low_parts,
+        mixture_low,
+        core,
+        far,
+        stages.ties + (far_one[0][0],),
+        apart=False,
+    )
+    far_one, near, pair = settle(
+        [ring.swap_core(f[0]) for f in far_one],
+        near,
+        ring.swap_side(*stages.hold(picked(scattered[0]))),
+    )
     pairs_got = [pair]
-    across = stages.hold(*across)
-
-    far = scatter_call(
-        ring, width, [input_one], raw_grad, 1 - core, ties=stages.ties, apart=False
-    )
-    far, work, out_next = settle(
-        [ring.swap_core(f[0]) for f in far],
-        back_first_call(
-            raw_grad, attention_full, token_rows, stages.ties + (far[0][0],)
-        ),
-        swap_tensor(out_sums[1]),
-    )
-    out_done.append(out_next)
-    *back_one, grad_first = work
+    ((mine, other),) = settle(
+        scatter_call(ring, width, [input_one], raw_grad, core, far_one, stages.ties)
+    )
+    *back_one, grad_first = back_first_call(raw_grad, attention_full, token_rows, stages.ties)
     gains = jnp.concatenate(
         [
             arrange_vector(grad_first[0], steps),
@@ -1178,18 +1264,15 @@
         ]
     )
     back_one_other = []
-    near_one, across, gains_got = settle(
-        scatter_call(ring, width, [input_one], raw_grad, core, far, stages.ties),
-        ring.swap_side(across[0]),
-        swap_tensor(gains),
-    )
-    gains = gains + gains_got
-    attention_sum = Scatter(ring, *near_one)
-
-    def places_of(value):
-        return [value[i * width : (i + 1) * width] for i in range(steps)]
-
-    output_sum = Scatter(ring, places_of(near[0]), None, places_of(across))
+    distances = [1] + [4 * 2**k for k in range((steps - 1).bit_length())] + [2]
+
+    def gains_sum(value, chosen):
+        for distance in chosen:
+            value = value + lax.ppermute(
+                value, "dp", [(k, k ^ distance) for k in range(dp_size)]
+            )
+        return value
+
     def token_call(first, last, into, ties):
         ins = [
             (back_one[first:last], "parts"),
@@ -1208,24 +1291,29 @@
             into=(into, first, rows),
         )[0]
 
-    distance = 1
     token_grad = block_output = None
+    sizes = (width, raw_grad.shape[1]), (width, query_columns)
+    joined_columns = sizes[0][1] + sizes[1][1]
+    sent = None
     for i in range(steps):
-        movers = [attention_sum] + ([output_sum] if output_sum.index < steps else [])
+        moves = [ring.swap_side(*stages.hold(other[i]))]
+        if i == 0:
+            moves.append(ring.swap_side(across[0]))
+        else:
+            moves.append(ring.shift(sent, 1))
         others = []
-        if i < PARTS:
-            others.append(swap_tensor(*stages.hold(back_one[i])))
-        if i < 2:
-            others.append(swap_tensor(out_sums[2 + i]))
-        if 0 < i < CHUNKS:
-            pair = picked(scattered[1])[:, (i - 1) * 3 * chunk : i * 3 * chunk]
-            others.append(ring.swap_side(*stages.hold(pair)))
-        if i == 2:
+        turns = [i] if i < PARTS else []
+        others.append([swap_tensor(back_one[k]) for k in turns])
+        k = i - (steps - CHUNKS + 1)
+        if k >= 0:
+            last_pair = picked(scattered[1])[:, k * 3 * chunk : (k + 1) * 3 * chunk]
+            others.append(ring.swap_side(*stages.hold(last_pair)))
+        if i == 1:
             (block_output,) = row_call(
                 functools.partial(output_kernel, turn),
                 rows,
                 128,
-                [(middle_parts, "parts"), (out_sums, "parts"), (out_done, "parts")],
+                [(middle_parts, "parts"), (out_sums, "halves"), (out_done, "halves")],
                 [(model_width, jnp.bfloat16)],
                 ties=stages.ties,
             )
@@ -1233,42 +1321,53 @@
         if i == steps - 1:
             early = len(back_one_other)
             token_grad = token_call(0, early, None, stages.ties)
-            grads = finish_call(ring, chunk, scattered, pairs_got)
-            others += [token_grad, grads]
-        if distance < dp_size:
-            others.append(
-                lax.ppermute(gains, "dp", [(k, k ^ distance) for k in range(dp_size)])
+            others.append(token_grad)
+            others.append(finish_call(ring, chunk, scattered, pairs_got))
+        if i == 0:
+            others.append(swap_tensor(out_sums[1]))
+        if i < 2:
+            others.append(gains_sum(gains, distances[:-1] if i == 0 else distances[-1:]))
+        if i == steps - 1:
+            others.append(gains + swap_tensor(gains))
+        moves, others = settle(moves, others)
+        others = list(others)
+        side, hop = moves
+        if i == 0:
+            across, group, late = hop, [mine[0], side], [(near, (0, 0)), (hop, (0, 0), sizes[1])]
+        else:
+            group = [mine[i], (hop, (0, 0)), side]
+            late = [
+                (near, (i, 0)),
+                (across, (i, 0)),
+                (hop, (0, sizes[0][1] // sizes[1][1]), sizes[1]),
+            ]
+        if i < steps - 1:
+            (sent,) = sums_call(
+                (("open", joined_columns), group), (("close", sizes[0][1]), late)
             )
-        others = list(step(movers, *others))
-        if distance < dp_size:
-            gains = gains + others.pop()
-            distance *= 2
+        else:
+            grad_query, grad_key, grad_value, grad_output = sums_call(
+                ((query_columns, key_columns, key_columns), group), ("turned", late)
+            )
+        if i < 2 or i == steps - 1:
+            gains = others.pop()
+        if i == 0:
+            out_done.append(others.pop())
         if i == steps - 1:
             grads = others.pop()
             token_grad = others.pop()
-        if i == 2:
+        if i == 1:
             block_output = others.pop()
-        if 0 < i < CHUNKS:
+        if k >= 0:
             pairs_got.append(others.pop())
-        if i < 2:
-            out_done.append(others.pop())
-        if i < PARTS:
-            back_one_other.append(others.pop())
+        back_one_other += others.pop()
     if early < PARTS:
         token_grad = token_call(early, PARTS, token_grad, stages.ties)
+    grads = finish_call(ring, chunk, None, pairs_got[-1:], grads)
     if not tiled:
         token_grad, block_output = turned(token_grad), turned(block_output)
-    grad_output = output_sum.total
-    grad_attention = attention_sum.total
-    grad_query = grad_attention[:, :query_columns]
-    grad_key = grad_attention[:, query_columns : query_columns + key_columns]
-    grad_value = grad_attention[:, query_columns + key_columns :]
-
     grad_gate, grad_up, grad_down = grads
 
-    while distance < dp_size:
-        gains = gains + lax.ppermute(gains, "dp", [(k, k ^ distance) for k in range(dp_size)])
-        distance *= 2
     index = lax.axis_index("dp")
 
     def own_part(start, size):
@@ -1283,7 +1382,7 @@
         grad_value,
         own_part(2 * model_width, HEAD_SIZE),
         own_part(2 * model_width + HEAD_SIZE, HEAD_SIZE),
-        grad_output.T,
+        grad_output,
         own_part(model_width, model_width),
         grad_gate,
         grad_up,

time: 574 us -> 558 us (0.972)
  other arithmetic: 24.7 us -> 16.6 us
  waiting for transfers between devices: 152 us -> 145 us
    ppermute x12 -> x9, waiting for transfers between devices: 66.9 us -> 35.6 us  [shift(): lax.ppermute(value, 'dp', [(i, (i + 4 * places) % self.size) for i in ran...]
    ppermute x33 -> x31, waiting for transfers between devices: 45.2 us -> 54.4 us  [swap_side(): return lax.ppermute(value, 'dp', [(i, i ^ 2) for i in range(self.size)])]
    pallas_call x3 -> x8, Pallas kernels: 23.1 us -> 31.1 us  [the longest x2 13.8 us: attention_call(): pl.pallas_call(attend_kernel, in_specs=specs + loose(ties), out_specs=[pl...]
    ppermute x4, waiting for transfers between devices: 7.42 us -> 14.1 us  [gains_sum(): lax.ppermute(value, 'dp', [(k, k ^ distance) for k in range(dp_size)])]
    ppermute x19 -> x17, waiting for transfers between devices: 29.8 us -> 35.6 us  [swap_tensor(): return lax.ppermute(value, 'tensor', [(0, 1), (1, 0)])]
    unnamed x205 -> x204, local copies, waits for them, and re-layouts: 10.7 us -> 13.2 us
    ppermute x19 -> x17, starting transfers between devices: 21.7 us -> 19.2 us  [swap_tensor(): return lax.ppermute(value, 'tensor', [(0, 1), (1, 0)])]
    ppermute x33 -> x31, starting transfers between devices: 34.3 us -> 34.1 us  [swap_side(): return lax.ppermute(value, 'dp', [(i, i ^ 2) for i in range(self.size)])]
  transfers between devices with their start and end apart: 93 -> 86, of which waited for: 28 -> 30; matrix products, arithmetic and copies ran while one was open for 5% -> 4% of each run, Pallas kernels for 49% -> 50%
where the time goes in v3:
time: 558 us; the launch traced here: 550 us
  Pallas kernels  284 us (51%)
  waiting for transfers between devices  145 us (26%)
  starting transfers between devices  66.8 us (12%)
  local copies, waits for them, and re-layouts  21.6 us (4%)
  other arithmetic  16.6 us (3%)
  between operations  15.2 us (3%)
    ppermute x31, waiting for transfers between devices, swap_side(): return lax.ppermute(value, 'dp', [(i, i ^ 2) for i in range(self.size)])  54.4 us
    pallas_call x12, Pallas kernels, row_call(): pl.pallas_call(body, grid=(rows // block,), in_specs=specs + loose(ties),...  53.9 us
    pallas_call x6, Pallas kernels, feed_call(): pl.pallas_call(functools.partial(feed_kernel, columns // 3, len(specs), l...  52.2 us
    pallas_call x4, Pallas kernels, wide_call(): pl.pallas_call(functools.partial(wide_kernel, count, start is not None, p...  38.7 us
    ppermute x9, waiting for transfers between devices, shift(): lax.ppermute(value, 'dp', [(i, (i + 4 * places) % self.size) for i in ran...  35.6 us
    ppermute x17, waiting for transfers between devices, swap_tensor(): return lax.ppermute(value, 'tensor', [(0, 1), (1, 0)])  35.6 us
    pallas_call x3, Pallas kernels, grad_call(): pl.pallas_call(functools.partial(grad_kernel, columns // 3 * 2, [len(g) f...  35 us
    ppermute x31, starting transfers between devices, swap_side(): return lax.ppermute(value, 'dp', [(i, i ^ 2) for i in range(self.size)])  34.1 us
  transfers between devices with their start and end apart: 86, of which 30 were waited for; matrix products, arithmetic and copies ran while one was open for 4% of the time, Pallas kernels for 50%

profile of v3, /device:TPU:0, one launch (start us, length us, event | category | flops | bytes accessed | tf_op | source)
XLA Modules:
  0.0 549.7 jit_solution(8935300188527896442)
XLA Ops:
  9.9 2.9 collective-permute-start.2
  22.7 5.7 %shard_map.237 = (bf16[512,2048]{1,0:T(8,128)(2,1)}, bf16[512,2048]{1,0:T(8,128)(2,1)}, bf16[512,2048]{1,0:T(8,128)(2,1)}) custom-call(bf16[512,2048]{1,0:T(8,128)(2,1)} %refs_0_.1, bf16[512,2048]{1,0:T(8,128)(2,1)} %refs_1_.1, f32[512,1]{1,0:T(8,128)} %copy.54.refs_2_, f32[1,2048]{1,0:T(1,128)} %bitcast.73), custom_call_target="tpu_custom_call" | custom-call | bytes 10496000 | tf_op jit(solution)/shard_map/pallas_call | solution.py:305
  28.4 5.4 collective-permute-done.3.rest_4_
  36.3 8.8 %collective-permute-done.8.rest_8_ = bf16[128,1024]{1,0:T(8,128)(2,1)S(1)} collective-permute-done((bf16[128,1024]{1,0:T(8,128)(2,1)}, bf16[128,1024]{1,0:T(8,128)(2,1)S(1)}, u32[]{:S(2)}, u32[]{:S(2)}) %collective-permute-start.8) | collective-permute-done | bytes 262176 | tf_op jit(solution)/shard_map/ppermute | solution.py:88
  45.7 9.4 %collective-permute-done.9 = bf16[128,1536]{1,0:T(8,128)(2,1)S(1)} collective-permute-done((bf16[128,1536]{1,0:T(8,128)(2,1)S(1)}, bf16[128,1536]{1,0:T(8,128)(2,1)S(1)}, u32[]{:S(2)}, u32[]{:S(2)}) %collective-permute-start.9) | collective-permute-done | bytes 393248 | tf_op jit(solution)/shard_map/ppermute | solution.py:85
  60.0 16.8 %collective-permute-done.14 = bf16[128,1536]{1,0:T(8,128)(2,1)S(1)} collective-permute-done((bf16[128,1536]{1,0:T(8,128)(2,1)S(1)}, bf16[128,1536]{1,0:T(8,128)(2,1)S(1)}, u32[]{:S(2)}, u32[]{:S(2)}) %collective-permute-start.14) | collective-permute-done | bytes 393248 | tf_op jit(solution)/shard_map/ppermute | solution.py:85
  82.6 12.6 %collective-permute-done.19.rest_12_ = bf16[128,1024]{1,0:T(8,128)(2,1)S(1)} collective-permute-done((bf16[128,1024]{1,0:T(8,128)(2,1)S(1)}, bf16[128,1024]{1,0:T(8,128)(2,1)S(1)}, u32[]{:S(2)}, u32[]{:S(2)}) %collective-permute-start.19) | collective-permute-done | bytes 262176 | tf_op jit(solution)/shard_map/ppermute | solution.py:88
  103.1 12.1 %shard_map.238 = (f32[512,2048]{1,0:T(8,128)}, bf16[2048,2048]{1,0:T(8,128)(2,1)}) custom-call(s32[16]{0:T(128)} %stack.139.order, bf16[512,2048]{1,0:T(8,128)(2,1)} %get-tuple-element.323.left.refs_0_, bf16[128,2048]{1,0:T(8,128)(2,1)} %copy-done.41, bf16[128,2048]{1,0:T(8,128)(2,1)} %collective-permute-done.2.rest_1_, ...), custom_call_target="tpu_custom_call" | custom-call | flops 4294967296 | bytes 20971520 | tf_op jit(solution)/shard_map/pallas_call | solution.py:873
  117.4 6.9 %shard_map.239 = (bf16[512,512]{1,0:T(8,128)(2,1)}, f32[16,512]{1,0:T(8,128)}) custom-call(f32[512,2048]{1,0:T(8,128)} %get-tuple-element.361.queries.keys.values, f32[512,2048]{1,0:T(8,128)} %get-tuple-element.361.queries.keys.values, f32[512,2048]{1,0:T(8,128)} %get-tuple-element.361.queries.keys.values, f32[1,128]{1,0:T(1,128)} %get-tuple-element.671.query_gain, ...), custom_call_target="tpu_custom_call" | custom-call | flops 536870912 | bytes 5242880 | tf_op jit(solution)/shard_map/pallas_call | solution.py:655
  127.4 6.9 %shard_map.240 = (bf16[512,512]{1,0:T(8,128)(2,1)}, f32[16,512]{1,0:T(8,128)}) custom-call(f32[512,2048]{1,0:T(8,128)} %get-tuple-element.361.queries.keys.values, f32[512,2048]{1,0:T(8,128)} %get-tuple-element.361.queries.keys.values, f32[512,2048]{1,0:T(8,128)} %get-tuple-element.361.queries.keys.values, f32[1,128]{1,0:T(1,128)} %get-tuple-element.671.query_gain, ...), custom_call_target="tpu_custom_call" | custom-call | flops 536870912 | bytes 5242880 | tf_op jit(solution)/shard_map/pallas_call | solution.py:655
  137.8 7.9 %shard_map.241 = (bf16[512,1024]{1,0:T(8,128)(2,1)}, bf16[2048,1024]{1,0:T(8,128)(2,1)}, bf16[128,2048]{1,0:T(8,128)(2,1)}, bf16[128,2048]{1,0:T(8,128)(2,1)}, b...) custom-call(s32[16]{0:T(128)} %stack.139.order, bf16[512,512]{1,0:T(8,128)(2,1)} %get-tuple-element.380.first, ...), custom_call_target="tpu_custom_call" | custom-call | flops 2147483648 | bytes 12582912 | tf_op jit(solution)/shard_map/pallas_call | solution.py:923
  147.0 3.6 collective-permute-done.34
  150.7 9.2 %collective-permute-done.33.refs_2_ = bf16[128,2048]{1,0:T(8,128)(2,1)S(1)} collective-permute-done((bf16[128,2048]{1,0:T(8,128)(2,1)}, bf16[128,2048]{1,0:T(8,128)(2,1)S(1)}, u32[]{:S(2)}, u32[]{:S(2)}) %collective-permute-start.33) | collective-permute-done | bytes 524320 | tf_op jit(solution)/shard_map/ppermute | solution.py:177
  162.8 2.8 shard_map.242
  165.6 7.4 %collective-permute-done.36 = bf16[128,2048]{1,0:T(8,128)(2,1)S(1)} collective-permute-done((bf16[128,2048]{1,0:T(8,128)(2,1)S(1)}, bf16[128,2048]{1,0:T(8,128)(2,1)S(1)}, u32[]{:S(2)}, u32[]{:S(2)}) %collective-permute-start.36) | collective-permute-done | bytes 524320 | tf_op jit(solution)/shard_map/ppermute | solution.py:85
  176.4 2.8 shard_map.243
  179.2 6.6 %collective-permute-done.37.refs_2_ = bf16[128,2048]{1,0:T(8,128)(2,1)S(1)} collective-permute-done((bf16[128,2048]{1,0:T(8,128)(2,1)S(1)}, bf16[128,2048]{1,0:T(8,128)(2,1)S(1)}, u32[]{:S(2)}, u32[]{:S(2)}) %collective-permute-start.37) | collective-permute-done | bytes 524320 | tf_op jit(solution)/shard_map/ppermute | solution.py:177
  189.0 2.8 shard_map.244
  191.8 5.9 %collective-permute-done.39.refs_2_ = bf16[128,2048]{1,0:T(8,128)(2,1)S(1)} collective-permute-done((bf16[128,2048]{1,0:T(8,128)(2,1)S(1)}, bf16[128,2048]{1,0:T(8,128)(2,1)S(1)}, u32[]{:S(2)}, u32[]{:S(2)}) %collective-permute-start.39) | collective-permute-done | bytes 524320 | tf_op jit(solution)/shard_map/ppermute | solution.py:177
  197.7 2.2 collective-permute-done.40.refs_1_.refs_5_
  201.1 2.9 shard_map.245
  206.9 8.4 %shard_map.246.refs_13_.refs_0_ = bf16[512,1536]{1,0:T(8,128)(2,1)} custom-call(bf16[128,2048]{1,0:T(8,128)(2,1)} %get-tuple-element.410.refs_0_, bf16[128,2048]{1,0:T(8,128)(2,1)} %get-tuple-element.419.refs_1_, bf16[128,2048]{1,0:T(8,128)(2,1)} %get-tuple-element.426.refs_2_, bf16[128,2048]{1,0:T(8,128)(2,1)} %get-tuple-element.429.refs_3_, ...), custom_call_target="tpu_custom_call" | custom-call | flops 3221225472 | bytes 12058624 | tf_op jit(solution)/shard_map/pallas_call | solution.py:414
  215.3 9.0 %shard_map.247.refs_1_.refs_13_ = bf16[512,1536]{1,0:T(8,128)(2,1)} custom-call(bf16[128,2048]{1,0:T(8,128)(2,1)} %get-tuple-element.410.refs_0_, bf16[128,2048]{1,0:T(8,128)(2,1)} %get-tuple-element.419.refs_1_, bf16[128,2048]{1,0:T(8,128)(2,1)} %get-tuple-element.426.refs_2_, bf16[128,2048]{1,0:T(8,128)(2,1)} %get-tuple-element.429.refs_3_, ...), custom_call_target="tpu_custom_call" | custom-call | flops 3221225472 | bytes 12058624 | tf_op jit(solution)/shard_map/pallas_call | solution.py:414
  226.6 8.7 %shard_map.248.refs_14_.refs_0_ = bf16[512,1536]{1,0:T(8,128)(2,1)} custom-call(bf16[128,2048]{1,0:T(8,128)(2,1)} %copy-done.2, bf16[128,2048]{1,0:T(8,128)(2,1)} %copy-done.3, bf16[128,2048]{1,0:T(8,128)(2,1)} %copy-done.4, bf16[128,2048]{1,0:T(8,128)(2,1)} %copy-done.5, bf16[128,2048]{1,0:T(8,128)(2,1)} %get-tuple-element.445.refs_4_.refs_9_, ...), custom_call_target="tpu_custom_call" | custom-call | flops 3221225472 | bytes 12058624 | tf_op jit(solution)/shard_map/pallas_call | solution.py:414
  235.3 11.5 %shard_map.249.refs_9_ = bf16[2048,1536]{1,0:T(8,128)(2,1)} custom-call(bf16[128,2048]{1,0:T(8,128)(2,1)} %get-tuple-element.410.refs_0_, bf16[128,2048]{1,0:T(8,128)(2,1)} %get-tuple-element.419.refs_1_, bf16[128,2048]{1,0:T(8,128)(2,1)} %get-tuple-element.426.refs_2_, bf16[128,2048]{1,0:T(8,128)(2,1)} %get-tuple-element.429.refs_3_, ...), custom_call_target="tpu_custom_call" | custom-call | flops 6442450944 | bytes 17825792 | tf_op jit(solution)/shard_map/pallas_call | solution.py:499
  246.9 8.9 %shard_map.250.refs_9_.refs_1_.refs_14_ = bf16[512,1536]{1,0:T(8,128)(2,1)} custom-call(bf16[128,2048]{1,0:T(8,128)(2,1)} %copy-done.2, bf16[128,2048]{1,0:T(8,128)(2,1)} %copy-done.3, bf16[128,2048]{1,0:T(8,128)(2,1)} %copy-done.4, bf16[128,2048]{1,0:T(8,128)(2,1)} %copy-done.5, bf16[128,2048]{1,0:T(8,128)(2,1)} %get-tuple-element.445.refs_4_.refs_9_, ...), custom_call_target="tpu_custom_call" | custom-call | flops 3221225472 | bytes 12058624 | tf_op jit(solution)/shard_map/pallas_call | solution.py:414
  255.8 3.6 all-gather.8.cloned.1.call-done.refs_8_.refs_5_
  259.4 8.7 %shard_map.251.refs_2_.refs_14_ = bf16[512,1536]{1,0:T(8,128)(2,1)} custom-call(bf16[128,2048]{1,0:T(8,128)(2,1)} %copy-done.2, bf16[128,2048]{1,0:T(8,128)(2,1)} %copy-done.3, bf16[128,2048]{1,0:T(8,128)(2,1)} %copy-done.4, bf16[128,2048]{1,0:T(8,128)(2,1)} %copy-done.5, bf16[128,2048]{1,0:T(8,128)(2,1)} %get-tuple-element.445.refs_4_.refs_9_, ...), custom_call_target="tpu_custom_call" | custom-call | flops 3221225472 | bytes 12058624 | tf_op jit(solution)/shard_map/pallas_call | solution.py:414
  268.1 11.4 %shard_map.252 = (bf16[128,2048]{1,0:T(8,128)(2,1)}, bf16[128,2048]{1,0:T(8,128)(2,1)}, bf16[128,2048]{1,0:T(8,128)(2,1)}, bf16[128,2048]{1,0:T(8,128)(2,1)}) custom-call(bf16[512,1536]{1,0:T(8,128)(2,1)} %shard_map.248.refs_14_.refs_0_, bf16[512,1536]{1,0:T(8,128)(2,1)} %shard_map.250.refs_9_.refs_1_.refs_14_, ...), custom_call_target="tpu_custom_call" | custom-call | flops 6442450944 | bytes 22020096 | tf_op jit(solution)/shard_map/pallas_call | solution.py:454
  281.0 8.5 %shard_map.253.refs_2_.refs_13_ = bf16[512,1536]{1,0:T(8,128)(2,1)} custom-call(bf16[128,2048]{1,0:T(8,128)(2,1)} %get-tuple-element.410.refs_0_, bf16[128,2048]{1,0:T(8,128)(2,1)} %get-tuple-element.419.refs_1_, bf16[128,2048]{1,0:T(8,128)(2,1)} %get-tuple-element.426.refs_2_, bf16[128,2048]{1,0:T(8,128)(2,1)} %get-tuple-element.429.refs_3_, ...), custom_call_target="tpu_custom_call" | custom-call | flops 3221225472 | bytes 12058624 | tf_op jit(solution)/shard_map/pallas_call | solution.py:414
  290.0 11.9 %shard_map.254 = (f32[128,2048]{1,0:T(8,128)}, f32[128,2048]{1,0:T(8,128)}, f32[128,2048]{1,0:T(8,128)}, f32[128,2048]{1,0:T(8,128)}) custom-call(bf16[512,1536]{1,0:T(8,128)(2,1)} %shard_map.246.refs_13_.refs_0_, bf16[512,1536]{1,0:T(8,128)(2,1)} %shard_map.247.refs_1_.refs_13_, bf16[512,1536]{1,0:T(8,128)(2,1)} %shard_map.253.refs_2_.refs_13_, ...), custom_call_target="tpu_custom_call" | custom-call | flops 6442450944 | bytes 22020096 | tf_op jit(solution)/shard_map/pallas_call | solution.py:454
  304.8 11.9 %shard_map.255.refs_15_ = bf16[2048,3072]{1,0:T(8,128)(2,1)} custom-call(bf16[128,2048]{1,0:T(8,128)(2,1)} %get-tuple-element.410.refs_0_, bf16[128,2048]{1,0:T(8,128)(2,1)} %get-tuple-element.419.refs_1_, bf16[128,2048]{1,0:T(8,128)(2,1)} %get-tuple-element.426.refs_2_, bf16[128,2048]{1,0:T(8,128)(2,1)} %get-tuple-element.429.refs_3_, ...), custom_call_target="tpu_custom_call" | custom-call | flops 6442450944 | bytes 17825792 | tf_op jit(solution)/shard_map/pallas_call | solution.py:499
  320.0 5.1 shard_map.257
  325.1 11.6 %shard_map.256 = bf16[2048,3072]{1,0:T(8,128)(2,1)} custom-call(bf16[128,2048]{1,0:T(8,128)(2,1)} %get-tuple-element.410.refs_0_, bf16[128,2048]{1,0:T(8,128)(2,1)} %get-tuple-element.419.refs_1_, bf16[128,2048]{1,0:T(8,128)(2,1)} %get-tuple-element.426.refs_2_, bf16[128,2048]{1,0:T(8,128)(2,1)} %get-tuple-element.429.refs_3_, ...), custom_call_target="tpu_custom_call", output_to_operand_aliasing={{}: (15, {})} | custom-call | flops 6442450944 | bytes 17825792 | tf_op jit(solution)/shard_map/pallas_call | solution.py:499
  339.3 5.3 shard_map.259
  344.6 7.5 %shard_map.258 = (bf16[256,2048]{1,0:T(8,128)(2,1)}, bf16[256,2048]{1,0:T(8,128)(2,1)}) custom-call(bf16[512,1536]{1,0:T(8,128)(2,1)} %shard_map.248.refs_14_.refs_0_, bf16[512,1536]{1,0:T(8,128)(2,1)} %shard_map.250.refs_9_.refs_1_.refs_14_, bf16[512,1536]{1,0:T(8,128)(2,1)} %shard_map.251.refs_2_.refs_14_, ...), custom_call_target="tpu_custom_call" | custom-call | flops 3221225472 | bytes 14155776 | tf_op jit(solution)/shard_map/pallas_call | solution.py:454
  355.7 5.1 shard_map.261
  360.8 7.8 %shard_map.260 = (f32[256,2048]{1,0:T(8,128)}, f32[256,2048]{1,0:T(8,128)}) custom-call(bf16[512,1536]{1,0:T(8,128)(2,1)} %shard_map.246.refs_13_.refs_0_, bf16[512,1536]{1,0:T(8,128)(2,1)} %shard_map.247.refs_1_.refs_13_, bf16[512,1536]{1,0:T(8,128)(2,1)} %shard_map.253.refs_2_.refs_13_, ...), custom_call_target="tpu_custom_call" | custom-call | flops 3221225472 | bytes 14155776 | tf_op jit(solution)/shard_map/pallas_call | solution.py:454
  369.4 5.2 shard_map.262
  374.6 5.1 shard_map.263
  382.9 17.0 %shard_map.264 = (bf16[512,2048]{1,0:T(8,128)(2,1)}, f32[1,128]{1,0:T(1,128)}, f32[1,128]{1,0:T(1,128)}) custom-call(f32[512,2048]{1,0:T(8,128)} %get-tuple-element.361.queries.keys.values, f32[512,2048]{1,0:T(8,128)} %get-tuple-element.361.queries.keys.values, f32[512,2048]{1,0:T(8,128)} %get-tuple-element.361.queries.keys.values, ...), custom_call_target="tpu_custom_call" | custom-call | flops 3221225472 | bytes 8388608 | tf_op jit(solution)/shard_map/pallas_call | solution.py:673
  401.9 3.7 collective-permute-done.56
  406.6 7.3 %shard_map.265 = (bf16[512,2048]{1,0:T(8,128)(2,1)}, bf16[512,2048]{1,0:T(8,128)(2,1)}) custom-call(s32[6]{0:T(128)} %stack.141.info, bf16[512,2048]{1,0:T(8,128)(2,1)} %get-tuple-element.323.left.refs_0_, bf16[512,2048]{1,0:T(8,128)(2,1)} %get-tuple-element.528.refs_1_.raw_grad, ...), custom_call_target="tpu_custom_call" | custom-call | flops 2147483648 | bytes 8388608 | tf_op jit(solution)/shard_map/pallas_call | solution.py:781
  418.7 5.7 %shard_map.266 = (bf16[512,1024]{1,0:T(8,128)(2,1)}, bf16[512,1024]{1,0:T(8,128)(2,1)}) custom-call(s32[6]{0:T(128)} %stack.58.info, bf16[128,2048]{1,0:T(8,128)(2,1)} %get-tuple-element.514.refs_0_, bf16[128,2048]{1,0:T(8,128)(2,1)} %get-tuple-element.515.refs_1_, bf16[128,2048]{1,0:T(8,128)(2,1)} %get-tuple-element.516.refs_2_, ...), custom_call_target="tpu_custom_call" | custom-call | flops 1073741824 | bytes 5242880 | tf_op jit(solution)/shard_map/pallas_call | solution.py:781
  426.1 8.5 %shard_map.267 = (bf16[128,2048]{1,0:T(8,128)(2,1)}, bf16[128,2048]{1,0:T(8,128)(2,1)}, bf16[128,2048]{1,0:T(8,128)(2,1)}, bf16[128,2048]{1,0:T(8,128)(2,1)}, bf...) custom-call(s32[6]{0:T(128)} %stack.58.info, ...), custom_call_target="tpu_custom_call" | custom-call | flops 2147483648 | bytes 8388608 | tf_op jit(solution)/shard_map/pallas_call | solution.py:781
  435.8 9.8 %shard_map.268 = (bf16[128,2048]{1,0:T(8,128)(2,1)}, bf16[128,2048]{1,0:T(8,128)(2,1)}, bf16[128,2048]{1,0:T(8,128)(2,1)}, bf16[128,2048]{1,0:T(8,128)(2,1)}, f32[1,2048]{1,0:T(1,128)}) custom-call(bf16[512,2048]{1,0:T(8,128)(2,1)} %get-tuple-element.528.refs_1_.raw_grad, bf16[2048,2048]{1,0:T(8,128)(2,1)} %get-tuple-element.553.full, ...), custom_call_target="tpu_custom_call" | custom-call | flops 4294967296 | bytes 16777216 | tf_op jit(solution)/shard_map/pallas_call | solution.py:707
  448.6 4.5 collective-permute-done.66
  454.9 4.1 collective-permute-done.67
  461.2 2.7 shard_map.269
  467.3 6.1 %shard_map.270 = bf16[512,2048]{1,0:T(8,128)(2,1)} custom-call(f32[128,2048]{1,0:T(8,128)} %get-tuple-element.475.refs_2_.refs_0_, f32[128,2048]{1,0:T(8,128)} %get-tuple-element.490.refs_2_.refs_1_, f32[128,2048]{1,0:T(8,128)} %get-tuple-element.501.refs_2_, f32[128,2048]{1,0:T(8,128)} %get-tuple-element.509.refs_2_.refs_3_, bf16[256,2048]{1,0:T(8,128)(2,1)} %copy-done.10, ...), custom_call_target="tpu_custom_call" | custom-call | bytes 10485760 | tf_op jit(solution)/shard_map/pallas_call | solution.py:305
  473.3 4.4 collective-permute-done.71
  477.7 6.1 %collective-permute-done.69.refs_1_.refs_5_ = bf16[128,3072]{1,0:T(8,128)(2,1)S(1)} collective-permute-done((bf16[128,3072]{1,0:T(8,128)(2,1)}, bf16[128,3072]{1,0:T(8,128)(2,1)S(1)}, u32[]{:S(2)}, u32[]{:S(2)}) %collective-permute-start.69) | collective-permute-done | bytes 786464 | tf_op jit(solution)/shard_map/ppermute | solution.py:88
  484.7 2.7 shard_map.271
  489.8 1.9 fusion.5
  492.7 6.3 %collective-permute-done.74.refs_5_ = bf16[128,2048]{1,0:T(8,128)(2,1)S(1)} collective-permute-done((bf16[128,2048]{1,0:T(8,128)(2,1)S(1)}, bf16[128,2048]{1,0:T(8,128)(2,1)S(1)}, u32[]{:S(2)}, u32[]{:S(2)}) %collective-permute-start.74) | collective-permute-done | bytes 524320 | tf_op jit(solution)/shard_map/ppermute | solution.py:177
  499.0 4.8 collective-permute-done.72.refs_2_
  503.9 2.7 collective-permute-done.73.refs_1_.refs_5_
  506.6 2.1 collective-permute-done.75.refs_3_
  508.7 2.7 shard_map.272
  515.7 6.6 %collective-permute-done.80 = f32[4352]{0:T(1024)S(1)} collective-permute-done((f32[4352]{0:T(1024)S(1)}, f32[4352]{0:T(1024)S(1)}, u32[]{:S(2)}, u32[]{:S(2)}) %collective-permute-start.80) | collective-permute-done | bytes 17440 | tf_op jit(solution)/shard_map/ppermute | solution.py:177
  522.3 6.9 %shard_map.273.refs_5_ = f32[512,2048]{1,0:T(8,128)} custom-call(bf16[128,2048]{1,0:T(8,128)(2,1)} %get-tuple-element.554.refs_0_, bf16[128,2048]{1,0:T(8,128)(2,1)} %get-tuple-element.570.refs_1_, bf16[128,2048]{1,0:T(8,128)(2,1)} %get-tuple-element.583.refs_2_, bf16[128,2048]{1,0:T(8,128)(2,1)} %copy-done.31, bf16[128,2048]{1,0:T(8,128)(2,1)} %copy-done.32, ...), custom_call_target="tpu_custom_call" | custom-call | bytes 11542528 | tf_op jit(solution)/shard_map/pallas_call | solution.py:305
  529.1 4.3 shard_map.274
  534.8 2.9 shard_map.276
  537.8 3.3 shard_map.275
  (420 shorter events, 110.6 us)
Async XLA Ops:
  7.2 199.7 %all-gather.4.cloned.1.call-start = ((), (), s32[]{:S(2)}) async-start(), calls=%async_computation.2 | async-start | bytes 7077888 | tf_op jit(solution)/shard_map/all_gather | solution.py:995
  9.9 23.9 %collective-permute-start.2 = (bf16[128,2048]{1,0:T(8,128)(2,1)S(1)}, bf16[128,2048]{1,0:T(8,128)(2,1)}, u32[]{:S(2)}, u32[]{:S(2)}) collective-permute-start(bf16[128,2048]{1,0:T(8,128)(2,1)S(1)} %pad_maximum_fusion.rest_0_), channel_id=1, source_target_pairs={{0,4},{2,6},{4,0},{6,2},{8,12},{10,14},{12,8},{14,10},{16,20},{18,... | collective-permute-start | bytes 1572872 | tf_op jit(solution)/shard_map/ppermute | solution.py:85
  12.8 21.0 %collective-permute-start.1 = (bf16[128,2048]{1,0:T(8,128)(2,1)S(1)}, bf16[128,2048]{1,0:T(8,128)(2,1)}, u32[]{:S(2)}, u32[]{:S(2)}) collective-permute-start(bf16[128,2048]{1,0:T(8,128)(2,1)S(1)} %pad_maximum_fusion.rest_0_), channel_id=1, source_target_pairs={{0,8},{2,10},{4,12},{6,14},{8,16},{10,18},{12,20},{14,22},{16,24},... | collective-permute-start | bytes 1572872 | tf_op jit(solution)/shard_map/ppermute | solution.py:88
  14.4 19.4 %collective-permute-start = (bf16[128,2048]{1,0:T(8,128)(2,1)S(1)}, bf16[128,2048]{1,0:T(8,128)(2,1)}, u32[]{:S(2)}, u32[]{:S(2)}) collective-permute-start(bf16[128,2048]{1,0:T(8,128)(2,1)S(1)} %pad_maximum_fusion.rest_0_), channel_id=1, source_target_pairs={{0,2},{2,0},{4,6},{6,4},{8,10},{10,8},{12,14},{14,12},{16,18},{18,... | collective-permute-start | bytes 1572872 | tf_op jit(solution)/shard_map/ppermute | solution.py:82
  15.5 18.3 %collective-permute-start.3 = (bf16[128,1024]{1,0:T(8,128)(2,1)S(1)}, bf16[128,1024]{1,0:T(8,128)(2,1)}, u32[]{:S(2)}, u32[]{:S(2)}) collective-permute-start(bf16[128,1024]{1,0:T(8,128)(2,1)S(1)} %bitcast.68), channel_id=1, source_target_pairs={{0,8},{2,10},{4,12},{6,14},{8,16},{10,18},{12,20},{14,22},{16,24},... | collective-permute-start | bytes 786440 | tf_op jit(solution)/shard_map/ppermute | solution.py:88
  33.9 21.2 %collective-permute-start.7 = (bf16[128,2048]{1,0:T(8,128)(2,1)}, bf16[128,2048]{1,0:T(8,128)(2,1)S(1)}, u32[]{:S(2)}, u32[]{:S(2)}) collective-permute-start(bf16[128,2048]{1,0:T(8,128)(2,1)} %collective-permute-done.1.rest_4_), channel_id=1, source_target_pairs={{0,4},{2,6},{4,0},{6,2},{8,12},{10,14},{12,8},{14,10},{16,20},{18,... | collective-permute-start | bytes 1572872 | tf_op jit(solution)/shard_map/ppermute | solution.py:85
  34.5 20.7 %collective-permute-start.6 = (bf16[128,2048]{1,0:T(8,128)(2,1)}, bf16[128,2048]{1,0:T(8,128)(2,1)}, u32[]{:S(2)}, u32[]{:S(2)}) collective-permute-start(bf16[128,2048]{1,0:T(8,128)(2,1)} %collective-permute-done.1.rest_4_), channel_id=1, source_target_pairs={{0,8},{2,10},{4,12},{6,14},{8,16},{10,18},{12,20},{14,22},{16,24},... | collective-permute-start | bytes 1572872 | tf_op jit(solution)/shard_map/ppermute | solution.py:88
  35.8 19.4 %collective-permute-start.5 = (bf16[128,2048]{1,0:T(8,128)(2,1)}, bf16[128,2048]{1,0:T(8,128)(2,1)}, u32[]{:S(2)}, u32[]{:S(2)}) collective-permute-start(bf16[128,2048]{1,0:T(8,128)(2,1)} %collective-permute-done.1.rest_4_), channel_id=1, source_target_pairs={{0,2},{2,0},{4,6},{6,4},{8,10},{10,8},{12,14},{14,12},{16,18},{18,... | collective-permute-start | bytes 1572872 | tf_op jit(solution)/shard_map/ppermute | solution.py:82
  35.8 19.4 %collective-permute-start.4 = (bf16[128,2048]{1,0:T(8,128)(2,1)}, bf16[128,2048]{1,0:T(8,128)(2,1)}, u32[]{:S(2)}, u32[]{:S(2)}) collective-permute-start(bf16[128,2048]{1,0:T(8,128)(2,1)} %collective-permute-done.2.rest_1_), channel_id=1, source_target_pairs={{0,2},{2,0},{4,6},{6,4},{8,10},{10,8},{12,14},{14,12},{16,18},{18,... | collective-permute-start | bytes 1572872 | tf_op jit(solution)/shard_map/ppermute | solution.py:82
  56.3 159.0 %all-gather.6.cloned.1.call-start = ((), (), s32[]{:S(2)}) async-start(), calls=%async_computation.3 | async-start | bytes 7077888 | tf_op jit(solution)/shard_map/all_gather | solution.py:995
  56.3 20.4 %collective-permute-start.13 = (bf16[128,2048]{1,0:T(8,128)(2,1)}, bf16[128,2048]{1,0:T(8,128)(2,1)S(1)}, u32[]{:S(2)}, u32[]{:S(2)}) collective-permute-start(bf16[128,2048]{1,0:T(8,128)(2,1)} %collective-permute-done.6.rest_8_), channel_id=1, source_target_pairs={{0,4},{2,6},{4,0},{6,2},{8,12},{10,14},{12,8},{14,10},{16,20},{18,... | collective-permute-start | bytes 1572872 | tf_op jit(solution)/shard_map/ppermute | solution.py:85
  57.2 19.6 %collective-permute-start.12 = (bf16[128,2048]{1,0:T(8,128)(2,1)}, bf16[128,2048]{1,0:T(8,128)(2,1)S(1)}, u32[]{:S(2)}, u32[]{:S(2)}) collective-permute-start(bf16[128,2048]{1,0:T(8,128)(2,1)} %collective-permute-done.6.rest_8_), channel_id=1, source_target_pairs={{0,8},{2,10},{4,12},{6,14},{8,16},{10,18},{12,20},{14,22},{16,24},... | collective-permute-start | bytes 1572872 | tf_op jit(solution)/shard_map/ppermute | solution.py:88
  57.9 18.9 %collective-permute-start.11 = (bf16[128,2048]{1,0:T(8,128)(2,1)}, bf16[128,2048]{1,0:T(8,128)(2,1)S(1)}, u32[]{:S(2)}, u32[]{:S(2)}) collective-permute-start(bf16[128,2048]{1,0:T(8,128)(2,1)} %collective-permute-done.6.rest_8_), channel_id=1, source_target_pairs={{0,2},{2,0},{4,6},{6,4},{8,10},{10,8},{12,14},{14,12},{16,18},{18,... | collective-permute-start | bytes 1572872 | tf_op jit(solution)/shard_map/ppermute | solution.py:82
  57.9 18.9 %collective-permute-start.10 = (bf16[128,2048]{1,0:T(8,128)(2,1)S(1)}, bf16[128,2048]{1,0:T(8,128)(2,1)S(1)}, u32[]{:S(2)}, u32[]{:S(2)}) collective-permute-start(bf16[128,2048]{1,0:T(8,128)(2,1)S(1)} %collective-permute-done.7.rest_5_), channel_id=1, source_target_pairs={{0,2},{2,0},{4,6},{6,4},{8,10},{10,8},{12,14},{14,12},{16,18},{18,... | collective-permute-start | bytes 1572872 | tf_op jit(solution)/shard_map/ppermute | solution.py:82
  58.4 18.3 %collective-permute-start.14 = (bf16[128,1536]{1,0:T(8,128)(2,1)S(1)}, bf16[128,1536]{1,0:T(8,128)(2,1)S(1)}, u32[]{:S(2)}, u32[]{:S(2)}) collective-permute-start(bf16[128,1536]{1,0:T(8,128)(2,1)S(1)} %pad_maximum_fusion.2), channel_id=1, source_target_pairs={{0,4},{2,6},{4,0},{6,2},{8,12},{10,14},{12,8},{14,10},{16,20},{18,... | collective-permute-start | bytes 1179656 | tf_op jit(solution)/shard_map/ppermute | solution.py:85
  79.5 179.9 %all-gather.8.cloned.1.call-start = ((), (), s32[]{:S(2)}) async-start(), calls=%async_computation.4 | async-start | bytes 7077888 | tf_op jit(solution)/shard_map/all_gather | solution.py:995
  79.5 15.7 %collective-permute-start.19 = (bf16[128,1024]{1,0:T(8,128)(2,1)S(1)}, bf16[128,1024]{1,0:T(8,128)(2,1)S(1)}, u32[]{:S(2)}, u32[]{:S(2)}) collective-permute-start(bf16[128,1024]{1,0:T(8,128)(2,1)S(1)} %copy-done.86), channel_id=1, source_target_pairs={{0,8},{2,10},{4,12},{6,14},{8,16},{10,18},{12,20},{14,22},{16,24},... | collective-permute-start | bytes 786440 | tf_op jit(solution)/shard_map/ppermute | solution.py:88
  80.0 16.7 %collective-permute-start.17 = (bf16[128,2048]{1,0:T(8,128)(2,1)}, bf16[128,2048]{1,0:T(8,128)(2,1)S(1)}, u32[]{:S(2)}, u32[]{:S(2)}) collective-permute-start(bf16[128,2048]{1,0:T(8,128)(2,1)} %copy-done.74), channel_id=1, source_target_pairs={{0,4},{2,6},{4,0},{6,2},{8,12},{10,14},{12,8},{14,10},{16,20},{18,... | collective-permute-start | bytes 1572872 | tf_op jit(solution)/shard_map/ppermute | solution.py:85
  80.7 16.0 %collective-permute-start.16 = (bf16[128,2048]{1,0:T(8,128)(2,1)}, bf16[128,2048]{1,0:T(8,128)(2,1)S(1)}, u32[]{:S(2)}, u32[]{:S(2)}) collective-permute-start(bf16[128,2048]{1,0:T(8,128)(2,1)} %copy-done.74), channel_id=1, source_target_pairs={{0,2},{2,0},{4,6},{6,4},{8,10},{10,8},{12,14},{14,12},{16,18},{18,... | collective-permute-start | bytes 1572872 | tf_op jit(solution)/shard_map/ppermute | solution.py:82
  80.7 16.0 %collective-permute-start.15 = (bf16[128,2048]{1,0:T(8,128)(2,1)S(1)}, bf16[128,2048]{1,0:T(8,128)(2,1)S(1)}, u32[]{:S(2)}, u32[]{:S(2)}) collective-permute-start(bf16[128,2048]{1,0:T(8,128)(2,1)S(1)} %copy-done.73), channel_id=1, source_target_pairs={{0,2},{2,0},{4,6},{6,4},{8,10},{10,8},{12,14},{14,12},{16,18},{18,... | collective-permute-start | bytes 1572872 | tf_op jit(solution)/shard_map/ppermute | solution.py:82
  81.2 15.2 %collective-permute-start.20 = (bf16[128,1024]{1,0:T(8,128)(2,1)S(1)}, bf16[128,1024]{1,0:T(8,128)(2,1)S(1)}, u32[]{:S(2)}, u32[]{:S(2)}) collective-permute-start(bf16[128,1024]{1,0:T(8,128)(2,1)S(1)} %bitcast.69), channel_id=1, source_target_pairs={{0,4},{2,6},{4,0},{6,2},{8,12},{10,14},{12,8},{14,10},{16,20},{18,... | collective-permute-start | bytes 786440 | tf_op jit(solution)/shard_map/ppermute | solution.py:85
  100.8 14.4 %collective-permute-start.21 = (bf16[128,1024]{1,0:T(8,128)(2,1)}, bf16[128,1024]{1,0:T(8,128)(2,1)S(1)}, u32[]{:S(2)}, u32[]{:S(2)}) collective-permute-start(bf16[128,1024]{1,0:T(8,128)(2,1)} %copy-done.89), channel_id=1, source_target_pairs={{0,2},{2,0},{4,6},{6,4},{8,10},{10,8},{12,14},{14,12},{16,18},{18,... | collective-permute-start | bytes 786440 | tf_op jit(solution)/shard_map/ppermute | solution.py:82
  101.0 14.2 %collective-permute-start.24 = (bf16[128,1024]{1,0:T(8,128)(2,1)}, bf16[128,1024]{1,0:T(8,128)(2,1)S(1)}, u32[]{:S(2)}, u32[]{:S(2)}) collective-permute-start(bf16[128,1024]{1,0:T(8,128)(2,1)} %collective-permute-done.3.rest_4_), channel_id=1, source_target_pairs={{0,4},{2,6},{4,0},{6,2},{8,12},{10,14},{12,8},{14,10},{16,20},{18,... | collective-permute-start | bytes 786440 | tf_op jit(solution)/shard_map/ppermute | solution.py:85
  101.9 13.3 %collective-permute-start.23 = (bf16[128,1024]{1,0:T(8,128)(2,1)}, bf16[128,1024]{1,0:T(8,128)(2,1)S(1)}, u32[]{:S(2)}, u32[]{:S(2)}) collective-permute-start(bf16[128,1024]{1,0:T(8,128)(2,1)} %collective-permute-done.3.rest_4_), channel_id=1, source_target_pairs={{0,2},{2,0},{4,6},{6,4},{8,10},{10,8},{12,14},{14,12},{16,18},{18,... | collective-permute-start | bytes 786440 | tf_op jit(solution)/shard_map/ppermute | solution.py:82
  102.1 22.2 %collective-permute-start.28 = (bf16[128,1536]{1,0:T(8,128)(2,1)S(1)}, bf16[128,1536]{1,0:T(8,128)(2,1)S(1)}, u32[]{:S(2)}, u32[]{:S(2)}) collective-permute-start(bf16[128,1536]{1,0:T(8,128)(2,1)S(1)} %pad_maximum_fusion.3), channel_id=1, source_target_pairs={{0,4},{2,6},{4,0},{6,2},{8,12},{10,14},{12,8},{14,10},{16,20},{18,... | collective-permute-start | bytes 1179656 | tf_op jit(solution)/shard_map/ppermute | solution.py:85
  125.5 281.1 %reduce-scatter.3.cloned.1.call-start = ((), (), s32[]{:S(2)}) async-start(), calls=%async_computation.5 | async-start | bytes 7077888 | tf_op jit(solution)/shard_map/reduce_scatter | solution.py:1202
  136.7 14.0 %collective-permute-start.34 = (bf16[128,2048]{1,0:T(8,128)(2,1)S(1)}, bf16[128,2048]{1,0:T(8,128)(2,1)S(1)}, u32[]{:S(2)}, u32[]{:S(2)}) collective-permute-start(bf16[128,2048]{1,0:T(8,128)(2,1)S(1)} %get-tuple-element.395), channel_id=1, source_target_pairs={{0,4},{2,6},{4,0},{6,2},{8,12},{10,14},{12,8},{14,10},{16,20},{18,... | collective-permute-start | bytes 1572872 | tf_op jit(solution)/shard_map/ppermute | solution.py:85
  145.7 14.2 %collective-permute-start.33 = (bf16[128,2048]{1,0:T(8,128)(2,1)}, bf16[128,2048]{1,0:T(8,128)(2,1)S(1)}, u32[]{:S(2)}, u32[]{:S(2)}) collective-permute-start(bf16[128,2048]{1,0:T(8,128)(2,1)} %get-tuple-element.403.refs_1_), channel_id=1, source_target_pairs={{0,1},{1,0},{2,3},{3,2},{4,5},{5,4},{6,7},{7,6},{8,9},{9,8},{10,11... | collective-permute-start | bytes 1572872 | tf_op jit(solution)/shard_map/ppermute | solution.py:177
  159.8 13.2 %collective-permute-start.36 = (bf16[128,2048]{1,0:T(8,128)(2,1)S(1)}, bf16[128,2048]{1,0:T(8,128)(2,1)S(1)}, u32[]{:S(2)}, u32[]{:S(2)}) collective-permute-start(bf16[128,2048]{1,0:T(8,128)(2,1)S(1)} %get-tuple-element.401), channel_id=1, source_target_pairs={{0,4},{2,6},{4,0},{6,2},{8,12},{10,14},{12,8},{14,10},{16,20},{18,... | collective-permute-start | bytes 1572872 | tf_op jit(solution)/shard_map/ppermute | solution.py:85
  161.1 12.9 %collective-permute-start.35 = (bf16[128,2048]{1,0:T(8,128)(2,1)}, bf16[128,2048]{1,0:T(8,128)(2,1)S(1)}, u32[]{:S(2)}, u32[]{:S(2)}) collective-permute-start(bf16[128,2048]{1,0:T(8,128)(2,1)} %get-tuple-element.411.refs_1_), channel_id=1, source_target_pairs={{0,1},{1,0},{2,3},{3,2},{4,5},{5,4},{6,7},{7,6},{8,9},{9,8},{10,11... | collective-permute-start | bytes 1572872 | tf_op jit(solution)/shard_map/ppermute | solution.py:177
  199.9 15.4 %collective-permute-start.41 = (bf16[128,2048]{1,0:T(8,128)(2,1)}, bf16[128,2048]{1,0:T(8,128)(2,1)S(1)}, u32[]{:S(2)}, u32[]{:S(2)}) collective-permute-start(bf16[128,2048]{1,0:T(8,128)(2,1)} %get-tuple-element.426.refs_2_), channel_id=1, source_target_pairs={{0,4},{2,6},{4,0},{6,2},{8,12},{10,14},{12,8},{14,10},{16,20},{18,... | collective-permute-start | bytes 1572872 | tf_op jit(solution)/shard_map/ppermute | solution.py:85
  204.0 20.3 %collective-permute-start.42 = (bf16[128,2048]{1,0:T(8,128)(2,1)}, bf16[128,2048]{1,0:T(8,128)(2,1)S(1)}, u32[]{:S(2)}, u32[]{:S(2)}) collective-permute-start(bf16[128,2048]{1,0:T(8,128)(2,1)} %get-tuple-element.429.refs_3_), channel_id=1, source_target_pairs={{0,4},{2,6},{4,0},{6,2},{8,12},{10,14},{12,8},{14,10},{16,20},{18,... | collective-permute-start | bytes 1572872 | tf_op jit(solution)/shard_map/ppermute | solution.py:85
  204.8 19.5 %collective-permute-start.43 = (bf16[128,2048]{1,0:T(8,128)(2,1)S(1)}, bf16[128,2048]{1,0:T(8,128)(2,1)S(1)}, u32[]{:S(2)}, u32[]{:S(2)}) collective-permute-start(bf16[128,2048]{1,0:T(8,128)(2,1)S(1)} %collective-permute-done.34), channel_id=1, source_target_pairs={{0,1},{1,0},{2,3},{3,2},{4,5},{5,4},{6,7},{7,6},{8,9},{9,8},{10,11... | collective-permute-start | bytes 1572872 | tf_op jit(solution)/shard_map/ppermute | solution.py:177
  205.7 18.6 %collective-permute-start.44 = (bf16[128,2048]{1,0:T(8,128)(2,1)S(1)}, bf16[128,2048]{1,0:T(8,128)(2,1)S(1)}, u32[]{:S(2)}, u32[]{:S(2)}) collective-permute-start(bf16[128,2048]{1,0:T(8,128)(2,1)S(1)} %collective-permute-done.36), channel_id=1, source_target_pairs={{0,1},{1,0},{2,3},{3,2},{4,5},{5,4},{6,7},{7,6},{8,9},{9,8},{10,11... | collective-permute-start | bytes 1572872 | tf_op jit(solution)/shard_map/ppermute | solution.py:177
  246.8 243.0 %reduce-scatter.5.cloned.1.call-start = ((), (), s32[]{:S(2)}) async-start(), calls=%async_computation.6 | async-start | bytes 14155776 | tf_op jit(solution)/shard_map/reduce_scatter | solution.py:1202
  279.5 22.4 %collective-permute-start.45 = (bf16[128,2048]{1,0:T(8,128)(2,1)}, bf16[128,2048]{1,0:T(8,128)(2,1)S(1)}, u32[]{:S(2)}, u32[]{:S(2)}) collective-permute-start(bf16[128,2048]{1,0:T(8,128)(2,1)} %get-tuple-element.452.refs_6_), channel_id=1, source_target_pairs={{0,4},{2,6},{4,0},{6,2},{8,12},{10,14},{12,8},{14,10},{16,20},{18,... | collective-permute-start | bytes 1572872 | tf_op jit(solution)/shard_map/ppermute | solution.py:85
  289.5 27.2 %collective-permute-start.47 = (bf16[128,2048]{1,0:T(8,128)(2,1)S(1)}, bf16[128,2048]{1,0:T(8,128)(2,1)S(1)}, u32[]{:S(2)}, u32[]{:S(2)}) collective-permute-start(bf16[128,2048]{1,0:T(8,128)(2,1)S(1)} %copy-done.84), channel_id=1, source_target_pairs={{0,4},{2,6},{4,0},{6,2},{8,12},{10,14},{12,8},{14,10},{16,20},{18,... | collective-permute-start | bytes 1572872 | tf_op jit(solution)/shard_map/ppermute | solution.py:85
  303.3 13.5 %collective-permute-start.46 = (bf16[128,2048]{1,0:T(8,128)(2,1)S(1)}, bf16[128,2048]{1,0:T(8,128)(2,1)S(1)}, u32[]{:S(2)}, u32[]{:S(2)}) collective-permute-start(bf16[128,2048]{1,0:T(8,128)(2,1)S(1)} %add_convert_fusion.5.refs_15_.refs_0_), channel_id=1, source_target_pairs={{0,1},{1,0},{2,3},{3,2},{4,5},{5,4},{6,7},{7,6},{8,9},{9,8},{10,11... | collective-permute-start | bytes 1572872 | tf_op jit(solution)/shard_map/ppermute | solution.py:177
  316.8 19.9 %collective-permute-start.49 = (bf16[128,2048]{1,0:T(8,128)(2,1)S(1)}, bf16[128,2048]{1,0:T(8,128)(2,1)S(1)}, u32[]{:S(2)}, u32[]{:S(2)}) collective-permute-start(bf16[128,2048]{1,0:T(8,128)(2,1)S(1)} %copy-done.83), channel_id=1, source_target_pairs={{0,4},{2,6},{4,0},{6,2},{8,12},{10,14},{12,8},{14,10},{16,20},{18,... | collective-permute-start | bytes 1572872 | tf_op jit(solution)/shard_map/ppermute | solution.py:85
  318.5 18.2 %collective-permute-start.48 = (bf16[128,2048]{1,0:T(8,128)(2,1)S(1)}, bf16[128,2048]{1,0:T(8,128)(2,1)S(1)}, u32[]{:S(2)}, u32[]{:S(2)}) collective-permute-start(bf16[128,2048]{1,0:T(8,128)(2,1)S(1)} %add_convert_fusion.4.refs_16_.refs_0_), channel_id=1, source_target_pairs={{0,1},{1,0},{2,3},{3,2},{4,5},{5,4},{6,7},{7,6},{8,9},{9,8},{10,11... | collective-permute-start | bytes 1572872 | tf_op jit(solution)/shard_map/ppermute | solution.py:177
  338.0 14.2 %collective-permute-start.51 = (bf16[128,2048]{1,0:T(8,128)(2,1)S(1)}, bf16[128,2048]{1,0:T(8,128)(2,1)S(1)}, u32[]{:S(2)}, u32[]{:S(2)}) collective-permute-start(bf16[128,2048]{1,0:T(8,128)(2,1)S(1)} %copy-done.82), channel_id=1, source_target_pairs={{0,4},{2,6},{4,0},{6,2},{8,12},{10,14},{12,8},{14,10},{16,20},{18,... | collective-permute-start | bytes 1572872 | tf_op jit(solution)/shard_map/ppermute | solution.py:85
  338.7 13.5 %collective-permute-start.50 = (bf16[128,2048]{1,0:T(8,128)(2,1)S(1)}, bf16[128,2048]{1,0:T(8,128)(2,1)S(1)}, u32[]{:S(2)}, u32[]{:S(2)}) collective-permute-start(bf16[128,2048]{1,0:T(8,128)(2,1)S(1)} %add_convert_fusion.3.refs_6_.refs_0_), channel_id=1, source_target_pairs={{0,1},{1,0},{2,3},{3,2},{4,5},{5,4},{6,7},{7,6},{8,9},{9,8},{10,11... | collective-permute-start | bytes 1572872 | tf_op jit(solution)/shard_map/ppermute | solution.py:177
  352.2 28.1 %collective-permute-start.53 = (bf16[256,2048]{1,0:T(8,128)(2,1)}, bf16[256,2048]{1,0:T(8,128)(2,1)S(1)}, u32[]{:S(2)}, u32[]{:S(2)}) collective-permute-start(bf16[256,2048]{1,0:T(8,128)(2,1)} %get-tuple-element.512), channel_id=1, source_target_pairs={{0,4},{2,6},{4,0},{6,2},{8,12},{10,14},{12,8},{14,10},{16,20},{18,... | collective-permute-start | bytes 3145736 | tf_op jit(solution)/shard_map/ppermute | solution.py:85
  353.7 14.9 %collective-permute-start.52 = (bf16[128,2048]{1,0:T(8,128)(2,1)S(1)}, bf16[128,2048]{1,0:T(8,128)(2,1)S(1)}, u32[]{:S(2)}, u32[]{:S(2)}) collective-permute-start(bf16[128,2048]{1,0:T(8,128)(2,1)S(1)} %add_convert_fusion.2.refs_6_.refs_0_), channel_id=1, source_target_pairs={{0,1},{1,0},{2,3},{3,2},{4,5},{5,4},{6,7},{7,6},{8,9},{9,8},{10,11... | collective-permute-start | bytes 1572872 | tf_op jit(solution)/shard_map/ppermute | solution.py:177
  379.7 20.2 %collective-permute-start.55 = (bf16[512,1024]{1,0:T(8,128)(2,1)}, bf16[512,1024]{1,0:T(8,128)(2,1)S(1)}, u32[]{:S(2)}, u32[]{:S(2)}) collective-permute-start(bf16[512,1024]{1,0:T(8,128)(2,1)} %get-tuple-element.523), channel_id=1, source_target_pairs={{0,2},{2,0},{4,6},{6,4},{8,10},{10,8},{12,14},{14,12},{16,18},{18,... | collective-permute-start | bytes 3145736 | tf_op jit(solution)/shard_map/ppermute | solution.py:82
  379.8 21.1 %collective-permute-start.54 = (bf16[512,1024]{1,0:T(8,128)(2,1)}, bf16[512,1024]{1,0:T(8,128)(2,1)S(1)}, u32[]{:S(2)}, u32[]{:S(2)}) collective-permute-start(bf16[512,1024]{1,0:T(8,128)(2,1)} %get-tuple-element.519.rest_5_), channel_id=1, source_target_pairs={{0,2},{2,0},{4,6},{6,4},{8,10},{10,8},{12,14},{14,12},{16,18},{18,... | collective-permute-start | bytes 3145736 | tf_op jit(solution)/shard_map/ppermute | solution.py:82
  380.3 25.4 %collective-permute-start.56 = (bf16[256,2048]{1,0:T(8,128)(2,1)}, bf16[256,2048]{1,0:T(8,128)(2,1)S(1)}, u32[]{:S(2)}, u32[]{:S(2)}) collective-permute-start(bf16[256,2048]{1,0:T(8,128)(2,1)} %get-tuple-element.525), channel_id=1, source_target_pairs={{0,4},{2,6},{4,0},{6,2},{8,12},{10,14},{12,8},{14,10},{16,20},{18,... | collective-permute-start | bytes 3145736 | tf_op jit(solution)/shard_map/ppermute | solution.py:85
  381.3 25.3 %collective-permute-start.57 = (bf16[256,2048]{1,0:T(8,128)(2,1)S(1)}, bf16[256,2048]{1,0:T(8,128)(2,1)}, u32[]{:S(2)}, u32[]{:S(2)}) collective-permute-start(bf16[256,2048]{1,0:T(8,128)(2,1)S(1)} %add_convert_fusion.1.refs_4_), channel_id=1, source_target_pairs={{0,1},{1,0},{2,3},{3,2},{4,5},{5,4},{6,7},{7,6},{8,9},{9,8},{10,11... | collective-permute-start | bytes 3145736 | tf_op jit(solution)/shard_map/ppermute | solution.py:177
  413.9 12.2 %collective-permute-start.59 = (bf16[512,2048]{1,0:T(8,128)(2,1)}, bf16[512,2048]{1,0:T(8,128)(2,1)}, u32[]{:S(2)}, u32[]{:S(2)}) collective-permute-start(bf16[512,2048]{1,0:T(8,128)(2,1)} %get-tuple-element.531), channel_id=1, source_target_pairs={{0,2},{2,0},{4,6},{6,4},{8,10},{10,8},{12,14},{14,12},{16,18},{18,... | collective-permute-start | bytes 6291464 | tf_op jit(solution)/shard_map/ppermute | solution.py:82
  413.9 12.2 %collective-permute-start.58 = (bf16[512,2048]{1,0:T(8,128)(2,1)}, bf16[512,2048]{1,0:T(8,128)(2,1)}, u32[]{:S(2)}, u32[]{:S(2)}) collective-permute-start(bf16[512,2048]{1,0:T(8,128)(2,1)} %get-tuple-element.530.refs_8_), channel_id=1, source_target_pairs={{0,2},{2,0},{4,6},{6,4},{8,10},{10,8},{12,14},{14,12},{16,18},{18,... | collective-permute-start | bytes 6291464 | tf_op jit(solution)/shard_map/ppermute | solution.py:82
  417.7 41.2 %collective-permute-start.64 = (bf16[256,2048]{1,0:T(8,128)(2,1)S(1)}, bf16[256,2048]{1,0:T(8,128)(2,1)S(1)}, u32[]{:S(2)}, u32[]{:S(2)}) collective-permute-start(bf16[256,2048]{1,0:T(8,128)(2,1)S(1)} %add_convert_fusion.refs_5_), channel_id=1, source_target_pairs={{0,1},{1,0},{2,3},{3,2},{4,5},{5,4},{6,7},{7,6},{8,9},{9,8},{10,11... | collective-permute-start | bytes 3145736 | tf_op jit(solution)/shard_map/ppermute | solution.py:177
  424.3 34.6 %collective-permute-start.62 = (bf16[512,1024]{1,0:T(8,128)(2,1)}, bf16[512,1024]{1,0:T(8,128)(2,1)S(1)}, u32[]{:S(2)}, u32[]{:S(2)}) collective-permute-start(bf16[512,1024]{1,0:T(8,128)(2,1)} %get-tuple-element.552), channel_id=1, source_target_pairs={{0,4},{2,6},{4,0},{6,2},{8,12},{10,14},{12,8},{14,10},{16,20},{18,... | collective-permute-start | bytes 3145736 | tf_op jit(solution)/shard_map/ppermute | solution.py:85
  434.7 25.7 %collective-permute-start.61 = (bf16[128,2048]{1,0:T(8,128)(2,1)}, bf16[128,2048]{1,0:T(8,128)(2,1)S(1)}, u32[]{:S(2)}, u32[]{:S(2)}) collective-permute-start(bf16[128,2048]{1,0:T(8,128)(2,1)} %get-tuple-element.551), channel_id=1, source_target_pairs={{0,4},{2,6},{4,0},{6,2},{8,12},{10,14},{12,8},{14,10},{16,20},{18,... | collective-permute-start | bytes 1572872 | tf_op jit(solution)/shard_map/ppermute | solution.py:85
  445.6 14.8 %collective-permute-start.63 = (bf16[128,2048]{1,0:T(8,128)(2,1)}, bf16[128,2048]{1,0:T(8,128)(2,1)S(1)}, u32[]{:S(2)}, u32[]{:S(2)}) collective-permute-start(bf16[128,2048]{1,0:T(8,128)(2,1)} %get-tuple-element.554.refs_0_), channel_id=1, source_target_pairs={{0,1},{1,0},{2,3},{3,2},{4,5},{5,4},{6,7},{7,6},{8,9},{9,8},{10,11... | collective-permute-start | bytes 1572872 | tf_op jit(solution)/shard_map/ppermute | solution.py:177
  463.8 20.0 %collective-permute-start.69 = (bf16[128,3072]{1,0:T(8,128)(2,1)}, bf16[128,3072]{1,0:T(8,128)(2,1)S(1)}, u32[]{:S(2)}, u32[]{:S(2)}) collective-permute-start(bf16[128,3072]{1,0:T(8,128)(2,1)} %shard_map.269), channel_id=1, source_target_pairs={{0,8},{2,10},{4,12},{6,14},{8,16},{10,18},{12,20},{14,22},{16,24},... | collective-permute-start | bytes 2359304 | tf_op jit(solution)/shard_map/ppermute | solution.py:88
  463.8 13.9 %collective-permute-start.70 = (bf16[128,2048]{1,0:T(8,128)(2,1)S(1)}, bf16[128,2048]{1,0:T(8,128)(2,1)S(1)}, u32[]{:S(2)}, u32[]{:S(2)}) collective-permute-start(bf16[128,2048]{1,0:T(8,128)(2,1)S(1)} %copy-done.29), channel_id=1, source_target_pairs={{0,1},{1,0},{2,3},{3,2},{4,5},{5,4},{6,7},{7,6},{8,9},{9,8},{10,11... | collective-permute-start | bytes 1572872 | tf_op jit(solution)/shard_map/ppermute | solution.py:177
  465.2 12.5 %collective-permute-start.68 = (bf16[128,2048]{1,0:T(8,128)(2,1)S(1)}, bf16[128,2048]{1,0:T(8,128)(2,1)S(1)}, u32[]{:S(2)}, u32[]{:S(2)}) collective-permute-start(bf16[128,2048]{1,0:T(8,128)(2,1)S(1)} %copy-done.81), channel_id=1, source_target_pairs={{0,4},{2,6},{4,0},{6,2},{8,12},{10,14},{12,8},{14,10},{16,20},{18,... | collective-permute-start | bytes 1572872 | tf_op jit(solution)/shard_map/ppermute | solution.py:85
  487.5 19.1 %collective-permute-start.73 = (bf16[128,3072]{1,0:T(8,128)(2,1)}, bf16[128,3072]{1,0:T(8,128)(2,1)S(1)}, u32[]{:S(2)}, u32[]{:S(2)}) collective-permute-start(bf16[128,3072]{1,0:T(8,128)(2,1)} %shard_map.271), channel_id=1, source_target_pairs={{0,8},{2,10},{4,12},{6,14},{8,16},{10,18},{12,20},{14,22},{16,24},... | collective-permute-start | bytes 2359304 | tf_op jit(solution)/shard_map/ppermute | solution.py:88
  488.8 15.1 %collective-permute-start.72 = (bf16[128,2048]{1,0:T(8,128)(2,1)}, bf16[128,2048]{1,0:T(8,128)(2,1)S(1)}, u32[]{:S(2)}, u32[]{:S(2)}) collective-permute-start(bf16[128,2048]{1,0:T(8,128)(2,1)} %get-tuple-element.579), channel_id=1, source_target_pairs={{0,4},{2,6},{4,0},{6,2},{8,12},{10,14},{12,8},{14,10},{16,20},{18,... | collective-permute-start | bytes 1572872 | tf_op jit(solution)/shard_map/ppermute | solution.py:85
  491.7 17.0 %collective-permute-start.75 = (bf16[128,1536]{1,0:T(8,128)(2,1)S(1)}, bf16[128,1536]{1,0:T(8,128)(2,1)}, u32[]{:S(2)}, u32[]{:S(2)}) collective-permute-start(bf16[128,1536]{1,0:T(8,128)(2,1)S(1)} %get-tuple-element.585), channel_id=1, source_target_pairs={{0,4},{2,6},{4,0},{6,2},{8,12},{10,14},{12,8},{14,10},{16,20},{18,... | collective-permute-start | bytes 1179656 | tf_op jit(solution)/shard_map/ppermute | solution.py:85
  511.5 22.0 %collective-permute-start.77 = (bf16[128,3072]{1,0:T(8,128)(2,1)}, bf16[128,3072]{1,0:T(8,128)(2,1)S(1)}, u32[]{:S(2)}, u32[]{:S(2)}) collective-permute-start(bf16[128,3072]{1,0:T(8,128)(2,1)} %shard_map.272), channel_id=1, source_target_pairs={{0,8},{2,10},{4,12},{6,14},{8,16},{10,18},{12,20},{14,22},{16,24},... | collective-permute-start | bytes 2359304 | tf_op jit(solution)/shard_map/ppermute | solution.py:88
  511.6 21.8 %collective-permute-start.78 = (bf16[128,2048]{1,0:T(8,128)(2,1)S(1)}, bf16[128,2048]{1,0:T(8,128)(2,1)S(1)}, u32[]{:S(2)}, u32[]{:S(2)}) collective-permute-start(bf16[128,2048]{1,0:T(8,128)(2,1)S(1)} %copy-done.28), channel_id=1, source_target_pairs={{0,1},{1,0},{2,3},{3,2},{4,5},{5,4},{6,7},{7,6},{8,9},{9,8},{10,11... | collective-permute-start | bytes 1572872 | tf_op jit(solution)/shard_map/ppermute | solution.py:177
  512.9 20.6 %collective-permute-start.76 = (bf16[128,2048]{1,0:T(8,128)(2,1)}, bf16[128,2048]{1,0:T(8,128)(2,1)S(1)}, u32[]{:S(2)}, u32[]{:S(2)}) collective-permute-start(bf16[128,2048]{1,0:T(8,128)(2,1)} %get-tuple-element.587), channel_id=1, source_target_pairs={{0,4},{2,6},{4,0},{6,2},{8,12},{10,14},{12,8},{14,10},{16,20},{18,... | collective-permute-start | bytes 1572872 | tf_op jit(solution)/shard_map/ppermute | solution.py:85
  513.7 19.7 %collective-permute-start.79 = (bf16[128,1536]{1,0:T(8,128)(2,1)}, bf16[128,1536]{1,0:T(8,128)(2,1)S(1)}, u32[]{:S(2)}, u32[]{:S(2)}) collective-permute-start(bf16[128,1536]{1,0:T(8,128)(2,1)} %get-tuple-element.591), channel_id=1, source_target_pairs={{0,4},{2,6},{4,0},{6,2},{8,12},{10,14},{12,8},{14,10},{16,20},{18,... | collective-permute-start | bytes 1179656 | tf_op jit(solution)/shard_map/ppermute | solution.py:85
  (123 other events, 961.5 us)
Sparse Core Ops, SparseCore 0:
  56.4 72.6 all-gather.3
  131.3 62.9 all-gather.5
  196.0 63.3 all-gather.7
  261.6 68.4 reduce-scatter.2
  336.9 129.3 reduce-scatter.4

commit v4 on v3

--- a/solution.py
+++ b/solution.py
@@ -110,39 +110,41 @@
 class Gather:
     def __init__(self, ring, piece):
         self.ring = ring
-        self.hops, self.across, self.index = [piece], None, 0
+        self.hops, self.across, self.index = [piece], [], 0
         self.pieces, self.order = [], []
 
     def put(self, back, core, side, value):
         self.pieces.append(value)
         self.order.append(self.ring.block(back, core, side))
 
-    def start(self, stages, hop=True, swap=True):
+    def start(self, stages, hop=True, swap=1):
         ring, moves = self.ring, {}
         self.hops = list(stages.hold(*self.hops))
         if hop and len(self.hops) < ring.steps:
             moves["hop"] = ring.shift(self.hops[-1], 1)
-        if swap and self.index < ring.steps:
-            moves["side"] = ring.swap_side(self.hops[self.index])
-            moves["core"] = ring.swap_core(self.hops[self.index])
-        if swap and self.across is not None:
-            moves["both"] = ring.swap_core(self.across)
+        if swap:
+            pieces = self.hops[self.index : self.index + swap]
+            moves["side"] = [ring.swap_side(p) for p in pieces]
+            moves["core"] = [ring.swap_core(p) for p in pieces]
+            moves["both"] = [ring.swap_core(p) for p in self.across]
         return moves
 
     def finish(self, moves):
-        ring, back = self.ring, self.index
+        ring = self.ring
         core, side = ring.core, ring.side
         if "hop" in moves:
             self.hops.append(moves["hop"])
-        if "both" in moves:
-            self.put(back - 1, 1 - core, 1 - side, moves["both"])
-            self.across = None
-        if "side" in moves:
+        if "side" not in moves:
+            return
+        first = self.index - len(self.across)
+        for back, value in enumerate(moves["both"], first):
+            self.put(back, 1 - core, 1 - side, value)
+        self.across = moves["side"]
+        for back, (aside, other) in enumerate(zip(moves["side"], moves["core"]), self.index):
             self.put(back, core, side, self.hops[back])
-            self.put(back, core, 1 - side, moves["side"])
-            self.put(back, 1 - core, side, moves["core"])
-            self.across = moves["side"]
-            self.index += 1
+            self.put(back, core, 1 - side, aside)
+            self.put(back, 1 - core, side, other)
+        self.index += len(moves["side"])
 
     @property
     def done(self):
@@ -535,35 +537,36 @@
 
 
 def attend_kernel(
-    queries, keys, values, query_gain, key_gain, cosine, sine, seg_column, seg_row, *rest
+    start, queries, keys, values, query_gain, key_gain, cosine, sine, seg_column, seg_row, *rest
 ):
     out, total_out = rest[-2:]
-    rows = queries.shape[0]
-    cosine, sine = cosine[...], sine[...]
-    key = norm_rope(keys[...], key_gain[...], cosine, sine)[0].astype(jnp.bfloat16)
+    size, rows = queries.shape[0], keys.shape[0]
+    key = norm_rope(keys[...], key_gain[...], cosine[:rows, :], sine[:rows, :])[0]
+    key = key.astype(jnp.bfloat16)
     value = values[...].T.astype(jnp.bfloat16)
     spans = [slice(lo, lo + HEAD_SIZE) for lo in range(0, queries.shape[1], HEAD_SIZE)]
+    turn = cosine[start : start + size, :], sine[start : start + size, :]
     heads = [
-        norm_rope(queries[:, span], query_gain[...], cosine, sine)[0].astype(jnp.bfloat16)
+        norm_rope(queries[:, span], query_gain[...], *turn)[0].astype(jnp.bfloat16)
         for span in spans
     ]
-    for first in range(0, rows, ROW_BLOCK):
-        end = first + ROW_BLOCK
-        allowed = allowed_pairs(seg_column, seg_row, first, ROW_BLOCK)
+    for first in range(0, size, ROW_BLOCK):
+        here = slice(first, first + ROW_BLOCK)
+        end = start + first + ROW_BLOCK
+        allowed = allowed_pairs(seg_column, seg_row, start + first, ROW_BLOCK)
         for k, (span, query) in enumerate(zip(spans, heads)):
-            scores = inner_right(key[:end], query[first:end]) * HEAD_SIZE ** (-0.5)
+            scores = inner_right(key[:end], query[here]) * HEAD_SIZE ** (-0.5)
             scores = jnp.where(allowed, scores, -1e30)
             largest = jnp.max(scores, axis=0, keepdims=True)
             raised = jnp.exp(scores - largest)
             total = jnp.sum(raised, axis=0, keepdims=True)
             weights = (raised * (1.0 / total)).astype(jnp.bfloat16)
             mixed = matrix_product(value[:, :end], weights)
-            out[first:end, span] = mixed.T.astype(jnp.bfloat16)
-            total_out[k : k + 1, first:end] = largest + jnp.log(total)
+            out[here, span] = mixed.T.astype(jnp.bfloat16)
+            total_out[k : k + 1, here] = largest + jnp.log(total)
 
 
 def attend_back_kernel(
-    first_head,
     query_columns,
     key_columns,
     queries,
@@ -579,8 +582,8 @@
     *rest,
 ):
     out, query_gain_out, key_gain_out = rest[-3:]
-    back_parts = rest[:PARTS]
-    head = first_head + pl.program_id(0)
+    back_parts = rest[:2]
+    head = pl.program_id(0)
     rows, wide = queries.shape
     scaling = HEAD_SIZE ** (-0.5)
     cosine, sine = cosine[...], sine[...]
@@ -634,17 +637,19 @@
     add_sum(key_gain_out, key_sum)
 
 
-def attention_call(raw, query_columns, key_columns, gains, tables, segment, heads, back=None, totals=None, ties=()):
+def attention_call(raw, query_columns, key_columns, gains, tables, segment, span, back=None, totals=None, ties=()):
     rows, columns = raw.shape
-    first, count = heads
+    start, end = span
+    count = key_columns // HEAD_SIZE
     wide = query_columns * HEAD_SIZE // key_columns
-    first_key = query_columns // HEAD_SIZE + first
+    first_key = query_columns // HEAD_SIZE
     first_value = first_key + key_columns // HEAD_SIZE
     ins = [raw, raw, raw, *gains, *tables, segment[:, None], segment[None, :]]
+    size = end - start
     specs = [
-        pl.BlockSpec((rows, wide), lambda h: (0, first + h)),
-        pl.BlockSpec((rows, HEAD_SIZE), lambda h: (0, first_key + h)),
-        pl.BlockSpec((rows, HEAD_SIZE), lambda h: (0, first_value + h)),
+        pl.BlockSpec((size, wide), lambda h: (start // size, h)),
+        pl.BlockSpec((end, HEAD_SIZE), lambda h: (0, first_key + h)),
+        pl.BlockSpec((end, HEAD_SIZE), lambda h: (0, first_value + h)),
     ] + [pl.BlockSpec(a.shape, lambda h: (0, 0)) for a in ins[3:]]
     params = dict(
         grid=(count,),
@@ -653,15 +658,15 @@
     pairs = count * wide // HEAD_SIZE * rows * rows
     if back is None:
         return pl.pallas_call(
-            attend_kernel,
+            functools.partial(attend_kernel, start),
             in_specs=specs + loose(ties),
             out_specs=[
-                pl.BlockSpec((rows, wide), lambda h: (0, h)),
-                pl.BlockSpec((8, rows), lambda h: (h, 0)),
+                pl.BlockSpec((size, wide), lambda h: (0, h)),
+                pl.BlockSpec((8, size), lambda h: (h, 0)),
             ],
             out_shape=[
-                jax.ShapeDtypeStruct((rows, count * wide), jnp.bfloat16),
-                jax.ShapeDtypeStruct((count * 8, rows), jnp.float32),
+                jax.ShapeDtypeStruct((size, count * wide), jnp.bfloat16),
+                jax.ShapeDtypeStruct((count * 8, size), jnp.float32),
             ],
             cost_estimate=pl.CostEstimate(
                 flops=4 * pairs * HEAD_SIZE, bytes_accessed=5 * raw.size, transcendentals=pairs
@@ -671,10 +676,10 @@
     gain_spec = pl.BlockSpec((1, HEAD_SIZE), lambda h: (0, 0))
     gain_shape = jax.ShapeDtypeStruct((1, HEAD_SIZE), jnp.float32)
     return pl.pallas_call(
-        functools.partial(attend_back_kernel, first, query_columns, key_columns),
+        functools.partial(attend_back_kernel, query_columns, key_columns),
         in_specs=specs
         + [pl.BlockSpec((8, rows), lambda h: (h, 0))]
-        + [pl.BlockSpec((b.shape[0], wide), lambda h: (0, first + h)) for b in back]
+        + [pl.BlockSpec((b.shape[0], wide), lambda h: (0, h)) for b in back]
         + loose(ties),
         out_specs=[pl.BlockSpec((rows, columns), lambda h: (0, 0)), gain_spec, gain_spec],
         out_shape=[jax.ShapeDtypeStruct((rows, columns), jnp.bfloat16), gain_shape, gain_shape],
@@ -727,9 +732,10 @@
     )(raw_grad, full, tokens, *ties)
 
 
-def scatter_kernel(width, steps, lefts, gots, ties, info, *refs):
-    turned, outs = refs[-1], refs[lefts + 1 + gots + ties : -1]
-    left, right, got = refs[:lefts], refs[lefts], refs[lefts + 1 : lefts + 1 + gots]
+def scatter_kernel(width, steps, lefts, rights, gots, ties, info, *refs):
+    turned, outs = refs[-1], refs[lefts + rights + gots + ties : -1]
+    left, right = refs[:lefts], refs[lefts : lefts + rights]
+    got = refs[lefts + rights : lefts + rights + gots]
     size = steps * width
 
     @pl.when(pl.program_id(0) == 0)
@@ -745,7 +751,10 @@
                     turned[row : row + width, first : first + part.shape[0]] = block
                     first += part.shape[0]
 
-    total = matrix_product(turned[...], right[...])
+    joined = right[0][...]
+    if rights > 1:
+        joined = jnp.concatenate([r[...] for r in right], axis=0)
+    total = matrix_product(turned[...], joined)
     for k in range(2):
         value = total[k * size : (k + 1) * size]
         if gots:
@@ -758,11 +767,12 @@
 
 
 def scatter_call(ring, width, left, right, core, got=(), ties=(), apart=True):
-    rows, columns = right.shape
+    rows, columns = sum(r.shape[0] for r in right), right[0].shape[1]
     steps = ring.steps
     each = steps if apart else 1
     if 2 * width % LANES:
         blocks = jnp.concatenate(left, axis=0).reshape(rows, steps, 2, 2, width)
+        right = jnp.concatenate(right, axis=0)
         outs = []
         for k, side in enumerate((ring.side, 1 - ring.side)):
             for i, place in enumerate(ring.places):
@@ -779,12 +789,14 @@
     info = jnp.stack([core, ring.side] + ring.places).astype(jnp.int32)
     tile, tall = 512, steps * width // each
     outs = pl.pallas_call(
-        functools.partial(scatter_kernel, width, steps, len(left), len(got), len(ties)),
+        functools.partial(
+            scatter_kernel, width, steps, len(left), len(right), len(got), len(ties)
+        ),
         grid_spec=pltpu.PrefetchScalarGridSpec(
             num_scalar_prefetch=1,
             grid=(columns // tile,),
             in_specs=[pl.BlockSpec(a.shape, lambda i, info: (0, 0)) for a in left]
-            + [pl.BlockSpec((rows, tile), lambda i, info: (0, i))]
+            + [pl.BlockSpec((r.shape[0], tile), lambda i, info: (0, i)) for r in right]
             + [pl.BlockSpec((steps * width, tile), lambda i, info: (0, i)) for _ in got]
             + loose(ties),
             out_specs=[pl.BlockSpec((tall, tile), lambda i, info: (0, i))] * (2 * each),
@@ -794,10 +806,10 @@
         compiler_params=pltpu.CompilerParams(vmem_limit_bytes=VMEM_LIMIT),
         cost_estimate=pl.CostEstimate(
             flops=4 * rows * steps * width * columns,
-            bytes_accessed=2 * (right.size + rows * 16 * width) + 4 * steps * width * columns,
+            bytes_accessed=2 * rows * (columns + 16 * width) + 4 * steps * width * columns,
             transcendentals=0,
         ),
-    )(info, *left, right, *got, *ties)
+    )(info, *left, *right, *got, *ties)
     return outs[:each], outs[each:]
 
 
@@ -819,43 +831,25 @@
         down[pl.ds(start, chunk), :] = value[:, 2 * chunk :].T
 
 
-def finish_last_kernel(chunk, info, other, _gate, _up, _down, gate, up, down):
-    value = other[...].astype(jnp.float32)
-    gate[...] = value[:, :chunk]
-    up[...] = value[:, chunk : 2 * chunk]
-    down[...] = value[:, 2 * chunk :].T
-
-
-def finish_call(ring, chunk, totals, others, into=None):
+def finish_call(ring, chunk, totals, others):
     width, hidden = others[0].shape[0], 2 * CHUNKS * chunk
+    counts = [a.shape[1] // (3 * chunk) for a in totals]
     shapes = [(width, hidden), (width, hidden), (hidden, width)]
-    if into is None:
-        counts = [a.shape[1] // (3 * chunk) for a in totals]
-        kernel = functools.partial(finish_kernel, chunk, counts)
-        ins = [*totals, *others]
-        specs = [pl.BlockSpec(a.shape, lambda i, info: (0, 0)) for a in ins]
-        out_specs = [pl.BlockSpec(shape, lambda i, info: (0, 0)) for shape in shapes]
-        aliases = {}
-    else:
-        kernel = functools.partial(finish_last_kernel, chunk)
-        ins = [*others, *into]
-        specs = [pl.BlockSpec(others[0].shape, lambda i, info: (0, 0))] + loose(into)
-        last = lambda info: (1 - info[0]) * CHUNKS + CHUNKS - 1
-        out_specs = [pl.BlockSpec((width, chunk), lambda i, info: (0, last(info)))] * 2
-        out_specs.append(pl.BlockSpec((chunk, width), lambda i, info: (last(info), 0)))
-        aliases = {2: 0, 3: 1, 4: 2}
+    whole = [pl.BlockSpec(a.shape, lambda i, info: (0, 0)) for a in (*totals, *others)]
     return pl.pallas_call(
-        kernel,
+        functools.partial(finish_kernel, chunk, counts),
         grid_spec=pltpu.PrefetchScalarGridSpec(
-            num_scalar_prefetch=1, grid=(1,), in_specs=specs, out_specs=out_specs
+            num_scalar_prefetch=1,
+            grid=(1,),
+            in_specs=whole,
+            out_specs=[pl.BlockSpec(shape, lambda i, info: (0, 0)) for shape in shapes],
         ),
         out_shape=[jax.ShapeDtypeStruct(shape, jnp.float32) for shape in shapes],
-        input_output_aliases=aliases,
         compiler_params=pltpu.CompilerParams(vmem_limit_bytes=VMEM_LIMIT),
         cost_estimate=pl.CostEstimate(
             flops=0, bytes_accessed=18 * hidden * width, transcendentals=0
         ),
-    )(jnp.stack([ring.side]).astype(jnp.int32), *ins)
+    )(jnp.stack([ring.side]).astype(jnp.int32), *totals, *others)
 
 
 def join_kernel(width, count, order, left, *rest):
@@ -895,57 +889,78 @@
     )(jnp.stack(gather.order).astype(jnp.int32), left, *gather.pieces)
 
 
-def join_wide_kernel(width, count, order, first, second, *rest):
-    pieces, mixture, whole = rest[:count], rest[count], rest[count + 1]
-    total, outs = rest[-1], rest[count + 2 : -1]
+def join_wide_kernel(width, count, order, left, *rest):
+    pieces, whole, total, outs = rest[:count], rest[count], rest[-1], rest[count + 1 : -1]
     for i, piece in enumerate(pieces):
         whole[pl.ds(pl.multiple_of(order[i] * width, width), width), :] = piece[...]
+    term = inner_right(left[...], whole[...])
 
     @pl.when(pl.program_id(0) == 0)
     def _():
-        mixture[...] = first[...]
-        total[...] = inner_right(first[...], whole[...])
+        total[...] = term
 
     @pl.when(pl.program_id(0) == 1)
     def _():
-        mixture[...] = second[...]
-        total[...] += inner_right(second[...], whole[...])
         part = outs[0].shape[0]
         for i, out in enumerate(outs):
-            out[...] = total[i * part : (i + 1) * part, :].astype(jnp.bfloat16)
-
-
-def join_wide_call(gather, left):
+            value = total[i * part : (i + 1) * part, :] + term[i * part : (i + 1) * part]
+            out[...] = value.astype(jnp.bfloat16)
+
+
+def join_wide_call(gather, left, part):
     width, columns = gather.pieces[0].shape
-    rows, model_width = left[0].shape[0], width * len(gather.pieces)
-    tile, part = columns // 2, rows // PARTS
+    rows, model_width = left.shape[0], width * len(gather.pieces)
+    tile, parts = columns // 2, rows // part
     count = len(gather.pieces)
     return pl.pallas_call(
         functools.partial(join_wide_kernel, width, count),
         grid_spec=pltpu.PrefetchScalarGridSpec(
             num_scalar_prefetch=1,
             grid=(2,),
-            in_specs=[pl.BlockSpec((rows, tile), lambda i, order: (0, 0))] * 2
+            in_specs=[pl.BlockSpec((rows, tile), lambda i, order: (0, i))]
             + [pl.BlockSpec((width, tile), lambda i, order: (0, i))] * count,
-            out_specs=[
-                pl.BlockSpec((rows, tile), lambda i, order: (0, i)),
-                pl.BlockSpec((model_width, tile), lambda i, order: (0, i)),
-            ]
-            + [pl.BlockSpec((part, model_width), lambda i, order: (0, 0))] * PARTS,
+            out_specs=[pl.BlockSpec((model_width, tile), lambda i, order: (0, i))]
+            + [pl.BlockSpec((part, model_width), lambda i, order: (0, 0))] * parts,
             scratch_shapes=[pltpu.VMEM((rows, model_width), jnp.float32)],
         ),
-        out_shape=[
-            jax.ShapeDtypeStruct((rows, columns), jnp.bfloat16),
-            jax.ShapeDtypeStruct((model_width, columns), jnp.bfloat16),
-        ]
-        + [jax.ShapeDtypeStruct((part, model_width), jnp.bfloat16)] * PARTS,
+        out_shape=[jax.ShapeDtypeStruct((model_width, columns), jnp.bfloat16)]
+        + [jax.ShapeDtypeStruct((part, model_width), jnp.bfloat16)] * parts,
         compiler_params=pltpu.CompilerParams(vmem_limit_bytes=VMEM_LIMIT),
         cost_estimate=pl.CostEstimate(
             flops=2 * rows * model_width * columns,
             bytes_accessed=4 * model_width * columns + 4 * rows * model_width,
             transcendentals=0,
         ),
-    )(jnp.stack(gather.order).astype(jnp.int32), *left, *gather.pieces)
+    )(jnp.stack(gather.order).astype(jnp.int32), left, *gather.pieces)
+
+
+def rows_product_kernel(left, right, *outs):
+    outs = outs[-2:]
+    total = inner_right(left[...], right[...])
+    part = outs[0].shape[0]
+    for i, out in enumerate(outs):
+        out[...] = total[i * part : (i + 1) * part].astype(jnp.bfloat16)
+
+
+def rows_product(left, right, part, ties=()):
+    rows, columns = left.shape
+    model_width = right.shape[0]
+    tile = 512
+    return pl.pallas_call(
+        rows_product_kernel,
+        grid=(model_width // tile,),
+        in_specs=[
+            pl.BlockSpec(left.shape, lambda i: (0, 0)),
+            pl.BlockSpec((tile, columns), lambda i: (i, 0)),
+        ]
+        + loose(ties),
+        out_specs=[pl.BlockSpec((part, tile), lambda i: (0, i))] * (rows // part),
+        out_shape=[jax.ShapeDtypeStruct((part, model_width), jnp.bfloat16)] * (rows // part),
+        compiler_params=pltpu.CompilerParams(vmem_limit_bytes=VMEM_LIMIT),
+        cost_estimate=pl.CostEstimate(
+            flops=2 * rows * right.size, bytes_accessed=2 * right.size, transcendentals=0
+        ),
+    )(left, right, *ties)
 
 
 def shards(
@@ -1028,7 +1043,7 @@
     for i in range(steps):
         movers = [attention]
         if i != 2:
-            movers.append((output, dict(swap=i > 2)))
+            movers.append((output, dict(swap=int(i > 2))))
         others = []
         if i in (1, 2):
             others.append(ring.swap_side(*stages.hold(feed_other[i - 1])))
@@ -1045,21 +1060,15 @@
         lax.dynamic_slice_in_dim(upstream, place * (rows // 2) + k * part, part) for k in range(2)
     ]
 
-    late = stages.hold(*feed_other[2:])
-    raw, attention_full = step([output], *join_call(attention, input_one))
-    half = key_heads // 2
+    raw, attention_full = step([(output, dict(swap=2))], *join_call(attention, input_one))
+    half = rows // 2
     attend_args = (raw, query_columns, key_columns, head_gains, tables, segment)
-    mixture_low, row_totals = [], []
-    for i in range(2):
-        mixed = attention_call(*attend_args, (i * half, half), ties=stages.ties)
-        mixed, got = step([output], mixed, [ring.swap_side(w) for w in late] if i == 0 else [])
-        mixture_low.append(mixed[0])
-        row_totals.append(mixed[1])
-        for j, value in enumerate(got):
-            feed_gather(2 + j, value)
+    mixed, row_total = attention_call(*attend_args, (0, half), ties=stages.ties)
     while not output.done:
-        step([output])
-    mixture_low, output_full, *branch_parts = join_wide_call(output, mixture_low)
+        (mixed,) = step([output], mixed)
+    mixture_low, row_totals = [mixed], [row_total]
+    output_full, *branch_parts = join_wide_call(output, mixed, part)
+    (late,) = stages.hold(feed_other[2:])
 
     middle_parts, normed_parts, normed_other = [], [], []
     got = None
@@ -1084,8 +1093,22 @@
                 moves.append(ring.swap_side(stages.hold(sent[i])[0]))
             else:
                 moves.append(ring.swap_side(normed_parts[i - 2]))
-            moves, work, branch_parts = settle(moves, work, branch_parts)
+            extra = []
+            if i == 0:
+                mixed, row_total = attention_call(*attend_args, (half, rows), ties=stages.ties)
+                mixture_low.append(mixed)
+                row_totals.append(row_total)
+                extra = [mixed, [ring.swap_side(w) for w in late]]
+            if i == 1:
+                extra = rows_product(mixture_low[1], output_full, part, stages.ties)
+            moves, work, extra = settle(moves, work, extra)
             got = moves[0]
+            if i == 0:
+                mixture_low[1], extra = extra
+                for j, value in enumerate(extra):
+                    feed_gather(2 + j, value)
+            if i == 1:
+                branch_parts += extra
             if i < 2:
                 sent[i] = moves[1]
             else:
@@ -1113,12 +1136,14 @@
     sides = (normed_parts, normed_other), (upstream, upstream_other)
     acts_other = [feed_call(normed_other, upstream_other, feed_full[0], stages.ties)]
     feed_grads = [grad_call(*sides, (acts[0], acts_other[0]))]
-    for j in range(1, CHUNKS):
+    last_grads = None
+    for j in range(1, CHUNKS - 1):
         acts_other.append(
             feed_call(normed_other, upstream_other, feed_full[j], (feed_grads + acts_other[1:])[-1:])
         )
-    back_other = wide_call(acts_other, feed_full, span, jnp.bfloat16)
-    last_grads = None
+    (early,) = wide_call(acts_other, feed_full[:-1], span, jnp.float32, parts=1)
+    acts_other.append(feed_call(normed_other, upstream_other, feed_full[-1], (early,)))
+    back_other = wide_call(acts_other[-1:], feed_full[-1:], span, jnp.bfloat16, early)
     (acts_last,) = settle(
         feed_call(normed_parts, upstream, feed_full[-1], tuple(back_other[:1]))
     )
@@ -1131,16 +1156,16 @@
     back_parts, low_parts, mixed_parts, grad_second = [], [], [], 0.0
     out_other, out_mine, out_sums, out_got = None, None, [], []
 
-    def back_middle_call(i, mine, other):
+    def back_middle_call(k, mine, other):
         return row_call(
             back_middle_kernel,
-            part,
+            2 * part,
             part,
             [
-                (mine, "rows"),
-                (other, "rows"),
-                (middle_parts[i], "rows"),
-                (upstream, i),
+                (mine, "parts"),
+                (other, "parts"),
+                (middle_parts[2 * k : 2 * k + 2], "parts"),
+                (upstream, 2 * k),
                 (gain_two, "all"),
                 (output_full, "all"),
             ],
@@ -1153,6 +1178,7 @@
             stages.ties,
         )
 
+    sums, sums_got = [], []
     for i in range(PARTS):
         work = []
         if i + 1 < CHUNKS:
@@ -1171,13 +1197,14 @@
             ]
         if i == PARTS - 1:
             work = [wide_call(acts, feed_full, out_span, jnp.float32, ties=(mine,), parts=2)]
-        done = back_middle_call(i - 1, *last) if i else []
+        done = back_middle_call(0, sums, sums_got) if i == 2 else []
         moves = [swap_tensor(mine)]
         if i + 1 < PARTS:
             moves.append(ring.swap_side(back_other[i + 1]))
         moves, work, done = settle(moves, work, done)
         back_other[i + 2 :] = stages.hold(*back_other[i + 2 :])
-        last = (mine, moves[0])
+        sums.append(mine)
+        sums_got.append(moves[0])
         if i + 1 < PARTS:
             mine = add_low(back_mine[i + 1], moves[1])
         if i + 1 < CHUNKS:
@@ -1186,12 +1213,12 @@
             out_other = list(work[0])
         if i == PARTS - 1:
             out_mine = work[0]
-        if i:
+        if i == 2:
             back_parts.append(done[0])
             low_parts.append(done[1])
             mixed_parts.append(done[2])
             grad_second = grad_second + done[3]
-    done = back_middle_call(PARTS - 1, *last)
+    done = back_middle_call(1, sums[2:], sums_got[2:])
     back_parts.append(done[0])
     low_parts.append(done[1])
     mixed_parts.append(done[2])
@@ -1219,9 +1246,9 @@
     work, scattered[0], far, got, out_next = settle(
         attention_call(
             *attend_args,
-            (0, key_heads),
+            (0, rows),
             mixed_parts,
-            jnp.concatenate(row_totals, axis=0),
+            jnp.concatenate(row_totals, axis=1),
             stages.ties + (far[0][0],),
         ),
         scattered[0],
@@ -1233,7 +1260,7 @@
     out_sums.append(add_low(out_mine[1], got))
     out_done = [out_next]
     far_one = scatter_call(
-        ring, width, [input_one], raw_grad, 1 - core, ties=stages.ties, apart=False
+        ring, width, [input_one], [raw_grad], 1 - core, ties=stages.ties, apart=False
     )
     (near,), across = scatter_call(
         ring,
@@ -1252,7 +1279,7 @@
     )
     pairs_got = [pair]
     ((mine, other),) = settle(
-        scatter_call(ring, width, [input_one], raw_grad, core, far_one, stages.ties)
+        scatter_call(ring, width, [input_one], [raw_grad], core, far_one, stages.ties)
     )
     *back_one, grad_first = back_first_call(raw_grad, attention_full, token_rows, stages.ties)
     gains = jnp.concatenate(
@@ -1278,7 +1305,7 @@
             (back_one[first:last], "parts"),
             (back_one_other[first:last], "parts"),
             (token_rows, first),
-            (back_parts[first:last], "parts"),
+            (back_parts, "halves"),
             (gain_one, "all"),
         ]
         return row_call(
@@ -1302,10 +1329,10 @@
         else:
             moves.append(ring.shift(sent, 1))
         others = []
-        turns = [i] if i < PARTS else []
+        turns = {0: [0], 1: [1], 2: [2, 3]}.get(i, [])
         others.append([swap_tensor(back_one[k]) for k in turns])
-        k = i - (steps - CHUNKS + 1)
-        if k >= 0:
+        k = i - (steps - CHUNKS)
+        if 0 <= k < CHUNKS - 1:
             last_pair = picked(scattered[1])[:, k * 3 * chunk : (k + 1) * 3 * chunk]
             others.append(ring.swap_side(*stages.hold(last_pair)))
         if i == 1:
@@ -1319,8 +1346,7 @@
             )
             others.append(block_output)
         if i == steps - 1:
-            early = len(back_one_other)
-            token_grad = token_call(0, early, None, stages.ties)
+            token_grad = token_call(0, PARTS, None, stages.ties)
             others.append(token_grad)
             others.append(finish_call(ring, chunk, scattered, pairs_got))
         if i == 0:
@@ -1358,12 +1384,9 @@
             token_grad = others.pop()
         if i == 1:
             block_output = others.pop()
-        if k >= 0:
+        if 0 <= k < CHUNKS - 1:
             pairs_got.append(others.pop())
         back_one_other += others.pop()
-    if early < PARTS:
-        token_grad = token_call(early, PARTS, token_grad, stages.ties)
-    grads = finish_call(ring, chunk, None, pairs_got[-1:], grads)
     if not tiled:
         token_grad, block_output = turned(token_grad), turned(block_output)
     grad_gate, grad_up, grad_down = grads

time: 558 us -> 554 us (level)
  waiting for transfers between devices: 145 us -> 129 us
    ppermute x31, waiting for transfers between devices: 54.4 us -> 37.4 us  [swap_side(): return lax.ppermute(value, 'dp', [(i, i ^ 2) for i in range(self.size)])]
    ppermute x9, waiting for transfers between devices: 35.6 us -> 27.1 us  [shift(): lax.ppermute(value, 'dp', [(i, (i + 4 * places) % self.size) for i in ran...]
    pallas_call x5, Pallas kernels: 37 us -> 44.6 us  [the longest x2 18.3 us: attention_call(): pl.pallas_call(functools.partial(attend_kernel, start), in_specs=specs +...]
    pallas_call x12 -> x9, Pallas kernels: 53.9 us -> 46.6 us  [row_call(): pl.pallas_call(body, grid=(rows // block,), in_specs=specs + loose(ties),...]
    ppermute x17, waiting for transfers between devices: 35.6 us -> 42.5 us  [swap_tensor(): return lax.ppermute(value, 'tensor', [(0, 1), (1, 0)])]
    pallas_call x4 -> x5, Pallas kernels: 38.7 us -> 43.6 us  [wide_call(): pl.pallas_call(functools.partial(wide_kernel, count, start is not None, p...]
    unnamed x204 -> x184, local copies, waits for them, and re-layouts: 13.2 us -> 15 us
  transfers between devices with their start and end apart: 86 -> 86, of which waited for: 30 -> 30; matrix products, arithmetic and copies ran while one was open for 4% -> 4% of each run, Pallas kernels for 50% -> 51%
where the time goes in v4:
time: 554 us; the launch traced here: 544 us
  Pallas kernels  287 us (52%)
  waiting for transfers between devices  129 us (23%)
  starting transfers between devices  71.3 us (13%)
  local copies, waits for them, and re-layouts  24.5 us (4%)
  other arithmetic  16.6 us (3%)
  between operations  15.4 us (3%)
    pallas_call x6, Pallas kernels, feed_call(): pl.pallas_call(functools.partial(feed_kernel, columns // 3, len(specs), l...  52.1 us
    pallas_call x9, Pallas kernels, row_call(): pl.pallas_call(body, grid=(rows // block,), in_specs=specs + loose(ties),...  46.6 us
    pallas_call x5, Pallas kernels, wide_call(): pl.pallas_call(functools.partial(wide_kernel, count, start is not None, p...  43.6 us
    ppermute x17, waiting for transfers between devices, swap_tensor(): return lax.ppermute(value, 'tensor', [(0, 1), (1, 0)])  42.5 us
    ppermute x31, waiting for transfers between devices, swap_side(): return lax.ppermute(value, 'dp', [(i, i ^ 2) for i in range(self.size)])  37.4 us
    ppermute x31, starting transfers between devices, swap_side(): return lax.ppermute(value, 'dp', [(i, i ^ 2) for i in range(self.size)])  35.8 us
    pallas_call x3, Pallas kernels, grad_call(): pl.pallas_call(functools.partial(grad_kernel, columns // 3 * 2, [len(g) f...  35.1 us
    ppermute x9, waiting for transfers between devices, shift(): lax.ppermute(value, 'dp', [(i, (i + 4 * places) % self.size) for i in ran...  27.1 us
  transfers between devices with their start and end apart: 86, of which 30 were waited for; matrix products, arithmetic and copies ran while one was open for 4% of the time, Pallas kernels for 51%

profile of v4, /device:TPU:0, one launch (start us, length us, event | category | flops | bytes accessed | tf_op | source)
XLA Modules:
  0.0 543.9 jit_solution(6799901955084918620)
XLA Ops:
  9.9 2.9 collective-permute-start.2
  22.8 5.6 %shard_map.237 = (bf16[512,2048]{1,0:T(8,128)(2,1)}, bf16[512,2048]{1,0:T(8,128)(2,1)}, bf16[512,2048]{1,0:T(8,128)(2,1)}) custom-call(bf16[512,2048]{1,0:T(8,128)(2,1)} %refs_0_.1, bf16[512,2048]{1,0:T(8,128)(2,1)} %refs_1_.1, f32[512,1]{1,0:T(8,128)} %copy.50.refs_2_, f32[1,2048]{1,0:T(1,128)} %bitcast.71), custom_call_target="tpu_custom_call" | custom-call | bytes 10496000 | tf_op jit(solution)/shard_map/pallas_call | solution.py:307
  29.1 4.7 collective-permute-done.3.rest_4_
  36.3 8.8 %collective-permute-done.8.rest_7_ = bf16[128,1024]{1,0:T(8,128)(2,1)S(1)} collective-permute-done((bf16[128,1024]{1,0:T(8,128)(2,1)}, bf16[128,1024]{1,0:T(8,128)(2,1)S(1)}, u32[]{:S(2)}, u32[]{:S(2)}) %collective-permute-start.8) | collective-permute-done | bytes 262176 | tf_op jit(solution)/shard_map/ppermute | solution.py:88
  45.7 9.4 %collective-permute-done.9 = bf16[128,1536]{1,0:T(8,128)(2,1)S(1)} collective-permute-done((bf16[128,1536]{1,0:T(8,128)(2,1)S(1)}, bf16[128,1536]{1,0:T(8,128)(2,1)S(1)}, u32[]{:S(2)}, u32[]{:S(2)}) %collective-permute-start.9) | collective-permute-done | bytes 393248 | tf_op jit(solution)/shard_map/ppermute | solution.py:85
  60.0 16.8 %collective-permute-done.14 = bf16[128,1536]{1,0:T(8,128)(2,1)S(1)} collective-permute-done((bf16[128,1536]{1,0:T(8,128)(2,1)S(1)}, bf16[128,1536]{1,0:T(8,128)(2,1)S(1)}, u32[]{:S(2)}, u32[]{:S(2)}) %collective-permute-start.14) | collective-permute-done | bytes 393248 | tf_op jit(solution)/shard_map/ppermute | solution.py:85
  81.0 13.5 %collective-permute-done.19.rest_12_ = bf16[128,1024]{1,0:T(8,128)(2,1)S(1)} collective-permute-done((bf16[128,1024]{1,0:T(8,128)(2,1)S(1)}, bf16[128,1024]{1,0:T(8,128)(2,1)S(1)}, u32[]{:S(2)}, u32[]{:S(2)}) %collective-permute-start.19) | collective-permute-done | bytes 262176 | tf_op jit(solution)/shard_map/ppermute | solution.py:88
  100.8 1.9 collective-permute-start.26
  102.9 12.0 %shard_map.238 = (f32[512,2048]{1,0:T(8,128)}, bf16[2048,2048]{1,0:T(8,128)(2,1)}) custom-call(s32[16]{0:T(128)} %stack.140.order, bf16[512,2048]{1,0:T(8,128)(2,1)} %get-tuple-element.290.left.refs_0_, bf16[128,2048]{1,0:T(8,128)(2,1)} %copy-done.36, bf16[128,2048]{1,0:T(8,128)(2,1)} %collective-permute-done.2.rest_1_, ...), custom_call_target="tpu_custom_call" | custom-call | flops 4294967296 | bytes 20971520 | tf_op jit(solution)/shard_map/pallas_call | solution.py:867
  116.7 7.7 %shard_map.239 = (bf16[256,1024]{1,0:T(8,128)(2,1)}, f32[32,256]{1,0:T(8,128)}) custom-call(f32[512,2048]{1,0:T(8,128)} %get-tuple-element.329.queries.keys.values, f32[512,2048]{1,0:T(8,128)} %get-tuple-element.329.queries.keys.values, f32[512,2048]{1,0:T(8,128)} %get-tuple-element.329.queries.keys.values, f32[1,128]{1,0:T(1,128)} %get-tuple-element.605.query_gain, ...), custom_call_target="tpu_custom_call" | custom-call | flops 1073741824 | bytes 5242880 | tf_op jit(solution)/shard_map/pallas_call | solution.py:660
  127.6 1.7 collective-permute-start.34
  129.3 6.1 %shard_map.241 = (bf16[2048,1024]{1,0:T(8,128)(2,1)}, bf16[128,2048]{1,0:T(8,128)(2,1)}, bf16[128,2048]{1,0:T(8,128)(2,1)}) custom-call(s32[16]{0:T(128)} %stack.141.order, bf16[256,1024]{1,0:T(8,128)(2,1)} %get-tuple-element.344.left.refs_2_, bf16[128,1024]{1,0:T(8,128)(2,1)} %bitcast.63, bf16[128,1024]{1,0:T(8,128)(2,1)} %copy-done.58, ...), custom_call_target="tpu_custom_call" | custom-call | flops 1073741824 | bytes 10485760 | tf_op jit(solution)/shard_map/pallas_call | solution.py:915
  136.6 10.6 %shard_map.240 = (bf16[256,1024]{1,0:T(8,128)(2,1)}, f32[32,256]{1,0:T(8,128)}) custom-call(f32[512,2048]{1,0:T(8,128)} %get-tuple-element.329.queries.keys.values, f32[512,2048]{1,0:T(8,128)} %get-tuple-element.329.queries.keys.values, f32[512,2048]{1,0:T(8,128)} %get-tuple-element.329.queries.keys.values, f32[1,128]{1,0:T(1,128)} %get-tuple-element.605.query_gain, ...), custom_call_target="tpu_custom_call" | custom-call | flops 1073741824 | bytes 5242880 | tf_op jit(solution)/shard_map/pallas_call | solution.py:660
  147.2 3.0 collective-permute-done.35
  154.2 2.8 shard_map.242
  157.0 5.1 shard_map.243
  162.1 3.0 collective-permute-done.32.refs_2_
  166.9 1.7 collective-permute-start.38
  168.6 2.8 shard_map.244
  171.8 8.9 %collective-permute-done.37.refs_2_ = bf16[128,2048]{1,0:T(8,128)(2,1)S(1)} collective-permute-done((bf16[128,2048]{1,0:T(8,128)(2,1)}, bf16[128,2048]{1,0:T(8,128)(2,1)S(1)}, u32[]{:S(2)}, u32[]{:S(2)}) %collective-permute-start.37) | collective-permute-done | bytes 524320 | tf_op jit(solution)/shard_map/ppermute | solution.py:179
  182.1 2.8 shard_map.245
  184.9 4.5 collective-permute-done.39.refs_2_
  190.7 1.8 collective-permute-start.41
  192.4 2.8 shard_map.246
  197.5 8.4 %shard_map.247.refs_13_.refs_0_ = bf16[512,1536]{1,0:T(8,128)(2,1)} custom-call(bf16[128,2048]{1,0:T(8,128)(2,1)} %get-tuple-element.370.refs_0_, bf16[128,2048]{1,0:T(8,128)(2,1)} %get-tuple-element.377.refs_1_, bf16[128,2048]{1,0:T(8,128)(2,1)} %get-tuple-element.383.refs_2_, bf16[128,2048]{1,0:T(8,128)(2,1)} %get-tuple-element.385.refs_3_, ...), custom_call_target="tpu_custom_call" | custom-call | flops 3221225472 | bytes 12058624 | tf_op jit(solution)/shard_map/pallas_call | solution.py:416
  206.0 8.5 %shard_map.248.refs_1_.refs_13_ = bf16[512,1536]{1,0:T(8,128)(2,1)} custom-call(bf16[128,2048]{1,0:T(8,128)(2,1)} %get-tuple-element.370.refs_0_, bf16[128,2048]{1,0:T(8,128)(2,1)} %get-tuple-element.377.refs_1_, bf16[128,2048]{1,0:T(8,128)(2,1)} %get-tuple-element.383.refs_2_, bf16[128,2048]{1,0:T(8,128)(2,1)} %get-tuple-element.385.refs_3_, ...), custom_call_target="tpu_custom_call" | custom-call | flops 3221225472 | bytes 12058624 | tf_op jit(solution)/shard_map/pallas_call | solution.py:416
  214.5 3.0 collective-permute-done.44
  219.7 8.8 %shard_map.249.refs_14_.refs_0_ = bf16[512,1536]{1,0:T(8,128)(2,1)} custom-call(bf16[128,2048]{1,0:T(8,128)(2,1)} %copy-done.3, bf16[128,2048]{1,0:T(8,128)(2,1)} %copy-done.4, bf16[128,2048]{1,0:T(8,128)(2,1)} %copy-done.5, bf16[128,2048]{1,0:T(8,128)(2,1)} %copy-done.6, bf16[128,2048]{1,0:T(8,128)(2,1)} %get-tuple-element.401.refs_4_.refs_9_, ...), custom_call_target="tpu_custom_call" | custom-call | flops 3221225472 | bytes 12058624 | tf_op jit(solution)/shard_map/pallas_call | solution.py:416
  228.5 11.8 %shard_map.250.refs_9_ = bf16[2048,1536]{1,0:T(8,128)(2,1)} custom-call(bf16[128,2048]{1,0:T(8,128)(2,1)} %get-tuple-element.370.refs_0_, bf16[128,2048]{1,0:T(8,128)(2,1)} %get-tuple-element.377.refs_1_, bf16[128,2048]{1,0:T(8,128)(2,1)} %get-tuple-element.383.refs_2_, bf16[128,2048]{1,0:T(8,128)(2,1)} %get-tuple-element.385.refs_3_, ...), custom_call_target="tpu_custom_call" | custom-call | flops 6442450944 | bytes 17825792 | tf_op jit(solution)/shard_map/pallas_call | solution.py:501
  240.3 9.2 %shard_map.251.refs_1_.refs_14_ = bf16[512,1536]{1,0:T(8,128)(2,1)} custom-call(bf16[128,2048]{1,0:T(8,128)(2,1)} %copy-done.3, bf16[128,2048]{1,0:T(8,128)(2,1)} %copy-done.4, bf16[128,2048]{1,0:T(8,128)(2,1)} %copy-done.5, bf16[128,2048]{1,0:T(8,128)(2,1)} %copy-done.6, bf16[128,2048]{1,0:T(8,128)(2,1)} %get-tuple-element.401.refs_4_.refs_9_, ...), custom_call_target="tpu_custom_call" | custom-call | flops 3221225472 | bytes 12058624 | tf_op jit(solution)/shard_map/pallas_call | solution.py:416
  249.6 9.3 %shard_map.252.refs_9_.refs_2_ = f32[512,2048]{1,0:T(8,128)} custom-call(bf16[512,1536]{1,0:T(8,128)(2,1)} %shard_map.249.refs_14_.refs_0_, bf16[512,1536]{1,0:T(8,128)(2,1)} %shard_map.251.refs_1_.refs_14_, bf16[2048,1536]{1,0:T(8,128)(2,1)} %all-gather.4.cloned.1.call-done.refs_5_.refs_8_.refs_2_.refs_3_, ...), custom_call_target="tpu_custom_call" | custom-call | flops 4294967296 | bytes 16777216 | tf_op jit(solution)/shard_map/pallas_call | solution.py:456
  259.4 8.7 %shard_map.253.refs_0_.refs_14_.refs_2_ = bf16[512,1536]{1,0:T(8,128)(2,1)} custom-call(bf16[128,2048]{1,0:T(8,128)(2,1)} %copy-done.3, bf16[128,2048]{1,0:T(8,128)(2,1)} %copy-done.4, bf16[128,2048]{1,0:T(8,128)(2,1)} %copy-done.5, bf16[128,2048]{1,0:T(8,128)(2,1)} %copy-done.6, bf16[128,2048]{1,0:T(8,128)(2,1)} %get-tuple-element.401.refs_4_.refs_9_, ...), custom_call_target="tpu_custom_call" | custom-call | flops 3221225472 | bytes 12058624 | tf_op jit(solution)/shard_map/pallas_call | solution.py:416
  268.1 6.7 %shard_map.254 = (bf16[128,2048]{1,0:T(8,128)(2,1)}, bf16[128,2048]{1,0:T(8,128)(2,1)}, bf16[128,2048]{1,0:T(8,128)(2,1)}, bf16[128,2048]{1,0:T(8,128)(2,1)}) custom-call(bf16[512,1536]{1,0:T(8,128)(2,1)} %shard_map.253.refs_0_.refs_14_.refs_2_, bf16[2048,1536]{1,0:T(8,128)(2,1)} %all-gather.8.cloned.1.call-done.refs_8_.refs_1_.refs_5_, ...), custom_call_target="tpu_custom_call" | custom-call | flops 2147483648 | bytes 11534336 | tf_op jit(solution)/shard_map/pallas_call | solution.py:456
  276.3 8.5 %shard_map.255.refs_2_.refs_13_ = bf16[512,1536]{1,0:T(8,128)(2,1)} custom-call(bf16[128,2048]{1,0:T(8,128)(2,1)} %get-tuple-element.370.refs_0_, bf16[128,2048]{1,0:T(8,128)(2,1)} %get-tuple-element.377.refs_1_, bf16[128,2048]{1,0:T(8,128)(2,1)} %get-tuple-element.383.refs_2_, bf16[128,2048]{1,0:T(8,128)(2,1)} %get-tuple-element.385.refs_3_, ...), custom_call_target="tpu_custom_call" | custom-call | flops 3221225472 | bytes 12058624 | tf_op jit(solution)/shard_map/pallas_call | solution.py:416
  285.3 11.8 %shard_map.256 = (f32[128,2048]{1,0:T(8,128)}, f32[128,2048]{1,0:T(8,128)}, f32[128,2048]{1,0:T(8,128)}, f32[128,2048]{1,0:T(8,128)}) custom-call(bf16[512,1536]{1,0:T(8,128)(2,1)} %shard_map.247.refs_13_.refs_0_, bf16[512,1536]{1,0:T(8,128)(2,1)} %shard_map.248.refs_1_.refs_13_, bf16[512,1536]{1,0:T(8,128)(2,1)} %shard_map.255.refs_2_.refs_13_, ...), custom_call_target="tpu_custom_call" | custom-call | flops 6442450944 | bytes 22020096 | tf_op jit(solution)/shard_map/pallas_call | solution.py:456
  300.0 11.7 %shard_map.257.refs_15_ = bf16[2048,3072]{1,0:T(8,128)(2,1)} custom-call(bf16[128,2048]{1,0:T(8,128)(2,1)} %get-tuple-element.370.refs_0_, bf16[128,2048]{1,0:T(8,128)(2,1)} %get-tuple-element.377.refs_1_, bf16[128,2048]{1,0:T(8,128)(2,1)} %get-tuple-element.383.refs_2_, bf16[128,2048]{1,0:T(8,128)(2,1)} %get-tuple-element.385.refs_3_, ...), custom_call_target="tpu_custom_call" | custom-call | flops 6442450944 | bytes 17825792 | tf_op jit(solution)/shard_map/pallas_call | solution.py:501
  315.3 11.6 %shard_map.258 = bf16[2048,3072]{1,0:T(8,128)(2,1)} custom-call(bf16[128,2048]{1,0:T(8,128)(2,1)} %get-tuple-element.370.refs_0_, bf16[128,2048]{1,0:T(8,128)(2,1)} %get-tuple-element.377.refs_1_, bf16[128,2048]{1,0:T(8,128)(2,1)} %get-tuple-element.383.refs_2_, bf16[128,2048]{1,0:T(8,128)(2,1)} %get-tuple-element.385.refs_3_, ...), custom_call_target="tpu_custom_call", output_to_operand_aliasing={{}: (15, {})} | custom-call | flops 6442450944 | bytes 17825792 | tf_op jit(solution)/shard_map/pallas_call | solution.py:501
  329.3 7.8 %shard_map.260 = (f32[256,2048]{1,0:T(8,128)}, bf16[256,2048]{1,0:T(8,128)(2,1)}, bf16[256,1024]{1,0:T(8,128)(2,1)}, f32[1,2048]{1,0:T(1,128)}) custom-call(bf16[128,2048]{1,0:T(8,128)(2,1)} %copy-done.9, bf16[128,2048]{1,0:T(8,128)(2,1)} %copy-done.7, bf16[128,2048]{1,0:T(8,128)(2,1)} %copy-done.33, bf16[128,2048]{1,0:T(8,128)(2,1)} %copy-done.35, ...), custom_call_target="tpu_custom_call" | custom-call | bytes 14163968 | tf_op jit(solution)/shard_map/pallas_call | solution.py:307
  337.1 7.9 %shard_map.259 = (bf16[256,2048]{1,0:T(8,128)(2,1)}, bf16[256,2048]{1,0:T(8,128)(2,1)}) custom-call(bf16[512,1536]{1,0:T(8,128)(2,1)} %shard_map.249.refs_14_.refs_0_, bf16[512,1536]{1,0:T(8,128)(2,1)} %shard_map.251.refs_1_.refs_14_, bf16[512,1536]{1,0:T(8,128)(2,1)} %shard_map.253.refs_0_.refs_14_.refs_2_, ...), custom_call_target="tpu_custom_call" | custom-call | flops 3221225472 | bytes 14155776 | tf_op jit(solution)/shard_map/pallas_call | solution.py:456
  348.6 8.0 %shard_map.261 = (f32[256,2048]{1,0:T(8,128)}, f32[256,2048]{1,0:T(8,128)}) custom-call(bf16[512,1536]{1,0:T(8,128)(2,1)} %shard_map.247.refs_13_.refs_0_, bf16[512,1536]{1,0:T(8,128)(2,1)} %shard_map.248.refs_1_.refs_13_, bf16[512,1536]{1,0:T(8,128)(2,1)} %shard_map.255.refs_2_.refs_13_, ...), custom_call_target="tpu_custom_call" | custom-call | flops 3221225472 | bytes 14155776 | tf_op jit(solution)/shard_map/pallas_call | solution.py:456
  358.9 7.6 %shard_map.262 = (f32[256,2048]{1,0:T(8,128)}, bf16[256,2048]{1,0:T(8,128)(2,1)}, bf16[256,1024]{1,0:T(8,128)(2,1)}, f32[1,2048]{1,0:T(1,128)}) custom-call(bf16[128,2048]{1,0:T(8,128)(2,1)} %copy-done.8, bf16[128,2048]{1,0:T(8,128)(2,1)} %copy-done.10, bf16[128,2048]{1,0:T(8,128)(2,1)} %copy-done.31, bf16[128,2048]{1,0:T(8,128)(2,1)} %copy-done.34, ...), custom_call_target="tpu_custom_call" | custom-call | bytes 14163968 | tf_op jit(solution)/shard_map/pallas_call | solution.py:307
  366.5 5.2 shard_map.263
  375.3 16.7 %shard_map.264 = (bf16[512,2048]{1,0:T(8,128)(2,1)}, f32[1,128]{1,0:T(1,128)}, f32[1,128]{1,0:T(1,128)}) custom-call(f32[512,2048]{1,0:T(8,128)} %get-tuple-element.329.queries.keys.values, f32[512,2048]{1,0:T(8,128)} %get-tuple-element.329.queries.keys.values, f32[512,2048]{1,0:T(8,128)} %get-tuple-element.329.queries.keys.values, ...), custom_call_target="tpu_custom_call" | custom-call | flops 3221225472 | bytes 8388608 | tf_op jit(solution)/shard_map/pallas_call | solution.py:678
  394.0 3.6 collective-permute-done.56
  399.0 7.4 %shard_map.265 = (bf16[512,2048]{1,0:T(8,128)(2,1)}, bf16[512,2048]{1,0:T(8,128)(2,1)}) custom-call(s32[6]{0:T(128)} %stack.143.info, bf16[512,2048]{1,0:T(8,128)(2,1)} %get-tuple-element.290.left.refs_0_, bf16[512,2048]{1,0:T(8,128)(2,1)} %get-tuple-element.470.refs_1_.raw_grad, ...), custom_call_target="tpu_custom_call" | custom-call | flops 2147483648 | bytes 8388608 | tf_op jit(solution)/shard_map/pallas_call | solution.py:791
  410.8 5.5 %shard_map.266 = (bf16[512,1024]{1,0:T(8,128)(2,1)}, bf16[512,1024]{1,0:T(8,128)(2,1)}) custom-call(s32[6]{0:T(128)} %stack.60.info, bf16[256,2048]{1,0:T(8,128)(2,1)} %get-tuple-element.459.refs_0_, bf16[256,2048]{1,0:T(8,128)(2,1)} %get-tuple-element.460.refs_1_, bf16[256,1024]{1,0:T(8,128)(2,1)} %get-tuple-element.344.left.refs_2_, ...), custom_call_target="tpu_custom_call" | custom-call | flops 1073741824 | bytes 5242880 | tf_op jit(solution)/shard_map/pallas_call | solution.py:791
  418.6 8.3 %shard_map.267 = (bf16[128,2048]{1,0:T(8,128)(2,1)}, bf16[128,2048]{1,0:T(8,128)(2,1)}, bf16[128,2048]{1,0:T(8,128)(2,1)}, bf16[128,2048]{1,0:T(8,128)(2,1)}, bf...) custom-call(s32[6]{0:T(128)} %stack.60.info, ...), custom_call_target="tpu_custom_call" | custom-call | flops 2147483648 | bytes 8388608 | tf_op jit(solution)/shard_map/pallas_call | solution.py:791
  427.9 9.9 %shard_map.268 = (bf16[128,2048]{1,0:T(8,128)(2,1)}, bf16[128,2048]{1,0:T(8,128)(2,1)}, bf16[128,2048]{1,0:T(8,128)(2,1)}, bf16[128,2048]{1,0:T(8,128)(2,1)}, f32[1,2048]{1,0:T(1,128)}) custom-call(bf16[512,2048]{1,0:T(8,128)(2,1)} %get-tuple-element.470.refs_1_.raw_grad, bf16[2048,2048]{1,0:T(8,128)(2,1)} %get-tuple-element.495.full, ...), custom_call_target="tpu_custom_call" | custom-call | flops 4294967296 | bytes 16777216 | tf_op jit(solution)/shard_map/pallas_call | solution.py:712
  440.8 4.5 collective-permute-done.66
  445.3 2.4 collective-permute-start.67
  447.7 3.3 collective-permute-done.67
  453.9 2.4 shard_map.269
  463.9 6.1 %shard_map.270 = bf16[512,2048]{1,0:T(8,128)(2,1)} custom-call(f32[128,2048]{1,0:T(8,128)} %get-tuple-element.439.refs_4_.refs_0_, f32[128,2048]{1,0:T(8,128)} %get-tuple-element.440.refs_5_.refs_1_, f32[128,2048]{1,0:T(8,128)} %get-tuple-element.453.refs_4_.refs_2_, f32[128,2048]{1,0:T(8,128)} %get-tuple-element.454.refs_5_.refs_3_, ...), custom_call_target="tpu_custom_call" | custom-call | bytes 10485760 | tf_op jit(solution)/shard_map/pallas_call | solution.py:307
  470.0 9.0 %collective-permute-done.72 = f32[4352]{0:T(1024)S(1)} collective-permute-done((f32[4352]{0:T(1024)S(1)}, f32[4352]{0:T(1024)S(1)}, u32[]{:S(2)}, u32[]{:S(2)}) %collective-permute-start.72) | collective-permute-done | bytes 17440 | tf_op jit(solution)/shard_map/ppermute | solution.py:1298
  480.8 2.7 shard_map.271
  483.6 1.8 collective-permute-start.74
  489.4 10.8 %collective-permute-done.75.refs_6_ = bf16[128,2048]{1,0:T(8,128)(2,1)S(1)} collective-permute-done((bf16[128,2048]{1,0:T(8,128)(2,1)S(1)}, bf16[128,2048]{1,0:T(8,128)(2,1)S(1)}, u32[]{:S(2)}, u32[]{:S(2)}) %collective-permute-start.75) | collective-permute-done | bytes 524320 | tf_op jit(solution)/shard_map/ppermute | solution.py:179
  500.2 7.0 %collective-permute-done.76.refs_7_ = bf16[128,2048]{1,0:T(8,128)(2,1)S(1)} collective-permute-done((bf16[128,2048]{1,0:T(8,128)(2,1)S(1)}, bf16[128,2048]{1,0:T(8,128)(2,1)S(1)}, u32[]{:S(2)}, u32[]{:S(2)}) %collective-permute-start.76) | collective-permute-done | bytes 524320 | tf_op jit(solution)/shard_map/ppermute | solution.py:179
  508.9 2.7 shard_map.272
  511.7 3.3 collective-permute-start.79
  516.9 3.0 collective-permute-done.80
  519.9 8.4 %shard_map.273 = f32[512,2048]{1,0:T(8,128)} custom-call(bf16[128,2048]{1,0:T(8,128)(2,1)} %get-tuple-element.496.refs_0_, bf16[128,2048]{1,0:T(8,128)(2,1)} %get-tuple-element.510.refs_1_, bf16[128,2048]{1,0:T(8,128)(2,1)} %get-tuple-element.524.refs_2_, bf16[128,2048]{1,0:T(8,128)(2,1)} %get-tuple-element.525.refs_3_, bf16[128,2048]{1,0:T(8,128)(2,1)} %copy-done.50, ...), custom_call_target="tpu_custom_call" | custom-call | bytes 14688256 | tf_op jit(solution)/shard_map/pallas_call | solution.py:307
  528.3 4.5 shard_map.274
  534.0 2.9 shard_map.275
  (399 shorter events, 107.0 us)
Async XLA Ops:
  7.2 190.3 %all-gather.4.cloned.1.call-start = ((), (), s32[]{:S(2)}) async-start(), calls=%async_computation.2 | async-start | bytes 7077888 | tf_op jit(solution)/shard_map/all_gather | solution.py:1010
  9.9 23.9 %collective-permute-start.2 = (bf16[128,2048]{1,0:T(8,128)(2,1)S(1)}, bf16[128,2048]{1,0:T(8,128)(2,1)}, u32[]{:S(2)}, u32[]{:S(2)}) collective-permute-start(bf16[128,2048]{1,0:T(8,128)(2,1)S(1)} %pad_maximum_fusion.rest_0_), channel_id=1, source_target_pairs={{0,4},{2,6},{4,0},{6,2},{8,12},{10,14},{12,8},{14,10},{16,20},{18,... | collective-permute-start | bytes 1572872 | tf_op jit(solution)/shard_map/ppermute | solution.py:85
  12.8 21.0 %collective-permute-start.1 = (bf16[128,2048]{1,0:T(8,128)(2,1)S(1)}, bf16[128,2048]{1,0:T(8,128)(2,1)}, u32[]{:S(2)}, u32[]{:S(2)}) collective-permute-start(bf16[128,2048]{1,0:T(8,128)(2,1)S(1)} %pad_maximum_fusion.rest_0_), channel_id=1, source_target_pairs={{0,8},{2,10},{4,12},{6,14},{8,16},{10,18},{12,20},{14,22},{16,24},... | collective-permute-start | bytes 1572872 | tf_op jit(solution)/shard_map/ppermute | solution.py:88
  14.4 19.4 %collective-permute-start = (bf16[128,2048]{1,0:T(8,128)(2,1)S(1)}, bf16[128,2048]{1,0:T(8,128)(2,1)}, u32[]{:S(2)}, u32[]{:S(2)}) collective-permute-start(bf16[128,2048]{1,0:T(8,128)(2,1)S(1)} %pad_maximum_fusion.rest_0_), channel_id=1, source_target_pairs={{0,2},{2,0},{4,6},{6,4},{8,10},{10,8},{12,14},{14,12},{16,18},{18,... | collective-permute-start | bytes 1572872 | tf_op jit(solution)/shard_map/ppermute | solution.py:82
  15.5 18.3 %collective-permute-start.3 = (bf16[128,1024]{1,0:T(8,128)(2,1)S(1)}, bf16[128,1024]{1,0:T(8,128)(2,1)}, u32[]{:S(2)}, u32[]{:S(2)}) collective-permute-start(bf16[128,1024]{1,0:T(8,128)(2,1)S(1)} %bitcast.60), channel_id=1, source_target_pairs={{0,8},{2,10},{4,12},{6,14},{8,16},{10,18},{12,20},{14,22},{16,24},... | collective-permute-start | bytes 786440 | tf_op jit(solution)/shard_map/ppermute | solution.py:88
  33.9 21.2 %collective-permute-start.7 = (bf16[128,2048]{1,0:T(8,128)(2,1)}, bf16[128,2048]{1,0:T(8,128)(2,1)}, u32[]{:S(2)}, u32[]{:S(2)}) collective-permute-start(bf16[128,2048]{1,0:T(8,128)(2,1)} %collective-permute-done.1.rest_4_), channel_id=1, source_target_pairs={{0,4},{2,6},{4,0},{6,2},{8,12},{10,14},{12,8},{14,10},{16,20},{18,... | collective-permute-start | bytes 1572872 | tf_op jit(solution)/shard_map/ppermute | solution.py:85
  34.5 20.6 %collective-permute-start.6 = (bf16[128,2048]{1,0:T(8,128)(2,1)}, bf16[128,2048]{1,0:T(8,128)(2,1)}, u32[]{:S(2)}, u32[]{:S(2)}) collective-permute-start(bf16[128,2048]{1,0:T(8,128)(2,1)} %collective-permute-done.1.rest_4_), channel_id=1, source_target_pairs={{0,8},{2,10},{4,12},{6,14},{8,16},{10,18},{12,20},{14,22},{16,24},... | collective-permute-start | bytes 1572872 | tf_op jit(solution)/shard_map/ppermute | solution.py:88
  35.8 19.4 %collective-permute-start.5 = (bf16[128,2048]{1,0:T(8,128)(2,1)}, bf16[128,2048]{1,0:T(8,128)(2,1)}, u32[]{:S(2)}, u32[]{:S(2)}) collective-permute-start(bf16[128,2048]{1,0:T(8,128)(2,1)} %collective-permute-done.1.rest_4_), channel_id=1, source_target_pairs={{0,2},{2,0},{4,6},{6,4},{8,10},{10,8},{12,14},{14,12},{16,18},{18,... | collective-permute-start | bytes 1572872 | tf_op jit(solution)/shard_map/ppermute | solution.py:82
  35.8 19.4 %collective-permute-start.4 = (bf16[128,2048]{1,0:T(8,128)(2,1)}, bf16[128,2048]{1,0:T(8,128)(2,1)}, u32[]{:S(2)}, u32[]{:S(2)}) collective-permute-start(bf16[128,2048]{1,0:T(8,128)(2,1)} %collective-permute-done.2.rest_1_), channel_id=1, source_target_pairs={{0,2},{2,0},{4,6},{6,4},{8,10},{10,8},{12,14},{14,12},{16,18},{18,... | collective-permute-start | bytes 1572872 | tf_op jit(solution)/shard_map/ppermute | solution.py:82
  56.3 149.7 %all-gather.6.cloned.1.call-start = ((), (), s32[]{:S(2)}) async-start(), calls=%async_computation.3 | async-start | bytes 7077888 | tf_op jit(solution)/shard_map/all_gather | solution.py:1010
  56.3 20.4 %collective-permute-start.13 = (bf16[128,2048]{1,0:T(8,128)(2,1)}, bf16[128,2048]{1,0:T(8,128)(2,1)S(1)}, u32[]{:S(2)}, u32[]{:S(2)}) collective-permute-start(bf16[128,2048]{1,0:T(8,128)(2,1)} %collective-permute-done.6.rest_8_), channel_id=1, source_target_pairs={{0,4},{2,6},{4,0},{6,2},{8,12},{10,14},{12,8},{14,10},{16,20},{18,... | collective-permute-start | bytes 1572872 | tf_op jit(solution)/shard_map/ppermute | solution.py:85
  57.2 19.6 %collective-permute-start.12 = (bf16[128,2048]{1,0:T(8,128)(2,1)}, bf16[128,2048]{1,0:T(8,128)(2,1)}, u32[]{:S(2)}, u32[]{:S(2)}) collective-permute-start(bf16[128,2048]{1,0:T(8,128)(2,1)} %collective-permute-done.6.rest_8_), channel_id=1, source_target_pairs={{0,8},{2,10},{4,12},{6,14},{8,16},{10,18},{12,20},{14,22},{16,24},... | collective-permute-start | bytes 1572872 | tf_op jit(solution)/shard_map/ppermute | solution.py:88
  57.9 18.9 %collective-permute-start.11 = (bf16[128,2048]{1,0:T(8,128)(2,1)}, bf16[128,2048]{1,0:T(8,128)(2,1)}, u32[]{:S(2)}, u32[]{:S(2)}) collective-permute-start(bf16[128,2048]{1,0:T(8,128)(2,1)} %collective-permute-done.6.rest_8_), channel_id=1, source_target_pairs={{0,2},{2,0},{4,6},{6,4},{8,10},{10,8},{12,14},{14,12},{16,18},{18,... | collective-permute-start | bytes 1572872 | tf_op jit(solution)/shard_map/ppermute | solution.py:82
  57.9 18.9 %collective-permute-start.10 = (bf16[128,2048]{1,0:T(8,128)(2,1)}, bf16[128,2048]{1,0:T(8,128)(2,1)}, u32[]{:S(2)}, u32[]{:S(2)}) collective-permute-start(bf16[128,2048]{1,0:T(8,128)(2,1)} %collective-permute-done.7.rest_5_), channel_id=1, source_target_pairs={{0,2},{2,0},{4,6},{6,4},{8,10},{10,8},{12,14},{14,12},{16,18},{18,... | collective-permute-start | bytes 1572872 | tf_op jit(solution)/shard_map/ppermute | solution.py:82
  58.4 18.4 %collective-permute-start.14 = (bf16[128,1536]{1,0:T(8,128)(2,1)S(1)}, bf16[128,1536]{1,0:T(8,128)(2,1)S(1)}, u32[]{:S(2)}, u32[]{:S(2)}) collective-permute-start(bf16[128,1536]{1,0:T(8,128)(2,1)S(1)} %pad_maximum_fusion.2), channel_id=1, source_target_pairs={{0,4},{2,6},{4,0},{6,2},{8,12},{10,14},{12,8},{14,10},{16,20},{18,... | collective-permute-start | bytes 1179656 | tf_op jit(solution)/shard_map/ppermute | solution.py:85
  77.9 181.5 %all-gather.8.cloned.1.call-start = ((), (), s32[]{:S(2)}) async-start(), calls=%async_computation.4 | async-start | bytes 7077888 | tf_op jit(solution)/shard_map/all_gather | solution.py:1010
  77.9 16.6 %collective-permute-start.19 = (bf16[128,1024]{1,0:T(8,128)(2,1)S(1)}, bf16[128,1024]{1,0:T(8,128)(2,1)S(1)}, u32[]{:S(2)}, u32[]{:S(2)}) collective-permute-start(bf16[128,1024]{1,0:T(8,128)(2,1)S(1)} %collective-permute-done.8.rest_7_), channel_id=1, source_target_pairs={{0,8},{2,10},{4,12},{6,14},{8,16},{10,18},{12,20},{14,22},{16,24},... | collective-permute-start | bytes 786440 | tf_op jit(solution)/shard_map/ppermute | solution.py:88
  78.5 17.6 %collective-permute-start.17 = (bf16[128,2048]{1,0:T(8,128)(2,1)}, bf16[128,2048]{1,0:T(8,128)(2,1)S(1)}, u32[]{:S(2)}, u32[]{:S(2)}) collective-permute-start(bf16[128,2048]{1,0:T(8,128)(2,1)} %collective-permute-done.12.rest_12_), channel_id=1, source_target_pairs={{0,4},{2,6},{4,0},{6,2},{8,12},{10,14},{12,8},{14,10},{16,20},{18,... | collective-permute-start | bytes 1572872 | tf_op jit(solution)/shard_map/ppermute | solution.py:85
  79.1 17.0 %collective-permute-start.16 = (bf16[128,2048]{1,0:T(8,128)(2,1)}, bf16[128,2048]{1,0:T(8,128)(2,1)S(1)}, u32[]{:S(2)}, u32[]{:S(2)}) collective-permute-start(bf16[128,2048]{1,0:T(8,128)(2,1)} %collective-permute-done.12.rest_12_), channel_id=1, source_target_pairs={{0,2},{2,0},{4,6},{6,4},{8,10},{10,8},{12,14},{14,12},{16,18},{18,... | collective-permute-start | bytes 1572872 | tf_op jit(solution)/shard_map/ppermute | solution.py:82
  79.1 17.0 %collective-permute-start.15 = (bf16[128,2048]{1,0:T(8,128)(2,1)S(1)}, bf16[128,2048]{1,0:T(8,128)(2,1)S(1)}, u32[]{:S(2)}, u32[]{:S(2)}) collective-permute-start(bf16[128,2048]{1,0:T(8,128)(2,1)S(1)} %collective-permute-done.13.rest_9_), channel_id=1, source_target_pairs={{0,2},{2,0},{4,6},{6,4},{8,10},{10,8},{12,14},{14,12},{16,18},{18,... | collective-permute-start | bytes 1572872 | tf_op jit(solution)/shard_map/ppermute | solution.py:82
  79.6 15.2 %collective-permute-start.20 = (bf16[128,1024]{1,0:T(8,128)(2,1)S(1)}, bf16[128,1024]{1,0:T(8,128)(2,1)S(1)}, u32[]{:S(2)}, u32[]{:S(2)}) collective-permute-start(bf16[128,1024]{1,0:T(8,128)(2,1)S(1)} %bitcast.61), channel_id=1, source_target_pairs={{0,4},{2,6},{4,0},{6,2},{8,12},{10,14},{12,8},{14,10},{16,20},{18,... | collective-permute-start | bytes 786440 | tf_op jit(solution)/shard_map/ppermute | solution.py:85
  100.3 14.7 %collective-permute-start.21 = (bf16[128,1024]{1,0:T(8,128)(2,1)S(1)}, bf16[128,1024]{1,0:T(8,128)(2,1)S(1)}, u32[]{:S(2)}, u32[]{:S(2)}) collective-permute-start(bf16[128,1024]{1,0:T(8,128)(2,1)S(1)} %collective-permute-done.20.rest_1_), channel_id=1, source_target_pairs={{0,2},{2,0},{4,6},{6,4},{8,10},{10,8},{12,14},{14,12},{16,18},{18,... | collective-permute-start | bytes 786440 | tf_op jit(solution)/shard_map/ppermute | solution.py:82
  100.7 14.3 %collective-permute-start.25 = (bf16[128,1024]{1,0:T(8,128)(2,1)}, bf16[128,1024]{1,0:T(8,128)(2,1)S(1)}, u32[]{:S(2)}, u32[]{:S(2)}) collective-permute-start(bf16[128,1024]{1,0:T(8,128)(2,1)} %collective-permute-done.3.rest_4_), channel_id=1, source_target_pairs={{0,4},{2,6},{4,0},{6,2},{8,12},{10,14},{12,8},{14,10},{16,20},{18,... | collective-permute-start | bytes 786440 | tf_op jit(solution)/shard_map/ppermute | solution.py:85
  100.7 14.3 %collective-permute-start.23 = (bf16[128,1024]{1,0:T(8,128)(2,1)}, bf16[128,1024]{1,0:T(8,128)(2,1)S(1)}, u32[]{:S(2)}, u32[]{:S(2)}) collective-permute-start(bf16[128,1024]{1,0:T(8,128)(2,1)} %collective-permute-done.3.rest_4_), channel_id=1, source_target_pairs={{0,2},{2,0},{4,6},{6,4},{8,10},{10,8},{12,14},{14,12},{16,18},{18,... | collective-permute-start | bytes 786440 | tf_op jit(solution)/shard_map/ppermute | solution.py:82
  100.8 14.2 %collective-permute-start.26 = (bf16[128,1024]{1,0:T(8,128)(2,1)S(1)}, bf16[128,1024]{1,0:T(8,128)(2,1)S(1)}, u32[]{:S(2)}, u32[]{:S(2)}) collective-permute-start(bf16[128,1024]{1,0:T(8,128)(2,1)S(1)} %collective-permute-done.8.rest_7_), channel_id=1, source_target_pairs={{0,4},{2,6},{4,0},{6,2},{8,12},{10,14},{12,8},{14,10},{16,20},{18,... | collective-permute-start | bytes 786440 | tf_op jit(solution)/shard_map/ppermute | solution.py:85
  127.6 22.6 %collective-permute-start.34 = (bf16[128,2048]{1,0:T(8,128)(2,1)S(1)}, bf16[128,2048]{1,0:T(8,128)(2,1)S(1)}, u32[]{:S(2)}, u32[]{:S(2)}) collective-permute-start(bf16[128,2048]{1,0:T(8,128)(2,1)S(1)} %get-tuple-element.356), channel_id=1, source_target_pairs={{0,4},{2,6},{4,0},{6,2},{8,12},{10,14},{12,8},{14,10},{16,20},{18,... | collective-permute-start | bytes 1572872 | tf_op jit(solution)/shard_map/ppermute | solution.py:85
  135.4 14.8 %collective-permute-start.33 = (bf16[128,2048]{1,0:T(8,128)(2,1)}, bf16[128,2048]{1,0:T(8,128)(2,1)S(1)}, u32[]{:S(2)}, u32[]{:S(2)}) collective-permute-start(bf16[128,2048]{1,0:T(8,128)(2,1)} %get-tuple-element.355.refs_1_), channel_id=1, source_target_pairs={{0,1},{1,0},{2,3},{3,2},{4,5},{5,4},{6,7},{7,6},{8,9},{9,8},{10,11... | collective-permute-start | bytes 1572872 | tf_op jit(solution)/shard_map/ppermute | solution.py:179
  135.8 14.4 %collective-permute-start.35 = (bf16[128,1536]{1,0:T(8,128)(2,1)S(1)}, bf16[128,1536]{1,0:T(8,128)(2,1)S(1)}, u32[]{:S(2)}, u32[]{:S(2)}) collective-permute-start(bf16[128,1536]{1,0:T(8,128)(2,1)S(1)} %pad_maximum_fusion.3), channel_id=1, source_target_pairs={{0,4},{2,6},{4,0},{6,2},{8,12},{10,14},{12,8},{14,10},{16,20},{18,... | collective-permute-start | bytes 1179656 | tf_op jit(solution)/shard_map/ppermute | solution.py:85
  151.3 247.7 %reduce-scatter.3.cloned.1.call-start = ((), (), s32[]{:S(2)}) async-start(), calls=%async_computation.5 | async-start | bytes 7077888 | tf_op jit(solution)/shard_map/reduce_scatter | solution.py:1229
  165.6 15.1 %collective-permute-start.37 = (bf16[128,2048]{1,0:T(8,128)(2,1)}, bf16[128,2048]{1,0:T(8,128)(2,1)S(1)}, u32[]{:S(2)}, u32[]{:S(2)}) collective-permute-start(bf16[128,2048]{1,0:T(8,128)(2,1)} %get-tuple-element.369.refs_1_), channel_id=1, source_target_pairs={{0,1},{1,0},{2,3},{3,2},{4,5},{5,4},{6,7},{7,6},{8,9},{9,8},{10,11... | collective-permute-start | bytes 1572872 | tf_op jit(solution)/shard_map/ppermute | solution.py:179
  166.9 13.8 %collective-permute-start.38 = (bf16[128,2048]{1,0:T(8,128)(2,1)S(1)}, bf16[128,2048]{1,0:T(8,128)(2,1)S(1)}, u32[]{:S(2)}, u32[]{:S(2)}) collective-permute-start(bf16[128,2048]{1,0:T(8,128)(2,1)S(1)} %copy-done.2), channel_id=1, source_target_pairs={{0,4},{2,6},{4,0},{6,2},{8,12},{10,14},{12,8},{14,10},{16,20},{18,... | collective-permute-start | bytes 1572872 | tf_op jit(solution)/shard_map/ppermute | solution.py:85
  171.4 18.0 %collective-permute-start.39 = (bf16[128,2048]{1,0:T(8,128)(2,1)S(1)}, bf16[128,2048]{1,0:T(8,128)(2,1)S(1)}, u32[]{:S(2)}, u32[]{:S(2)}) collective-permute-start(bf16[128,2048]{1,0:T(8,128)(2,1)S(1)} %copy-done.39), channel_id=1, source_target_pairs={{0,1},{1,0},{2,3},{3,2},{4,5},{5,4},{6,7},{7,6},{8,9},{9,8},{10,11... | collective-permute-start | bytes 1572872 | tf_op jit(solution)/shard_map/ppermute | solution.py:179
  190.7 15.3 %collective-permute-start.41 = (bf16[128,2048]{1,0:T(8,128)(2,1)}, bf16[128,2048]{1,0:T(8,128)(2,1)S(1)}, u32[]{:S(2)}, u32[]{:S(2)}) collective-permute-start(bf16[128,2048]{1,0:T(8,128)(2,1)} %get-tuple-element.383.refs_2_), channel_id=1, source_target_pairs={{0,4},{2,6},{4,0},{6,2},{8,12},{10,14},{12,8},{14,10},{16,20},{18,... | collective-permute-start | bytes 1572872 | tf_op jit(solution)/shard_map/ppermute | solution.py:85
  195.3 19.3 %collective-permute-start.42 = (bf16[128,2048]{1,0:T(8,128)(2,1)}, bf16[128,2048]{1,0:T(8,128)(2,1)S(1)}, u32[]{:S(2)}, u32[]{:S(2)}) collective-permute-start(bf16[128,2048]{1,0:T(8,128)(2,1)} %get-tuple-element.385.refs_3_), channel_id=1, source_target_pairs={{0,4},{2,6},{4,0},{6,2},{8,12},{10,14},{12,8},{14,10},{16,20},{18,... | collective-permute-start | bytes 1572872 | tf_op jit(solution)/shard_map/ppermute | solution.py:85
  195.5 19.0 %collective-permute-start.43 = (bf16[128,2048]{1,0:T(8,128)(2,1)S(1)}, bf16[128,2048]{1,0:T(8,128)(2,1)S(1)}, u32[]{:S(2)}, u32[]{:S(2)}) collective-permute-start(bf16[128,2048]{1,0:T(8,128)(2,1)S(1)} %collective-permute-done.34), channel_id=1, source_target_pairs={{0,1},{1,0},{2,3},{3,2},{4,5},{5,4},{6,7},{7,6},{8,9},{9,8},{10,11... | collective-permute-start | bytes 1572872 | tf_op jit(solution)/shard_map/ppermute | solution.py:179
  196.3 21.3 %collective-permute-start.44 = (bf16[128,2048]{1,0:T(8,128)(2,1)S(1)}, bf16[128,2048]{1,0:T(8,128)(2,1)S(1)}, u32[]{:S(2)}, u32[]{:S(2)}) collective-permute-start(bf16[128,2048]{1,0:T(8,128)(2,1)S(1)} %collective-permute-done.36), channel_id=1, source_target_pairs={{0,1},{1,0},{2,3},{3,2},{4,5},{5,4},{6,7},{7,6},{8,9},{9,8},{10,11... | collective-permute-start | bytes 1572872 | tf_op jit(solution)/shard_map/ppermute | solution.py:179
  240.3 220.4 %reduce-scatter.5.cloned.1.call-start = ((), (), s32[]{:S(2)}) async-start(), calls=%async_computation.6 | async-start | bytes 14155776 | tf_op jit(solution)/shard_map/reduce_scatter | solution.py:1229
  274.8 22.4 %collective-permute-start.45 = (bf16[128,2048]{1,0:T(8,128)(2,1)}, bf16[128,2048]{1,0:T(8,128)(2,1)S(1)}, u32[]{:S(2)}, u32[]{:S(2)}) collective-permute-start(bf16[128,2048]{1,0:T(8,128)(2,1)} %get-tuple-element.408.refs_6_), channel_id=1, source_target_pairs={{0,4},{2,6},{4,0},{6,2},{8,12},{10,14},{12,8},{14,10},{16,20},{18,... | collective-permute-start | bytes 1572872 | tf_op jit(solution)/shard_map/ppermute | solution.py:85
  284.8 27.0 %collective-permute-start.47 = (bf16[128,2048]{1,0:T(8,128)(2,1)S(1)}, bf16[128,2048]{1,0:T(8,128)(2,1)S(1)}, u32[]{:S(2)}, u32[]{:S(2)}) collective-permute-start(bf16[128,2048]{1,0:T(8,128)(2,1)S(1)} %copy-done.90), channel_id=1, source_target_pairs={{0,4},{2,6},{4,0},{6,2},{8,12},{10,14},{12,8},{14,10},{16,20},{18,... | collective-permute-start | bytes 1572872 | tf_op jit(solution)/shard_map/ppermute | solution.py:85
  298.5 13.6 %collective-permute-start.46 = (bf16[128,2048]{1,0:T(8,128)(2,1)S(1)}, bf16[128,2048]{1,0:T(8,128)(2,1)S(1)}, u32[]{:S(2)}, u32[]{:S(2)}) collective-permute-start(bf16[128,2048]{1,0:T(8,128)(2,1)S(1)} %add_convert_fusion.5.refs_15_.refs_0_), channel_id=1, source_target_pairs={{0,1},{1,0},{2,3},{3,2},{4,5},{5,4},{6,7},{7,6},{8,9},{9,8},{10,11... | collective-permute-start | bytes 1572872 | tf_op jit(solution)/shard_map/ppermute | solution.py:179
  312.1 14.8 %collective-permute-start.49 = (bf16[128,2048]{1,0:T(8,128)(2,1)}, bf16[128,2048]{1,0:T(8,128)(2,1)S(1)}, u32[]{:S(2)}, u32[]{:S(2)}) collective-permute-start(bf16[128,2048]{1,0:T(8,128)(2,1)} %get-tuple-element.429), channel_id=1, source_target_pairs={{0,4},{2,6},{4,0},{6,2},{8,12},{10,14},{12,8},{14,10},{16,20},{18,... | collective-permute-start | bytes 1572872 | tf_op jit(solution)/shard_map/ppermute | solution.py:85
  327.7 17.2 %collective-permute-start.51 = (bf16[128,2048]{1,0:T(8,128)(2,1)}, bf16[128,2048]{1,0:T(8,128)(2,1)S(1)}, u32[]{:S(2)}, u32[]{:S(2)}) collective-permute-start(bf16[128,2048]{1,0:T(8,128)(2,1)} %get-tuple-element.434), channel_id=1, source_target_pairs={{0,4},{2,6},{4,0},{6,2},{8,12},{10,14},{12,8},{14,10},{16,20},{18,... | collective-permute-start | bytes 1572872 | tf_op jit(solution)/shard_map/ppermute | solution.py:85
  328.4 16.5 %collective-permute-start.50 = (bf16[128,2048]{1,0:T(8,128)(2,1)S(1)}, bf16[128,2048]{1,0:T(8,128)(2,1)S(1)}, u32[]{:S(2)}, u32[]{:S(2)}) collective-permute-start(bf16[128,2048]{1,0:T(8,128)(2,1)S(1)} %add_convert_fusion.3.refs_6_.refs_0_), channel_id=1, source_target_pairs={{0,1},{1,0},{2,3},{3,2},{4,5},{5,4},{6,7},{7,6},{8,9},{9,8},{10,11... | collective-permute-start | bytes 1572872 | tf_op jit(solution)/shard_map/ppermute | solution.py:179
  344.9 27.3 %collective-permute-start.53 = (bf16[256,2048]{1,0:T(8,128)(2,1)}, bf16[256,2048]{1,0:T(8,128)(2,1)S(1)}, u32[]{:S(2)}, u32[]{:S(2)}) collective-permute-start(bf16[256,2048]{1,0:T(8,128)(2,1)} %get-tuple-element.457), channel_id=1, source_target_pairs={{0,4},{2,6},{4,0},{6,2},{8,12},{10,14},{12,8},{14,10},{16,20},{18,... | collective-permute-start | bytes 3145736 | tf_op jit(solution)/shard_map/ppermute | solution.py:85
  371.7 20.4 %collective-permute-start.55 = (bf16[512,1024]{1,0:T(8,128)(2,1)}, bf16[512,1024]{1,0:T(8,128)(2,1)S(1)}, u32[]{:S(2)}, u32[]{:S(2)}) collective-permute-start(bf16[512,1024]{1,0:T(8,128)(2,1)} %get-tuple-element.465), channel_id=1, source_target_pairs={{0,2},{2,0},{4,6},{6,4},{8,10},{10,8},{12,14},{14,12},{16,18},{18,... | collective-permute-start | bytes 3145736 | tf_op jit(solution)/shard_map/ppermute | solution.py:82
  371.7 21.3 %collective-permute-start.54 = (bf16[512,1024]{1,0:T(8,128)(2,1)}, bf16[512,1024]{1,0:T(8,128)(2,1)S(1)}, u32[]{:S(2)}, u32[]{:S(2)}) collective-permute-start(bf16[512,1024]{1,0:T(8,128)(2,1)} %get-tuple-element.461.rest_3_), channel_id=1, source_target_pairs={{0,2},{2,0},{4,6},{6,4},{8,10},{10,8},{12,14},{14,12},{16,18},{18,... | collective-permute-start | bytes 3145736 | tf_op jit(solution)/shard_map/ppermute | solution.py:82
  372.2 25.4 %collective-permute-start.56 = (bf16[256,2048]{1,0:T(8,128)(2,1)}, bf16[256,2048]{1,0:T(8,128)(2,1)S(1)}, u32[]{:S(2)}, u32[]{:S(2)}) collective-permute-start(bf16[256,2048]{1,0:T(8,128)(2,1)} %get-tuple-element.467), channel_id=1, source_target_pairs={{0,4},{2,6},{4,0},{6,2},{8,12},{10,14},{12,8},{14,10},{16,20},{18,... | collective-permute-start | bytes 3145736 | tf_op jit(solution)/shard_map/ppermute | solution.py:85
  373.9 25.0 %collective-permute-start.57 = (bf16[256,2048]{1,0:T(8,128)(2,1)S(1)}, bf16[256,2048]{1,0:T(8,128)(2,1)}, u32[]{:S(2)}, u32[]{:S(2)}) collective-permute-start(bf16[256,2048]{1,0:T(8,128)(2,1)S(1)} %add_convert_fusion.1.refs_4_), channel_id=1, source_target_pairs={{0,1},{1,0},{2,3},{3,2},{4,5},{5,4},{6,7},{7,6},{8,9},{9,8},{10,11... | collective-permute-start | bytes 3145736 | tf_op jit(solution)/shard_map/ppermute | solution.py:179
  410.1 40.9 %collective-permute-start.64 = (bf16[256,2048]{1,0:T(8,128)(2,1)S(1)}, bf16[256,2048]{1,0:T(8,128)(2,1)S(1)}, u32[]{:S(2)}, u32[]{:S(2)}) collective-permute-start(bf16[256,2048]{1,0:T(8,128)(2,1)S(1)} %add_convert_fusion.refs_5_), channel_id=1, source_target_pairs={{0,1},{1,0},{2,3},{3,2},{4,5},{5,4},{6,7},{7,6},{8,9},{9,8},{10,11... | collective-permute-start | bytes 3145736 | tf_op jit(solution)/shard_map/ppermute | solution.py:179
  416.3 34.7 %collective-permute-start.62 = (bf16[512,1024]{1,0:T(8,128)(2,1)}, bf16[512,1024]{1,0:T(8,128)(2,1)S(1)}, u32[]{:S(2)}, u32[]{:S(2)}) collective-permute-start(bf16[512,1024]{1,0:T(8,128)(2,1)} %get-tuple-element.494), channel_id=1, source_target_pairs={{0,4},{2,6},{4,0},{6,2},{8,12},{10,14},{12,8},{14,10},{16,20},{18,... | collective-permute-start | bytes 3145736 | tf_op jit(solution)/shard_map/ppermute | solution.py:85
  426.9 25.4 %collective-permute-start.61 = (bf16[128,2048]{1,0:T(8,128)(2,1)}, bf16[128,2048]{1,0:T(8,128)(2,1)S(1)}, u32[]{:S(2)}, u32[]{:S(2)}) collective-permute-start(bf16[128,2048]{1,0:T(8,128)(2,1)} %get-tuple-element.493), channel_id=1, source_target_pairs={{0,4},{2,6},{4,0},{6,2},{8,12},{10,14},{12,8},{14,10},{16,20},{18,... | collective-permute-start | bytes 1572872 | tf_op jit(solution)/shard_map/ppermute | solution.py:85
  437.9 14.5 %collective-permute-start.63 = (bf16[128,2048]{1,0:T(8,128)(2,1)}, bf16[128,2048]{1,0:T(8,128)(2,1)S(1)}, u32[]{:S(2)}, u32[]{:S(2)}) collective-permute-start(bf16[128,2048]{1,0:T(8,128)(2,1)} %get-tuple-element.496.refs_0_), channel_id=1, source_target_pairs={{0,1},{1,0},{2,3},{3,2},{4,5},{5,4},{6,7},{7,6},{8,9},{9,8},{10,11... | collective-permute-start | bytes 1572872 | tf_op jit(solution)/shard_map/ppermute | solution.py:179
  456.3 22.7 %collective-permute-start.69 = (bf16[128,3072]{1,0:T(8,128)(2,1)}, bf16[128,3072]{1,0:T(8,128)(2,1)S(1)}, u32[]{:S(2)}, u32[]{:S(2)}) collective-permute-start(bf16[128,3072]{1,0:T(8,128)(2,1)} %shard_map.269), channel_id=1, source_target_pairs={{0,8},{2,10},{4,12},{6,14},{8,16},{10,18},{12,20},{14,22},{16,24},... | collective-permute-start | bytes 2359304 | tf_op jit(solution)/shard_map/ppermute | solution.py:88
  456.8 22.2 %collective-permute-start.70 = (bf16[128,2048]{1,0:T(8,128)(2,1)S(1)}, bf16[128,2048]{1,0:T(8,128)(2,1)}, u32[]{:S(2)}, u32[]{:S(2)}) collective-permute-start(bf16[128,2048]{1,0:T(8,128)(2,1)S(1)} %copy-done.47), channel_id=1, source_target_pairs={{0,1},{1,0},{2,3},{3,2},{4,5},{5,4},{6,7},{7,6},{8,9},{9,8},{10,11... | collective-permute-start | bytes 1572872 | tf_op jit(solution)/shard_map/ppermute | solution.py:179
  458.1 21.0 %collective-permute-start.68 = (bf16[128,2048]{1,0:T(8,128)(2,1)}, bf16[128,2048]{1,0:T(8,128)(2,1)S(1)}, u32[]{:S(2)}, u32[]{:S(2)}) collective-permute-start(bf16[128,2048]{1,0:T(8,128)(2,1)} %get-tuple-element.505), channel_id=1, source_target_pairs={{0,4},{2,6},{4,0},{6,2},{8,12},{10,14},{12,8},{14,10},{16,20},{18,... | collective-permute-start | bytes 1572872 | tf_op jit(solution)/shard_map/ppermute | solution.py:85
  461.8 17.2 %collective-permute-start.71 = (bf16[128,1536]{1,0:T(8,128)(2,1)S(1)}, bf16[128,1536]{1,0:T(8,128)(2,1)S(1)}, u32[]{:S(2)}, u32[]{:S(2)}) collective-permute-start(bf16[128,1536]{1,0:T(8,128)(2,1)S(1)} %get-tuple-element.512), channel_id=1, source_target_pairs={{0,4},{2,6},{4,0},{6,2},{8,12},{10,14},{12,8},{14,10},{16,20},{18,... | collective-permute-start | bytes 1179656 | tf_op jit(solution)/shard_map/ppermute | solution.py:85
  463.5 15.5 %collective-permute-start.72 = (f32[4352]{0:T(1024)S(1)}, f32[4352]{0:T(1024)S(1)}, u32[]{:S(2)}, u32[]{:S(2)}) collective-permute-start(f32[4352]{0:T(1024)S(1)} %add.328), channel_id=1, source_target_pairs={{0,4},{2,6},{4,0},{6,2},{8,12},{10,14},{12,8},{14,10},{16,20},{18,... | collective-permute-start | bytes 52232 | tf_op jit(solution)/shard_map/ppermute | solution.py:1298
  483.6 23.7 %collective-permute-start.74 = (bf16[128,3072]{1,0:T(8,128)(2,1)}, bf16[128,3072]{1,0:T(8,128)(2,1)S(1)}, u32[]{:S(2)}, u32[]{:S(2)}) collective-permute-start(bf16[128,3072]{1,0:T(8,128)(2,1)} %shard_map.271), channel_id=1, source_target_pairs={{0,8},{2,10},{4,12},{6,14},{8,16},{10,18},{12,20},{14,22},{16,24},... | collective-permute-start | bytes 2359304 | tf_op jit(solution)/shard_map/ppermute | solution.py:88
  485.4 14.9 %collective-permute-start.75 = (bf16[128,2048]{1,0:T(8,128)(2,1)S(1)}, bf16[128,2048]{1,0:T(8,128)(2,1)S(1)}, u32[]{:S(2)}, u32[]{:S(2)}) collective-permute-start(bf16[128,2048]{1,0:T(8,128)(2,1)S(1)} %copy-done.48), channel_id=1, source_target_pairs={{0,1},{1,0},{2,3},{3,2},{4,5},{5,4},{6,7},{7,6},{8,9},{9,8},{10,11... | collective-permute-start | bytes 1572872 | tf_op jit(solution)/shard_map/ppermute | solution.py:179
  486.4 20.8 %collective-permute-start.76 = (bf16[128,2048]{1,0:T(8,128)(2,1)S(1)}, bf16[128,2048]{1,0:T(8,128)(2,1)S(1)}, u32[]{:S(2)}, u32[]{:S(2)}) collective-permute-start(bf16[128,2048]{1,0:T(8,128)(2,1)S(1)} %copy-done.49), channel_id=1, source_target_pairs={{0,1},{1,0},{2,3},{3,2},{4,5},{5,4},{6,7},{7,6},{8,9},{9,8},{10,11... | collective-permute-start | bytes 1572872 | tf_op jit(solution)/shard_map/ppermute | solution.py:179
  487.4 19.8 %collective-permute-start.73 = (bf16[128,2048]{1,0:T(8,128)(2,1)S(1)}, bf16[128,2048]{1,0:T(8,128)(2,1)S(1)}, u32[]{:S(2)}, u32[]{:S(2)}) collective-permute-start(bf16[128,2048]{1,0:T(8,128)(2,1)S(1)} %copy-done.89), channel_id=1, source_target_pairs={{0,4},{2,6},{4,0},{6,2},{8,12},{10,14},{12,8},{14,10},{16,20},{18,... | collective-permute-start | bytes 1572872 | tf_op jit(solution)/shard_map/ppermute | solution.py:85
  488.4 18.8 %collective-permute-start.77 = (bf16[128,1536]{1,0:T(8,128)(2,1)S(1)}, bf16[128,1536]{1,0:T(8,128)(2,1)S(1)}, u32[]{:S(2)}, u32[]{:S(2)}) collective-permute-start(bf16[128,1536]{1,0:T(8,128)(2,1)S(1)} %get-tuple-element.526), channel_id=1, source_target_pairs={{0,4},{2,6},{4,0},{6,2},{8,12},{10,14},{12,8},{14,10},{16,20},{18,... | collective-permute-start | bytes 1179656 | tf_op jit(solution)/shard_map/ppermute | solution.py:85
  511.7 21.1 %collective-permute-start.79 = (bf16[128,3072]{1,0:T(8,128)(2,1)}, bf16[128,3072]{1,0:T(8,128)(2,1)S(1)}, u32[]{:S(2)}, u32[]{:S(2)}) collective-permute-start(bf16[128,3072]{1,0:T(8,128)(2,1)} %shard_map.272), channel_id=1, source_target_pairs={{0,8},{2,10},{4,12},{6,14},{8,16},{10,18},{12,20},{14,22},{16,24},... | collective-permute-start | bytes 2359304 | tf_op jit(solution)/shard_map/ppermute | solution.py:88
  515.0 17.7 %collective-permute-start.78 = (bf16[128,2048]{1,0:T(8,128)(2,1)}, bf16[128,2048]{1,0:T(8,128)(2,1)S(1)}, u32[]{:S(2)}, u32[]{:S(2)}) collective-permute-start(bf16[128,2048]{1,0:T(8,128)(2,1)} %get-tuple-element.528), channel_id=1, source_target_pairs={{0,4},{2,6},{4,0},{6,2},{8,12},{10,14},{12,8},{14,10},{16,20},{18,... | collective-permute-start | bytes 1572872 | tf_op jit(solution)/shard_map/ppermute | solution.py:85
  (113 other events, 923.4 us)
Sparse Core Ops, SparseCore 0:
  56.4 72.6 all-gather.3
  131.3 62.9 all-gather.5
  196.0 63.3 all-gather.7
  261.6 68.4 reduce-scatter.2
  332.2 128.4 reduce-scatter.4

commit v5 on v4

--- a/solution.py
+++ b/solution.py
@@ -732,7 +732,7 @@
     )(raw_grad, full, tokens, *ties)
 
 
-def scatter_kernel(width, steps, lefts, rights, gots, ties, info, *refs):
+def scatter_kernel(width, steps, lefts, rights, gots, ties, flipped, info, *refs):
     turned, outs = refs[-1], refs[lefts + rights + gots + ties : -1]
     left, right = refs[:lefts], refs[lefts : lefts + rights]
     got = refs[lefts + rights : lefts + rights + gots]
@@ -744,10 +744,12 @@
             side = info[1] if k == 0 else 1 - info[1]
             for i in range(steps):
                 start = pl.multiple_of((info[2 + i] * 4 + info[0] * 2 + side) * width, width)
-                first = 0
+                first, row = 0, k * size + i * width
+                if flipped:
+                    turned[row : row + width, :] = left[0][pl.ds(start, width), :]
+                    continue
                 for part in left:
                     block = part[:, pl.ds(start, width)].T
-                    row = k * size + i * width
                     turned[row : row + width, first : first + part.shape[0]] = block
                     first += part.shape[0]
 
@@ -766,12 +768,13 @@
             outs[k * each + i][...] = value[i * rows : (i + 1) * rows]
 
 
-def scatter_call(ring, width, left, right, core, got=(), ties=(), apart=True):
+def scatter_call(ring, width, left, right, core, got=(), ties=(), apart=True, flipped=False):
     rows, columns = sum(r.shape[0] for r in right), right[0].shape[1]
     steps = ring.steps
     each = steps if apart else 1
     if 2 * width % LANES:
-        blocks = jnp.concatenate(left, axis=0).reshape(rows, steps, 2, 2, width)
+        left = left[0].T if flipped else jnp.concatenate(left, axis=0)
+        blocks = left.reshape(rows, steps, 2, 2, width)
         right = jnp.concatenate(right, axis=0)
         outs = []
         for k, side in enumerate((ring.side, 1 - ring.side)):
@@ -790,7 +793,7 @@
     tile, tall = 512, steps * width // each
     outs = pl.pallas_call(
         functools.partial(
-            scatter_kernel, width, steps, len(left), len(right), len(got), len(ties)
+            scatter_kernel, width, steps, len(left), len(right), len(got), len(ties), flipped
         ),
         grid_spec=pltpu.PrefetchScalarGridSpec(
             num_scalar_prefetch=1,
@@ -862,7 +865,7 @@
 def join_call(gather, left):
     width, columns = gather.pieces[0].shape
     rows, model_width = left.shape
-    tile = columns // 4
+    tile = columns // 2
     count = len(gather.pieces)
     return pl.pallas_call(
         functools.partial(join_kernel, width, count),
@@ -1099,6 +1102,8 @@
                 mixture_low.append(mixed)
                 row_totals.append(row_total)
                 extra = [mixed, [ring.swap_side(w) for w in late]]
+            if i == 2:
+                extra = [input_one.T]
             if i == 1:
                 extra = rows_product(mixture_low[1], output_full, part, stages.ties)
             moves, work, extra = settle(moves, work, extra)
@@ -1109,6 +1114,8 @@
                     feed_gather(2 + j, value)
             if i == 1:
                 branch_parts += extra
+            if i == 2:
+                (flipped,) = extra
             if i < 2:
                 sent[i] = moves[1]
             else:
@@ -1260,7 +1267,7 @@
     out_sums.append(add_low(out_mine[1], got))
     out_done = [out_next]
     far_one = scatter_call(
-        ring, width, [input_one], [raw_grad], 1 - core, ties=stages.ties, apart=False
+        ring, width, [flipped], [raw_grad], 1 - core, ties=stages.ties, apart=False, flipped=True
     )
     (near,), across = scatter_call(
         ring,
@@ -1279,7 +1286,9 @@
     )
     pairs_got = [pair]
     ((mine, other),) = settle(
-        scatter_call(ring, width, [input_one], [raw_grad], core, far_one, stages.ties)
+        scatter_call(
+            ring, width, [flipped], [raw_grad], core, far_one, stages.ties, flipped=True
+        )
     )
     *back_one, grad_first = back_first_call(raw_grad, attention_full, token_rows, stages.ties)
     gains = jnp.concatenate(
@@ -1329,7 +1338,7 @@
         else:
             moves.append(ring.shift(sent, 1))
         others = []
-        turns = {0: [0], 1: [1], 2: [2, 3]}.get(i, [])
+        turns = {0: [0], 1: [1, 2], 2: [3]}.get(i, [])
         others.append([swap_tensor(back_one[k]) for k in turns])
         k = i - (steps - CHUNKS)
         if 0 <= k < CHUNKS - 1:
@@ -1351,7 +1360,7 @@
             others.append(finish_call(ring, chunk, scattered, pairs_got))
         if i == 0:
             others.append(swap_tensor(out_sums[1]))
-        if i < 2:
+        if i in (0, 2):
             others.append(gains_sum(gains, distances[:-1] if i == 0 else distances[-1:]))
         if i == steps - 1:
             others.append(gains + swap_tensor(gains))
@@ -1375,7 +1384,7 @@
             grad_query, grad_key, grad_value, grad_output = sums_call(
                 ((query_columns, key_columns, key_columns), group), ("turned", late)
             )
-        if i < 2 or i == steps - 1:
+        if i in (0, 2, steps - 1):
             gains = others.pop()
         if i == 0:
             out_done.append(others.pop())

time: 554 us -> 545 us (0.984)
    ppermute x17, waiting for transfers between devices: 42.5 us -> 26.9 us  [swap_tensor(): return lax.ppermute(value, 'tensor', [(0, 1), (1, 0)])]
    ppermute x4, waiting for transfers between devices: 17.9 us -> 26.1 us  [gains_sum(): lax.ppermute(value, 'dp', [(k, k ^ distance) for k in range(dp_size)])]
    unnamed x184 -> x182, local copies, waits for them, and re-layouts: 15 us -> 13.9 us
  transfers between devices with their start and end apart: 86 -> 86, of which waited for: 30 -> 30; matrix products, arithmetic and copies ran while one was open for 4% -> 5% of each run, Pallas kernels for 51% -> 51%
where the time goes in v5:
time: 545 us; the launch traced here: 539 us
  Pallas kernels  285 us (52%)
  waiting for transfers between devices  126 us (23%)
  starting transfers between devices  69 us (13%)
  local copies, waits for them, and re-layouts  26.1 us (5%)
  other arithmetic  17.6 us (3%)
  between operations  15.1 us (3%)
    pallas_call x6, Pallas kernels, feed_call(): pl.pallas_call(functools.partial(feed_kernel, columns // 3, len(specs), l...  51.5 us
    pallas_call x9, Pallas kernels, row_call(): pl.pallas_call(body, grid=(rows // block,), in_specs=specs + loose(ties),...  46.4 us
    pallas_call x5, Pallas kernels, wide_call(): pl.pallas_call(functools.partial(wide_kernel, count, start is not None, p...  43.4 us
    ppermute x31, waiting for transfers between devices, swap_side(): return lax.ppermute(value, 'dp', [(i, i ^ 2) for i in range(self.size)])  38.7 us
    ppermute x31, starting transfers between devices, swap_side(): return lax.ppermute(value, 'dp', [(i, i ^ 2) for i in range(self.size)])  35.9 us
    pallas_call x3, Pallas kernels, grad_call(): pl.pallas_call(functools.partial(grad_kernel, columns // 3 * 2, [len(g) f...  35 us
    ppermute x9, waiting for transfers between devices, shift(): lax.ppermute(value, 'dp', [(i, (i + 4 * places) % self.size) for i in ran...  28.7 us
    ppermute x17, waiting for transfers between devices, swap_tensor(): return lax.ppermute(value, 'tensor', [(0, 1), (1, 0)])  26.9 us
  transfers between devices with their start and end apart: 86, of which 30 were waited for; matrix products, arithmetic and copies ran while one was open for 5% of the time, Pallas kernels for 51%

profile of v5, /device:TPU:0, one launch (start us, length us, event | category | flops | bytes accessed | tf_op | source)
XLA Modules:
  0.0 539.4 jit_solution(14612132303516376070)
XLA Ops:
  9.9 2.9 collective-permute-start.2
  22.8 5.7 %shard_map.237 = (bf16[512,2048]{1,0:T(8,128)(2,1)}, bf16[512,2048]{1,0:T(8,128)(2,1)}, bf16[512,2048]{1,0:T(8,128)(2,1)}) custom-call(bf16[512,2048]{1,0:T(8,128)(2,1)} %refs_0_.1, bf16[512,2048]{1,0:T(8,128)(2,1)} %refs_1_.1, f32[512,1]{1,0:T(8,128)} %copy.53.refs_2_, f32[1,2048]{1,0:T(1,128)} %bitcast.74), custom_call_target="tpu_custom_call" | custom-call | bytes 10496000 | tf_op jit(solution)/shard_map/pallas_call | solution.py:307
  28.5 5.4 collective-permute-done.3.rest_4_
  36.3 8.8 %collective-permute-done.8.rest_7_ = bf16[128,1024]{1,0:T(8,128)(2,1)S(1)} collective-permute-done((bf16[128,1024]{1,0:T(8,128)(2,1)}, bf16[128,1024]{1,0:T(8,128)(2,1)S(1)}, u32[]{:S(2)}, u32[]{:S(2)}) %collective-permute-start.8) | collective-permute-done | bytes 262176 | tf_op jit(solution)/shard_map/ppermute | solution.py:88
  45.7 9.4 %collective-permute-done.9 = bf16[128,1536]{1,0:T(8,128)(2,1)S(1)} collective-permute-done((bf16[128,1536]{1,0:T(8,128)(2,1)S(1)}, bf16[128,1536]{1,0:T(8,128)(2,1)S(1)}, u32[]{:S(2)}, u32[]{:S(2)}) %collective-permute-start.9) | collective-permute-done | bytes 393248 | tf_op jit(solution)/shard_map/ppermute | solution.py:85
  60.0 16.8 %collective-permute-done.14 = bf16[128,1536]{1,0:T(8,128)(2,1)S(1)} collective-permute-done((bf16[128,1536]{1,0:T(8,128)(2,1)S(1)}, bf16[128,1536]{1,0:T(8,128)(2,1)S(1)}, u32[]{:S(2)}, u32[]{:S(2)}) %collective-permute-start.14) | collective-permute-done | bytes 393248 | tf_op jit(solution)/shard_map/ppermute | solution.py:85
  81.3 13.5 %collective-permute-done.19.rest_12_ = bf16[128,1024]{1,0:T(8,128)(2,1)S(1)} collective-permute-done((bf16[128,1024]{1,0:T(8,128)(2,1)S(1)}, bf16[128,1024]{1,0:T(8,128)(2,1)S(1)}, u32[]{:S(2)}, u32[]{:S(2)}) %collective-permute-start.19) | collective-permute-done | bytes 262176 | tf_op jit(solution)/shard_map/ppermute | solution.py:88
  99.3 1.9 collective-permute-start.26
  101.4 11.1 %shard_map.238 = (f32[512,2048]{1,0:T(8,128)}, bf16[2048,2048]{1,0:T(8,128)(2,1)}) custom-call(s32[16]{0:T(128)} %stack.141.order, bf16[512,2048]{1,0:T(8,128)(2,1)} %get-tuple-element.319.left, bf16[128,2048]{1,0:T(8,128)(2,1)} %copy-done.39, bf16[128,2048]{1,0:T(8,128)(2,1)} %collective-permute-done.2.rest_1_, ...), custom_call_target="tpu_custom_call" | custom-call | flops 4294967296 | bytes 20971520 | tf_op jit(solution)/shard_map/pallas_call | solution.py:870
  114.8 7.7 %shard_map.239 = (bf16[256,1024]{1,0:T(8,128)(2,1)}, f32[32,256]{1,0:T(8,128)}) custom-call(f32[512,2048]{1,0:T(8,128)} %get-tuple-element.335.queries.keys.values, f32[512,2048]{1,0:T(8,128)} %get-tuple-element.335.queries.keys.values, f32[512,2048]{1,0:T(8,128)} %get-tuple-element.335.queries.keys.values, f32[1,128]{1,0:T(1,128)} %get-tuple-element.607.query_gain, ...), custom_call_target="tpu_custom_call" | custom-call | flops 1073741824 | bytes 5242880 | tf_op jit(solution)/shard_map/pallas_call | solution.py:660
  126.0 1.7 collective-permute-start.34
  127.7 6.1 %shard_map.240 = (bf16[2048,1024]{1,0:T(8,128)(2,1)}, bf16[128,2048]{1,0:T(8,128)(2,1)}, bf16[128,2048]{1,0:T(8,128)(2,1)}) custom-call(s32[16]{0:T(128)} %stack.140.order, bf16[256,1024]{1,0:T(8,128)(2,1)} %get-tuple-element.342.left.refs_2_, bf16[128,1024]{1,0:T(8,128)(2,1)} %bitcast.66, bf16[128,1024]{1,0:T(8,128)(2,1)} %copy-done.57, ...), custom_call_target="tpu_custom_call" | custom-call | flops 1073741824 | bytes 10485760 | tf_op jit(solution)/shard_map/pallas_call | solution.py:918
  135.0 10.6 %shard_map.241 = (bf16[256,1024]{1,0:T(8,128)(2,1)}, f32[32,256]{1,0:T(8,128)}) custom-call(f32[512,2048]{1,0:T(8,128)} %get-tuple-element.335.queries.keys.values, f32[512,2048]{1,0:T(8,128)} %get-tuple-element.335.queries.keys.values, f32[512,2048]{1,0:T(8,128)} %get-tuple-element.335.queries.keys.values, f32[1,128]{1,0:T(1,128)} %get-tuple-element.607.query_gain, ...), custom_call_target="tpu_custom_call" | custom-call | flops 1073741824 | bytes 5242880 | tf_op jit(solution)/shard_map/pallas_call | solution.py:660
  145.6 2.7 collective-permute-done.35
  152.1 2.8 shard_map.242
  154.9 5.9 %shard_map.243 = (bf16[128,2048]{1,0:T(8,128)(2,1)}, bf16[128,2048]{1,0:T(8,128)(2,1)}) custom-call(bf16[256,1024]{1,0:T(8,128)(2,1)} %get-tuple-element.364.left.refs_3_, bf16[2048,1024]{1,0:T(8,128)(2,1)} %get-tuple-element.365.right.refs_8_, f32[8,128]{1,0:T(8,128)} %broadcast_in_dim.27.rest_0_.outs_0_.refs_6_.refs_9_.refs_16_.refs_17_.refs_4_.rest_2_.refs_2_.refs_8_.refs_12_), custom_call_target="tpu_custom_call" | custom-call | flops 1073741824 | bytes 4194304 | tf_op jit(solution)/shard_map/pallas_call | solution.py:952
  160.8 2.0 collective-permute-done.32.refs_2_
  167.0 2.5 copy.58
  169.6 2.8 shard_map.244
  172.9 6.3 %collective-permute-done.37.refs_2_ = bf16[128,2048]{1,0:T(8,128)(2,1)} collective-permute-done((bf16[128,2048]{1,0:T(8,128)(2,1)}, bf16[128,2048]{1,0:T(8,128)(2,1)}, u32[]{:S(2)}, u32[]{:S(2)}) %collective-permute-start.37) | collective-permute-done | bytes 524320 | tf_op jit(solution)/shard_map/ppermute | solution.py:179
  180.6 2.8 shard_map.245
  183.4 4.1 collective-permute-done.39.refs_2_
  187.5 1.9 collective-permute-done.40.refs_1_.refs_5_
  190.6 2.8 shard_map.246
  196.3 8.3 %shard_map.247.refs_13_.refs_0_ = bf16[512,1536]{1,0:T(8,128)(2,1)} custom-call(bf16[128,2048]{1,0:T(8,128)(2,1)} %get-tuple-element.369.refs_0_, bf16[128,2048]{1,0:T(8,128)(2,1)} %get-tuple-element.379.refs_1_, bf16[128,2048]{1,0:T(8,128)(2,1)} %get-tuple-element.385.refs_2_, bf16[128,2048]{1,0:T(8,128)(2,1)} %get-tuple-element.387.refs_3_, ...), custom_call_target="tpu_custom_call" | custom-call | flops 3221225472 | bytes 12058624 | tf_op jit(solution)/shard_map/pallas_call | solution.py:416
  204.6 8.5 %shard_map.248.refs_1_.refs_13_ = bf16[512,1536]{1,0:T(8,128)(2,1)} custom-call(bf16[128,2048]{1,0:T(8,128)(2,1)} %get-tuple-element.369.refs_0_, bf16[128,2048]{1,0:T(8,128)(2,1)} %get-tuple-element.379.refs_1_, bf16[128,2048]{1,0:T(8,128)(2,1)} %get-tuple-element.385.refs_2_, bf16[128,2048]{1,0:T(8,128)(2,1)} %get-tuple-element.387.refs_3_, ...), custom_call_target="tpu_custom_call" | custom-call | flops 3221225472 | bytes 12058624 | tf_op jit(solution)/shard_map/pallas_call | solution.py:416
  213.2 2.0 collective-permute-done.44
  215.1 2.1 broadcast_select_fusion.1
  218.3 8.8 %shard_map.249.refs_14_.refs_0_ = bf16[512,1536]{1,0:T(8,128)(2,1)} custom-call(bf16[128,2048]{1,0:T(8,128)(2,1)} %copy-done.3, bf16[128,2048]{1,0:T(8,128)(2,1)} %copy-done.4, bf16[128,2048]{1,0:T(8,128)(2,1)} %copy-done.5, bf16[128,2048]{1,0:T(8,128)(2,1)} %copy-done.6, bf16[128,2048]{1,0:T(8,128)(2,1)} %get-tuple-element.403.refs_4_.refs_9_, ...), custom_call_target="tpu_custom_call" | custom-call | flops 3221225472 | bytes 12058624 | tf_op jit(solution)/shard_map/pallas_call | solution.py:416
  227.1 11.6 %shard_map.250.refs_9_ = bf16[2048,1536]{1,0:T(8,128)(2,1)} custom-call(bf16[128,2048]{1,0:T(8,128)(2,1)} %get-tuple-element.369.refs_0_, bf16[128,2048]{1,0:T(8,128)(2,1)} %get-tuple-element.379.refs_1_, bf16[128,2048]{1,0:T(8,128)(2,1)} %get-tuple-element.385.refs_2_, bf16[128,2048]{1,0:T(8,128)(2,1)} %get-tuple-element.387.refs_3_, ...), custom_call_target="tpu_custom_call" | custom-call | flops 6442450944 | bytes 17825792 | tf_op jit(solution)/shard_map/pallas_call | solution.py:501
  238.9 8.8 %shard_map.251.refs_1_.refs_14_ = bf16[512,1536]{1,0:T(8,128)(2,1)} custom-call(bf16[128,2048]{1,0:T(8,128)(2,1)} %copy-done.3, bf16[128,2048]{1,0:T(8,128)(2,1)} %copy-done.4, bf16[128,2048]{1,0:T(8,128)(2,1)} %copy-done.5, bf16[128,2048]{1,0:T(8,128)(2,1)} %copy-done.6, bf16[128,2048]{1,0:T(8,128)(2,1)} %get-tuple-element.403.refs_4_.refs_9_, ...), custom_call_target="tpu_custom_call" | custom-call | flops 3221225472 | bytes 12058624 | tf_op jit(solution)/shard_map/pallas_call | solution.py:416
  247.7 9.1 %shard_map.252.refs_9_.refs_2_ = f32[512,2048]{1,0:T(8,128)} custom-call(bf16[512,1536]{1,0:T(8,128)(2,1)} %shard_map.249.refs_14_.refs_0_, bf16[512,1536]{1,0:T(8,128)(2,1)} %shard_map.251.refs_1_.refs_14_, bf16[2048,1536]{1,0:T(8,128)(2,1)} %all-gather.4.cloned.1.call-done.refs_5_.refs_8_.refs_2_.refs_3_, ...), custom_call_target="tpu_custom_call" | custom-call | flops 4294967296 | bytes 16777216 | tf_op jit(solution)/shard_map/pallas_call | solution.py:456
  256.8 2.6 all-gather.8.cloned.1.call-done.refs_8_.refs_1_.refs_5_
  259.4 8.7 %shard_map.253.refs_0_.refs_14_.refs_2_ = bf16[512,1536]{1,0:T(8,128)(2,1)} custom-call(bf16[128,2048]{1,0:T(8,128)(2,1)} %copy-done.3, bf16[128,2048]{1,0:T(8,128)(2,1)} %copy-done.4, bf16[128,2048]{1,0:T(8,128)(2,1)} %copy-done.5, bf16[128,2048]{1,0:T(8,128)(2,1)} %copy-done.6, bf16[128,2048]{1,0:T(8,128)(2,1)} %get-tuple-element.403.refs_4_.refs_9_, ...), custom_call_target="tpu_custom_call" | custom-call | flops 3221225472 | bytes 12058624 | tf_op jit(solution)/shard_map/pallas_call | solution.py:416
  268.1 6.7 %shard_map.254 = (bf16[128,2048]{1,0:T(8,128)(2,1)}, bf16[128,2048]{1,0:T(8,128)(2,1)}, bf16[128,2048]{1,0:T(8,128)(2,1)}, bf16[128,2048]{1,0:T(8,128)(2,1)}) custom-call(bf16[512,1536]{1,0:T(8,128)(2,1)} %shard_map.253.refs_0_.refs_14_.refs_2_, bf16[2048,1536]{1,0:T(8,128)(2,1)} %all-gather.8.cloned.1.call-done.refs_8_.refs_1_.refs_5_, ...), custom_call_target="tpu_custom_call" | custom-call | flops 2147483648 | bytes 11534336 | tf_op jit(solution)/shard_map/pallas_call | solution.py:456
  276.3 8.5 %shard_map.255.refs_2_.refs_13_ = bf16[512,1536]{1,0:T(8,128)(2,1)} custom-call(bf16[128,2048]{1,0:T(8,128)(2,1)} %get-tuple-element.369.refs_0_, bf16[128,2048]{1,0:T(8,128)(2,1)} %get-tuple-element.379.refs_1_, bf16[128,2048]{1,0:T(8,128)(2,1)} %get-tuple-element.385.refs_2_, bf16[128,2048]{1,0:T(8,128)(2,1)} %get-tuple-element.387.refs_3_, ...), custom_call_target="tpu_custom_call" | custom-call | flops 3221225472 | bytes 12058624 | tf_op jit(solution)/shard_map/pallas_call | solution.py:416
  285.3 11.8 %shard_map.256 = (f32[128,2048]{1,0:T(8,128)}, f32[128,2048]{1,0:T(8,128)}, f32[128,2048]{1,0:T(8,128)}, f32[128,2048]{1,0:T(8,128)}) custom-call(bf16[512,1536]{1,0:T(8,128)(2,1)} %shard_map.247.refs_13_.refs_0_, bf16[512,1536]{1,0:T(8,128)(2,1)} %shard_map.248.refs_1_.refs_13_, bf16[512,1536]{1,0:T(8,128)(2,1)} %shard_map.255.refs_2_.refs_13_, ...), custom_call_target="tpu_custom_call" | custom-call | flops 6442450944 | bytes 22020096 | tf_op jit(solution)/shard_map/pallas_call | solution.py:456
  300.0 11.8 %shard_map.257.refs_15_ = bf16[2048,3072]{1,0:T(8,128)(2,1)} custom-call(bf16[128,2048]{1,0:T(8,128)(2,1)} %get-tuple-element.369.refs_0_, bf16[128,2048]{1,0:T(8,128)(2,1)} %get-tuple-element.379.refs_1_, bf16[128,2048]{1,0:T(8,128)(2,1)} %get-tuple-element.385.refs_2_, bf16[128,2048]{1,0:T(8,128)(2,1)} %get-tuple-element.387.refs_3_, ...), custom_call_target="tpu_custom_call" | custom-call | flops 6442450944 | bytes 17825792 | tf_op jit(solution)/shard_map/pallas_call | solution.py:501
  315.3 11.6 %shard_map.258 = bf16[2048,3072]{1,0:T(8,128)(2,1)} custom-call(bf16[128,2048]{1,0:T(8,128)(2,1)} %get-tuple-element.369.refs_0_, bf16[128,2048]{1,0:T(8,128)(2,1)} %get-tuple-element.379.refs_1_, bf16[128,2048]{1,0:T(8,128)(2,1)} %get-tuple-element.385.refs_2_, bf16[128,2048]{1,0:T(8,128)(2,1)} %get-tuple-element.387.refs_3_, ...), custom_call_target="tpu_custom_call", output_to_operand_aliasing={{}: (15, {})} | custom-call | flops 6442450944 | bytes 17825792 | tf_op jit(solution)/shard_map/pallas_call | solution.py:501
  329.3 7.7 %shard_map.260 = (f32[256,2048]{1,0:T(8,128)}, bf16[256,2048]{1,0:T(8,128)(2,1)}, bf16[256,1024]{1,0:T(8,128)(2,1)}, f32[1,2048]{1,0:T(1,128)}) custom-call(bf16[128,2048]{1,0:T(8,128)(2,1)} %copy-done.9, bf16[128,2048]{1,0:T(8,128)(2,1)} %copy-done.7, bf16[128,2048]{1,0:T(8,128)(2,1)} %copy-done.36, bf16[128,2048]{1,0:T(8,128)(2,1)} %copy-done.38, ...), custom_call_target="tpu_custom_call" | custom-call | bytes 14163968 | tf_op jit(solution)/shard_map/pallas_call | solution.py:307
  337.0 7.9 %shard_map.259 = (bf16[256,2048]{1,0:T(8,128)(2,1)}, bf16[256,2048]{1,0:T(8,128)(2,1)}) custom-call(bf16[512,1536]{1,0:T(8,128)(2,1)} %shard_map.249.refs_14_.refs_0_, bf16[512,1536]{1,0:T(8,128)(2,1)} %shard_map.251.refs_1_.refs_14_, bf16[512,1536]{1,0:T(8,128)(2,1)} %shard_map.253.refs_0_.refs_14_.refs_2_, ...), custom_call_target="tpu_custom_call" | custom-call | flops 3221225472 | bytes 14155776 | tf_op jit(solution)/shard_map/pallas_call | solution.py:456
  348.6 7.9 %shard_map.261 = (f32[256,2048]{1,0:T(8,128)}, f32[256,2048]{1,0:T(8,128)}) custom-call(bf16[512,1536]{1,0:T(8,128)(2,1)} %shard_map.247.refs_13_.refs_0_, bf16[512,1536]{1,0:T(8,128)(2,1)} %shard_map.248.refs_1_.refs_13_, bf16[512,1536]{1,0:T(8,128)(2,1)} %shard_map.255.refs_2_.refs_13_, ...), custom_call_target="tpu_custom_call" | custom-call | flops 3221225472 | bytes 14155776 | tf_op jit(solution)/shard_map/pallas_call | solution.py:456
  358.9 7.6 %shard_map.262 = (f32[256,2048]{1,0:T(8,128)}, bf16[256,2048]{1,0:T(8,128)(2,1)}, bf16[256,1024]{1,0:T(8,128)(2,1)}, f32[1,2048]{1,0:T(1,128)}) custom-call(bf16[128,2048]{1,0:T(8,128)(2,1)} %copy-done.8, bf16[128,2048]{1,0:T(8,128)(2,1)} %copy-done.10, bf16[128,2048]{1,0:T(8,128)(2,1)} %copy-done.34, bf16[128,2048]{1,0:T(8,128)(2,1)} %copy-done.37, ...), custom_call_target="tpu_custom_call" | custom-call | bytes 14163968 | tf_op jit(solution)/shard_map/pallas_call | solution.py:307
  366.5 5.2 shard_map.263
  375.3 16.9 %shard_map.264 = (bf16[512,2048]{1,0:T(8,128)(2,1)}, f32[1,128]{1,0:T(1,128)}, f32[1,128]{1,0:T(1,128)}) custom-call(f32[512,2048]{1,0:T(8,128)} %get-tuple-element.335.queries.keys.values, f32[512,2048]{1,0:T(8,128)} %get-tuple-element.335.queries.keys.values, f32[512,2048]{1,0:T(8,128)} %get-tuple-element.335.queries.keys.values, ...), custom_call_target="tpu_custom_call" | custom-call | flops 3221225472 | bytes 8388608 | tf_op jit(solution)/shard_map/pallas_call | solution.py:678
  394.2 3.4 collective-permute-done.56
  399.0 7.1 %shard_map.265 = (bf16[512,2048]{1,0:T(8,128)(2,1)}, bf16[512,2048]{1,0:T(8,128)(2,1)}) custom-call(s32[6]{0:T(128)} %stack.143.info, bf16[2048,512]{1,0:T(8,128)(2,1)} %bitcast.60, bf16[512,2048]{1,0:T(8,128)(2,1)} %get-tuple-element.472.refs_1_.raw_grad, ...), custom_call_target="tpu_custom_call" | custom-call | flops 2147483648 | bytes 8388608 | tf_op jit(solution)/shard_map/pallas_call | solution.py:794
  410.5 5.5 %shard_map.266 = (bf16[512,1024]{1,0:T(8,128)(2,1)}, bf16[512,1024]{1,0:T(8,128)(2,1)}) custom-call(s32[6]{0:T(128)} %stack.60.info, bf16[256,2048]{1,0:T(8,128)(2,1)} %get-tuple-element.461.refs_0_, bf16[256,2048]{1,0:T(8,128)(2,1)} %get-tuple-element.462.refs_1_, bf16[256,1024]{1,0:T(8,128)(2,1)} %get-tuple-element.342.left.refs_2_, ...), custom_call_target="tpu_custom_call" | custom-call | flops 1073741824 | bytes 5242880 | tf_op jit(solution)/shard_map/pallas_call | solution.py:794
  418.4 8.0 %shard_map.267 = (bf16[128,2048]{1,0:T(8,128)(2,1)}, bf16[128,2048]{1,0:T(8,128)(2,1)}, bf16[128,2048]{1,0:T(8,128)(2,1)}, bf16[128,2048]{1,0:T(8,128)(2,1)}, bf...) custom-call(s32[6]{0:T(128)} %stack.60.info, ...), custom_call_target="tpu_custom_call" | custom-call | flops 2147483648 | bytes 8388608 | tf_op jit(solution)/shard_map/pallas_call | solution.py:794
  427.5 9.9 %shard_map.268 = (bf16[128,2048]{1,0:T(8,128)(2,1)}, bf16[128,2048]{1,0:T(8,128)(2,1)}, bf16[128,2048]{1,0:T(8,128)(2,1)}, bf16[128,2048]{1,0:T(8,128)(2,1)}, f32[1,2048]{1,0:T(1,128)}) custom-call(bf16[512,2048]{1,0:T(8,128)(2,1)} %get-tuple-element.472.refs_1_.raw_grad, bf16[2048,2048]{1,0:T(8,128)(2,1)} %get-tuple-element.497.full, ...), custom_call_target="tpu_custom_call" | custom-call | flops 4294967296 | bytes 16777216 | tf_op jit(solution)/shard_map/pallas_call | solution.py:712
  440.1 4.3 collective-permute-done.66
  446.1 4.2 collective-permute-done.67
  450.3 1.8 collective-permute-done.61.refs_1_
  453.6 2.4 shard_map.269
  463.6 6.1 %shard_map.270 = bf16[512,2048]{1,0:T(8,128)(2,1)} custom-call(f32[128,2048]{1,0:T(8,128)} %get-tuple-element.441.refs_4_.refs_0_, f32[128,2048]{1,0:T(8,128)} %get-tuple-element.442.refs_5_.refs_1_, f32[128,2048]{1,0:T(8,128)} %get-tuple-element.455.refs_4_.refs_2_, f32[128,2048]{1,0:T(8,128)} %get-tuple-element.456.refs_5_.refs_3_, ...), custom_call_target="tpu_custom_call" | custom-call | bytes 10485760 | tf_op jit(solution)/shard_map/pallas_call | solution.py:307
  471.0 8.9 %collective-permute-done.71.refs_6_ = bf16[128,2048]{1,0:T(8,128)(2,1)} collective-permute-done((bf16[128,2048]{1,0:T(8,128)(2,1)S(1)}, bf16[128,2048]{1,0:T(8,128)(2,1)}, u32[]{:S(2)}, u32[]{:S(2)}) %collective-permute-start.71) | collective-permute-done | bytes 524320 | tf_op jit(solution)/shard_map/ppermute | solution.py:179
  481.7 2.7 shard_map.271
  484.5 1.8 collective-permute-start.74
  490.2 16.4 %collective-permute-done.77 = f32[4352]{0:T(1024)S(1)} collective-permute-done((f32[4352]{0:T(1024)S(1)}, f32[4352]{0:T(1024)S(1)}, u32[]{:S(2)}, u32[]{:S(2)}) %collective-permute-start.77) | collective-permute-done | bytes 17440 | tf_op jit(solution)/shard_map/ppermute | solution.py:1307
  508.3 2.8 shard_map.272
  511.1 1.7 collective-permute-start.79
  514.8 8.1 %shard_map.273 = f32[512,2048]{1,0:T(8,128)} custom-call(bf16[128,2048]{1,0:T(8,128)(2,1)} %get-tuple-element.498.refs_0_, bf16[128,2048]{1,0:T(8,128)(2,1)} %get-tuple-element.512.refs_1_, bf16[128,2048]{1,0:T(8,128)(2,1)} %get-tuple-element.513.refs_2_, bf16[128,2048]{1,0:T(8,128)(2,1)} %get-tuple-element.526.refs_3_, bf16[128,2048]{1,0:T(8,128)(2,1)} %copy-done.50, ...), custom_call_target="tpu_custom_call" | custom-call | bytes 14688256 | tf_op jit(solution)/shard_map/pallas_call | solution.py:307
  522.9 4.5 shard_map.274
  529.8 2.9 shard_map.275
  (398 shorter events, 109.8 us)
Async XLA Ops:
  7.2 189.1 %all-gather.4.cloned.1.call-start = ((), (), s32[]{:S(2)}) async-start(), calls=%async_computation.2 | async-start | bytes 7077888 | tf_op jit(solution)/shard_map/all_gather | solution.py:1013
  9.9 23.9 %collective-permute-start.2 = (bf16[128,2048]{1,0:T(8,128)(2,1)S(1)}, bf16[128,2048]{1,0:T(8,128)(2,1)}, u32[]{:S(2)}, u32[]{:S(2)}) collective-permute-start(bf16[128,2048]{1,0:T(8,128)(2,1)S(1)} %pad_maximum_fusion.rest_0_), channel_id=1, source_target_pairs={{0,4},{2,6},{4,0},{6,2},{8,12},{10,14},{12,8},{14,10},{16,20},{18,... | collective-permute-start | bytes 1572872 | tf_op jit(solution)/shard_map/ppermute | solution.py:85
  12.8 21.0 %collective-permute-start.1 = (bf16[128,2048]{1,0:T(8,128)(2,1)S(1)}, bf16[128,2048]{1,0:T(8,128)(2,1)}, u32[]{:S(2)}, u32[]{:S(2)}) collective-permute-start(bf16[128,2048]{1,0:T(8,128)(2,1)S(1)} %pad_maximum_fusion.rest_0_), channel_id=1, source_target_pairs={{0,8},{2,10},{4,12},{6,14},{8,16},{10,18},{12,20},{14,22},{16,24},... | collective-permute-start | bytes 1572872 | tf_op jit(solution)/shard_map/ppermute | solution.py:88
  14.4 19.4 %collective-permute-start = (bf16[128,2048]{1,0:T(8,128)(2,1)S(1)}, bf16[128,2048]{1,0:T(8,128)(2,1)}, u32[]{:S(2)}, u32[]{:S(2)}) collective-permute-start(bf16[128,2048]{1,0:T(8,128)(2,1)S(1)} %pad_maximum_fusion.rest_0_), channel_id=1, source_target_pairs={{0,2},{2,0},{4,6},{6,4},{8,10},{10,8},{12,14},{14,12},{16,18},{18,... | collective-permute-start | bytes 1572872 | tf_op jit(solution)/shard_map/ppermute | solution.py:82
  15.5 18.3 %collective-permute-start.3 = (bf16[128,1024]{1,0:T(8,128)(2,1)S(1)}, bf16[128,1024]{1,0:T(8,128)(2,1)}, u32[]{:S(2)}, u32[]{:S(2)}) collective-permute-start(bf16[128,1024]{1,0:T(8,128)(2,1)S(1)} %bitcast.63), channel_id=1, source_target_pairs={{0,8},{2,10},{4,12},{6,14},{8,16},{10,18},{12,20},{14,22},{16,24},... | collective-permute-start | bytes 786440 | tf_op jit(solution)/shard_map/ppermute | solution.py:88
  33.9 21.2 %collective-permute-start.7 = (bf16[128,2048]{1,0:T(8,128)(2,1)}, bf16[128,2048]{1,0:T(8,128)(2,1)}, u32[]{:S(2)}, u32[]{:S(2)}) collective-permute-start(bf16[128,2048]{1,0:T(8,128)(2,1)} %collective-permute-done.1.rest_4_), channel_id=1, source_target_pairs={{0,4},{2,6},{4,0},{6,2},{8,12},{10,14},{12,8},{14,10},{16,20},{18,... | collective-permute-start | bytes 1572872 | tf_op jit(solution)/shard_map/ppermute | solution.py:85
  34.5 20.6 %collective-permute-start.6 = (bf16[128,2048]{1,0:T(8,128)(2,1)}, bf16[128,2048]{1,0:T(8,128)(2,1)}, u32[]{:S(2)}, u32[]{:S(2)}) collective-permute-start(bf16[128,2048]{1,0:T(8,128)(2,1)} %collective-permute-done.1.rest_4_), channel_id=1, source_target_pairs={{0,8},{2,10},{4,12},{6,14},{8,16},{10,18},{12,20},{14,22},{16,24},... | collective-permute-start | bytes 1572872 | tf_op jit(solution)/shard_map/ppermute | solution.py:88
  35.8 19.4 %collective-permute-start.5 = (bf16[128,2048]{1,0:T(8,128)(2,1)}, bf16[128,2048]{1,0:T(8,128)(2,1)}, u32[]{:S(2)}, u32[]{:S(2)}) collective-permute-start(bf16[128,2048]{1,0:T(8,128)(2,1)} %collective-permute-done.1.rest_4_), channel_id=1, source_target_pairs={{0,2},{2,0},{4,6},{6,4},{8,10},{10,8},{12,14},{14,12},{16,18},{18,... | collective-permute-start | bytes 1572872 | tf_op jit(solution)/shard_map/ppermute | solution.py:82
  35.8 19.4 %collective-permute-start.4 = (bf16[128,2048]{1,0:T(8,128)(2,1)}, bf16[128,2048]{1,0:T(8,128)(2,1)}, u32[]{:S(2)}, u32[]{:S(2)}) collective-permute-start(bf16[128,2048]{1,0:T(8,128)(2,1)} %collective-permute-done.2.rest_1_), channel_id=1, source_target_pairs={{0,2},{2,0},{4,6},{6,4},{8,10},{10,8},{12,14},{14,12},{16,18},{18,... | collective-permute-start | bytes 1572872 | tf_op jit(solution)/shard_map/ppermute | solution.py:82
  56.3 148.4 %all-gather.6.cloned.1.call-start = ((), (), s32[]{:S(2)}) async-start(), calls=%async_computation.3 | async-start | bytes 7077888 | tf_op jit(solution)/shard_map/all_gather | solution.py:1013
  56.3 20.4 %collective-permute-start.13 = (bf16[128,2048]{1,0:T(8,128)(2,1)}, bf16[128,2048]{1,0:T(8,128)(2,1)}, u32[]{:S(2)}, u32[]{:S(2)}) collective-permute-start(bf16[128,2048]{1,0:T(8,128)(2,1)} %collective-permute-done.6.rest_8_), channel_id=1, source_target_pairs={{0,4},{2,6},{4,0},{6,2},{8,12},{10,14},{12,8},{14,10},{16,20},{18,... | collective-permute-start | bytes 1572872 | tf_op jit(solution)/shard_map/ppermute | solution.py:85
  57.2 19.6 %collective-permute-start.12 = (bf16[128,2048]{1,0:T(8,128)(2,1)}, bf16[128,2048]{1,0:T(8,128)(2,1)}, u32[]{:S(2)}, u32[]{:S(2)}) collective-permute-start(bf16[128,2048]{1,0:T(8,128)(2,1)} %collective-permute-done.6.rest_8_), channel_id=1, source_target_pairs={{0,8},{2,10},{4,12},{6,14},{8,16},{10,18},{12,20},{14,22},{16,24},... | collective-permute-start | bytes 1572872 | tf_op jit(solution)/shard_map/ppermute | solution.py:88
  57.9 18.9 %collective-permute-start.11 = (bf16[128,2048]{1,0:T(8,128)(2,1)}, bf16[128,2048]{1,0:T(8,128)(2,1)}, u32[]{:S(2)}, u32[]{:S(2)}) collective-permute-start(bf16[128,2048]{1,0:T(8,128)(2,1)} %collective-permute-done.6.rest_8_), channel_id=1, source_target_pairs={{0,2},{2,0},{4,6},{6,4},{8,10},{10,8},{12,14},{14,12},{16,18},{18,... | collective-permute-start | bytes 1572872 | tf_op jit(solution)/shard_map/ppermute | solution.py:82
  57.9 18.9 %collective-permute-start.10 = (bf16[128,2048]{1,0:T(8,128)(2,1)}, bf16[128,2048]{1,0:T(8,128)(2,1)}, u32[]{:S(2)}, u32[]{:S(2)}) collective-permute-start(bf16[128,2048]{1,0:T(8,128)(2,1)} %collective-permute-done.7.rest_5_), channel_id=1, source_target_pairs={{0,2},{2,0},{4,6},{6,4},{8,10},{10,8},{12,14},{14,12},{16,18},{18,... | collective-permute-start | bytes 1572872 | tf_op jit(solution)/shard_map/ppermute | solution.py:82
  58.4 18.3 %collective-permute-start.14 = (bf16[128,1536]{1,0:T(8,128)(2,1)S(1)}, bf16[128,1536]{1,0:T(8,128)(2,1)S(1)}, u32[]{:S(2)}, u32[]{:S(2)}) collective-permute-start(bf16[128,1536]{1,0:T(8,128)(2,1)S(1)} %pad_maximum_fusion.2), channel_id=1, source_target_pairs={{0,4},{2,6},{4,0},{6,2},{8,12},{10,14},{12,8},{14,10},{16,20},{18,... | collective-permute-start | bytes 1179656 | tf_op jit(solution)/shard_map/ppermute | solution.py:85
  77.8 181.6 %all-gather.8.cloned.1.call-start = ((), (), s32[]{:S(2)}) async-start(), calls=%async_computation.4 | async-start | bytes 7077888 | tf_op jit(solution)/shard_map/all_gather | solution.py:1013
  77.9 16.8 %collective-permute-start.19 = (bf16[128,1024]{1,0:T(8,128)(2,1)S(1)}, bf16[128,1024]{1,0:T(8,128)(2,1)S(1)}, u32[]{:S(2)}, u32[]{:S(2)}) collective-permute-start(bf16[128,1024]{1,0:T(8,128)(2,1)S(1)} %collective-permute-done.8.rest_7_), channel_id=1, source_target_pairs={{0,8},{2,10},{4,12},{6,14},{8,16},{10,18},{12,20},{14,22},{16,24},... | collective-permute-start | bytes 786440 | tf_op jit(solution)/shard_map/ppermute | solution.py:88
  78.7 17.6 %collective-permute-start.17 = (bf16[128,2048]{1,0:T(8,128)(2,1)}, bf16[128,2048]{1,0:T(8,128)(2,1)S(1)}, u32[]{:S(2)}, u32[]{:S(2)}) collective-permute-start(bf16[128,2048]{1,0:T(8,128)(2,1)} %collective-permute-done.12.rest_12_), channel_id=1, source_target_pairs={{0,4},{2,6},{4,0},{6,2},{8,12},{10,14},{12,8},{14,10},{16,20},{18,... | collective-permute-start | bytes 1572872 | tf_op jit(solution)/shard_map/ppermute | solution.py:85
  79.4 16.9 %collective-permute-start.16 = (bf16[128,2048]{1,0:T(8,128)(2,1)}, bf16[128,2048]{1,0:T(8,128)(2,1)S(1)}, u32[]{:S(2)}, u32[]{:S(2)}) collective-permute-start(bf16[128,2048]{1,0:T(8,128)(2,1)} %collective-permute-done.12.rest_12_), channel_id=1, source_target_pairs={{0,2},{2,0},{4,6},{6,4},{8,10},{10,8},{12,14},{14,12},{16,18},{18,... | collective-permute-start | bytes 1572872 | tf_op jit(solution)/shard_map/ppermute | solution.py:82
  79.4 16.9 %collective-permute-start.15 = (bf16[128,2048]{1,0:T(8,128)(2,1)}, bf16[128,2048]{1,0:T(8,128)(2,1)}, u32[]{:S(2)}, u32[]{:S(2)}) collective-permute-start(bf16[128,2048]{1,0:T(8,128)(2,1)} %collective-permute-done.13.rest_9_), channel_id=1, source_target_pairs={{0,2},{2,0},{4,6},{6,4},{8,10},{10,8},{12,14},{14,12},{16,18},{18,... | collective-permute-start | bytes 1572872 | tf_op jit(solution)/shard_map/ppermute | solution.py:82
  79.9 15.2 %collective-permute-start.20 = (bf16[128,1024]{1,0:T(8,128)(2,1)S(1)}, bf16[128,1024]{1,0:T(8,128)(2,1)S(1)}, u32[]{:S(2)}, u32[]{:S(2)}) collective-permute-start(bf16[128,1024]{1,0:T(8,128)(2,1)S(1)} %bitcast.64), channel_id=1, source_target_pairs={{0,4},{2,6},{4,0},{6,2},{8,12},{10,14},{12,8},{14,10},{16,20},{18,... | collective-permute-start | bytes 786440 | tf_op jit(solution)/shard_map/ppermute | solution.py:85
  98.7 13.8 %collective-permute-start.21 = (bf16[128,1024]{1,0:T(8,128)(2,1)S(1)}, bf16[128,1024]{1,0:T(8,128)(2,1)S(1)}, u32[]{:S(2)}, u32[]{:S(2)}) collective-permute-start(bf16[128,1024]{1,0:T(8,128)(2,1)S(1)} %collective-permute-done.20.rest_1_), channel_id=1, source_target_pairs={{0,2},{2,0},{4,6},{6,4},{8,10},{10,8},{12,14},{14,12},{16,18},{18,... | collective-permute-start | bytes 786440 | tf_op jit(solution)/shard_map/ppermute | solution.py:82
  99.1 13.4 %collective-permute-start.25 = (bf16[128,1024]{1,0:T(8,128)(2,1)}, bf16[128,1024]{1,0:T(8,128)(2,1)S(1)}, u32[]{:S(2)}, u32[]{:S(2)}) collective-permute-start(bf16[128,1024]{1,0:T(8,128)(2,1)} %collective-permute-done.3.rest_4_), channel_id=1, source_target_pairs={{0,4},{2,6},{4,0},{6,2},{8,12},{10,14},{12,8},{14,10},{16,20},{18,... | collective-permute-start | bytes 786440 | tf_op jit(solution)/shard_map/ppermute | solution.py:85
  99.3 14.0 %collective-permute-start.26 = (bf16[128,1024]{1,0:T(8,128)(2,1)S(1)}, bf16[128,1024]{1,0:T(8,128)(2,1)S(1)}, u32[]{:S(2)}, u32[]{:S(2)}) collective-permute-start(bf16[128,1024]{1,0:T(8,128)(2,1)S(1)} %collective-permute-done.8.rest_7_), channel_id=1, source_target_pairs={{0,4},{2,6},{4,0},{6,2},{8,12},{10,14},{12,8},{14,10},{16,20},{18,... | collective-permute-start | bytes 786440 | tf_op jit(solution)/shard_map/ppermute | solution.py:85
  126.0 22.3 %collective-permute-start.34 = (bf16[128,2048]{1,0:T(8,128)(2,1)S(1)}, bf16[128,2048]{1,0:T(8,128)(2,1)}, u32[]{:S(2)}, u32[]{:S(2)}) collective-permute-start(bf16[128,2048]{1,0:T(8,128)(2,1)S(1)} %get-tuple-element.355), channel_id=1, source_target_pairs={{0,4},{2,6},{4,0},{6,2},{8,12},{10,14},{12,8},{14,10},{16,20},{18,... | collective-permute-start | bytes 1572872 | tf_op jit(solution)/shard_map/ppermute | solution.py:85
  133.8 14.4 %collective-permute-start.33 = (bf16[128,2048]{1,0:T(8,128)(2,1)}, bf16[128,2048]{1,0:T(8,128)(2,1)S(1)}, u32[]{:S(2)}, u32[]{:S(2)}) collective-permute-start(bf16[128,2048]{1,0:T(8,128)(2,1)} %get-tuple-element.353.refs_1_), channel_id=1, source_target_pairs={{0,1},{1,0},{2,3},{3,2},{4,5},{5,4},{6,7},{7,6},{8,9},{9,8},{10,11... | collective-permute-start | bytes 1572872 | tf_op jit(solution)/shard_map/ppermute | solution.py:179
  134.3 14.0 %collective-permute-start.35 = (bf16[128,1536]{1,0:T(8,128)(2,1)S(1)}, bf16[128,1536]{1,0:T(8,128)(2,1)S(1)}, u32[]{:S(2)}, u32[]{:S(2)}) collective-permute-start(bf16[128,1536]{1,0:T(8,128)(2,1)S(1)} %pad_maximum_fusion.3), channel_id=1, source_target_pairs={{0,4},{2,6},{4,0},{6,2},{8,12},{10,14},{12,8},{14,10},{16,20},{18,... | collective-permute-start | bytes 1179656 | tf_op jit(solution)/shard_map/ppermute | solution.py:85
  149.3 249.6 %reduce-scatter.3.cloned.1.call-start = ((), (), s32[]{:S(2)}) async-start(), calls=%async_computation.5 | async-start | bytes 7077888 | tf_op jit(solution)/shard_map/reduce_scatter | solution.py:1236
  164.0 15.2 %collective-permute-start.37 = (bf16[128,2048]{1,0:T(8,128)(2,1)}, bf16[128,2048]{1,0:T(8,128)(2,1)}, u32[]{:S(2)}, u32[]{:S(2)}) collective-permute-start(bf16[128,2048]{1,0:T(8,128)(2,1)} %get-tuple-element.368.refs_1_), channel_id=1, source_target_pairs={{0,1},{1,0},{2,3},{3,2},{4,5},{5,4},{6,7},{7,6},{8,9},{9,8},{10,11... | collective-permute-start | bytes 1572872 | tf_op jit(solution)/shard_map/ppermute | solution.py:179
  165.3 13.9 %collective-permute-start.38 = (bf16[128,2048]{1,0:T(8,128)(2,1)S(1)}, bf16[128,2048]{1,0:T(8,128)(2,1)S(1)}, u32[]{:S(2)}, u32[]{:S(2)}) collective-permute-start(bf16[128,2048]{1,0:T(8,128)(2,1)S(1)} %copy-done.2), channel_id=1, source_target_pairs={{0,4},{2,6},{4,0},{6,2},{8,12},{10,14},{12,8},{14,10},{16,20},{18,... | collective-permute-start | bytes 1572872 | tf_op jit(solution)/shard_map/ppermute | solution.py:85
  172.4 15.1 %collective-permute-start.39 = (bf16[128,2048]{1,0:T(8,128)(2,1)S(1)}, bf16[128,2048]{1,0:T(8,128)(2,1)S(1)}, u32[]{:S(2)}, u32[]{:S(2)}) collective-permute-start(bf16[128,2048]{1,0:T(8,128)(2,1)S(1)} %copy-done.41), channel_id=1, source_target_pairs={{0,1},{1,0},{2,3},{3,2},{4,5},{5,4},{6,7},{7,6},{8,9},{9,8},{10,11... | collective-permute-start | bytes 1572872 | tf_op jit(solution)/shard_map/ppermute | solution.py:179
  189.4 15.2 %collective-permute-start.41 = (bf16[128,2048]{1,0:T(8,128)(2,1)}, bf16[128,2048]{1,0:T(8,128)(2,1)S(1)}, u32[]{:S(2)}, u32[]{:S(2)}) collective-permute-start(bf16[128,2048]{1,0:T(8,128)(2,1)} %get-tuple-element.385.refs_2_), channel_id=1, source_target_pairs={{0,4},{2,6},{4,0},{6,2},{8,12},{10,14},{12,8},{14,10},{16,20},{18,... | collective-permute-start | bytes 1572872 | tf_op jit(solution)/shard_map/ppermute | solution.py:85
  193.4 19.7 %collective-permute-start.42 = (bf16[128,2048]{1,0:T(8,128)(2,1)}, bf16[128,2048]{1,0:T(8,128)(2,1)S(1)}, u32[]{:S(2)}, u32[]{:S(2)}) collective-permute-start(bf16[128,2048]{1,0:T(8,128)(2,1)} %get-tuple-element.387.refs_3_), channel_id=1, source_target_pairs={{0,4},{2,6},{4,0},{6,2},{8,12},{10,14},{12,8},{14,10},{16,20},{18,... | collective-permute-start | bytes 1572872 | tf_op jit(solution)/shard_map/ppermute | solution.py:85
  194.2 18.9 %collective-permute-start.43 = (bf16[128,2048]{1,0:T(8,128)(2,1)}, bf16[128,2048]{1,0:T(8,128)(2,1)S(1)}, u32[]{:S(2)}, u32[]{:S(2)}) collective-permute-start(bf16[128,2048]{1,0:T(8,128)(2,1)} %collective-permute-done.34), channel_id=1, source_target_pairs={{0,1},{1,0},{2,3},{3,2},{4,5},{5,4},{6,7},{7,6},{8,9},{9,8},{10,11... | collective-permute-start | bytes 1572872 | tf_op jit(solution)/shard_map/ppermute | solution.py:179
  195.5 19.6 %collective-permute-start.44 = (bf16[128,2048]{1,0:T(8,128)(2,1)S(1)}, bf16[128,2048]{1,0:T(8,128)(2,1)S(1)}, u32[]{:S(2)}, u32[]{:S(2)}) collective-permute-start(bf16[128,2048]{1,0:T(8,128)(2,1)S(1)} %copy-done.32), channel_id=1, source_target_pairs={{0,1},{1,0},{2,3},{3,2},{4,5},{5,4},{6,7},{7,6},{8,9},{9,8},{10,11... | collective-permute-start | bytes 1572872 | tf_op jit(solution)/shard_map/ppermute | solution.py:179
  238.7 222.1 %reduce-scatter.5.cloned.1.call-start = ((), (), s32[]{:S(2)}) async-start(), calls=%async_computation.6 | async-start | bytes 14155776 | tf_op jit(solution)/shard_map/reduce_scatter | solution.py:1236
  274.8 22.3 %collective-permute-start.45 = (bf16[128,2048]{1,0:T(8,128)(2,1)}, bf16[128,2048]{1,0:T(8,128)(2,1)S(1)}, u32[]{:S(2)}, u32[]{:S(2)}) collective-permute-start(bf16[128,2048]{1,0:T(8,128)(2,1)} %get-tuple-element.410.refs_6_), channel_id=1, source_target_pairs={{0,4},{2,6},{4,0},{6,2},{8,12},{10,14},{12,8},{14,10},{16,20},{18,... | collective-permute-start | bytes 1572872 | tf_op jit(solution)/shard_map/ppermute | solution.py:85
  284.8 27.0 %collective-permute-start.47 = (bf16[128,2048]{1,0:T(8,128)(2,1)S(1)}, bf16[128,2048]{1,0:T(8,128)(2,1)S(1)}, u32[]{:S(2)}, u32[]{:S(2)}) collective-permute-start(bf16[128,2048]{1,0:T(8,128)(2,1)S(1)} %copy-done.89), channel_id=1, source_target_pairs={{0,4},{2,6},{4,0},{6,2},{8,12},{10,14},{12,8},{14,10},{16,20},{18,... | collective-permute-start | bytes 1572872 | tf_op jit(solution)/shard_map/ppermute | solution.py:85
  298.5 13.6 %collective-permute-start.46 = (bf16[128,2048]{1,0:T(8,128)(2,1)S(1)}, bf16[128,2048]{1,0:T(8,128)(2,1)S(1)}, u32[]{:S(2)}, u32[]{:S(2)}) collective-permute-start(bf16[128,2048]{1,0:T(8,128)(2,1)S(1)} %add_convert_fusion.5.refs_15_.refs_0_), channel_id=1, source_target_pairs={{0,1},{1,0},{2,3},{3,2},{4,5},{5,4},{6,7},{7,6},{8,9},{9,8},{10,11... | collective-permute-start | bytes 1572872 | tf_op jit(solution)/shard_map/ppermute | solution.py:179
  312.1 14.8 %collective-permute-start.49 = (bf16[128,2048]{1,0:T(8,128)(2,1)}, bf16[128,2048]{1,0:T(8,128)(2,1)S(1)}, u32[]{:S(2)}, u32[]{:S(2)}) collective-permute-start(bf16[128,2048]{1,0:T(8,128)(2,1)} %get-tuple-element.431), channel_id=1, source_target_pairs={{0,4},{2,6},{4,0},{6,2},{8,12},{10,14},{12,8},{14,10},{16,20},{18,... | collective-permute-start | bytes 1572872 | tf_op jit(solution)/shard_map/ppermute | solution.py:85
  327.7 17.2 %collective-permute-start.51 = (bf16[128,2048]{1,0:T(8,128)(2,1)}, bf16[128,2048]{1,0:T(8,128)(2,1)S(1)}, u32[]{:S(2)}, u32[]{:S(2)}) collective-permute-start(bf16[128,2048]{1,0:T(8,128)(2,1)} %get-tuple-element.436), channel_id=1, source_target_pairs={{0,4},{2,6},{4,0},{6,2},{8,12},{10,14},{12,8},{14,10},{16,20},{18,... | collective-permute-start | bytes 1572872 | tf_op jit(solution)/shard_map/ppermute | solution.py:85
  328.5 16.4 %collective-permute-start.50 = (bf16[128,2048]{1,0:T(8,128)(2,1)S(1)}, bf16[128,2048]{1,0:T(8,128)(2,1)S(1)}, u32[]{:S(2)}, u32[]{:S(2)}) collective-permute-start(bf16[128,2048]{1,0:T(8,128)(2,1)S(1)} %add_convert_fusion.3.refs_6_.refs_0_), channel_id=1, source_target_pairs={{0,1},{1,0},{2,3},{3,2},{4,5},{5,4},{6,7},{7,6},{8,9},{9,8},{10,11... | collective-permute-start | bytes 1572872 | tf_op jit(solution)/shard_map/ppermute | solution.py:179
  344.9 27.3 %collective-permute-start.53 = (bf16[256,2048]{1,0:T(8,128)(2,1)}, bf16[256,2048]{1,0:T(8,128)(2,1)S(1)}, u32[]{:S(2)}, u32[]{:S(2)}) collective-permute-start(bf16[256,2048]{1,0:T(8,128)(2,1)} %get-tuple-element.459), channel_id=1, source_target_pairs={{0,4},{2,6},{4,0},{6,2},{8,12},{10,14},{12,8},{14,10},{16,20},{18,... | collective-permute-start | bytes 3145736 | tf_op jit(solution)/shard_map/ppermute | solution.py:85
  371.7 20.5 %collective-permute-start.55 = (bf16[512,1024]{1,0:T(8,128)(2,1)}, bf16[512,1024]{1,0:T(8,128)(2,1)S(1)}, u32[]{:S(2)}, u32[]{:S(2)}) collective-permute-start(bf16[512,1024]{1,0:T(8,128)(2,1)} %get-tuple-element.467), channel_id=1, source_target_pairs={{0,2},{2,0},{4,6},{6,4},{8,10},{10,8},{12,14},{14,12},{16,18},{18,... | collective-permute-start | bytes 3145736 | tf_op jit(solution)/shard_map/ppermute | solution.py:82
  371.7 21.5 %collective-permute-start.54 = (bf16[512,1024]{1,0:T(8,128)(2,1)}, bf16[512,1024]{1,0:T(8,128)(2,1)S(1)}, u32[]{:S(2)}, u32[]{:S(2)}) collective-permute-start(bf16[512,1024]{1,0:T(8,128)(2,1)} %get-tuple-element.463.rest_3_), channel_id=1, source_target_pairs={{0,2},{2,0},{4,6},{6,4},{8,10},{10,8},{12,14},{14,12},{16,18},{18,... | collective-permute-start | bytes 3145736 | tf_op jit(solution)/shard_map/ppermute | solution.py:82
  372.2 25.4 %collective-permute-start.56 = (bf16[256,2048]{1,0:T(8,128)(2,1)}, bf16[256,2048]{1,0:T(8,128)(2,1)S(1)}, u32[]{:S(2)}, u32[]{:S(2)}) collective-permute-start(bf16[256,2048]{1,0:T(8,128)(2,1)} %get-tuple-element.469), channel_id=1, source_target_pairs={{0,4},{2,6},{4,0},{6,2},{8,12},{10,14},{12,8},{14,10},{16,20},{18,... | collective-permute-start | bytes 3145736 | tf_op jit(solution)/shard_map/ppermute | solution.py:85
  373.9 25.0 %collective-permute-start.57 = (bf16[256,2048]{1,0:T(8,128)(2,1)S(1)}, bf16[256,2048]{1,0:T(8,128)(2,1)}, u32[]{:S(2)}, u32[]{:S(2)}) collective-permute-start(bf16[256,2048]{1,0:T(8,128)(2,1)S(1)} %add_convert_fusion.1.refs_4_), channel_id=1, source_target_pairs={{0,1},{1,0},{2,3},{3,2},{4,5},{5,4},{6,7},{7,6},{8,9},{9,8},{10,11... | collective-permute-start | bytes 3145736 | tf_op jit(solution)/shard_map/ppermute | solution.py:179
  409.8 40.5 %collective-permute-start.64 = (bf16[256,2048]{1,0:T(8,128)(2,1)S(1)}, bf16[256,2048]{1,0:T(8,128)(2,1)S(1)}, u32[]{:S(2)}, u32[]{:S(2)}) collective-permute-start(bf16[256,2048]{1,0:T(8,128)(2,1)S(1)} %add_convert_fusion.refs_5_), channel_id=1, source_target_pairs={{0,1},{1,0},{2,3},{3,2},{4,5},{5,4},{6,7},{7,6},{8,9},{9,8},{10,11... | collective-permute-start | bytes 3145736 | tf_op jit(solution)/shard_map/ppermute | solution.py:179
  415.9 34.3 %collective-permute-start.62 = (bf16[512,1024]{1,0:T(8,128)(2,1)}, bf16[512,1024]{1,0:T(8,128)(2,1)S(1)}, u32[]{:S(2)}, u32[]{:S(2)}) collective-permute-start(bf16[512,1024]{1,0:T(8,128)(2,1)} %get-tuple-element.496), channel_id=1, source_target_pairs={{0,4},{2,6},{4,0},{6,2},{8,12},{10,14},{12,8},{14,10},{16,20},{18,... | collective-permute-start | bytes 3145736 | tf_op jit(solution)/shard_map/ppermute | solution.py:85
  426.4 25.6 %collective-permute-start.61 = (bf16[128,2048]{1,0:T(8,128)(2,1)}, bf16[128,2048]{1,0:T(8,128)(2,1)S(1)}, u32[]{:S(2)}, u32[]{:S(2)}) collective-permute-start(bf16[128,2048]{1,0:T(8,128)(2,1)} %get-tuple-element.495), channel_id=1, source_target_pairs={{0,4},{2,6},{4,0},{6,2},{8,12},{10,14},{12,8},{14,10},{16,20},{18,... | collective-permute-start | bytes 1572872 | tf_op jit(solution)/shard_map/ppermute | solution.py:85
  437.4 14.7 %collective-permute-start.63 = (bf16[128,2048]{1,0:T(8,128)(2,1)}, bf16[128,2048]{1,0:T(8,128)(2,1)S(1)}, u32[]{:S(2)}, u32[]{:S(2)}) collective-permute-start(bf16[128,2048]{1,0:T(8,128)(2,1)} %get-tuple-element.498.refs_0_), channel_id=1, source_target_pairs={{0,1},{1,0},{2,3},{3,2},{4,5},{5,4},{6,7},{7,6},{8,9},{9,8},{10,11... | collective-permute-start | bytes 1572872 | tf_op jit(solution)/shard_map/ppermute | solution.py:179
  456.0 23.9 %collective-permute-start.69 = (bf16[128,3072]{1,0:T(8,128)(2,1)}, bf16[128,3072]{1,0:T(8,128)(2,1)S(1)}, u32[]{:S(2)}, u32[]{:S(2)}) collective-permute-start(bf16[128,3072]{1,0:T(8,128)(2,1)} %shard_map.269), channel_id=1, source_target_pairs={{0,8},{2,10},{4,12},{6,14},{8,16},{10,18},{12,20},{14,22},{16,24},... | collective-permute-start | bytes 2359304 | tf_op jit(solution)/shard_map/ppermute | solution.py:88
  456.0 15.0 %collective-permute-start.70 = (bf16[128,2048]{1,0:T(8,128)(2,1)S(1)}, bf16[128,2048]{1,0:T(8,128)(2,1)}, u32[]{:S(2)}, u32[]{:S(2)}) collective-permute-start(bf16[128,2048]{1,0:T(8,128)(2,1)S(1)} %copy-done.47), channel_id=1, source_target_pairs={{0,1},{1,0},{2,3},{3,2},{4,5},{5,4},{6,7},{7,6},{8,9},{9,8},{10,11... | collective-permute-start | bytes 1572872 | tf_op jit(solution)/shard_map/ppermute | solution.py:179
  457.3 22.6 %collective-permute-start.71 = (bf16[128,2048]{1,0:T(8,128)(2,1)S(1)}, bf16[128,2048]{1,0:T(8,128)(2,1)}, u32[]{:S(2)}, u32[]{:S(2)}) collective-permute-start(bf16[128,2048]{1,0:T(8,128)(2,1)S(1)} %copy-done.48), channel_id=1, source_target_pairs={{0,1},{1,0},{2,3},{3,2},{4,5},{5,4},{6,7},{7,6},{8,9},{9,8},{10,11... | collective-permute-start | bytes 1572872 | tf_op jit(solution)/shard_map/ppermute | solution.py:179
  458.1 21.9 %collective-permute-start.68 = (bf16[128,2048]{1,0:T(8,128)(2,1)}, bf16[128,2048]{1,0:T(8,128)(2,1)S(1)}, u32[]{:S(2)}, u32[]{:S(2)}) collective-permute-start(bf16[128,2048]{1,0:T(8,128)(2,1)} %get-tuple-element.507), channel_id=1, source_target_pairs={{0,4},{2,6},{4,0},{6,2},{8,12},{10,14},{12,8},{14,10},{16,20},{18,... | collective-permute-start | bytes 1572872 | tf_op jit(solution)/shard_map/ppermute | solution.py:85
  461.9 18.0 %collective-permute-start.72 = (bf16[128,1536]{1,0:T(8,128)(2,1)S(1)}, bf16[128,1536]{1,0:T(8,128)(2,1)S(1)}, u32[]{:S(2)}, u32[]{:S(2)}) collective-permute-start(bf16[128,1536]{1,0:T(8,128)(2,1)S(1)} %get-tuple-element.515), channel_id=1, source_target_pairs={{0,4},{2,6},{4,0},{6,2},{8,12},{10,14},{12,8},{14,10},{16,20},{18,... | collective-permute-start | bytes 1179656 | tf_op jit(solution)/shard_map/ppermute | solution.py:85
  484.5 22.2 %collective-permute-start.74 = (bf16[128,3072]{1,0:T(8,128)(2,1)}, bf16[128,3072]{1,0:T(8,128)(2,1)S(1)}, u32[]{:S(2)}, u32[]{:S(2)}) collective-permute-start(bf16[128,3072]{1,0:T(8,128)(2,1)} %shard_map.271), channel_id=1, source_target_pairs={{0,8},{2,10},{4,12},{6,14},{8,16},{10,18},{12,20},{14,22},{16,24},... | collective-permute-start | bytes 2359304 | tf_op jit(solution)/shard_map/ppermute | solution.py:88
  486.2 20.3 %collective-permute-start.75 = (bf16[128,2048]{1,0:T(8,128)(2,1)S(1)}, bf16[128,2048]{1,0:T(8,128)(2,1)S(1)}, u32[]{:S(2)}, u32[]{:S(2)}) collective-permute-start(bf16[128,2048]{1,0:T(8,128)(2,1)S(1)} %copy-done.49), channel_id=1, source_target_pairs={{0,1},{1,0},{2,3},{3,2},{4,5},{5,4},{6,7},{7,6},{8,9},{9,8},{10,11... | collective-permute-start | bytes 1572872 | tf_op jit(solution)/shard_map/ppermute | solution.py:179
  487.0 19.7 %collective-permute-start.73 = (bf16[128,2048]{1,0:T(8,128)(2,1)S(1)}, bf16[128,2048]{1,0:T(8,128)(2,1)S(1)}, u32[]{:S(2)}, u32[]{:S(2)}) collective-permute-start(bf16[128,2048]{1,0:T(8,128)(2,1)S(1)} %copy-done.88), channel_id=1, source_target_pairs={{0,4},{2,6},{4,0},{6,2},{8,12},{10,14},{12,8},{14,10},{16,20},{18,... | collective-permute-start | bytes 1572872 | tf_op jit(solution)/shard_map/ppermute | solution.py:85
  488.1 18.5 %collective-permute-start.76 = (bf16[128,1536]{1,0:T(8,128)(2,1)S(1)}, bf16[128,1536]{1,0:T(8,128)(2,1)S(1)}, u32[]{:S(2)}, u32[]{:S(2)}) collective-permute-start(bf16[128,1536]{1,0:T(8,128)(2,1)S(1)} %get-tuple-element.527), channel_id=1, source_target_pairs={{0,4},{2,6},{4,0},{6,2},{8,12},{10,14},{12,8},{14,10},{16,20},{18,... | collective-permute-start | bytes 1179656 | tf_op jit(solution)/shard_map/ppermute | solution.py:85
  489.0 17.6 %collective-permute-start.77 = (f32[4352]{0:T(1024)S(1)}, f32[4352]{0:T(1024)S(1)}, u32[]{:S(2)}, u32[]{:S(2)}) collective-permute-start(f32[4352]{0:T(1024)S(1)} %add.328), channel_id=1, source_target_pairs={{0,4},{2,6},{4,0},{6,2},{8,12},{10,14},{12,8},{14,10},{16,20},{18,... | collective-permute-start | bytes 52232 | tf_op jit(solution)/shard_map/ppermute | solution.py:1307
  511.1 17.5 %collective-permute-start.79 = (bf16[128,3072]{1,0:T(8,128)(2,1)}, bf16[128,3072]{1,0:T(8,128)(2,1)S(1)}, u32[]{:S(2)}, u32[]{:S(2)}) collective-permute-start(bf16[128,3072]{1,0:T(8,128)(2,1)} %shard_map.272), channel_id=1, source_target_pairs={{0,8},{2,10},{4,12},{6,14},{8,16},{10,18},{12,20},{14,22},{16,24},... | collective-permute-start | bytes 2359304 | tf_op jit(solution)/shard_map/ppermute | solution.py:88
  512.8 14.6 %collective-permute-start.78 = (bf16[128,2048]{1,0:T(8,128)(2,1)S(1)}, bf16[128,2048]{1,0:T(8,128)(2,1)S(1)}, u32[]{:S(2)}, u32[]{:S(2)}) collective-permute-start(bf16[128,2048]{1,0:T(8,128)(2,1)S(1)} %copy-done.85), channel_id=1, source_target_pairs={{0,4},{2,6},{4,0},{6,2},{8,12},{10,14},{12,8},{14,10},{16,20},{18,... | collective-permute-start | bytes 1572872 | tf_op jit(solution)/shard_map/ppermute | solution.py:85
  513.9 13.5 %collective-permute-start.80 = (f32[4352]{0:T(1024)S(1)}, f32[4352]{0:T(1024)S(1)}, u32[]{:S(2)}, u32[]{:S(2)}) collective-permute-start(f32[4352]{0:T(1024)S(1)} %add.329), channel_id=1, source_target_pairs={{0,1},{1,0},{2,3},{3,2},{4,5},{5,4},{6,7},{7,6},{8,9},{9,8},{10,11... | collective-permute-start | bytes 52232 | tf_op jit(solution)/shard_map/ppermute | solution.py:179
  (112 other events, 900.8 us)
Sparse Core Ops, SparseCore 0:
  56.4 72.6 all-gather.3
  131.3 62.9 all-gather.5
  196.0 63.3 all-gather.7
  261.6 68.4 reduce-scatter.2
  332.2 128.4 reduce-scatter.4
